TPU v7x, 32 devices: a whole 2x2x4 slice. The times are simulated.
32 devices in a mesh: groups: 2 (over y), tok: 16 (over z, x, core), feat: 1.
Axes of the slice: x: 2, y: 2, z: 4, core: 2. Of those that a mesh axis runs over, the one named last changes fastest.
Arguments:
- activations: bfloat16 [8192, 16384], P(('groups', 'tok'), 'feat'), parts along dimension 0, may hold values from -200 to 200, as said below
- sketch: bfloat16 [1, 16384, 128], P('feat', 'tok'), may hold values from -0.046875 to 0.046875
Outputs:
- basis: float32 [2, 16384, 128], P(('groups', 'feat'), 'tok'), parts along dimension 0
- coords: float32 [8192, 128], P(('groups', 'tok')), parts along dimension 0
- resid_rms: float32 [8192], P(('groups', 'tok')), parts along dimension 0
There are 2 independent parts, one for each index of `groups`. A program takes and returns all parts, laid end to end along the dimension named above; an argument that names none is the same for every part. Nothing has to cross between parts.
Inputs may be any that keep to these rules, and one draw needn't show every extreme that they name: real-valued activations.
All inputs are finite; a program needn't handle non-finite values.
Results may differ from a plain program's by a relative error of at most 0.0027.
Values may be sent and summed in bfloat16 or wider, within the bound.
No kernel may reach another device: no remote copies, remote signals or barrier semaphores. Data moves between devices by JAX's collectives and lax.ppermute only.
A program may use at most 64 MiB of HBM per device.

v0:
```python
import math

import jax
import jax.numpy as jnp
from jax import lax
from jax.sharding import PartitionSpec as P

D = 16384


def shards(activations, sketch):
    columns = activations
    partial_value = jnp.dot(
        columns,
        lax.all_gather(sketch, "tok", axis=1, tiled=True)[0],
        preferred_element_type=jnp.float32,
    )
    sketched = lax.psum(partial_value, "feat").astype(jnp.bfloat16)
    columns = activations
    range_rows = lax.psum_scatter(
        lax.dot_general(
            columns, sketched, (((0,), (0,)), ((), ())), preferred_element_type=jnp.float32
        ),
        "tok",
        scatter_dimension=0,
        tiled=True,
    )
    local_gram = jnp.dot(
        range_rows.T,
        range_rows,
        preferred_element_type=jnp.float32,
        precision=lax.Precision.HIGHEST,
    )
    gram_matrix = lax.psum(local_gram, ("tok", "feat"))
    factor = jnp.linalg.cholesky(gram_matrix)
    own_rows = jax.scipy.linalg.solve_triangular(factor, range_rows.T, lower=True).T
    half_basis = lax.all_gather(own_rows.astype(jnp.bfloat16), "tok", axis=0, tiled=True)
    basis = (own_rows * jnp.float32(math.sqrt(D)))[None]
    coords_part = jnp.dot(activations, half_basis, preferred_element_type=jnp.float32)
    coords = lax.psum(coords_part, "feat")
    coords_b = coords.astype(jnp.bfloat16)
    rebuilt = jnp.dot(coords_b, half_basis.T, preferred_element_type=jnp.float32)
    leftover = activations.astype(jnp.float32) - rebuilt
    energy = lax.psum(jnp.sum(leftover * leftover, axis=1), "feat")
    resid_rms = jnp.sqrt(energy / D + 1e-06)
    return (basis, coords, resid_rms)


def solution(mesh):
    placed = (P(("groups", "tok"), "feat"), P("feat", "tok", None))
    return jax.shard_map(
        shards,
        mesh=mesh,
        in_specs=placed,
        out_specs=(
            P(("groups", "feat"), "tok", None),
            P(("groups", "tok"), None),
            P(("groups", "tok")),
        ),
        check_vma=False,
    )
```

profile of v0, /device:TPU:0, one launch (start us, length us, event | category | flops | bytes accessed | tf_op | source)
XLA Modules:
  0.0 370.7 jit_solution(17255615056119931746)
XLA Ops:
  7.2 0.0 all-gather.3.cloned.1.call-start
  7.2 0.7 all-gather.3.cloned.1.call-update
  7.9 0.0 reduce-scatter.2.cloned.1.call-start
  7.9 55.5 %all-gather.3.cloned.1.call-done = bf16[1,16384,128]{2,1,0:T(8,128)(2,1)} async-done(((bf16[1,1024,128]{2,1,0:T(8,128)(2,1)}), bf16[1,16384,128]{2,1,0:T(8,128)(2,1)}) %all-gather.3.cloned.1.call-update) | async-done | bytes 4194320 | tf_op jit(solution)/shard_map/all_gather | solution.py:15
  63.4 13.9 %convolution_bitcast_fusion = f32[16384,128]{0,1:T(8,128)} fusion(bf16[256,16384]{1,0:T(8,128)(2,1)} %param.2, bf16[1,16384,128]{2,1,0:T(8,128)(2,1)} %all-gather.3.cloned.1.call-done), kind=kOutput, calls=%fused_computation.2 | convolution fusion | flops 2147516416 | bytes 20971520 | tf_op jit(solution)/shard_map/dot_general | solution.py:21
  77.3 0.0 reduce-scatter.2.cloned.1.call-update
  77.4 0.0 all-reduce.2.cloned.1.call-start
  77.4 103.6 %reduce-scatter.2.cloned.1.call-done = f32[1024,128]{0,1:T(8,128)} async-done(((f32[16384,128]{0,1:T(8,128)}), f32[1024,128]{0,1:T(8,128)}) %reduce-scatter.2.cloned.1.call-update) | async-done | bytes 524304 | tf_op jit(solution)/shard_map/reduce_scatter | solution.py:20
  181.0 2.4 fusion.17
  183.4 0.0 all-reduce.2.cloned.1.call-update
  183.4 0.2 all-gather.5.cloned.1.call-start
  183.6 85.5 %all-reduce.2.cloned.1.call-done = f32[128,128]{0,1:T(8,128)} async-done(((f32[128,128]{0,1:T(8,128)}), f32[128,128]{0,1:T(8,128)}) %all-reduce.2.cloned.1.call-update) | async-done | bytes 65552 | tf_op jit(solution)/shard_map/psum | solution.py:34
  269.2 0.9 copy.6
  270.1 0.9 fusion.12
  271.0 11.7 %cholesky.16 = f32[128,128]{1,0:T(8,128)S(1)} custom-call(f32[128,128]{1,0:T(8,128)S(1)} %fusion.12), custom_call_target="Cholesky" | custom-call | tf_op jit(solution)/shard_map/jit(cholesky)/cholesky | solution.py:35
  282.7 0.6 compare_reduce_fusion
  283.4 0.7 fusion.9
  284.0 9.8 %custom-call.7 = f32[1,128,128]{1,2,0:T(8,128)S(1)} custom-call(f32[1,128,128]{2,1,0:T(8,128)S(1)} %fusion.9), custom_call_target="InvertDiagBlocksLowerTriangular" | custom-call | tf_op jit(solution)/shard_map/jit(_solve_triangular)/triangular_solve | solution.py:36
  293.8 2.9 fusion.14
  296.8 0.0 all-gather.5.cloned.1.call-update
  296.8 52.3 %all-gather.5.cloned.1.call-done = bf16[16384,128]{1,0:T(8,128)(2,1)} async-done(((bf16[1024,128]{1,0:T(8,128)(2,1)}), bf16[16384,128]{1,0:T(8,128)(2,1)}) %all-gather.5.cloned.1.call-update) | async-done | bytes 4194320 | tf_op jit(solution)/shard_map/all_gather | solution.py:37
  349.1 7.5 %convolution_bitcast_fusion.1 = f32[256,128]{0,1:T(8,128)S(1)} fusion(bf16[16384,128]{1,0:T(8,128)(2,1)} %all-gather.5.cloned.1.call-done, bf16[256,16384]{1,0:T(8,128)(2,1)} %param.2), kind=kOutput, calls=%fused_computation.6 | convolution fusion | flops 1073741824 | bytes 12713984 | tf_op jit(solution)/shard_map/dot_general | solution.py:39
  356.6 0.8 copy.7
  357.4 6.2 %fusion.3 = f32[256]{0:T(256)S(1)} fusion(bf16[16384,128]{1,0:T(8,128)(2,1)} %all-gather.5.cloned.1.call-done, bf16[256,16384]{1,0:T(8,128)(2,1)} %param.2, f32[256,128]{0,1:T(8,128)S(1)} %convolution_bitcast_fusion.1), kind=kOutput, calls=%fused_computation.5 | convolution fusion | flops 1090551552 | bytes 12715008 | tf_op jit(solution)/shard_map/dot_general | solution.py:42
  363.6 0.6 add_sqrt_fusion
  (1 shorter events, 0.0 us)
Async XLA Ops:
  7.2 56.3 %all-gather.3.cloned.1.call-start = ((), (), s32[]{:S(2)}) async-start(), calls=%async_computation.1 | async-start | bytes 4456448 | tf_op jit(solution)/shard_map/all_gather | solution.py:15
  7.9 173.1 %reduce-scatter.2.cloned.1.call-start = ((), (), s32[]{:S(2)}) async-start(), calls=%async_computation.2 | async-start | bytes 8912896 | tf_op jit(solution)/shard_map/reduce_scatter | solution.py:20
  77.4 191.8 %all-reduce.2.cloned.1.call-start = ((), (), s32[]{:S(2)}) async-start(), calls=%async_computation.3 | async-start | bytes 131072 | tf_op jit(solution)/shard_map/psum | solution.py:34
  183.4 165.7 %all-gather.5.cloned.1.call-start = ((), (), s32[]{:S(2)}) async-start(), calls=%async_computation.4 | async-start | bytes 4456448 | tf_op jit(solution)/shard_map/all_gather | solution.py:37
Sparse Core Ops, SparseCore 0:
  10.2 53.2 all-gather.2
  77.5 103.4 reduce-scatter.1
  185.0 84.1 all-reduce.1
  296.9 52.1 all-gather.4
where the time goes:
time: 371 us
  waiting for transfers between devices  298 us (80%)
  matrix products  32.9 us (9%)
  other arithmetic  24.3 us (7%)
  between operations  13.8 us (4%)
    reduce_scatter x1, waiting for transfers between devices, shards(): lax.psum_scatter(lax.dot_general(columns, sketched, (((0,), (0,)), ((), (...  104 us
    psum x1, waiting for transfers between devices, shards(): gram_matrix = lax.psum(local_gram, ('tok', 'feat'))  85.5 us
    all_gather x1, waiting for transfers between devices, shards(): lax.all_gather(sketch, 'tok', axis=1, tiled=True)[0]  55.5 us
    all_gather x1, waiting for transfers between devices, shards(): lax.all_gather(own_rows.astype(jnp.bfloat16), 'tok', axis=0, tiled=True)  52.3 us
    dot_general x1, matrix products, shards(): lax.dot_general(columns, sketched, (((0,), (0,)), ((), ())), preferred_el...  13.9 us
    another operation x3, other arithmetic, shards(): factor = jnp.linalg.cholesky(gram_matrix)  12.4 us
    another operation x2, other arithmetic, shards(): jax.scipy.linalg.solve_triangular(factor, range_rows.T, lower=True)  10.5 us
    dot_general x1, matrix products, shards(): jnp.dot(activations, half_basis, preferred_element_type=jnp.float32)  7.49 us
  transfers between devices with their start and end apart: 4, of which 4 were waited for; matrix products, arithmetic and copies ran while one was open for 0% of the time, Pallas kernels for 0%

commit v1 on v0

v1 whole, which is shorter than its diff:
```python
import functools
import math

import jax
import jax.numpy as jnp
from jax import lax
from jax.experimental import pallas as pl
from jax.experimental.pallas import tpu as pltpu
from jax.sharding import PartitionSpec as P

F32, BF16 = jnp.float32, jnp.bfloat16
HIGH = lax.Precision.HIGHEST
ARB = pltpu.CompilerParams(dimension_semantics=("arbitrary",), vmem_limit_bytes=48 * 2**20)

X_BIT, ZLO, ZHI = 1, 2, 4
NEAR_A, FAR_A = (0, 4, 2, 6), (1, 5, 3, 7)
NEAR_B, FAR_B = (0, 4, 1, 5), (2, 6, 3, 7)


def swap(value, bit, n):
    return lax.ppermute(value, "tok", [(i, i ^ bit) for i in range(n)])


def encode(value):
    return (value * jnp.abs(value)).astype(BF16)


def decode(coded):
    wide = coded.astype(F32)
    root = jnp.sqrt(jnp.abs(wide))
    return jnp.where(wide < 0, -root, root)


def split_kernel(core_ref, x_ref, other_ref, norm_ref, acc_ref):
    step = pl.program_id(0)
    width = other_ref.shape[1]
    start = pl.multiple_of((1 - core_ref[0]) * width, width)
    other_ref[...] = x_ref[:, pl.ds(start, width)]
    wide = x_ref[...].astype(F32)
    square = wide * wide
    total = square[:, :128]
    for i in range(1, 2 * width // 128):
        total = total + square[:, i * 128 : (i + 1) * 128]

    @pl.when(step == 0)
    def _():
        acc_ref[...] = total

    @pl.when(step > 0)
    def _():
        acc_ref[...] += total

    @pl.when(step == pl.num_programs(0) - 1)
    def _():
        norm_ref[...] = jnp.sum(acc_ref[...], axis=1, keepdims=True)


def split(core, x, width):
    rows, features = x.shape
    return pl.pallas_call(
        split_kernel,
        grid_spec=pltpu.PrefetchScalarGridSpec(
            num_scalar_prefetch=1,
            grid=(features // (2 * width),),
            in_specs=[pl.BlockSpec((rows, 2 * width), lambda i, s: (0, i))],
            out_specs=[
                pl.BlockSpec((rows, width), lambda i, s: (0, i)),
                pl.BlockSpec((rows, 1), lambda i, s: (0, 0)),
            ],
            scratch_shapes=[pltpu.VMEM((rows, 128), F32)],
        ),
        out_shape=[
            jax.ShapeDtypeStruct((rows, features // 2), BF16),
            jax.ShapeDtypeStruct((rows, 1), F32),
        ],
        compiler_params=ARB,
        cost_estimate=pl.CostEstimate(flops=2 * rows * features, bytes_accessed=3 * rows * features, transcendentals=0),
    )(core, x)


def x_specs(rows, half):
    return [
        pl.BlockSpec((rows, half), functools.partial(lambda k, i, s: (0, s[k, i]), k)) for k in range(4)
    ]


def project_kernel(has_init, table_ref, xa, xb, oa, ob, sa, sb, *rest):
    init_ref, out_ref = rest if has_init else (None, rest[0])
    rows = xa.shape[0]
    own = jnp.dot(xa[...], sa[...], preferred_element_type=F32) + jnp.dot(xb[...], sb[...], preferred_element_type=F32)
    other = jnp.dot(oa[...], sa[...], preferred_element_type=F32) + jnp.dot(ob[...], sb[...], preferred_element_type=F32)
    first = pl.program_id(0) == 0

    @pl.when(first)
    def _():
        out_ref[:rows, :] = own + (init_ref[:rows, :] if has_init else 0.0)
        out_ref[rows:, :] = other + (init_ref[rows:, :] if has_init else 0.0)

    @pl.when(jnp.logical_not(first))
    def _():
        out_ref[:rows, :] += own
        out_ref[rows:, :] += other


def project(table, x, other, sa, sb, init=None):
    rows, half, rank = x.shape[0], sa.shape[0] // 4, sa.shape[1]
    rows_spec = pl.BlockSpec((half, rank), lambda i, s: (i, 0))
    whole = pl.BlockSpec((2 * rows, rank), lambda i, s: (0, 0))
    return pl.pallas_call(
        functools.partial(project_kernel, init is not None),
        grid_spec=pltpu.PrefetchScalarGridSpec(
            num_scalar_prefetch=1,
            grid=(4,),
            in_specs=x_specs(rows, half) + [rows_spec, rows_spec] + ([whole] if init is not None else []),
            out_specs=whole,
        ),
        out_shape=jax.ShapeDtypeStruct((2 * rows, rank), F32),
        compiler_params=ARB,
        cost_estimate=pl.CostEstimate(
            flops=2 * 2 * rows * 8 * half * rank, bytes_accessed=2 * 2 * rows * 8 * half, transcendentals=0
        ),
    )(table, x, x, other, other, sa, sb, *([init] if init is not None else []))


def spread_kernel(coded, table_ref, xa, xb, oa, ob, y_ref, za, zb):
    rows = xa.shape[0]
    for own, other, out in ((xa, oa, za), (xb, ob, zb)):
        term = lax.dot_general(
            own[...], y_ref[:rows, :], (((0,), (0,)), ((), ())), preferred_element_type=F32
        ) + lax.dot_general(other[...], y_ref[rows:, :], (((0,), (0,)), ((), ())), preferred_element_type=F32)
        out[...] = encode(term) if coded else term


def spread(table, x, other, y, half, coded):
    rows, rank = x.shape[0], y.shape[1]
    rows_spec = pl.BlockSpec((half, rank), lambda i, s: (i, 0))
    shape = jax.ShapeDtypeStruct((4 * half, rank), BF16 if coded else F32)
    return pl.pallas_call(
        functools.partial(spread_kernel, coded),
        grid_spec=pltpu.PrefetchScalarGridSpec(
            num_scalar_prefetch=1,
            grid=(4,),
            in_specs=x_specs(rows, half) + [pl.BlockSpec((2 * rows, rank), lambda i, s: (0, 0))],
            out_specs=[rows_spec, rows_spec],
        ),
        out_shape=[shape, shape],
        compiler_params=ARB,
        cost_estimate=pl.CostEstimate(
            flops=2 * 2 * rows * 8 * half * rank, bytes_accessed=2 * 2 * rows * 8 * half, transcendentals=0
        ),
    )(table, x, x, other, other, y)


def gather(piece, bits, n):
    held = piece
    for bit in bits[:-1]:
        held = jnp.concatenate([held, swap(held, 2 * bit, n)], axis=0)
    return held, swap(held, 2 * bits[-1], n)


def reduce(kept, sent, bits, n):
    for bit in bits:
        total = kept + decode(swap(sent, 2 * bit, n))
        if bit != bits[-1]:
            size = total.shape[0] // 2
            kept, sent = total[:size], encode(total[size:])
    return total


def shards(n, activations, sketch):
    x, rows = activations, activations.shape[0]
    width, rank = sketch.shape[1], sketch.shape[2]
    half = width // 2
    depth = n * width
    own = sketch[0]
    index = lax.axis_index("tok")
    core = index % 2

    def table(list_a, list_b):
        a = jnp.bitwise_xor(index, 2 * jnp.array(list_a, jnp.int32))
        b = jnp.bitwise_xor(index, 2 * jnp.array(list_b, jnp.int32))
        return jnp.stack([2 * a, 2 * b + 1, a // 2 * 2, b // 2 * 2 + 1]).astype(jnp.int32)

    near, far = table(NEAR_A, NEAR_B), table(FAR_A, FAR_B)

    with jax.named_scope("gather_sketch"):
        near_a, far_a = gather(own[:half], (ZHI, ZLO, X_BIT), n)
        near_b, far_b = gather(own[half:], (ZHI, X_BIT, ZLO), n)
    with jax.named_scope("split_features"):
        outgoing, norm = split(core.reshape(1).astype(jnp.int32), x, width)
        other = swap(outgoing, 1, n)
    with jax.named_scope("sketched"):
        part = project(near, x, other, near_a, near_b)
        part = project(far, x, other, far_a, far_b, part)
        theirs = swap(part, 1, n)
        sketched = (part + jnp.concatenate([theirs[rows:], theirs[:rows]])).astype(BF16)
    with jax.named_scope("range"):
        sent_a, sent_b = spread(far, x, other, sketched, half, True)
        kept_a, kept_b = spread(near, x, other, sketched, half, False)
        range_a = reduce(kept_a, sent_a, (X_BIT, ZLO, ZHI), n)
        range_b = reduce(kept_b, sent_b, (ZLO, X_BIT, ZHI), n)
        range_rows = jnp.concatenate([range_a, range_b], axis=0)
    with jax.named_scope("gather_range"):
        near_a, far_a = gather(range_a.astype(BF16), (ZHI, ZLO, X_BIT), n)
        near_b, far_b = gather(range_b.astype(BF16), (ZHI, X_BIT, ZLO), n)
    with jax.named_scope("gram"):
        gram = jnp.dot(range_rows.T, range_rows, preferred_element_type=F32, precision=HIGH)
        for bit in (1, 2, 4, 8):
            gram = gram + swap(gram, bit, n)
    with jax.named_scope("factor"):
        factor = jnp.linalg.cholesky(gram)
        inverse = jax.scipy.linalg.solve_triangular(factor, jnp.eye(rank, dtype=F32), lower=True)
        basis = jnp.dot(range_rows, inverse.T, precision=HIGH) * F32(math.sqrt(depth))
    with jax.named_scope("coords"):
        part = project(near, x, other, near_a, near_b)
        part = project(far, x, other, far_a, far_b, part)
        raw = part[:rows] + swap(part[rows:], 1, n)
        coords = jnp.dot(raw, inverse.T, precision=HIGH)
    with jax.named_scope("residual"):
        lost = coords - coords.astype(BF16).astype(F32)
        energy = norm[:, 0] + jnp.sum(lost * lost - coords * coords, axis=1)
        resid_rms = jnp.sqrt(jnp.maximum(energy, 0.0) / depth + 1e-06)
    return basis[None], coords, resid_rms


def shards_any(depth, activations, sketch):
    sketch_all = lax.all_gather(sketch, "tok", axis=1, tiled=True)[0]
    sketched = lax.psum(jnp.dot(activations, sketch_all, preferred_element_type=F32), "feat").astype(BF16)
    term = lax.dot_general(activations, sketched, (((0,), (0,)), ((), ())), preferred_element_type=F32)
    range_rows = lax.psum_scatter(term, "tok", scatter_dimension=0, tiled=True)
    gram = jnp.dot(range_rows.T, range_rows, preferred_element_type=F32, precision=HIGH)
    factor = jnp.linalg.cholesky(lax.psum(gram, ("tok", "feat")))
    own_rows = jax.scipy.linalg.solve_triangular(factor, range_rows.T, lower=True).T
    half_basis = lax.all_gather(own_rows.astype(BF16), "tok", axis=0, tiled=True)
    basis = (own_rows * F32(math.sqrt(depth)))[None]
    coords = lax.psum(jnp.dot(activations, half_basis, preferred_element_type=F32), "feat")
    rebuilt = jnp.dot(coords.astype(BF16), half_basis.T, preferred_element_type=F32)
    leftover = activations.astype(F32) - rebuilt
    energy = lax.psum(jnp.sum(leftover * leftover, axis=1), "feat")
    return basis, coords, jnp.sqrt(energy / depth + 1e-06)


def solution(mesh):
    n, feat = mesh.shape["tok"], mesh.shape["feat"]

    def call(activations, sketch):
        depth = activations.shape[1]
        if n == 16 and feat == 1:
            body = functools.partial(shards, n)
        else:
            body = functools.partial(shards_any, depth)
        return jax.shard_map(
            body,
            mesh=mesh,
            in_specs=(P(("groups", "tok"), "feat"), P("feat", "tok", None)),
            out_specs=(
                P(("groups", "feat"), "tok", None),
                P(("groups", "tok"), None),
                P(("groups", "tok")),
            ),
            check_vma=False,
        )(activations, sketch)

    return call
```

time: 371 us -> 159 us (0.43)
  waiting for transfers between devices: 298 us -> 56.2 us
  Pallas kernels: 0 us -> 35.9 us
  starting transfers between devices: 0.34 us -> 33.8 us
  matrix products: 32.9 us -> 2.95 us
  between operations: 13.8 us -> 1.04 us
    all_gather x2 -> x0, waiting for transfers between devices: 108 us -> none  [the longest x1 55.5 us: shards(): lax.all_gather(sketch, 'tok', axis=1, tiled=True)[0]]
    reduce_scatter x1 -> x0, waiting for transfers between devices: 104 us -> none  [shards(): lax.psum_scatter(lax.dot_general(columns, sketched, (((0,), (0,)), ((), (...]
    psum x1 -> x0, waiting for transfers between devices: 85.5 us -> none  [shards(): gram_matrix = lax.psum(local_gram, ('tok', 'feat'))]
    ppermute x0 -> x25, waiting for transfers between devices: none -> 56.2 us  [swap(): return lax.ppermute(value, 'tok', [(i, i ^ bit) for i in range(n)])]
    pallas_call x0 -> x7, Pallas kernels: none -> 35.9 us  [the longest x4 17.6 us: project(): pl.pallas_call(functools.partial(project_kernel, init is not None), grid_...]
    ppermute x0 -> x25, starting transfers between devices: none -> 33.8 us  [swap(): return lax.ppermute(value, 'tok', [(i, i ^ bit) for i in range(n)])]
    dot_general x4 -> x3, matrix products: 30 us -> 2.7 us  [the longest x1 1.38 us: shards(): jnp.dot(range_rows, inverse.T, precision=HIGH) * F32(math.sqrt(depth))]
    another operation x5 -> x9, other arithmetic: 22.9 us -> 22.9 us  [the longest x3 12.4 us: shards(): factor = jnp.linalg.cholesky(gram)]
  transfers between devices with their start and end apart: 4 -> 25, of which waited for: 4 -> 16; matrix products, arithmetic and copies ran while one was open for 0% -> 18% of each run, Pallas kernels for 0% -> 9%
where the time goes in v1:
time: 159 us
  waiting for transfers between devices  56.2 us (35%)
  Pallas kernels  35.9 us (23%)
  starting transfers between devices  33.8 us (21%)
  other arithmetic  25.7 us (16%)
  local copies, waits for them, and re-layouts  3.11 us (2%)
  matrix products  2.95 us (2%)
    ppermute x25, waiting for transfers between devices, swap(): return lax.ppermute(value, 'tok', [(i, i ^ bit) for i in range(n)])  56.2 us
    ppermute x25, starting transfers between devices, swap(): return lax.ppermute(value, 'tok', [(i, i ^ bit) for i in range(n)])  33.8 us
    pallas_call x4, Pallas kernels, project(): pl.pallas_call(functools.partial(project_kernel, init is not None), grid_...  17.6 us
    another operation x3, other arithmetic, shards(): factor = jnp.linalg.cholesky(gram)  12.4 us
    another operation x2, other arithmetic, shards(): jax.scipy.linalg.solve_triangular(factor, jnp.eye(rank, dtype=F32), lower...  10.5 us
    pallas_call x2, Pallas kernels, spread(): pl.pallas_call(functools.partial(spread_kernel, coded), grid_spec=pltpu.P...  9.19 us
    pallas_call x1, Pallas kernels, split(): pl.pallas_call(split_kernel, grid_spec=pltpu.PrefetchScalarGridSpec(num_s...  9.11 us
  transfers between devices with their start and end apart: 25, of which 16 were waited for; matrix products, arithmetic and copies ran while one was open for 18% of the time, Pallas kernels for 9%

profile of v1, /device:TPU:0, one launch (start us, length us, event | category | flops | bytes accessed | tf_op | source)
XLA Modules:
  0.0 158.7 jit_solution(14849504356655587772)
XLA Ops:
  0.7 9.1 %split_features.1 = (bf16[256,8192]{1,0:T(8,128)(2,1)}, f32[256,1]{1,0:T(8,128)S(1)}) custom-call(s32[1]{0:T(128)} %bitcast.4.core_ref, bf16[256,16384]{1,0:T(8,128)(2,1)} %xb.11), custom_call_target="tpu_custom_call" | custom-call | flops 8388608 | bytes 12582912 | tf_op jit(solution)/shard_map/split_features/pallas_call | solution.py:60
  9.8 0.5 collective-permute-start
  10.3 3.7 %collective-permute-start.1 = (bf16[512,128]{1,0:T(8,128)(2,1)S(1)}, bf16[512,128]{1,0:T(8,128)(2,1)S(1)}, u32[]{:S(2)}, u32[]{:S(2)}) collective-permute-start(bf16[512,128]{1,0:T(8,128)(2,1)S(1)} %get-tuple-element.28), channel_id=1, source_target_pairs={{0,8},{1,9},{2,10},{3,11},{4,12},{5,13},{6,14},{7,15},{8,0},{9,1},... | collective-permute-start | bytes 393224 | tf_op jit(solution)/shard_map/gather_sketch/ppermute | solution.py:21
  13.9 0.1 collective-permute-start.4
  14.0 9.9 %collective-permute-done.1 = bf16[512,128]{1,0:T(8,128)(2,1)S(1)} collective-permute-done((bf16[512,128]{1,0:T(8,128)(2,1)S(1)}, bf16[512,128]{1,0:T(8,128)(2,1)S(1)}, u32[]{:S(2)}, u32[]{:S(2)}) %collective-permute-start.1) | collective-permute-done | bytes 131104 | tf_op jit(solution)/shard_map/gather_sketch/ppermute | solution.py:21
  23.9 0.7 collective-permute-start.2
  24.6 2.0 %collective-permute-done.4 = bf16[512,128]{1,0:T(8,128)(2,1)S(1)} collective-permute-done((bf16[512,128]{1,0:T(8,128)(2,1)S(1)}, bf16[512,128]{1,0:T(8,128)(2,1)S(1)}, u32[]{:S(2)}, u32[]{:S(2)}) %collective-permute-start.4) | collective-permute-done | bytes 131104 | tf_op jit(solution)/shard_map/gather_sketch/ppermute | solution.py:21
  26.6 1.6 %collective-permute-start.5 = (bf16[1024,128]{1,0:T(8,128)(2,1)S(1)}, bf16[1024,128]{1,0:T(8,128)(2,1)S(1)}, u32[]{:S(2)}, u32[]{:S(2)}) collective-permute-start(bf16[1024,128]{1,0:T(8,128)(2,1)S(1)} %pad_maximum_fusion.8), channel_id=1, source_target_pairs={{0,2},{1,3},{2,0},{3,1},{4,6},{5,7},{6,4},{7,5},{8,10},{9,11},{10,... | collective-permute-start | bytes 786440 | tf_op jit(solution)/shard_map/gather_sketch/ppermute | solution.py:21
  28.2 4.0 %collective-permute-done.2 = bf16[1024,128]{1,0:T(8,128)(2,1)S(1)} collective-permute-done((bf16[1024,128]{1,0:T(8,128)(2,1)S(1)}, bf16[1024,128]{1,0:T(8,128)(2,1)S(1)}, u32[]{:S(2)}, u32[]{:S(2)}) %collective-permute-start.2) | collective-permute-done | bytes 262176 | tf_op jit(solution)/shard_map/gather_sketch/ppermute | solution.py:21
  32.2 1.6 %collective-permute-start.3 = (bf16[2048,128]{1,0:T(8,128)(2,1)S(1)}, bf16[2048,128]{1,0:T(8,128)(2,1)S(1)}, u32[]{:S(2)}, u32[]{:S(2)}) collective-permute-start(bf16[2048,128]{1,0:T(8,128)(2,1)S(1)} %pad_maximum_fusion.sa), channel_id=1, source_target_pairs={{0,2},{1,3},{2,0},{3,1},{4,6},{5,7},{6,4},{7,5},{8,10},{9,11},{10,... | collective-permute-start | bytes 1572872 | tf_op jit(solution)/shard_map/gather_sketch/ppermute | solution.py:21
  33.8 1.7 %collective-permute-done.5 = bf16[1024,128]{1,0:T(8,128)(2,1)S(1)} collective-permute-done((bf16[1024,128]{1,0:T(8,128)(2,1)S(1)}, bf16[1024,128]{1,0:T(8,128)(2,1)S(1)}, u32[]{:S(2)}, u32[]{:S(2)}) %collective-permute-start.5) | collective-permute-done | bytes 262176 | tf_op jit(solution)/shard_map/gather_sketch/ppermute | solution.py:21
  35.6 1.1 collective-permute-start.6
  36.8 4.6 %sketched.2.rest_0_ = f32[512,128]{1,0:T(8,128)S(1)} custom-call(s32[4,4]{1,0:T(4,128)S(1)} %pad_add_fusion.table_ref, bf16[256,16384]{1,0:T(8,128)(2,1)} %xb.11, bf16[256,16384]{1,0:T(8,128)(2,1)} %xb.11, bf16[256,8192]{1,0:T(8,128)(2,1)S(1)} %collective-permute-done.oa.ob, bf16[256,8192]{1,0:T(8,128)(2,1)S(1)} %collective-permute-done.oa.ob, ...), custom_call_target="tpu_custom_call" | custom-call | flops 536870912 | bytes 4194304 | tf_op jit(solution)/shard_map/sketched/pallas_call | solution.py:109
  41.4 4.6 %collective-permute-done.3.sa = bf16[2048,128]{1,0:T(8,128)(2,1)S(1)} collective-permute-done((bf16[2048,128]{1,0:T(8,128)(2,1)S(1)}, bf16[2048,128]{1,0:T(8,128)(2,1)S(1)}, u32[]{:S(2)}, u32[]{:S(2)}) %collective-permute-start.3) | collective-permute-done | bytes 524320 | tf_op jit(solution)/shard_map/gather_sketch/ppermute | solution.py:21
  46.0 1.7 %collective-permute-done.6.sb = bf16[2048,128]{1,0:T(8,128)(2,1)S(1)} collective-permute-done((bf16[2048,128]{1,0:T(8,128)(2,1)S(1)}, bf16[2048,128]{1,0:T(8,128)(2,1)S(1)}, u32[]{:S(2)}, u32[]{:S(2)}) %collective-permute-start.6) | collective-permute-done | bytes 524320 | tf_op jit(solution)/shard_map/gather_sketch/ppermute | solution.py:21
  47.7 4.2 %sketched.3 = f32[512,128]{1,0:T(8,128)S(1)} custom-call(s32[4,4]{1,0:T(4,128)S(1)} %pad_add_fusion.1.table_ref, bf16[256,16384]{1,0:T(8,128)(2,1)} %xb.11, bf16[256,16384]{1,0:T(8,128)(2,1)} %xb.11, bf16[256,8192]{1,0:T(8,128)(2,1)S(1)} %collective-permute-done.oa.ob, bf16[256,8192]{1,0:T(8,128)(2,1)S(1)} %collective-permute-done.oa.ob, ...), custom_call_target="tpu_custom_call" | custom-call | flops 536870912 | bytes 4194304 | tf_op jit(solution)/shard_map/sketched/pallas_call | solution.py:109
  52.0 0.1 collective-permute-start.7
  52.1 1.5 collective-permute-done.7
  53.6 4.4 %range.3 = (bf16[2048,128]{1,0:T(8,128)(2,1)S(1)}, bf16[2048,128]{1,0:T(8,128)(2,1)S(1)}) custom-call(s32[4,4]{1,0:T(4,128)S(1)} %pad_add_fusion.1.table_ref, bf16[256,16384]{1,0:T(8,128)(2,1)} %xb.11, bf16[256,16384]{1,0:T(8,128)(2,1)} %xb.11, bf16[256,8192]{1,0:T(8,128)(2,1)S(1)} %collective-permute-done.oa.ob, ...), custom_call_target="tpu_custom_call" | custom-call | flops 536870912 | bytes 4194304 | tf_op jit(solution)/shard_map/range/pallas_call | solution.py:138
  58.0 1.1 collective-permute-start.11
  59.1 1.5 collective-permute-start.8
  60.6 4.8 %range.2 = (f32[2048,128]{1,0:T(8,128)S(1)}, f32[2048,128]{1,0:T(8,128)S(1)}) custom-call(s32[4,4]{1,0:T(4,128)S(1)} %pad_add_fusion.table_ref, bf16[256,16384]{1,0:T(8,128)(2,1)} %xb.11, bf16[256,16384]{1,0:T(8,128)(2,1)} %xb.11, bf16[256,8192]{1,0:T(8,128)(2,1)} %copy-done, bf16[256,8192]{1,0:T(8,128)(2,1)} %copy-done, bf16[512,128]{1,0:T(8,128)(2,1)S(1)} %fusion.18.y_ref), custom_call_target="tpu_custom_call" | custom-call | flops 536870912 | bytes 4194304 | tf_op jit(solution)/shard_map/range/pallas_call | solution.py:138
  65.4 6.6 %collective-permute-done.11 = bf16[2048,128]{1,0:T(8,128)(2,1)S(1)} collective-permute-done((bf16[2048,128]{1,0:T(8,128)(2,1)S(1)}, bf16[2048,128]{1,0:T(8,128)(2,1)S(1)}, u32[]{:S(2)}, u32[]{:S(2)}) %collective-permute-start.11) | collective-permute-done | bytes 524320 | tf_op jit(solution)/shard_map/range/ppermute | solution.py:21
  72.0 0.4 fusion.4
  72.6 1.1 collective-permute-start.12
  73.7 0.4 fusion.3
  74.2 1.5 collective-permute-start.9
  75.7 4.4 %collective-permute-done.12 = bf16[1024,128]{1,0:T(8,128)(2,1)S(1)} collective-permute-done((bf16[1024,128]{1,0:T(8,128)(2,1)S(1)}, bf16[1024,128]{1,0:T(8,128)(2,1)S(1)}, u32[]{:S(2)}, u32[]{:S(2)}) %collective-permute-start.12) | collective-permute-done | bytes 262176 | tf_op jit(solution)/shard_map/range/ppermute | solution.py:21
  80.1 0.2 fusion.10
  80.4 2.8 %collective-permute-start.13 = (bf16[512,128]{1,0:T(8,128)(2,1)S(1)}, bf16[512,128]{1,0:T(8,128)(2,1)S(1)}, u32[]{:S(2)}, u32[]{:S(2)}) collective-permute-start(bf16[512,128]{1,0:T(8,128)(2,1)S(1)} %fusion.16), channel_id=1, source_target_pairs={{0,8},{1,9},{2,10},{3,11},{4,12},{5,13},{6,14},{7,15},{8,0},{9,1},... | collective-permute-start | bytes 393224 | tf_op jit(solution)/shard_map/range/ppermute | solution.py:21
  83.2 0.2 fusion.8
  83.5 1.9 %collective-permute-start.10 = (bf16[512,128]{1,0:T(8,128)(2,1)S(1)}, bf16[512,128]{1,0:T(8,128)(2,1)S(1)}, u32[]{:S(2)}, u32[]{:S(2)}) collective-permute-start(bf16[512,128]{1,0:T(8,128)(2,1)S(1)} %fusion.14), channel_id=1, source_target_pairs={{0,8},{1,9},{2,10},{3,11},{4,12},{5,13},{6,14},{7,15},{8,0},{9,1},... | collective-permute-start | bytes 393224 | tf_op jit(solution)/shard_map/range/ppermute | solution.py:21
  85.4 7.1 %collective-permute-done.13 = bf16[512,128]{1,0:T(8,128)(2,1)S(1)} collective-permute-done((bf16[512,128]{1,0:T(8,128)(2,1)S(1)}, bf16[512,128]{1,0:T(8,128)(2,1)S(1)}, u32[]{:S(2)}, u32[]{:S(2)}) %collective-permute-start.13) | collective-permute-done | bytes 131104 | tf_op jit(solution)/shard_map/range/ppermute | solution.py:21
  92.5 0.1 fusion.32
  92.7 2.6 %collective-permute-done.10 = bf16[512,128]{1,0:T(8,128)(2,1)S(1)} collective-permute-done((bf16[512,128]{1,0:T(8,128)(2,1)S(1)}, bf16[512,128]{1,0:T(8,128)(2,1)S(1)}, u32[]{:S(2)}, u32[]{:S(2)}) %collective-permute-start.10) | collective-permute-done | bytes 131104 | tf_op jit(solution)/shard_map/range/ppermute | solution.py:21
  95.3 0.1 fusion.34
  95.4 1.0 fusion.11
  96.5 0.4 collective-permute-start.18
  96.9 0.9 collective-permute-done.14
  97.8 1.2 collective-permute-start.15
  99.0 2.5 %collective-permute-done.21 = bf16[512,128]{1,0:T(8,128)(2,1)S(1)} collective-permute-done((bf16[512,128]{1,0:T(8,128)(2,1)S(1)}, bf16[512,128]{1,0:T(8,128)(2,1)S(1)}, u32[]{:S(2)}, u32[]{:S(2)}) %collective-permute-start.21) | collective-permute-done | bytes 131104 | tf_op jit(solution)/shard_map/gather_range/ppermute | solution.py:21
  101.6 1.8 %collective-permute-start.22 = (bf16[1024,128]{1,0:T(8,128)(2,1)S(1)}, bf16[1024,128]{1,0:T(8,128)(2,1)S(1)}, u32[]{:S(2)}, u32[]{:S(2)}) collective-permute-start(bf16[1024,128]{1,0:T(8,128)(2,1)S(1)} %pad_maximum_fusion.10), channel_id=1, source_target_pairs={{0,2},{1,3},{2,0},{3,1},{4,6},{5,7},{6,4},{7,5},{8,10},{9,11},{10,... | collective-permute-start | bytes 786440 | tf_op jit(solution)/shard_map/gather_range/ppermute | solution.py:21
  103.4 3.3 %collective-permute-start.16 = (f32[128,128]{0,1:T(8,128)S(1)}, f32[128,128]{0,1:T(8,128)S(1)}, u32[]{:S(2)}, u32[]{:S(2)}) collective-permute-start(f32[128,128]{0,1:T(8,128)S(1)} %add.90), channel_id=1, source_target_pairs={{0,4},{1,5},{2,6},{3,7},{4,0},{5,1},{6,2},{7,3},{8,12},{9,13},{10,... | collective-permute-start | bytes 196616 | tf_op jit(solution)/shard_map/gram/ppermute | solution.py:21
  106.7 2.2 %collective-permute-done.16 = f32[128,128]{0,1:T(8,128)S(1)} collective-permute-done((f32[128,128]{0,1:T(8,128)S(1)}, f32[128,128]{0,1:T(8,128)S(1)}, u32[]{:S(2)}, u32[]{:S(2)}) %collective-permute-start.16) | collective-permute-done | bytes 65568 | tf_op jit(solution)/shard_map/gram/ppermute | solution.py:21
  108.9 1.4 collective-permute-start.17
  110.4 2.1 %collective-permute-start.19 = (bf16[1024,128]{1,0:T(8,128)(2,1)S(1)}, bf16[1024,128]{1,0:T(8,128)(2,1)S(1)}, u32[]{:S(2)}, u32[]{:S(2)}) collective-permute-start(bf16[1024,128]{1,0:T(8,128)(2,1)S(1)} %pad_maximum_fusion.9), channel_id=1, source_target_pairs={{0,4},{1,5},{2,6},{3,7},{4,0},{5,1},{6,2},{7,3},{8,12},{9,13},{10,... | collective-permute-start | bytes 786440 | tf_op jit(solution)/shard_map/gather_range/ppermute | solution.py:21
  112.5 0.1 reduce.6
  112.6 1.7 %collective-permute-done.17 = f32[128,128]{0,1:T(8,128)S(1)} collective-permute-done((f32[128,128]{0,1:T(8,128)S(1)}, f32[128,128]{0,1:T(8,128)S(1)}, u32[]{:S(2)}, u32[]{:S(2)}) %collective-permute-start.17) | collective-permute-done | bytes 65568 | tf_op jit(solution)/shard_map/gram/ppermute | solution.py:21
  114.3 0.1 copy.15
  114.4 2.7 %collective-permute-start.23 = (bf16[2048,128]{1,0:T(8,128)(2,1)S(1)}, bf16[2048,128]{1,0:T(8,128)(2,1)S(1)}, u32[]{:S(2)}, u32[]{:S(2)}) collective-permute-start(bf16[2048,128]{1,0:T(8,128)(2,1)S(1)} %pad_maximum_fusion.4.sb), channel_id=1, source_target_pairs={{0,4},{1,5},{2,6},{3,7},{4,0},{5,1},{6,2},{7,3},{8,12},{9,13},{10,... | collective-permute-start | bytes 1572872 | tf_op jit(solution)/shard_map/gather_range/ppermute | solution.py:21
  117.2 2.8 %collective-permute-done.19 = bf16[1024,128]{1,0:T(8,128)(2,1)S(1)} collective-permute-done((bf16[1024,128]{1,0:T(8,128)(2,1)S(1)}, bf16[1024,128]{1,0:T(8,128)(2,1)S(1)}, u32[]{:S(2)}, u32[]{:S(2)}) %collective-permute-start.19) | collective-permute-done | bytes 262176 | tf_op jit(solution)/shard_map/gather_range/ppermute | solution.py:21
  120.0 1.5 collective-permute-start.20
  121.5 11.7 %cholesky.17 = f32[128,128]{1,0:T(8,128)S(1)} custom-call(f32[128,128]{1,0:T(8,128)S(1)} %fusion.23), custom_call_target="Cholesky" | custom-call | tf_op jit(solution)/shard_map/factor/jit(cholesky)/cholesky | solution.py:211
  133.3 0.6 compare_reduce_fusion
  133.9 0.7 fusion.20
  134.6 9.8 %custom-call.7 = f32[1,128,128]{1,2,0:T(8,128)S(1)} custom-call(f32[1,128,128]{2,1,0:T(8,128)S(1)} %fusion.20), custom_call_target="InvertDiagBlocksLowerTriangular" | custom-call | tf_op jit(solution)/shard_map/factor/jit(_solve_triangular)/triangular_solve | solution.py:212
  144.4 2.2 %copy-done.1 = bf16[256,8192]{1,0:T(8,128)(2,1)S(1)} copy-done((bf16[256,8192]{1,0:T(8,128)(2,1)S(1)}, bf16[256,8192]{1,0:T(8,128)(2,1)}, u32[]{:S(2)}) %copy-start.1) | copy-done | bytes 4194328
  146.6 4.5 %coords.2.rest_0_ = f32[512,128]{1,0:T(8,128)S(1)} custom-call(s32[4,4]{1,0:T(4,128)S(1)} %pad_add_fusion.table_ref, bf16[256,16384]{1,0:T(8,128)(2,1)} %xb.11, bf16[256,16384]{1,0:T(8,128)(2,1)} %xb.11, bf16[256,8192]{1,0:T(8,128)(2,1)S(1)} %copy-done.1, bf16[256,8192]{1,0:T(8,128)(2,1)S(1)} %copy-done.1, bf16[2048,128]{1,0:T(8,128)(2,1)S(1)} %pad_maximum_fusion.3.sa, ...), custom_call_target="tpu_custom_call" | custom-call | flops 536870912 | bytes 4194304 | tf_op jit(solution)/shard_map/coords/pallas_call | solution.py:109
  151.1 4.2 %coords.3 = f32[512,128]{1,0:T(8,128)S(1)} custom-call(s32[4,4]{1,0:T(4,128)S(1)} %pad_add_fusion.1.table_ref, bf16[256,16384]{1,0:T(8,128)(2,1)} %xb.11, bf16[256,16384]{1,0:T(8,128)(2,1)} %xb.11, bf16[256,8192]{1,0:T(8,128)(2,1)S(1)} %copy-done.2, bf16[256,8192]{1,0:T(8,128)(2,1)S(1)} %copy-done.2, bf16[2048,128]{1,0:T(8,128)(2,1)S(1)} %collective-permute-done.20.sa, ...), custom_call_target="tpu_custom_call" | custom-call | flops 536870912 | bytes 4194304 | tf_op jit(solution)/shard_map/coords/pallas_call | solution.py:109
  155.4 0.2 fusion.21
  155.7 1.4 fusion
  157.1 0.3 subtract_reduce_fusion
  157.4 0.8 copy.16
  158.1 0.6 add_sqrt_fusion
  (53 shorter events, 0.9 us)
Async XLA Ops:
  0.6 9.6 %copy-start.3 = (bf16[1,1024,128]{2,1,0:T(8,128)(2,1)S(1)}, bf16[1,1024,128]{2,1,0:T(8,128)(2,1)}, u32[]{:S(2)}) copy-start(bf16[1,1024,128]{2,1,0:T(8,128)(2,1)} %param.7) | copy-start | bytes 786436
  0.7 36.0 %copy-start.6 = (s32[4]{0:T(128)S(1)}, s32[4]{0:T(128)}, u32[]{:S(2)}) copy-start(s32[4]{0:T(128)} %constant.118) | copy-start | bytes 52
  0.7 36.0 %copy-start.7 = (s32[4]{0:T(128)S(1)}, s32[4]{0:T(128)}, u32[]{:S(2)}) copy-start(s32[4]{0:T(128)} %constant.119) | copy-start | bytes 52
  0.7 36.0 %copy-start.4 = (s32[4]{0:T(128)S(1)}, s32[4]{0:T(128)}, u32[]{:S(2)}) copy-start(s32[4]{0:T(128)} %constant.120) | copy-start | bytes 52
  0.7 36.0 %copy-start.5 = (s32[4]{0:T(128)S(1)}, s32[4]{0:T(128)}, u32[]{:S(2)}) copy-start(s32[4]{0:T(128)} %constant.121) | copy-start | bytes 52
  9.8 26.9 %collective-permute-start = (bf16[256,8192]{1,0:T(8,128)(2,1)}, bf16[256,8192]{1,0:T(8,128)(2,1)S(1)}, u32[]{:S(2)}, u32[]{:S(2)}) collective-permute-start(bf16[256,8192]{1,0:T(8,128)(2,1)} %get-tuple-element.9), channel_id=1, source_target_pairs={{0,1},{1,0},{2,3},{3,2},{4,5},{5,4},{6,7},{7,6},{8,9},{9,8},{10,11... | collective-permute-start | bytes 12582920 | tf_op jit(solution)/shard_map/split_features/ppermute | solution.py:21
  10.3 13.6 %collective-permute-start.1 = (bf16[512,128]{1,0:T(8,128)(2,1)S(1)}, bf16[512,128]{1,0:T(8,128)(2,1)S(1)}, u32[]{:S(2)}, u32[]{:S(2)}) collective-permute-start(bf16[512,128]{1,0:T(8,128)(2,1)S(1)} %get-tuple-element.28), channel_id=1, source_target_pairs={{0,8},{1,9},{2,10},{3,11},{4,12},{5,13},{6,14},{7,15},{8,0},{9,1},... | collective-permute-start | bytes 393224 | tf_op jit(solution)/shard_map/gather_sketch/ppermute | solution.py:21
  13.9 12.6 %collective-permute-start.4 = (bf16[512,128]{1,0:T(8,128)(2,1)S(1)}, bf16[512,128]{1,0:T(8,128)(2,1)S(1)}, u32[]{:S(2)}, u32[]{:S(2)}) collective-permute-start(bf16[512,128]{1,0:T(8,128)(2,1)S(1)} %get-tuple-element.27), channel_id=1, source_target_pairs={{0,8},{1,9},{2,10},{3,11},{4,12},{5,13},{6,14},{7,15},{8,0},{9,1},... | collective-permute-start | bytes 393224 | tf_op jit(solution)/shard_map/gather_sketch/ppermute | solution.py:21
  23.9 8.2 %collective-permute-start.2 = (bf16[1024,128]{1,0:T(8,128)(2,1)S(1)}, bf16[1024,128]{1,0:T(8,128)(2,1)S(1)}, u32[]{:S(2)}, u32[]{:S(2)}) collective-permute-start(bf16[1024,128]{1,0:T(8,128)(2,1)S(1)} %pad_maximum_fusion.7), channel_id=1, source_target_pairs={{0,4},{1,5},{2,6},{3,7},{4,0},{5,1},{6,2},{7,3},{8,12},{9,13},{10,... | collective-permute-start | bytes 786440 | tf_op jit(solution)/shard_map/gather_sketch/ppermute | solution.py:21
  26.6 9.0 %collective-permute-start.5 = (bf16[1024,128]{1,0:T(8,128)(2,1)S(1)}, bf16[1024,128]{1,0:T(8,128)(2,1)S(1)}, u32[]{:S(2)}, u32[]{:S(2)}) collective-permute-start(bf16[1024,128]{1,0:T(8,128)(2,1)S(1)} %pad_maximum_fusion.8), channel_id=1, source_target_pairs={{0,2},{1,3},{2,0},{3,1},{4,6},{5,7},{6,4},{7,5},{8,10},{9,11},{10,... | collective-permute-start | bytes 786440 | tf_op jit(solution)/shard_map/gather_sketch/ppermute | solution.py:21
  32.2 13.8 %collective-permute-start.3 = (bf16[2048,128]{1,0:T(8,128)(2,1)S(1)}, bf16[2048,128]{1,0:T(8,128)(2,1)S(1)}, u32[]{:S(2)}, u32[]{:S(2)}) collective-permute-start(bf16[2048,128]{1,0:T(8,128)(2,1)S(1)} %pad_maximum_fusion.sa), channel_id=1, source_target_pairs={{0,2},{1,3},{2,0},{3,1},{4,6},{5,7},{6,4},{7,5},{8,10},{9,11},{10,... | collective-permute-start | bytes 1572872 | tf_op jit(solution)/shard_map/gather_sketch/ppermute | solution.py:21
  35.6 12.2 %collective-permute-start.6 = (bf16[2048,128]{1,0:T(8,128)(2,1)S(1)}, bf16[2048,128]{1,0:T(8,128)(2,1)S(1)}, u32[]{:S(2)}, u32[]{:S(2)}) collective-permute-start(bf16[2048,128]{1,0:T(8,128)(2,1)S(1)} %pad_maximum_fusion.1.sb), channel_id=1, source_target_pairs={{0,4},{1,5},{2,6},{3,7},{4,0},{5,1},{6,2},{7,3},{8,12},{9,13},{10,... | collective-permute-start | bytes 1572872 | tf_op jit(solution)/shard_map/gather_sketch/ppermute | solution.py:21
  36.8 16.9 %copy-start = (bf16[256,8192]{1,0:T(8,128)(2,1)}, bf16[256,8192]{1,0:T(8,128)(2,1)S(1)}, u32[]{:S(2)}) copy-start(bf16[256,8192]{1,0:T(8,128)(2,1)S(1)} %collective-permute-done.oa.ob) | copy-start | bytes 12582916
  52.0 1.6 %collective-permute-start.7 = (f32[512,128]{1,0:T(8,128)S(1)}, f32[512,128]{1,0:T(8,128)S(1)}, u32[]{:S(2)}, u32[]{:S(2)}) collective-permute-start(f32[512,128]{1,0:T(8,128)S(1)} %sketched.3), channel_id=1, source_target_pairs={{0,1},{1,0},{2,3},{3,2},{4,5},{5,4},{6,7},{7,6},{8,9},{9,8},{10,11... | collective-permute-start | bytes 786440 | tf_op jit(solution)/shard_map/sketched/ppermute | solution.py:21
  58.0 14.0 %collective-permute-start.11 = (bf16[2048,128]{1,0:T(8,128)(2,1)S(1)}, bf16[2048,128]{1,0:T(8,128)(2,1)S(1)}, u32[]{:S(2)}, u32[]{:S(2)}) collective-permute-start(bf16[2048,128]{1,0:T(8,128)(2,1)S(1)} %get-tuple-element.13), channel_id=1, source_target_pairs={{0,4},{1,5},{2,6},{3,7},{4,0},{5,1},{6,2},{7,3},{8,12},{9,13},{10,... | collective-permute-start | bytes 1572872 | tf_op jit(solution)/shard_map/range/ppermute | solution.py:21
  59.1 14.6 %collective-permute-start.8 = (bf16[2048,128]{1,0:T(8,128)(2,1)S(1)}, bf16[2048,128]{1,0:T(8,128)(2,1)S(1)}, u32[]{:S(2)}, u32[]{:S(2)}) collective-permute-start(bf16[2048,128]{1,0:T(8,128)(2,1)S(1)} %get-tuple-element.11), channel_id=1, source_target_pairs={{0,2},{1,3},{2,0},{3,1},{4,6},{5,7},{6,4},{7,5},{8,10},{9,11},{10,... | collective-permute-start | bytes 1572872 | tf_op jit(solution)/shard_map/range/ppermute | solution.py:21
  72.6 7.6 %collective-permute-start.12 = (bf16[1024,128]{1,0:T(8,128)(2,1)S(1)}, bf16[1024,128]{1,0:T(8,128)(2,1)S(1)}, u32[]{:S(2)}, u32[]{:S(2)}) collective-permute-start(bf16[1024,128]{1,0:T(8,128)(2,1)S(1)} %fusion.9), channel_id=1, source_target_pairs={{0,2},{1,3},{2,0},{3,1},{4,6},{5,7},{6,4},{7,5},{8,10},{9,11},{10,... | collective-permute-start | bytes 786440 | tf_op jit(solution)/shard_map/range/ppermute | solution.py:21
  74.2 9.0 %collective-permute-start.9 = (bf16[1024,128]{1,0:T(8,128)(2,1)S(1)}, bf16[1024,128]{1,0:T(8,128)(2,1)S(1)}, u32[]{:S(2)}, u32[]{:S(2)}) collective-permute-start(bf16[1024,128]{1,0:T(8,128)(2,1)S(1)} %fusion.7), channel_id=1, source_target_pairs={{0,4},{1,5},{2,6},{3,7},{4,0},{5,1},{6,2},{7,3},{8,12},{9,13},{10,... | collective-permute-start | bytes 786440 | tf_op jit(solution)/shard_map/range/ppermute | solution.py:21
  80.4 12.1 %collective-permute-start.13 = (bf16[512,128]{1,0:T(8,128)(2,1)S(1)}, bf16[512,128]{1,0:T(8,128)(2,1)S(1)}, u32[]{:S(2)}, u32[]{:S(2)}) collective-permute-start(bf16[512,128]{1,0:T(8,128)(2,1)S(1)} %fusion.16), channel_id=1, source_target_pairs={{0,8},{1,9},{2,10},{3,11},{4,12},{5,13},{6,14},{7,15},{8,0},{9,1},... | collective-permute-start | bytes 393224 | tf_op jit(solution)/shard_map/range/ppermute | solution.py:21
  83.5 11.8 %collective-permute-start.10 = (bf16[512,128]{1,0:T(8,128)(2,1)S(1)}, bf16[512,128]{1,0:T(8,128)(2,1)S(1)}, u32[]{:S(2)}, u32[]{:S(2)}) collective-permute-start(bf16[512,128]{1,0:T(8,128)(2,1)S(1)} %fusion.14), channel_id=1, source_target_pairs={{0,8},{1,9},{2,10},{3,11},{4,12},{5,13},{6,14},{7,15},{8,0},{9,1},... | collective-permute-start | bytes 393224 | tf_op jit(solution)/shard_map/range/ppermute | solution.py:21
  92.6 8.9 %collective-permute-start.21 = (bf16[512,128]{1,0:T(8,128)(2,1)S(1)}, bf16[512,128]{1,0:T(8,128)(2,1)S(1)}, u32[]{:S(2)}, u32[]{:S(2)}) collective-permute-start(bf16[512,128]{1,0:T(8,128)(2,1)S(1)} %get-tuple-element.21), channel_id=1, source_target_pairs={{0,8},{1,9},{2,10},{3,11},{4,12},{5,13},{6,14},{7,15},{8,0},{9,1},... | collective-permute-start | bytes 393224 | tf_op jit(solution)/shard_map/gather_range/ppermute | solution.py:21
  96.4 1.3 collective-permute-start.14
  96.5 13.9 %collective-permute-start.18 = (bf16[512,128]{1,0:T(8,128)(2,1)S(1)}, bf16[512,128]{1,0:T(8,128)(2,1)S(1)}, u32[]{:S(2)}, u32[]{:S(2)}) collective-permute-start(bf16[512,128]{1,0:T(8,128)(2,1)S(1)} %get-tuple-element.23), channel_id=1, source_target_pairs={{0,8},{1,9},{2,10},{3,11},{4,12},{5,13},{6,14},{7,15},{8,0},{9,1},... | collective-permute-start | bytes 393224 | tf_op jit(solution)/shard_map/gather_range/ppermute | solution.py:21
  97.8 5.6 %collective-permute-start.15 = (f32[128,128]{0,1:T(8,128)S(1)}, f32[128,128]{0,1:T(8,128)S(1)}, u32[]{:S(2)}, u32[]{:S(2)}) collective-permute-start(f32[128,128]{0,1:T(8,128)S(1)} %add.89), channel_id=1, source_target_pairs={{0,2},{1,3},{2,0},{3,1},{4,6},{5,7},{6,4},{7,5},{8,10},{9,11},{10,... | collective-permute-start | bytes 196616 | tf_op jit(solution)/shard_map/gram/ppermute | solution.py:21
  101.6 12.8 %collective-permute-start.22 = (bf16[1024,128]{1,0:T(8,128)(2,1)S(1)}, bf16[1024,128]{1,0:T(8,128)(2,1)S(1)}, u32[]{:S(2)}, u32[]{:S(2)}) collective-permute-start(bf16[1024,128]{1,0:T(8,128)(2,1)S(1)} %pad_maximum_fusion.10), channel_id=1, source_target_pairs={{0,2},{1,3},{2,0},{3,1},{4,6},{5,7},{6,4},{7,5},{8,10},{9,11},{10,... | collective-permute-start | bytes 786440 | tf_op jit(solution)/shard_map/gather_range/ppermute | solution.py:21
  103.4 5.5 %collective-permute-start.16 = (f32[128,128]{0,1:T(8,128)S(1)}, f32[128,128]{0,1:T(8,128)S(1)}, u32[]{:S(2)}, u32[]{:S(2)}) collective-permute-start(f32[128,128]{0,1:T(8,128)S(1)} %add.90), channel_id=1, source_target_pairs={{0,4},{1,5},{2,6},{3,7},{4,0},{5,1},{6,2},{7,3},{8,12},{9,13},{10,... | collective-permute-start | bytes 196616 | tf_op jit(solution)/shard_map/gram/ppermute | solution.py:21
  108.9 5.3 %collective-permute-start.17 = (f32[128,128]{0,1:T(8,128)S(1)}, f32[128,128]{0,1:T(8,128)S(1)}, u32[]{:S(2)}, u32[]{:S(2)}) collective-permute-start(f32[128,128]{0,1:T(8,128)S(1)} %add.91), channel_id=1, source_target_pairs={{0,8},{1,9},{2,10},{3,11},{4,12},{5,13},{6,14},{7,15},{8,0},{9,1},... | collective-permute-start | bytes 196616 | tf_op jit(solution)/shard_map/gram/ppermute | solution.py:21
  110.4 9.5 %collective-permute-start.19 = (bf16[1024,128]{1,0:T(8,128)(2,1)S(1)}, bf16[1024,128]{1,0:T(8,128)(2,1)S(1)}, u32[]{:S(2)}, u32[]{:S(2)}) collective-permute-start(bf16[1024,128]{1,0:T(8,128)(2,1)S(1)} %pad_maximum_fusion.9), channel_id=1, source_target_pairs={{0,4},{1,5},{2,6},{3,7},{4,0},{5,1},{6,2},{7,3},{8,12},{9,13},{10,... | collective-permute-start | bytes 786440 | tf_op jit(solution)/shard_map/gather_range/ppermute | solution.py:21
  114.4 36.6 %collective-permute-start.23 = (bf16[2048,128]{1,0:T(8,128)(2,1)S(1)}, bf16[2048,128]{1,0:T(8,128)(2,1)S(1)}, u32[]{:S(2)}, u32[]{:S(2)}) collective-permute-start(bf16[2048,128]{1,0:T(8,128)(2,1)S(1)} %pad_maximum_fusion.4.sb), channel_id=1, source_target_pairs={{0,4},{1,5},{2,6},{3,7},{4,0},{5,1},{6,2},{7,3},{8,12},{9,13},{10,... | collective-permute-start | bytes 1572872 | tf_op jit(solution)/shard_map/gather_range/ppermute | solution.py:21
  120.0 31.1 %collective-permute-start.20 = (bf16[2048,128]{1,0:T(8,128)(2,1)S(1)}, bf16[2048,128]{1,0:T(8,128)(2,1)S(1)}, u32[]{:S(2)}, u32[]{:S(2)}) collective-permute-start(bf16[2048,128]{1,0:T(8,128)(2,1)S(1)} %pad_maximum_fusion.3.sa), channel_id=1, source_target_pairs={{0,2},{1,3},{2,0},{3,1},{4,6},{5,7},{6,4},{7,5},{8,10},{9,11},{10,... | collective-permute-start | bytes 1572872 | tf_op jit(solution)/shard_map/gather_range/ppermute | solution.py:21
  144.4 2.2 %copy-start.1 = (bf16[256,8192]{1,0:T(8,128)(2,1)S(1)}, bf16[256,8192]{1,0:T(8,128)(2,1)}, u32[]{:S(2)}) copy-start(bf16[256,8192]{1,0:T(8,128)(2,1)} %copy-done) | copy-start | bytes 12582916
  146.6 4.5 %copy-start.2 = (bf16[256,8192]{1,0:T(8,128)(2,1)S(1)}, bf16[256,8192]{1,0:T(8,128)(2,1)}, u32[]{:S(2)}) copy-start(bf16[256,8192]{1,0:T(8,128)(2,1)} %copy-done) | copy-start | bytes 12582916
  155.4 1.7 %collective-permute-start.24 = (f32[256,128]{1,0:T(8,128)S(1)}, f32[256,128]{1,0:T(8,128)S(1)}, u32[]{:S(2)}, u32[]{:S(2)}) collective-permute-start(f32[256,128]{1,0:T(8,128)S(1)} %slice.87), channel_id=1, source_target_pairs={{0,1},{1,0},{2,3},{3,2},{4,5},{5,4},{6,7},{7,6},{8,9},{9,8},{10,11... | collective-permute-start | bytes 393224 | tf_op jit(solution)/shard_map/coords/ppermute | solution.py:21

commit v2 on v0

v2 whole, which is shorter than its diff:
```python
import functools
import math

import jax
import jax.numpy as jnp
from jax import lax
from jax.experimental import pallas as pl
from jax.experimental.pallas import tpu as pltpu
from jax.sharding import PartitionSpec as P

F32, BF16 = jnp.float32, jnp.bfloat16
HIGH = lax.Precision.HIGHEST
VMEM = pl.BlockSpec(memory_space=pltpu.VMEM)
SMEM = pl.BlockSpec(memory_space=pltpu.SMEM)
ANY = pl.BlockSpec(memory_space=pl.ANY)
PARAMS = pltpu.CompilerParams(vmem_limit_bytes=10 * 2**20)

X_BIT, ZLO, ZHI = 1, 2, 4
HLX, HXL, LHX = (ZHI, ZLO, X_BIT), (ZHI, X_BIT, ZLO), (ZLO, ZHI, X_BIT)
PIECES = ((4, HLX), (4, HXL))
LOADS, PARTS = 8, 4


def swap(value, bit, n):
    return lax.ppermute(value, "tok", [(i, i ^ bit) for i in range(n)])


def owners(bits):
    near = [0]
    for bit in bits[:-1]:
        near += [owner ^ bit for owner in near]
    return near, [owner ^ bits[-1] for owner in near]


def encode(value):
    return (value * jnp.abs(value)).astype(BF16)


def decode(coded):
    wide = coded.astype(F32)
    root = jnp.sqrt(jnp.abs(wide))
    return jnp.where(wide < 0, -root, root)


def after(value, *earlier):
    return lax.optimization_barrier((value, *earlier))[0]


def pinned(value):
    return pltpu.with_memory_space_constraint(value, pltpu.VMEM)


def load_kernel(width, core_ref, x_ref, copy_ref, norm_ref, *refs):
    outs, sems = refs[:-1], refs[-1]
    rows, features = x_ref.shape
    chunk = rows // LOADS

    def copy(i):
        part = pl.ds(i * chunk, chunk)
        return pltpu.make_async_copy(x_ref.at[part, :], copy_ref.at[part, :], sems.at[i])

    for i in range(LOADS):
        copy(i).start()
    for i in range(LOADS):
        copy(i).wait()
        out = outs[i * len(outs) // LOADS]
        base = i * chunk % out.shape[0]
        for k in range(features // (2 * width)):
            start = pl.multiple_of((2 * k + 1 - core_ref[0]) * width, width)
            out[base : base + chunk, k * width : (k + 1) * width] = copy_ref[
                i * chunk : (i + 1) * chunk, pl.ds(start, width)
            ]
        total = jnp.zeros((chunk, 128), F32)
        for k in range(0, features, 128):
            wide = copy_ref[i * chunk : (i + 1) * chunk, k : k + 128].astype(F32)
            total = total + wide * wide
        norm_ref[i * chunk : (i + 1) * chunk, :] = total


def load(core, x, width):
    rows, features = x.shape
    part = (rows // PARTS, features // 2)
    return pl.pallas_call(
        functools.partial(load_kernel, width),
        in_specs=[SMEM, ANY],
        out_specs=[VMEM] * (2 + PARTS),
        out_shape=[pltpu.VMEM(x.shape, BF16), pltpu.VMEM((rows, 128), F32)] + [pltpu.VMEM(part, BF16)] * PARTS,
        scratch_shapes=[pltpu.SemaphoreType.DMA((LOADS,))],
        compiler_params=PARAMS,
        cost_estimate=pl.CostEstimate(flops=2 * rows * features, bytes_accessed=4 * rows * features, transcendentals=0),
    )(core, pltpu.with_memory_space_constraint(x, pltpu.HBM))


def tokens(x_ref, other_refs, table_ref, row, step, j, size):
    mine = x_ref[:, pl.ds(pl.multiple_of(table_ref[row, j] * 128, 128), size)]
    start = pl.multiple_of(table_ref[row + step, j] * 128, 128)
    return jnp.concatenate([mine] + [ref[:, pl.ds(start, size)] for ref in other_refs], axis=0)


def project_kernel(n_pieces, has_init, table_ref, x_ref, *refs):
    others, refs, out_ref = refs[:PARTS], refs[PARTS:-1], refs[-1]
    pieces = refs[:n_pieces]
    total = refs[n_pieces][...] if has_init else None
    for j in range(4):
        sizes = [piece.shape[0] // 4 for piece in pieces]
        block = jnp.concatenate([ref[j * size : (j + 1) * size, :] for ref, size in zip(pieces, sizes)], axis=0)
        left = jnp.concatenate(
            [tokens(x_ref, others, table_ref, p, n_pieces, j, size) for p, size in enumerate(sizes)], axis=1
        )
        term = jnp.dot(left, block, preferred_element_type=F32)
        total = term if total is None else total + term
    out_ref[...] = total


def project(table, x, others, pieces, init=None):
    rows, rank = x.shape[0], pieces[0].shape[1]
    depth = sum(piece.shape[0] for piece in pieces)
    extra = [] if init is None else [init]
    return pl.pallas_call(
        functools.partial(project_kernel, len(pieces), init is not None),
        in_specs=[SMEM] + [VMEM] * (1 + PARTS + len(pieces) + len(extra)),
        out_specs=VMEM,
        out_shape=jax.ShapeDtypeStruct((2 * rows, rank), F32),
        compiler_params=PARAMS,
        cost_estimate=pl.CostEstimate(
            flops=4 * rows * depth * rank, bytes_accessed=4 * rows * depth, transcendentals=0
        ),
    )(table, pinned(x), *map(pinned, others), *pieces, *extra)


def spread_kernel(coded, n_pieces, table_ref, x_ref, *refs):
    others, y_ref, outs = refs[:PARTS], refs[PARTS], refs[PARTS + 1 :]
    turned = y_ref[...].astype(F32).T.astype(BF16)
    for p, out in enumerate(outs):
        size = out.shape[0] // 4
        for j in range(4):
            term = jnp.dot(
                turned, tokens(x_ref, others, table_ref, p, n_pieces, j, size), preferred_element_type=F32
            ).T
            out[j * size : (j + 1) * size, :] = encode(term) if coded else term


def spread(table, x, others, y, sizes, coded):
    rows, rank = x.shape[0], y.shape[1]
    return pl.pallas_call(
        functools.partial(spread_kernel, coded, len(sizes)),
        in_specs=[SMEM] + [VMEM] * (2 + PARTS),
        out_specs=[VMEM] * len(sizes),
        out_shape=[jax.ShapeDtypeStruct((4 * size, rank), BF16 if coded else F32) for size in sizes],
        compiler_params=PARAMS,
        cost_estimate=pl.CostEstimate(
            flops=16 * rows * sum(sizes) * rank, bytes_accessed=16 * rows * sum(sizes), transcendentals=0
        ),
    )(table, pinned(x), *map(pinned, others), y)


def factor_kernel(scale, gram_ref, range_ref, out_ref, basis_ref):
    n, b = gram_ref.shape[0], 8
    lane = lax.broadcasted_iota(jnp.int32, (b, n), 1)
    sub = lax.broadcasted_iota(jnp.int32, (b, n), 0)

    def full(value):
        return jnp.broadcast_to(value, (b, n))

    tiles = [gram_ref[b * i : b * i + b, :] for i in range(n // b)]
    for t in range(n // b):
        k = b * t
        group = (lane >= k) & (lane < k + b)
        cols = [full(tiles[t][:, k + c : k + c + 1]) for c in range(b)]
        entry = {(r, c): full(cols[c][r : r + 1, :]) for r in range(b) for c in range(r + 1)}
        rows = [jnp.where(lane == k + r, 1.0, jnp.where(group, 0.0, full(tiles[t][r : r + 1, :]))) for r in range(b)]
        invs, low = [], {}
        for c in range(b):
            invs.append(1.0 / entry[c, c])
            for r in range(c + 1, b):
                low[r, c] = entry[r, c] * invs[c]
            for r in range(c + 1, b):
                for s in range(c + 1, r + 1):
                    entry[r, s] = entry[r, s] - low[r, c] * entry[s, c]
            for r in range(c + 1, b):
                rows[r] = rows[r] - low[r, c] * rows[c]
        solved = [row * inv for row, inv in zip(rows, invs)]
        for c in range(b - 1, 0, -1):
            for r in range(c):
                solved[r] = solved[r] - low[c, r] * solved[c]
        for i in range(t + 1, n // b):
            new = jnp.where(group, 0.0, tiles[i])
            for c in range(b):
                new = new - full(tiles[i][:, k + c : k + c + 1]) * solved[c]
            tiles[i] = new
        done, pivots = rows[0], entry[0, 0]
        for r in range(1, b):
            done = jnp.where(sub == r, rows[r], done)
            pivots = jnp.where(sub == r, entry[r, r], pivots)
        out_ref[k : k + b, :] = jnp.where(lane <= k + sub, done, 0.0) * lax.rsqrt(pivots)
    basis_ref[...] = scale * lax.dot_general(
        range_ref[...], out_ref[...], (((1,), (1,)), ((), ())), precision=HIGH, preferred_element_type=F32
    )


def factored(scale, gram, range_rows):
    return pl.pallas_call(
        functools.partial(factor_kernel, scale),
        in_specs=[VMEM] * 2,
        out_specs=[VMEM] * 2,
        out_shape=[jax.ShapeDtypeStruct(gram.shape, F32), jax.ShapeDtypeStruct(range_rows.shape, F32)],
        compiler_params=PARAMS,
        cost_estimate=pl.CostEstimate(flops=10**7, bytes_accessed=2 * 10**7, transcendentals=0),
    )(gram, range_rows)


def close_kernel(depth, part_ref, theirs_ref, inverse_ref, norm_ref, coords_ref, resid_ref):
    raw = part_ref[: theirs_ref.shape[0], :] + theirs_ref[...]
    coords = lax.dot_general(raw, inverse_ref[...], (((1,), (1,)), ((), ())), precision=HIGH)
    coords_ref[...] = coords
    lost = coords - coords.astype(BF16).astype(F32)
    terms = norm_ref[...] + (lost * lost - coords * coords)
    energy = jnp.sum(terms.T, axis=0, keepdims=True)
    resid_ref[...] = jnp.sqrt(jnp.maximum(energy, 0.0) / depth + 1e-06)


def close(depth, part, theirs, inverse, norm):
    rows, rank = theirs.shape
    return pl.pallas_call(
        functools.partial(close_kernel, depth),
        in_specs=[VMEM] * 4,
        out_specs=[VMEM] * 2,
        out_shape=[jax.ShapeDtypeStruct((rows, rank), F32), jax.ShapeDtypeStruct((1, rows), F32)],
        compiler_params=PARAMS,
        cost_estimate=pl.CostEstimate(flops=2 * rows * rank * rank, bytes_accessed=16 * rows * rank, transcendentals=0),
    )(part, theirs, inverse, norm)


def shards(n, activations, sketch):
    x, rows = activations, activations.shape[0]
    width = sketch.shape[1]
    depth = n * width
    index = lax.axis_index("tok")
    core = index % 2
    orders = [order for _, order in PIECES]
    sizes = [width * share // 8 for share, _ in PIECES]
    starts = [sum(sizes[:p]) for p in range(len(sizes))]
    every = range(len(PIECES))

    def table(which):
        mine, theirs = [], []
        for order, start in zip(orders, starts):
            owner = jnp.bitwise_xor(index, 2 * jnp.array(owners(order)[which], jnp.int32))
            mine.append((width * owner + start) // 128)
            theirs.append((width * (owner // 2) + start) // 128)
        return jnp.stack(mine + theirs).astype(jnp.int32)

    near, far = table(0), table(1)

    with jax.named_scope("gather_sketch"):
        held = [sketch[0, start : start + size] for start, size in zip(starts, sizes)]
        came = [swap(held[p], 2 * orders[p][0], n) for p in every]
    with jax.named_scope("split_features"):
        x, norm, *others = load(core.reshape(1).astype(jnp.int32), x, width)
        others = lax.optimization_barrier((*others, *came))[:PARTS]
        others = [swap(part, 1, n) for part in others]
    with jax.named_scope("gather_sketch"):
        held = [jnp.concatenate([held[p], came[p]]) for p in every]
        held = [jnp.concatenate([held[p], swap(held[p], 2 * orders[p][1], n)]) for p in every]
        came = [swap(held[p], 2 * orders[p][2], n) for p in every]
    with jax.named_scope("sketched"):
        part = project(near, x, others, held)
        part = project(far, x, others, came, part)
        theirs = swap(part, 1, n)
        sketched = (part + jnp.concatenate([theirs[rows:], theirs[:rows]])).astype(BF16)
    with jax.named_scope("range"):
        sent = spread(far, x, others, sketched, sizes, True)
        kept = spread(near, x, others, sketched, sizes, False)
        sums = []
        for p in every:
            mine, coded = kept[p], sent[p]
            for bit in orders[p][::-1]:
                total = mine + decode(swap(coded, 2 * bit, n))
                cut = total.shape[0] // 2
                mine, coded = total[:cut], encode(total[cut:])
            sums.append(total)
        range_rows = jnp.concatenate(sums, axis=0)
    with jax.named_scope("gram"):
        gram = jnp.dot(range_rows.T, range_rows, preferred_element_type=F32, precision=HIGH)
        grams = [gram]
        for bit in (1, 2, 4, 8):
            gram = gram + swap(gram, bit, n)
            grams.append(gram)
    with jax.named_scope("gather_range"):
        held = [total.astype(BF16) for total in sums]
        held = [jnp.concatenate([held[p], swap(held[p], 2 * orders[p][0], n)]) for p in every]
        held[0] = after(held[0], grams[2])
        held[-1] = after(held[-1], grams[3])
        held = [jnp.concatenate([held[p], swap(held[p], 2 * orders[p][1], n)]) for p in every]
        held[-1] = after(held[-1], grams[4])
        came = [swap(held[p], 2 * orders[p][2], n) for p in every]
    with jax.named_scope("factor"):
        inverse, basis = factored(math.sqrt(depth), gram, range_rows)
    with jax.named_scope("coords"):
        part = project(near, x, others, held)
        part = project(far, x, others, came, after(part, inverse))
        coords, resid_rms = close(depth, part, swap(part[rows:], 1, n), inverse, norm)
    return basis[None], coords, resid_rms.reshape(rows)


def shards_any(depth, activations, sketch):
    sketch_all = lax.all_gather(sketch, "tok", axis=1, tiled=True)[0]
    sketched = lax.psum(jnp.dot(activations, sketch_all, preferred_element_type=F32), "feat").astype(BF16)
    term = lax.dot_general(activations, sketched, (((0,), (0,)), ((), ())), preferred_element_type=F32)
    range_rows = lax.psum_scatter(term, "tok", scatter_dimension=0, tiled=True)
    gram = jnp.dot(range_rows.T, range_rows, preferred_element_type=F32, precision=HIGH)
    factor = jnp.linalg.cholesky(lax.psum(gram, ("tok", "feat")))
    own_rows = jax.scipy.linalg.solve_triangular(factor, range_rows.T, lower=True).T
    half_basis = lax.all_gather(own_rows.astype(BF16), "tok", axis=0, tiled=True)
    basis = (own_rows * F32(math.sqrt(depth)))[None]
    coords = lax.psum(jnp.dot(activations, half_basis, preferred_element_type=F32), "feat")
    rebuilt = jnp.dot(coords.astype(BF16), half_basis.T, preferred_element_type=F32)
    leftover = activations.astype(F32) - rebuilt
    energy = lax.psum(jnp.sum(leftover * leftover, axis=1), "feat")
    return basis, coords, jnp.sqrt(energy / depth + 1e-06)


def solution(mesh):
    n, feat = mesh.shape["tok"], mesh.shape["feat"]

    def call(activations, sketch):
        depth = activations.shape[1]
        if n == 16 and feat == 1:
            body = functools.partial(shards, n)
        else:
            body = functools.partial(shards_any, depth)
        return jax.shard_map(
            body,
            mesh=mesh,
            in_specs=(P(("groups", "tok"), "feat"), P("feat", "tok", None)),
            out_specs=(
                P(("groups", "feat"), "tok", None),
                P(("groups", "tok"), None),
                P(("groups", "tok")),
            ),
            check_vma=False,
        )(activations, sketch)

    return call
```

time: 371 us -> 125 us (0.34)
  waiting for transfers between devices: 298 us -> 73.5 us
  matrix products: 32.9 us -> 1.02 us
  starting transfers between devices: 0.34 us -> 24.4 us
  other arithmetic: 24.3 us -> 2.14 us
  Pallas kernels: 0 us -> 21.5 us
  between operations: 13.8 us -> 0.99 us
    all_gather x2 -> x0, waiting for transfers between devices: 108 us -> none  [the longest x1 55.5 us: shards(): lax.all_gather(sketch, 'tok', axis=1, tiled=True)[0]]
    reduce_scatter x1 -> x0, waiting for transfers between devices: 104 us -> none  [shards(): lax.psum_scatter(lax.dot_general(columns, sketched, (((0,), (0,)), ((), (...]
    psum x1 -> x0, waiting for transfers between devices: 85.5 us -> none  [shards(): gram_matrix = lax.psum(local_gram, ('tok', 'feat'))]
    ppermute x0 -> x28, waiting for transfers between devices: none -> 73.5 us  [swap(): return lax.ppermute(value, 'tok', [(i, i ^ bit) for i in range(n)])]
    dot_general x4 -> x1, matrix products: 30 us -> 1.02 us  [shards(): jnp.dot(range_rows.T, range_rows, preferred_element_type=F32, precision=H...]
    ppermute x0 -> x28, starting transfers between devices: none -> 24.4 us  [swap(): return lax.ppermute(value, 'tok', [(i, i ^ bit) for i in range(n)])]
    another operation x5 -> x4, other arithmetic: 22.9 us -> 0.06 us  [table(): return jnp.stack(mine + theirs).astype(jnp.int32)]
    pallas_call x0 -> x9, Pallas kernels: none -> 21.5 us  [the longest x4 7.25 us: project(): pl.pallas_call(functools.partial(project_kernel, len(pieces), init is not...]
  transfers between devices with their start and end apart: 4 -> 28, of which waited for: 4 -> 20; matrix products, arithmetic and copies ran while one was open for 0% -> 2% of each run, Pallas kernels for 0% -> 12%
where the time goes in v2:
time: 125 us
  waiting for transfers between devices  73.5 us (59%)
  starting transfers between devices  24.4 us (20%)
  Pallas kernels  21.5 us (17%)
  other arithmetic  2.14 us (2%)
    ppermute x28, waiting for transfers between devices, swap(): return lax.ppermute(value, 'tok', [(i, i ^ bit) for i in range(n)])  73.5 us
    ppermute x28, starting transfers between devices, swap(): return lax.ppermute(value, 'tok', [(i, i ^ bit) for i in range(n)])  24.4 us
    pallas_call x4, Pallas kernels, project(): pl.pallas_call(functools.partial(project_kernel, len(pieces), init is not...  7.25 us
    pallas_call x1, Pallas kernels, factored(): pl.pallas_call(functools.partial(factor_kernel, scale), in_specs=[VMEM] *...  6.58 us
    pallas_call x1, Pallas kernels, load(): pl.pallas_call(functools.partial(load_kernel, width), in_specs=[SMEM, ANY...  3.78 us
    pallas_call x2, Pallas kernels, spread(): pl.pallas_call(functools.partial(spread_kernel, coded, len(sizes)), in_sp...  2.94 us
  transfers between devices with their start and end apart: 28, of which 20 were waited for; matrix products, arithmetic and copies ran while one was open for 2% of the time, Pallas kernels for 12%

profile of v2, /device:TPU:0, one launch (start us, length us, event | category | flops | bytes accessed | tf_op | source)
XLA Modules:
  0.0 124.6 jit_solution(2780258721545210065)
XLA Ops:
  0.7 1.0 slice_bitcast_fusion
  1.7 4.1 %collective-permute-start.1 = (bf16[512,128]{1,0:T(8,128)(2,1)S(1)}, bf16[512,128]{1,0:T(8,128)(2,1)S(1)}, u32[]{:S(2)}, u32[]{:S(2)}) collective-permute-start(bf16[512,128]{1,0:T(8,128)(2,1)S(1)} %get-tuple-element.53), channel_id=1, source_target_pairs={{0,8},{1,9},{2,10},{3,11},{4,12},{5,13},{6,14},{7,15},{8,0},{9,1},... | collective-permute-start | bytes 393224 | tf_op jit(solution)/shard_map/gather_sketch/ppermute | solution.py:25
  5.8 0.1 collective-permute-start
  5.9 3.8 %split_features.1 = (bf16[256,16384]{1,0:T(8,128)(2,1)S(1)}, f32[256,128]{1,0:T(8,128)S(1)}, bf16[64,8192]{1,0:T(8,128)(2,1)S(1)}, bf16[64,8192]{1,0:T(8,128)(2,...) custom-call(s32[1]{0:T(128)} %bitcast.4.core_ref, bf16[256,16384]{1,0:T(8,128)(2,1)} %x_ref.1), custom_call_target="tpu_custom_call" | custom-call | flops 8388608 | bytes 16777216 | tf_op jit(solution)/shard_map/split_features/pallas_call | solution.py:83
  9.7 6.1 %collective-permute-done.1 = bf16[512,128]{1,0:T(8,128)(2,1)S(1)} collective-permute-done((bf16[512,128]{1,0:T(8,128)(2,1)S(1)}, bf16[512,128]{1,0:T(8,128)(2,1)S(1)}, u32[]{:S(2)}, u32[]{:S(2)}) %collective-permute-start.1) | collective-permute-done | bytes 131104 | tf_op jit(solution)/shard_map/gather_sketch/ppermute | solution.py:25
  15.7 2.0 %collective-permute-done = bf16[512,128]{1,0:T(8,128)(2,1)S(1)} collective-permute-done((bf16[512,128]{1,0:T(8,128)(2,1)S(1)}, bf16[512,128]{1,0:T(8,128)(2,1)S(1)}, u32[]{:S(2)}, u32[]{:S(2)}) %collective-permute-start) | collective-permute-done | bytes 131104 | tf_op jit(solution)/shard_map/gather_sketch/ppermute | solution.py:25
  17.7 0.8 collective-permute-start.6
  18.6 1.6 %collective-permute-start.8 = (bf16[1024,128]{1,0:T(8,128)(2,1)S(1)}, bf16[1024,128]{1,0:T(8,128)(2,1)S(1)}, u32[]{:S(2)}, u32[]{:S(2)}) collective-permute-start(bf16[1024,128]{1,0:T(8,128)(2,1)S(1)} %pad_maximum_fusion.5), channel_id=1, source_target_pairs={{0,2},{1,3},{2,0},{3,1},{4,6},{5,7},{6,4},{7,5},{8,10},{9,11},{10,... | collective-permute-start | bytes 786440 | tf_op jit(solution)/shard_map/gather_sketch/ppermute | solution.py:25
  20.1 0.5 collective-permute-start.4
  20.6 5.9 %collective-permute-done.6 = bf16[1024,128]{1,0:T(8,128)(2,1)S(1)} collective-permute-done((bf16[1024,128]{1,0:T(8,128)(2,1)S(1)}, bf16[1024,128]{1,0:T(8,128)(2,1)S(1)}, u32[]{:S(2)}, u32[]{:S(2)}) %collective-permute-start.6) | collective-permute-done | bytes 262176 | tf_op jit(solution)/shard_map/gather_sketch/ppermute | solution.py:25
  26.6 0.5 collective-permute-done.8
  27.0 1.5 %collective-permute-start.7 = (bf16[2048,128]{1,0:T(8,128)(2,1)S(1)}, bf16[2048,128]{1,0:T(8,128)(2,1)S(1)}, u32[]{:S(2)}, u32[]{:S(2)}) collective-permute-start(bf16[2048,128]{1,0:T(8,128)(2,1)S(1)} %pad_maximum_fusion.refs_4_), channel_id=1, source_target_pairs={{0,2},{1,3},{2,0},{3,1},{4,6},{5,7},{6,4},{7,5},{8,10},{9,11},{10,... | collective-permute-start | bytes 1572872 | tf_op jit(solution)/shard_map/gather_sketch/ppermute | solution.py:25
  28.6 1.4 %collective-permute-start.9 = (bf16[2048,128]{1,0:T(8,128)(2,1)S(1)}, bf16[2048,128]{1,0:T(8,128)(2,1)S(1)}, u32[]{:S(2)}, u32[]{:S(2)}) collective-permute-start(bf16[2048,128]{1,0:T(8,128)(2,1)S(1)} %pad_maximum_fusion.1.refs_5_), channel_id=1, source_target_pairs={{0,4},{1,5},{2,6},{3,7},{4,0},{5,1},{6,2},{7,3},{8,12},{9,13},{10,... | collective-permute-start | bytes 1572872 | tf_op jit(solution)/shard_map/gather_sketch/ppermute | solution.py:25
  30.2 1.8 %sketched.2.refs_6_ = f32[512,128]{1,0:T(8,128)S(1)} custom-call(s32[4,4]{1,0:T(4,128)S(1)} %pad_add_fusion.table_ref, bf16[256,16384]{1,0:T(8,128)(2,1)S(1)} %get-tuple-element.25.x_ref, bf16[64,8192]{1,0:T(8,128)(2,1)S(1)} %collective-permute-done.2.refs_0_, bf16[64,8192]{1,0:T(8,128)(2,1)S(1)} %collective-permute-done.3.refs_1_, ...), custom_call_target="tpu_custom_call" | custom-call | flops 536870912 | bytes 4194304 | tf_op jit(solution)/shard_map/sketched/pallas_call | solution.py:119
  32.0 9.0 %collective-permute-done.7.refs_4_ = bf16[2048,128]{1,0:T(8,128)(2,1)S(1)} collective-permute-done((bf16[2048,128]{1,0:T(8,128)(2,1)S(1)}, bf16[2048,128]{1,0:T(8,128)(2,1)S(1)}, u32[]{:S(2)}, u32[]{:S(2)}) %collective-permute-start.7) | collective-permute-done | bytes 524320 | tf_op jit(solution)/shard_map/gather_sketch/ppermute | solution.py:25
  41.0 1.4 %collective-permute-done.9.refs_5_ = bf16[2048,128]{1,0:T(8,128)(2,1)S(1)} collective-permute-done((bf16[2048,128]{1,0:T(8,128)(2,1)S(1)}, bf16[2048,128]{1,0:T(8,128)(2,1)S(1)}, u32[]{:S(2)}, u32[]{:S(2)}) %collective-permute-start.9) | collective-permute-done | bytes 524320 | tf_op jit(solution)/shard_map/gather_sketch/ppermute | solution.py:25
  42.3 1.8 %sketched.3 = f32[512,128]{1,0:T(8,128)S(1)} custom-call(s32[4,4]{1,0:T(4,128)S(1)} %pad_add_fusion.1.table_ref, bf16[256,16384]{1,0:T(8,128)(2,1)S(1)} %get-tuple-element.25.x_ref, bf16[64,8192]{1,0:T(8,128)(2,1)S(1)} %collective-permute-done.2.refs_0_, bf16[64,8192]{1,0:T(8,128)(2,1)S(1)} %collective-permute-done.3.refs_1_, ...), custom_call_target="tpu_custom_call" | custom-call | flops 536870912 | bytes 4194304 | tf_op jit(solution)/shard_map/sketched/pallas_call | solution.py:119
  44.2 0.1 collective-permute-start.10
  44.2 1.5 %collective-permute-done.10 = f32[512,128]{1,0:T(8,128)S(1)} collective-permute-done((f32[512,128]{1,0:T(8,128)S(1)}, f32[512,128]{1,0:T(8,128)S(1)}, u32[]{:S(2)}, u32[]{:S(2)}) %collective-permute-start.10) | collective-permute-done | bytes 262176 | tf_op jit(solution)/shard_map/sketched/ppermute | solution.py:25
  45.8 1.5 %range.3 = (bf16[2048,128]{1,0:T(8,128)(2,1)S(1)}, bf16[2048,128]{1,0:T(8,128)(2,1)S(1)}) custom-call(s32[4,4]{1,0:T(4,128)S(1)} %pad_add_fusion.1.table_ref, bf16[256,16384]{1,0:T(8,128)(2,1)S(1)} %get-tuple-element.25.x_ref, bf16[64,8192]{1,0:T(8,128)(2,1)S(1)} %collective-permute-done.2.refs_0_, bf16[64,8192]{1,0:T(8,128)(2,1)S(1)} %collective-permute-done.3.refs_1_, ...), custom_call_target="tpu_custom_call" | custom-call | flops 536870912 | bytes 4194304 | tf_op jit(solution)/shard_map/range/pallas_call | solution.py:145
  47.3 0.6 collective-permute-start.11
  47.9 0.7 collective-permute-start.14
  48.6 1.5 %range.2 = (f32[2048,128]{1,0:T(8,128)S(1)}, f32[2048,128]{1,0:T(8,128)S(1)}) custom-call(s32[4,4]{1,0:T(4,128)S(1)} %pad_add_fusion.table_ref, bf16[256,16384]{1,0:T(8,128)(2,1)S(1)} %get-tuple-element.25.x_ref, bf16[64,8192]{1,0:T(8,128)(2,1)S(1)} %collective-permute-done.2.refs_0_, bf16[64,8192]{1,0:T(8,128)(2,1)S(1)} %collective-permute-done.3.refs_1_, ...), custom_call_target="tpu_custom_call" | custom-call | flops 536870912 | bytes 4194304 | tf_op jit(solution)/shard_map/range/pallas_call | solution.py:145
  50.1 11.3 %collective-permute-done.11 = bf16[2048,128]{1,0:T(8,128)(2,1)S(1)} collective-permute-done((bf16[2048,128]{1,0:T(8,128)(2,1)S(1)}, bf16[2048,128]{1,0:T(8,128)(2,1)S(1)}, u32[]{:S(2)}, u32[]{:S(2)}) %collective-permute-start.11) | collective-permute-done | bytes 524320 | tf_op jit(solution)/shard_map/range/ppermute | solution.py:25
  61.3 0.4 fusion.2
  61.8 0.1 fusion.6
  61.9 0.7 collective-permute-start.12
  62.6 0.4 fusion.3
  63.1 0.1 fusion.8
  63.1 0.6 collective-permute-start.15
  63.7 5.7 %collective-permute-done.12 = bf16[1024,128]{1,0:T(8,128)(2,1)S(1)} collective-permute-done((bf16[1024,128]{1,0:T(8,128)(2,1)S(1)}, bf16[1024,128]{1,0:T(8,128)(2,1)S(1)}, u32[]{:S(2)}, u32[]{:S(2)}) %collective-permute-start.12) | collective-permute-done | bytes 262176 | tf_op jit(solution)/shard_map/range/ppermute | solution.py:25
  69.4 0.2 fusion.7
  69.7 2.7 %collective-permute-start.13 = (bf16[512,128]{1,0:T(8,128)(2,1)S(1)}, bf16[512,128]{1,0:T(8,128)(2,1)S(1)}, u32[]{:S(2)}, u32[]{:S(2)}) collective-permute-start(bf16[512,128]{1,0:T(8,128)(2,1)S(1)} %fusion.12), channel_id=1, source_target_pairs={{0,8},{1,9},{2,10},{3,11},{4,12},{5,13},{6,14},{7,15},{8,0},{9,1},... | collective-permute-start | bytes 393224 | tf_op jit(solution)/shard_map/range/ppermute | solution.py:25
  72.4 0.2 fusion.9
  72.7 1.5 %collective-permute-start.16 = (bf16[512,128]{1,0:T(8,128)(2,1)S(1)}, bf16[512,128]{1,0:T(8,128)(2,1)S(1)}, u32[]{:S(2)}, u32[]{:S(2)}) collective-permute-start(bf16[512,128]{1,0:T(8,128)(2,1)S(1)} %fusion.14), channel_id=1, source_target_pairs={{0,8},{1,9},{2,10},{3,11},{4,12},{5,13},{6,14},{7,15},{8,0},{9,1},... | collective-permute-start | bytes 393224 | tf_op jit(solution)/shard_map/range/ppermute | solution.py:25
  74.1 7.2 %collective-permute-done.13 = bf16[512,128]{1,0:T(8,128)(2,1)S(1)} collective-permute-done((bf16[512,128]{1,0:T(8,128)(2,1)S(1)}, bf16[512,128]{1,0:T(8,128)(2,1)S(1)}, u32[]{:S(2)}, u32[]{:S(2)}) %collective-permute-start.13) | collective-permute-done | bytes 131104 | tf_op jit(solution)/shard_map/range/ppermute | solution.py:25
  81.3 0.1 fusion.30
  81.5 1.4 %collective-permute-done.16 = bf16[512,128]{1,0:T(8,128)(2,1)S(1)} collective-permute-done((bf16[512,128]{1,0:T(8,128)(2,1)S(1)}, bf16[512,128]{1,0:T(8,128)(2,1)S(1)}, u32[]{:S(2)}, u32[]{:S(2)}) %collective-permute-start.16) | collective-permute-done | bytes 131104 | tf_op jit(solution)/shard_map/range/ppermute | solution.py:25
  82.9 0.1 fusion.28
  83.0 1.0 fusion.27
  84.0 0.1 collective-permute-start.17
  84.1 0.1 collective-permute-start.21
  84.2 1.2 collective-permute-done.17
  85.4 0.6 collective-permute-start.18
  86.0 1.8 %collective-permute-start.24 = (bf16[512,128]{1,0:T(8,128)(2,1)S(1)}, bf16[512,128]{1,0:T(8,128)(2,1)S(1)}, u32[]{:S(2)}, u32[]{:S(2)}) collective-permute-start(bf16[512,128]{1,0:T(8,128)(2,1)S(1)} %get-tuple-element.47), channel_id=1, source_target_pairs={{0,8},{1,9},{2,10},{3,11},{4,12},{5,13},{6,14},{7,15},{8,0},{9,1},... | collective-permute-start | bytes 393224 | tf_op jit(solution)/shard_map/gather_range/ppermute | solution.py:25
  87.7 2.0 %collective-permute-done.18 = f32[128,128]{1,0:T(8,128)S(1)} collective-permute-done((f32[128,128]{1,0:T(8,128)S(1)}, f32[128,128]{1,0:T(8,128)S(1)}, u32[]{:S(2)}, u32[]{:S(2)}) %collective-permute-start.18) | collective-permute-done | bytes 65568 | tf_op jit(solution)/shard_map/gram/ppermute | solution.py:25
  89.7 3.0 %collective-permute-start.19 = (f32[128,128]{1,0:T(8,128)S(1)}, f32[128,128]{1,0:T(8,128)S(1)}, u32[]{:S(2)}, u32[]{:S(2)}) collective-permute-start(f32[128,128]{1,0:T(8,128)S(1)} %add.74), channel_id=1, source_target_pairs={{0,4},{1,5},{2,6},{3,7},{4,0},{5,1},{6,2},{7,3},{8,12},{9,13},{10,... | collective-permute-start | bytes 196616 | tf_op jit(solution)/shard_map/gram/ppermute | solution.py:25
  92.7 4.3 %collective-permute-done.21 = bf16[512,128]{1,0:T(8,128)(2,1)S(1)} collective-permute-done((bf16[512,128]{1,0:T(8,128)(2,1)S(1)}, bf16[512,128]{1,0:T(8,128)(2,1)S(1)}, u32[]{:S(2)}, u32[]{:S(2)}) %collective-permute-start.21) | collective-permute-done | bytes 131104 | tf_op jit(solution)/shard_map/gather_range/ppermute | solution.py:25
  97.0 0.1 collective-permute-start.22
  97.1 2.3 %collective-permute-done.24 = bf16[512,128]{1,0:T(8,128)(2,1)S(1)} collective-permute-done((bf16[512,128]{1,0:T(8,128)(2,1)S(1)}, bf16[512,128]{1,0:T(8,128)(2,1)S(1)}, u32[]{:S(2)}, u32[]{:S(2)}) %collective-permute-start.24) | collective-permute-done | bytes 131104 | tf_op jit(solution)/shard_map/gather_range/ppermute | solution.py:25
  99.5 0.6 collective-permute-start.25
  100.1 0.4 collective-permute-start.20
  100.6 5.7 %collective-permute-done.20 = f32[128,128]{1,0:T(8,128)S(1)} collective-permute-done((f32[128,128]{1,0:T(8,128)S(1)}, f32[128,128]{1,0:T(8,128)S(1)}, u32[]{:S(2)}, u32[]{:S(2)}) %collective-permute-start.20) | collective-permute-done | bytes 65568 | tf_op jit(solution)/shard_map/gram/ppermute | solution.py:25
  106.3 0.1 collective-permute-done.22
  106.4 0.9 collective-permute-start.23
  107.4 0.1 collective-permute-start.26
  107.5 6.6 %factor.1 = (f32[128,128]{1,0:T(8,128)S(1)}, f32[1024,128]{1,0:T(8,128)}) custom-call(f32[128,128]{1,0:T(8,128)S(1)} %add.76.gram_ref, f32[1024,128]{1,0:T(8,128)S(1)} %pad_maximum_fusion.2.range_ref), custom_call_target="tpu_custom_call" | custom-call | flops 10000000 | bytes 20000000 | tf_op jit(solution)/shard_map/factor/pallas_call | solution.py:202
  114.1 1.8 %coords.3.refs_6_ = f32[512,128]{1,0:T(8,128)S(1)} custom-call(s32[4,4]{1,0:T(4,128)S(1)} %pad_add_fusion.table_ref, bf16[256,16384]{1,0:T(8,128)(2,1)S(1)} %get-tuple-element.25.x_ref, bf16[64,8192]{1,0:T(8,128)(2,1)S(1)} %collective-permute-done.2.refs_0_, bf16[64,8192]{1,0:T(8,128)(2,1)S(1)} %collective-permute-done.3.refs_1_, ...), custom_call_target="tpu_custom_call" | custom-call | flops 536870912 | bytes 4194304 | tf_op jit(solution)/shard_map/coords/pallas_call | solution.py:119
  115.9 2.9 %collective-permute-done.23.refs_4_ = bf16[2048,128]{1,0:T(8,128)(2,1)S(1)} collective-permute-done((bf16[2048,128]{1,0:T(8,128)(2,1)S(1)}, bf16[2048,128]{1,0:T(8,128)(2,1)S(1)}, u32[]{:S(2)}, u32[]{:S(2)}) %collective-permute-start.23) | collective-permute-done | bytes 524320 | tf_op jit(solution)/shard_map/gather_range/ppermute | solution.py:25
  118.8 1.6 %collective-permute-done.26.refs_5_ = bf16[2048,128]{1,0:T(8,128)(2,1)S(1)} collective-permute-done((bf16[2048,128]{1,0:T(8,128)(2,1)S(1)}, bf16[2048,128]{1,0:T(8,128)(2,1)S(1)}, u32[]{:S(2)}, u32[]{:S(2)}) %collective-permute-start.26) | collective-permute-done | bytes 524320 | tf_op jit(solution)/shard_map/gather_range/ppermute | solution.py:25
  120.4 1.8 %coords.4.part_ref = f32[512,128]{1,0:T(8,128)S(1)} custom-call(s32[4,4]{1,0:T(4,128)S(1)} %pad_add_fusion.1.table_ref, bf16[256,16384]{1,0:T(8,128)(2,1)S(1)} %get-tuple-element.25.x_ref, bf16[64,8192]{1,0:T(8,128)(2,1)S(1)} %collective-permute-done.2.refs_0_, bf16[64,8192]{1,0:T(8,128)(2,1)S(1)} %collective-permute-done.3.refs_1_, ...), custom_call_target="tpu_custom_call" | custom-call | flops 536870912 | bytes 4194304 | tf_op jit(solution)/shard_map/coords/pallas_call | solution.py:119
  122.2 0.1 collective-permute-start.27
  122.3 1.3 %collective-permute-done.27.theirs_ref = f32[256,128]{1,0:T(8,128)S(1)} collective-permute-done((f32[256,128]{1,0:T(8,128)S(1)}, f32[256,128]{1,0:T(8,128)S(1)}, u32[]{:S(2)}, u32[]{:S(2)}) %collective-permute-start.27) | collective-permute-done | bytes 131104 | tf_op jit(solution)/shard_map/coords/ppermute | solution.py:25
  123.7 1.0 coords.5
  (42 shorter events, 0.6 us)
Async XLA Ops:
  0.6 29.4 %copy-start.2 = (s32[4]{0:T(128)S(1)}, s32[4]{0:T(128)}, u32[]{:S(2)}) copy-start(s32[4]{0:T(128)} %constant.131) | copy-start | bytes 52
  0.6 29.4 %copy-start.3 = (s32[4]{0:T(128)S(1)}, s32[4]{0:T(128)}, u32[]{:S(2)}) copy-start(s32[4]{0:T(128)} %constant.130) | copy-start | bytes 52
  0.7 29.4 %copy-start = (s32[4]{0:T(128)S(1)}, s32[4]{0:T(128)}, u32[]{:S(2)}) copy-start(s32[4]{0:T(128)} %constant.133) | copy-start | bytes 52
  0.7 29.4 %copy-start.1 = (s32[4]{0:T(128)S(1)}, s32[4]{0:T(128)}, u32[]{:S(2)}) copy-start(s32[4]{0:T(128)} %constant.132) | copy-start | bytes 52
  1.7 14.0 %collective-permute-start.1 = (bf16[512,128]{1,0:T(8,128)(2,1)S(1)}, bf16[512,128]{1,0:T(8,128)(2,1)S(1)}, u32[]{:S(2)}, u32[]{:S(2)}) collective-permute-start(bf16[512,128]{1,0:T(8,128)(2,1)S(1)} %get-tuple-element.53), channel_id=1, source_target_pairs={{0,8},{1,9},{2,10},{3,11},{4,12},{5,13},{6,14},{7,15},{8,0},{9,1},... | collective-permute-start | bytes 393224 | tf_op jit(solution)/shard_map/gather_sketch/ppermute | solution.py:25
  5.8 11.9 %collective-permute-start = (bf16[512,128]{1,0:T(8,128)(2,1)S(1)}, bf16[512,128]{1,0:T(8,128)(2,1)S(1)}, u32[]{:S(2)}, u32[]{:S(2)}) collective-permute-start(bf16[512,128]{1,0:T(8,128)(2,1)S(1)} %get-tuple-element.54), channel_id=1, source_target_pairs={{0,8},{1,9},{2,10},{3,11},{4,12},{5,13},{6,14},{7,15},{8,0},{9,1},... | collective-permute-start | bytes 393224 | tf_op jit(solution)/shard_map/gather_sketch/ppermute | solution.py:25
  17.7 10.9 %collective-permute-start.2 = (bf16[64,8192]{1,0:T(8,128)(2,1)S(1)}, bf16[64,8192]{1,0:T(8,128)(2,1)S(1)}, u32[]{:S(2)}, u32[]{:S(2)}) collective-permute-start(bf16[64,8192]{1,0:T(8,128)(2,1)S(1)} %get-tuple-element.30), channel_id=1, source_target_pairs={{0,1},{1,0},{2,3},{3,2},{4,5},{5,4},{6,7},{7,6},{8,9},{9,8},{10,11... | collective-permute-start | bytes 3145736 | tf_op jit(solution)/shard_map/split_features/ppermute | solution.py:25
  17.7 8.8 %collective-permute-start.6 = (bf16[1024,128]{1,0:T(8,128)(2,1)S(1)}, bf16[1024,128]{1,0:T(8,128)(2,1)S(1)}, u32[]{:S(2)}, u32[]{:S(2)}) collective-permute-start(bf16[1024,128]{1,0:T(8,128)(2,1)S(1)} %pad_maximum_fusion.4), channel_id=1, source_target_pairs={{0,4},{1,5},{2,6},{3,7},{4,0},{5,1},{6,2},{7,3},{8,12},{9,13},{10,... | collective-permute-start | bytes 786440 | tf_op jit(solution)/shard_map/gather_sketch/ppermute | solution.py:25
  18.6 8.5 %collective-permute-start.8 = (bf16[1024,128]{1,0:T(8,128)(2,1)S(1)}, bf16[1024,128]{1,0:T(8,128)(2,1)S(1)}, u32[]{:S(2)}, u32[]{:S(2)}) collective-permute-start(bf16[1024,128]{1,0:T(8,128)(2,1)S(1)} %pad_maximum_fusion.5), channel_id=1, source_target_pairs={{0,2},{1,3},{2,0},{3,1},{4,6},{5,7},{6,4},{7,5},{8,10},{9,11},{10,... | collective-permute-start | bytes 786440 | tf_op jit(solution)/shard_map/gather_sketch/ppermute | solution.py:25
  20.1 10.0 %collective-permute-start.3 = (bf16[64,8192]{1,0:T(8,128)(2,1)S(1)}, bf16[64,8192]{1,0:T(8,128)(2,1)S(1)}, u32[]{:S(2)}, u32[]{:S(2)}) collective-permute-start(bf16[64,8192]{1,0:T(8,128)(2,1)S(1)} %get-tuple-element.31), channel_id=1, source_target_pairs={{0,1},{1,0},{2,3},{3,2},{4,5},{5,4},{6,7},{7,6},{8,9},{9,8},{10,11... | collective-permute-start | bytes 3145736 | tf_op jit(solution)/shard_map/split_features/ppermute | solution.py:25
  20.1 10.0 %collective-permute-start.4 = (bf16[64,8192]{1,0:T(8,128)(2,1)S(1)}, bf16[64,8192]{1,0:T(8,128)(2,1)S(1)}, u32[]{:S(2)}, u32[]{:S(2)}) collective-permute-start(bf16[64,8192]{1,0:T(8,128)(2,1)S(1)} %get-tuple-element.32), channel_id=1, source_target_pairs={{0,1},{1,0},{2,3},{3,2},{4,5},{5,4},{6,7},{7,6},{8,9},{9,8},{10,11... | collective-permute-start | bytes 3145736 | tf_op jit(solution)/shard_map/split_features/ppermute | solution.py:25
  26.5 3.6 %collective-permute-start.5 = (bf16[64,8192]{1,0:T(8,128)(2,1)S(1)}, bf16[64,8192]{1,0:T(8,128)(2,1)S(1)}, u32[]{:S(2)}, u32[]{:S(2)}) collective-permute-start(bf16[64,8192]{1,0:T(8,128)(2,1)S(1)} %get-tuple-element.33), channel_id=1, source_target_pairs={{0,1},{1,0},{2,3},{3,2},{4,5},{5,4},{6,7},{7,6},{8,9},{9,8},{10,11... | collective-permute-start | bytes 3145736 | tf_op jit(solution)/shard_map/split_features/ppermute | solution.py:25
  27.0 13.9 %collective-permute-start.7 = (bf16[2048,128]{1,0:T(8,128)(2,1)S(1)}, bf16[2048,128]{1,0:T(8,128)(2,1)S(1)}, u32[]{:S(2)}, u32[]{:S(2)}) collective-permute-start(bf16[2048,128]{1,0:T(8,128)(2,1)S(1)} %pad_maximum_fusion.refs_4_), channel_id=1, source_target_pairs={{0,2},{1,3},{2,0},{3,1},{4,6},{5,7},{6,4},{7,5},{8,10},{9,11},{10,... | collective-permute-start | bytes 1572872 | tf_op jit(solution)/shard_map/gather_sketch/ppermute | solution.py:25
  28.6 13.8 %collective-permute-start.9 = (bf16[2048,128]{1,0:T(8,128)(2,1)S(1)}, bf16[2048,128]{1,0:T(8,128)(2,1)S(1)}, u32[]{:S(2)}, u32[]{:S(2)}) collective-permute-start(bf16[2048,128]{1,0:T(8,128)(2,1)S(1)} %pad_maximum_fusion.1.refs_5_), channel_id=1, source_target_pairs={{0,4},{1,5},{2,6},{3,7},{4,0},{5,1},{6,2},{7,3},{8,12},{9,13},{10,... | collective-permute-start | bytes 1572872 | tf_op jit(solution)/shard_map/gather_sketch/ppermute | solution.py:25
  44.2 1.6 %collective-permute-start.10 = (f32[512,128]{1,0:T(8,128)S(1)}, f32[512,128]{1,0:T(8,128)S(1)}, u32[]{:S(2)}, u32[]{:S(2)}) collective-permute-start(f32[512,128]{1,0:T(8,128)S(1)} %sketched.3), channel_id=1, source_target_pairs={{0,1},{1,0},{2,3},{3,2},{4,5},{5,4},{6,7},{7,6},{8,9},{9,8},{10,11... | collective-permute-start | bytes 786440 | tf_op jit(solution)/shard_map/sketched/ppermute | solution.py:25
  47.3 14.0 %collective-permute-start.11 = (bf16[2048,128]{1,0:T(8,128)(2,1)S(1)}, bf16[2048,128]{1,0:T(8,128)(2,1)S(1)}, u32[]{:S(2)}, u32[]{:S(2)}) collective-permute-start(bf16[2048,128]{1,0:T(8,128)(2,1)S(1)} %get-tuple-element.35), channel_id=1, source_target_pairs={{0,2},{1,3},{2,0},{3,1},{4,6},{5,7},{6,4},{7,5},{8,10},{9,11},{10,... | collective-permute-start | bytes 1572872 | tf_op jit(solution)/shard_map/range/ppermute | solution.py:25
  47.9 14.7 %collective-permute-start.14 = (bf16[2048,128]{1,0:T(8,128)(2,1)S(1)}, bf16[2048,128]{1,0:T(8,128)(2,1)S(1)}, u32[]{:S(2)}, u32[]{:S(2)}) collective-permute-start(bf16[2048,128]{1,0:T(8,128)(2,1)S(1)} %get-tuple-element.37), channel_id=1, source_target_pairs={{0,4},{1,5},{2,6},{3,7},{4,0},{5,1},{6,2},{7,3},{8,12},{9,13},{10,... | collective-permute-start | bytes 1572872 | tf_op jit(solution)/shard_map/range/ppermute | solution.py:25
  61.9 7.6 %collective-permute-start.12 = (bf16[1024,128]{1,0:T(8,128)(2,1)S(1)}, bf16[1024,128]{1,0:T(8,128)(2,1)S(1)}, u32[]{:S(2)}, u32[]{:S(2)}) collective-permute-start(bf16[1024,128]{1,0:T(8,128)(2,1)S(1)} %fusion.6), channel_id=1, source_target_pairs={{0,4},{1,5},{2,6},{3,7},{4,0},{5,1},{6,2},{7,3},{8,12},{9,13},{10,... | collective-permute-start | bytes 786440 | tf_op jit(solution)/shard_map/range/ppermute | solution.py:25
  63.1 9.3 %collective-permute-start.15 = (bf16[1024,128]{1,0:T(8,128)(2,1)S(1)}, bf16[1024,128]{1,0:T(8,128)(2,1)S(1)}, u32[]{:S(2)}, u32[]{:S(2)}) collective-permute-start(bf16[1024,128]{1,0:T(8,128)(2,1)S(1)} %fusion.8), channel_id=1, source_target_pairs={{0,2},{1,3},{2,0},{3,1},{4,6},{5,7},{6,4},{7,5},{8,10},{9,11},{10,... | collective-permute-start | bytes 786440 | tf_op jit(solution)/shard_map/range/ppermute | solution.py:25
  69.7 11.6 %collective-permute-start.13 = (bf16[512,128]{1,0:T(8,128)(2,1)S(1)}, bf16[512,128]{1,0:T(8,128)(2,1)S(1)}, u32[]{:S(2)}, u32[]{:S(2)}) collective-permute-start(bf16[512,128]{1,0:T(8,128)(2,1)S(1)} %fusion.12), channel_id=1, source_target_pairs={{0,8},{1,9},{2,10},{3,11},{4,12},{5,13},{6,14},{7,15},{8,0},{9,1},... | collective-permute-start | bytes 393224 | tf_op jit(solution)/shard_map/range/ppermute | solution.py:25
  72.7 10.2 %collective-permute-start.16 = (bf16[512,128]{1,0:T(8,128)(2,1)S(1)}, bf16[512,128]{1,0:T(8,128)(2,1)S(1)}, u32[]{:S(2)}, u32[]{:S(2)}) collective-permute-start(bf16[512,128]{1,0:T(8,128)(2,1)S(1)} %fusion.14), channel_id=1, source_target_pairs={{0,8},{1,9},{2,10},{3,11},{4,12},{5,13},{6,14},{7,15},{8,0},{9,1},... | collective-permute-start | bytes 393224 | tf_op jit(solution)/shard_map/range/ppermute | solution.py:25
  84.0 1.3 %collective-permute-start.17 = (f32[128,128]{1,0:T(8,128)S(1)}, f32[128,128]{1,0:T(8,128)S(1)}, u32[]{:S(2)}, u32[]{:S(2)}) collective-permute-start(f32[128,128]{1,0:T(8,128)S(1)} %fusion.27), channel_id=1, source_target_pairs={{0,1},{1,0},{2,3},{3,2},{4,5},{5,4},{6,7},{7,6},{8,9},{9,8},{10,11... | collective-permute-start | bytes 196616 | tf_op jit(solution)/shard_map/gram/ppermute | solution.py:25
  84.1 12.9 %collective-permute-start.21 = (bf16[512,128]{1,0:T(8,128)(2,1)S(1)}, bf16[512,128]{1,0:T(8,128)(2,1)S(1)}, u32[]{:S(2)}, u32[]{:S(2)}) collective-permute-start(bf16[512,128]{1,0:T(8,128)(2,1)S(1)} %get-tuple-element.49), channel_id=1, source_target_pairs={{0,8},{1,9},{2,10},{3,11},{4,12},{5,13},{6,14},{7,15},{8,0},{9,1},... | collective-permute-start | bytes 393224 | tf_op jit(solution)/shard_map/gather_range/ppermute | solution.py:25
  85.4 4.3 %collective-permute-start.18 = (f32[128,128]{1,0:T(8,128)S(1)}, f32[128,128]{1,0:T(8,128)S(1)}, u32[]{:S(2)}, u32[]{:S(2)}) collective-permute-start(f32[128,128]{1,0:T(8,128)S(1)} %add.73), channel_id=1, source_target_pairs={{0,2},{1,3},{2,0},{3,1},{4,6},{5,7},{6,4},{7,5},{8,10},{9,11},{10,... | collective-permute-start | bytes 196616 | tf_op jit(solution)/shard_map/gram/ppermute | solution.py:25
  86.0 13.4 %collective-permute-start.24 = (bf16[512,128]{1,0:T(8,128)(2,1)S(1)}, bf16[512,128]{1,0:T(8,128)(2,1)S(1)}, u32[]{:S(2)}, u32[]{:S(2)}) collective-permute-start(bf16[512,128]{1,0:T(8,128)(2,1)S(1)} %get-tuple-element.47), channel_id=1, source_target_pairs={{0,8},{1,9},{2,10},{3,11},{4,12},{5,13},{6,14},{7,15},{8,0},{9,1},... | collective-permute-start | bytes 393224 | tf_op jit(solution)/shard_map/gather_range/ppermute | solution.py:25
  89.7 9.7 %collective-permute-start.19 = (f32[128,128]{1,0:T(8,128)S(1)}, f32[128,128]{1,0:T(8,128)S(1)}, u32[]{:S(2)}, u32[]{:S(2)}) collective-permute-start(f32[128,128]{1,0:T(8,128)S(1)} %add.74), channel_id=1, source_target_pairs={{0,4},{1,5},{2,6},{3,7},{4,0},{5,1},{6,2},{7,3},{8,12},{9,13},{10,... | collective-permute-start | bytes 196616 | tf_op jit(solution)/shard_map/gram/ppermute | solution.py:25
  97.0 9.4 %collective-permute-start.22 = (bf16[1024,128]{1,0:T(8,128)(2,1)S(1)}, bf16[1024,128]{1,0:T(8,128)(2,1)S(1)}, u32[]{:S(2)}, u32[]{:S(2)}) collective-permute-start(bf16[1024,128]{1,0:T(8,128)(2,1)S(1)} %pad_maximum_fusion.6), channel_id=1, source_target_pairs={{0,4},{1,5},{2,6},{3,7},{4,0},{5,1},{6,2},{7,3},{8,12},{9,13},{10,... | collective-permute-start | bytes 786440 | tf_op jit(solution)/shard_map/gather_range/ppermute | solution.py:25
  99.5 7.9 %collective-permute-start.25 = (bf16[1024,128]{1,0:T(8,128)(2,1)S(1)}, bf16[1024,128]{1,0:T(8,128)(2,1)S(1)}, u32[]{:S(2)}, u32[]{:S(2)}) collective-permute-start(bf16[1024,128]{1,0:T(8,128)(2,1)S(1)} %pad_maximum_fusion.7), channel_id=1, source_target_pairs={{0,2},{1,3},{2,0},{3,1},{4,6},{5,7},{6,4},{7,5},{8,10},{9,11},{10,... | collective-permute-start | bytes 786440 | tf_op jit(solution)/shard_map/gather_range/ppermute | solution.py:25
  100.1 6.2 %collective-permute-start.20 = (f32[128,128]{1,0:T(8,128)S(1)}, f32[128,128]{1,0:T(8,128)S(1)}, u32[]{:S(2)}, u32[]{:S(2)}) collective-permute-start(f32[128,128]{1,0:T(8,128)S(1)} %add.75), channel_id=1, source_target_pairs={{0,8},{1,9},{2,10},{3,11},{4,12},{5,13},{6,14},{7,15},{8,0},{9,1},... | collective-permute-start | bytes 196616 | tf_op jit(solution)/shard_map/gram/ppermute | solution.py:25
  106.4 12.4 %collective-permute-start.23 = (bf16[2048,128]{1,0:T(8,128)(2,1)S(1)}, bf16[2048,128]{1,0:T(8,128)(2,1)S(1)}, u32[]{:S(2)}, u32[]{:S(2)}) collective-permute-start(bf16[2048,128]{1,0:T(8,128)(2,1)S(1)} %constant_dynamic-update-slice_fusion.refs_4_), channel_id=1, source_target_pairs={{0,2},{1,3},{2,0},{3,1},{4,6},{5,7},{6,4},{7,5},{8,10},{9,11},{10,... | collective-permute-start | bytes 1572872 | tf_op jit(solution)/shard_map/gather_range/ppermute | solution.py:25
  107.4 13.0 %collective-permute-start.26 = (bf16[2048,128]{1,0:T(8,128)(2,1)S(1)}, bf16[2048,128]{1,0:T(8,128)(2,1)S(1)}, u32[]{:S(2)}, u32[]{:S(2)}) collective-permute-start(bf16[2048,128]{1,0:T(8,128)(2,1)S(1)} %pad_maximum_fusion.3.refs_5_), channel_id=1, source_target_pairs={{0,4},{1,5},{2,6},{3,7},{4,0},{5,1},{6,2},{7,3},{8,12},{9,13},{10,... | collective-permute-start | bytes 1572872 | tf_op jit(solution)/shard_map/gather_range/ppermute | solution.py:25
  122.2 1.4 %collective-permute-start.27 = (f32[256,128]{1,0:T(8,128)S(1)}, f32[256,128]{1,0:T(8,128)S(1)}, u32[]{:S(2)}, u32[]{:S(2)}) collective-permute-start(f32[256,128]{1,0:T(8,128)S(1)} %slice.62), channel_id=1, source_target_pairs={{0,1},{1,0},{2,3},{3,2},{4,5},{5,4},{6,7},{7,6},{8,9},{9,8},{10,11... | collective-permute-start | bytes 393224 | tf_op jit(solution)/shard_map/coords/ppermute | solution.py:25

commit v3 on v2

--- a/solution.py
+++ b/solution.py
@@ -17,8 +17,9 @@
 
 X_BIT, ZLO, ZHI = 1, 2, 4
 HLX, HXL, LHX = (ZHI, ZLO, X_BIT), (ZHI, X_BIT, ZLO), (ZLO, ZHI, X_BIT)
-PIECES = ((4, HLX), (4, HXL))
-LOADS, PARTS = 8, 4
+PIECES = ((2, HLX), (2, HXL), (2, HLX), (2, HXL))
+LOADS, PARTS = 8, 1
+NEAR, FAR = 0, 1
 
 
 def swap(value, bit, n):
@@ -32,6 +33,14 @@
     return near, [owner ^ bits[-1] for owner in near]
 
 
+def layout(width):
+    place, out = 0, []
+    for share, order in PIECES:
+        out.append((place, width * share // 8, owners(order)))
+        place += width * share // 8
+    return out
+
+
 def encode(value):
     return (value * jnp.abs(value)).astype(BF16)
 
@@ -50,7 +59,7 @@
     return pltpu.with_memory_space_constraint(value, pltpu.VMEM)
 
 
-def load_kernel(width, core_ref, x_ref, copy_ref, norm_ref, *refs):
+def load_kernel(width, index_ref, x_ref, copy_ref, norm_ref, *refs):
     outs, sems = refs[:-1], refs[-1]
     rows, features = x_ref.shape
     chunk = rows // LOADS
@@ -66,7 +75,7 @@
         out = outs[i * len(outs) // LOADS]
         base = i * chunk % out.shape[0]
         for k in range(features // (2 * width)):
-            start = pl.multiple_of((2 * k + 1 - core_ref[0]) * width, width)
+            start = pl.multiple_of((2 * k + 1 - index_ref[0] % 2) * width, width)
             out[base : base + chunk, k * width : (k + 1) * width] = copy_ref[
                 i * chunk : (i + 1) * chunk, pl.ds(start, width)
             ]
@@ -77,7 +86,7 @@
         norm_ref[i * chunk : (i + 1) * chunk, :] = total
 
 
-def load(core, x, width):
+def load(index, x, width):
     rows, features = x.shape
     part = (rows // PARTS, features // 2)
     return pl.pallas_call(
@@ -88,36 +97,38 @@
         scratch_shapes=[pltpu.SemaphoreType.DMA((LOADS,))],
         compiler_params=PARAMS,
         cost_estimate=pl.CostEstimate(flops=2 * rows * features, bytes_accessed=4 * rows * features, transcendentals=0),
-    )(core, pltpu.with_memory_space_constraint(x, pltpu.HBM))
-
-
-def tokens(x_ref, other_refs, table_ref, row, step, j, size):
-    mine = x_ref[:, pl.ds(pl.multiple_of(table_ref[row, j] * 128, 128), size)]
-    start = pl.multiple_of(table_ref[row + step, j] * 128, 128)
-    return jnp.concatenate([mine] + [ref[:, pl.ds(start, size)] for ref in other_refs], axis=0)
-
-
-def project_kernel(n_pieces, has_init, table_ref, x_ref, *refs):
+    )(index, pltpu.with_memory_space_constraint(x, pltpu.HBM))
+
+
+def tokens(place, owner, start, size, x_ref, other_refs):
+    index_ref, width = place
+    block = jnp.bitwise_xor(index_ref[0], 2 * owner)
+    mine = x_ref[:, pl.ds(pl.multiple_of(block * width + start, 128), size)]
+    where = pl.ds(pl.multiple_of(block // 2 * width + start, 128), size)
+    return jnp.concatenate([mine] + [ref[:, where] for ref in other_refs], axis=0)
+
+
+def project_kernel(width, which, has_init, index_ref, x_ref, *refs):
     others, refs, out_ref = refs[:PARTS], refs[PARTS:-1], refs[-1]
-    pieces = refs[:n_pieces]
-    total = refs[n_pieces][...] if has_init else None
+    count = len(PIECES)
+    total = refs[count][...] if has_init else None
     for j in range(4):
-        sizes = [piece.shape[0] // 4 for piece in pieces]
-        block = jnp.concatenate([ref[j * size : (j + 1) * size, :] for ref, size in zip(pieces, sizes)], axis=0)
-        left = jnp.concatenate(
-            [tokens(x_ref, others, table_ref, p, n_pieces, j, size) for p, size in enumerate(sizes)], axis=1
-        )
+        left, block = [], []
+        for ref, (start, size, lists) in zip(refs, layout(width)):
+            left.append(tokens((index_ref, width), lists[which][j], start, size, x_ref, others))
+            block.append(ref[j * size : (j + 1) * size, :])
+        left, block = jnp.concatenate(left, axis=1), jnp.concatenate(block, axis=0)
         term = jnp.dot(left, block, preferred_element_type=F32)
         total = term if total is None else total + term
     out_ref[...] = total
 
 
-def project(table, x, others, pieces, init=None):
+def project(place, which, x, others, pieces, init=None):
     rows, rank = x.shape[0], pieces[0].shape[1]
     depth = sum(piece.shape[0] for piece in pieces)
     extra = [] if init is None else [init]
     return pl.pallas_call(
-        functools.partial(project_kernel, len(pieces), init is not None),
+        functools.partial(project_kernel, place[1], which, init is not None),
         in_specs=[SMEM] + [VMEM] * (1 + PARTS + len(pieces) + len(extra)),
         out_specs=VMEM,
         out_shape=jax.ShapeDtypeStruct((2 * rows, rank), F32),
@@ -125,33 +136,32 @@
         cost_estimate=pl.CostEstimate(
             flops=4 * rows * depth * rank, bytes_accessed=4 * rows * depth, transcendentals=0
         ),
-    )(table, pinned(x), *map(pinned, others), *pieces, *extra)
-
-
-def spread_kernel(coded, n_pieces, table_ref, x_ref, *refs):
+    )(place[0], pinned(x), *map(pinned, others), *pieces, *extra)
+
+
+def spread_kernel(width, which, index_ref, x_ref, *refs):
     others, y_ref, outs = refs[:PARTS], refs[PARTS], refs[PARTS + 1 :]
     turned = y_ref[...].astype(F32).T.astype(BF16)
-    for p, out in enumerate(outs):
-        size = out.shape[0] // 4
+    for out, (start, size, lists) in zip(outs, layout(width)):
         for j in range(4):
-            term = jnp.dot(
-                turned, tokens(x_ref, others, table_ref, p, n_pieces, j, size), preferred_element_type=F32
-            ).T
-            out[j * size : (j + 1) * size, :] = encode(term) if coded else term
-
-
-def spread(table, x, others, y, sizes, coded):
+            right = tokens((index_ref, width), lists[which][j], start, size, x_ref, others)
+            term = jnp.dot(turned, right, preferred_element_type=F32).T
+            out[j * size : (j + 1) * size, :] = encode(term) if which == FAR else term
+
+
+def spread(place, which, x, others, y):
     rows, rank = x.shape[0], y.shape[1]
-    return pl.pallas_call(
-        functools.partial(spread_kernel, coded, len(sizes)),
+    sizes = [size for _, size, _ in layout(place[1])]
+    return pl.pallas_call(
+        functools.partial(spread_kernel, place[1], which),
         in_specs=[SMEM] + [VMEM] * (2 + PARTS),
         out_specs=[VMEM] * len(sizes),
-        out_shape=[jax.ShapeDtypeStruct((4 * size, rank), BF16 if coded else F32) for size in sizes],
+        out_shape=[jax.ShapeDtypeStruct((4 * size, rank), BF16 if which == FAR else F32) for size in sizes],
         compiler_params=PARAMS,
         cost_estimate=pl.CostEstimate(
             flops=16 * rows * sum(sizes) * rank, bytes_accessed=16 * rows * sum(sizes), transcendentals=0
         ),
-    )(table, pinned(x), *map(pinned, others), y)
+    )(place[0], pinned(x), *map(pinned, others), y)
 
 
 def factor_kernel(scale, gram_ref, range_ref, out_ref, basis_ref):
@@ -235,28 +245,16 @@
     x, rows = activations, activations.shape[0]
     width = sketch.shape[1]
     depth = n * width
-    index = lax.axis_index("tok")
-    core = index % 2
+    index = lax.axis_index("tok").astype(jnp.int32).reshape(1)
+    place = (index, width)
     orders = [order for _, order in PIECES]
-    sizes = [width * share // 8 for share, _ in PIECES]
-    starts = [sum(sizes[:p]) for p in range(len(sizes))]
     every = range(len(PIECES))
 
-    def table(which):
-        mine, theirs = [], []
-        for order, start in zip(orders, starts):
-            owner = jnp.bitwise_xor(index, 2 * jnp.array(owners(order)[which], jnp.int32))
-            mine.append((width * owner + start) // 128)
-            theirs.append((width * (owner // 2) + start) // 128)
-        return jnp.stack(mine + theirs).astype(jnp.int32)
-
-    near, far = table(0), table(1)
-
     with jax.named_scope("gather_sketch"):
-        held = [sketch[0, start : start + size] for start, size in zip(starts, sizes)]
+        held = [sketch[0, start : start + size] for start, size, _ in layout(width)]
         came = [swap(held[p], 2 * orders[p][0], n) for p in every]
     with jax.named_scope("split_features"):
-        x, norm, *others = load(core.reshape(1).astype(jnp.int32), x, width)
+        x, norm, *others = load(index, x, width)
         others = lax.optimization_barrier((*others, *came))[:PARTS]
         others = [swap(part, 1, n) for part in others]
     with jax.named_scope("gather_sketch"):
@@ -264,13 +262,13 @@
         held = [jnp.concatenate([held[p], swap(held[p], 2 * orders[p][1], n)]) for p in every]
         came = [swap(held[p], 2 * orders[p][2], n) for p in every]
     with jax.named_scope("sketched"):
-        part = project(near, x, others, held)
-        part = project(far, x, others, came, part)
+        part = project(place, NEAR, x, others, held)
+        part = project(place, FAR, x, others, came, part)
         theirs = swap(part, 1, n)
         sketched = (part + jnp.concatenate([theirs[rows:], theirs[:rows]])).astype(BF16)
     with jax.named_scope("range"):
-        sent = spread(far, x, others, sketched, sizes, True)
-        kept = spread(near, x, others, sketched, sizes, False)
+        sent = spread(place, FAR, x, others, sketched)
+        kept = spread(place, NEAR, x, others, sketched)
         sums = []
         for p in every:
             mine, coded = kept[p], sent[p]
@@ -283,22 +281,24 @@
     with jax.named_scope("gram"):
         gram = jnp.dot(range_rows.T, range_rows, preferred_element_type=F32, precision=HIGH)
         grams = [gram]
-        for bit in (1, 2, 4, 8):
+        for bit in (1, 2):
             gram = gram + swap(gram, bit, n)
             grams.append(gram)
+        far = [swap(gram, bit, n) for bit in (4, 8, 12)]
+        gram = (gram + far[0]) + (far[1] + far[2])
+        grams += [gram, gram]
     with jax.named_scope("gather_range"):
         held = [total.astype(BF16) for total in sums]
         held = [jnp.concatenate([held[p], swap(held[p], 2 * orders[p][0], n)]) for p in every]
         held[0] = after(held[0], grams[2])
-        held[-1] = after(held[-1], grams[3])
+        held[-1] = after(held[-1], grams[2])
         held = [jnp.concatenate([held[p], swap(held[p], 2 * orders[p][1], n)]) for p in every]
-        held[-1] = after(held[-1], grams[4])
         came = [swap(held[p], 2 * orders[p][2], n) for p in every]
     with jax.named_scope("factor"):
         inverse, basis = factored(math.sqrt(depth), gram, range_rows)
     with jax.named_scope("coords"):
-        part = project(near, x, others, held)
-        part = project(far, x, others, came, after(part, inverse))
+        part = project(place, NEAR, x, others, held)
+        part = project(place, FAR, x, others, came, after(part, inverse))
         coords, resid_rms = close(depth, part, swap(part[rows:], 1, n), inverse, norm)
     return basis[None], coords, resid_rms.reshape(rows)
 

time: 125 us -> 118 us (0.944)
  waiting for transfers between devices: 73.5 us -> 48.9 us
  starting transfers between devices: 24.4 us -> 45.3 us
  Pallas kernels: 21.5 us -> 18 us
    ppermute x28 -> x44, waiting for transfers between devices: 73.5 us -> 48.9 us  [swap(): return lax.ppermute(value, 'tok', [(i, i ^ bit) for i in range(n)])]
    ppermute x28 -> x44, starting transfers between devices: 24.4 us -> 45.3 us  [swap(): return lax.ppermute(value, 'tok', [(i, i ^ bit) for i in range(n)])]
    pallas_call x6, Pallas kernels: 10.2 us -> 6.82 us  [the longest x4 5.02 us: project(): pl.pallas_call(functools.partial(project_kernel, place[1], which, init is...]
  transfers between devices with their start and end apart: 28 -> 44, of which waited for: 20 -> 24; matrix products, arithmetic and copies ran while one was open for 2% -> 3% of each run, Pallas kernels for 12% -> 12%
where the time goes in v3:
time: 118 us; the launch traced here: 117 us
  waiting for transfers between devices  48.9 us (41%)
  starting transfers between devices  45.3 us (38%)
  Pallas kernels  18 us (15%)
  other arithmetic  2.15 us (2%)
    ppermute x44, waiting for transfers between devices, swap(): return lax.ppermute(value, 'tok', [(i, i ^ bit) for i in range(n)])  48.9 us
    ppermute x44, starting transfers between devices, swap(): return lax.ppermute(value, 'tok', [(i, i ^ bit) for i in range(n)])  45.3 us
    pallas_call x1, Pallas kernels, factored(): pl.pallas_call(functools.partial(factor_kernel, scale), in_specs=[VMEM] *...  6.41 us
    pallas_call x4, Pallas kernels, project(): pl.pallas_call(functools.partial(project_kernel, place[1], which, init is...  5.02 us
    pallas_call x1, Pallas kernels, load(): pl.pallas_call(functools.partial(load_kernel, width), in_specs=[SMEM, ANY...  3.78 us
  transfers between devices with their start and end apart: 44, of which 24 were waited for; matrix products, arithmetic and copies ran while one was open for 3% of the time, Pallas kernels for 12%

profile of v3, /device:TPU:0, one launch (start us, length us, event | category | flops | bytes accessed | tf_op | source)
XLA Modules:
  0.0 117.3 jit_solution(10794552517738917717)
XLA Ops:
  0.6 1.0 slice_bitcast_fusion
  1.6 4.1 %collective-permute-start = (bf16[256,128]{1,0:T(8,128)(2,1)S(1)}, bf16[256,128]{1,0:T(8,128)(2,1)S(1)}, u32[]{:S(2)}, u32[]{:S(2)}) collective-permute-start(bf16[256,128]{1,0:T(8,128)(2,1)S(1)} %get-tuple-element.53), channel_id=1, source_target_pairs={{0,8},{1,9},{2,10},{3,11},{4,12},{5,13},{6,14},{7,15},{8,0},{9,1},... | collective-permute-start | bytes 196616 | tf_op jit(solution)/shard_map/gather_sketch/ppermute | solution.py:26
  5.8 2.8 %collective-permute-start.2 = (bf16[256,128]{1,0:T(8,128)(2,1)S(1)}, bf16[256,128]{1,0:T(8,128)(2,1)S(1)}, u32[]{:S(2)}, u32[]{:S(2)}) collective-permute-start(bf16[256,128]{1,0:T(8,128)(2,1)S(1)} %get-tuple-element.54), channel_id=1, source_target_pairs={{0,8},{1,9},{2,10},{3,11},{4,12},{5,13},{6,14},{7,15},{8,0},{9,1},... | collective-permute-start | bytes 196616 | tf_op jit(solution)/shard_map/gather_sketch/ppermute | solution.py:26
  8.7 3.8 %split_features.1 = (bf16[256,16384]{1,0:T(8,128)(2,1)S(1)}, f32[256,128]{1,0:T(8,128)S(1)}, bf16[256,8192]{1,0:T(8,128)(2,1)S(1)}) custom-call(s32[1]{0:T(128)} %bitcast.index_ref, bf16[256,16384]{1,0:T(8,128)(2,1)} %x_ref.1), custom_call_target="tpu_custom_call" | custom-call | flops 8388608 | bytes 16777216 | tf_op jit(solution)/shard_map/split_features/pallas_call | solution.py:92
  12.5 3.0 %collective-permute-done.1 = bf16[256,128]{1,0:T(8,128)(2,1)S(1)} collective-permute-done((bf16[256,128]{1,0:T(8,128)(2,1)S(1)}, bf16[256,128]{1,0:T(8,128)(2,1)S(1)}, u32[]{:S(2)}, u32[]{:S(2)}) %collective-permute-start.1) | collective-permute-done | bytes 65568 | tf_op jit(solution)/shard_map/gather_sketch/ppermute | solution.py:26
  15.5 1.4 %collective-permute-done.2 = bf16[256,128]{1,0:T(8,128)(2,1)S(1)} collective-permute-done((bf16[256,128]{1,0:T(8,128)(2,1)S(1)}, bf16[256,128]{1,0:T(8,128)(2,1)S(1)}, u32[]{:S(2)}, u32[]{:S(2)}) %collective-permute-start.2) | collective-permute-done | bytes 65568 | tf_op jit(solution)/shard_map/gather_sketch/ppermute | solution.py:26
  16.9 0.8 collective-permute-done.3
  17.8 0.6 collective-permute-start.5
  18.4 1.5 %collective-permute-start.9 = (bf16[512,128]{1,0:T(8,128)(2,1)S(1)}, bf16[512,128]{1,0:T(8,128)(2,1)S(1)}, u32[]{:S(2)}, u32[]{:S(2)}) collective-permute-start(bf16[512,128]{1,0:T(8,128)(2,1)S(1)} %pad_maximum_fusion.9), channel_id=1, source_target_pairs={{0,4},{1,5},{2,6},{3,7},{4,0},{5,1},{6,2},{7,3},{8,12},{9,13},{10,... | collective-permute-start | bytes 393224 | tf_op jit(solution)/shard_map/gather_sketch/ppermute | solution.py:26
  20.0 1.8 %collective-permute-start.11 = (bf16[512,128]{1,0:T(8,128)(2,1)S(1)}, bf16[512,128]{1,0:T(8,128)(2,1)S(1)}, u32[]{:S(2)}, u32[]{:S(2)}) collective-permute-start(bf16[512,128]{1,0:T(8,128)(2,1)S(1)} %pad_maximum_fusion.10), channel_id=1, source_target_pairs={{0,2},{1,3},{2,0},{3,1},{4,6},{5,7},{6,4},{7,5},{8,10},{9,11},{10,... | collective-permute-start | bytes 393224 | tf_op jit(solution)/shard_map/gather_sketch/ppermute | solution.py:26
  21.7 0.4 collective-permute-start.7
  22.1 4.4 %collective-permute-done.9 = bf16[512,128]{1,0:T(8,128)(2,1)S(1)} collective-permute-done((bf16[512,128]{1,0:T(8,128)(2,1)S(1)}, bf16[512,128]{1,0:T(8,128)(2,1)S(1)}, u32[]{:S(2)}, u32[]{:S(2)}) %collective-permute-start.9) | collective-permute-done | bytes 131104 | tf_op jit(solution)/shard_map/gather_sketch/ppermute | solution.py:26
  26.6 1.8 %collective-permute-start.10 = (bf16[1024,128]{1,0:T(8,128)(2,1)S(1)}, bf16[1024,128]{1,0:T(8,128)(2,1)S(1)}, u32[]{:S(2)}, u32[]{:S(2)}) collective-permute-start(bf16[1024,128]{1,0:T(8,128)(2,1)S(1)} %pad_maximum_fusion.3.refs_3_), channel_id=1, source_target_pairs={{0,2},{1,3},{2,0},{3,1},{4,6},{5,7},{6,4},{7,5},{8,10},{9,11},{10,... | collective-permute-start | bytes 786440 | tf_op jit(solution)/shard_map/gather_sketch/ppermute | solution.py:26
  28.4 0.4 collective-permute-start.12
  28.8 0.6 collective-permute-start.6
  29.5 1.5 %collective-permute-start.8 = (bf16[1024,128]{1,0:T(8,128)(2,1)S(1)}, bf16[1024,128]{1,0:T(8,128)(2,1)S(1)}, u32[]{:S(2)}, u32[]{:S(2)}) collective-permute-start(bf16[1024,128]{1,0:T(8,128)(2,1)S(1)} %pad_maximum_fusion.2.refs_2_), channel_id=1, source_target_pairs={{0,4},{1,5},{2,6},{3,7},{4,0},{5,1},{6,2},{7,3},{8,12},{9,13},{10,... | collective-permute-start | bytes 786440 | tf_op jit(solution)/shard_map/gather_sketch/ppermute | solution.py:26
  31.0 1.2 %sketched.2.refs_5_ = f32[512,128]{1,0:T(8,128)S(1)} custom-call(s32[1]{0:T(128)} %bitcast.index_ref, bf16[256,16384]{1,0:T(8,128)(2,1)S(1)} %get-tuple-element.22.x_ref, bf16[256,8192]{1,0:T(8,128)(2,1)S(1)} %collective-permute-done.4.refs_0_, bf16[1024,128]{1,0:T(8,128)(2,1)S(1)} %pad_maximum_fusion.1.refs_1_, ...), custom_call_target="tpu_custom_call" | custom-call | flops 536870912 | bytes 4194304 | tf_op jit(solution)/shard_map/sketched/pallas_call | solution.py:130
  32.2 3.6 %collective-permute-done.10.refs_3_ = bf16[1024,128]{1,0:T(8,128)(2,1)S(1)} collective-permute-done((bf16[1024,128]{1,0:T(8,128)(2,1)S(1)}, bf16[1024,128]{1,0:T(8,128)(2,1)S(1)}, u32[]{:S(2)}, u32[]{:S(2)}) %collective-permute-start.10) | collective-permute-done | bytes 262176 | tf_op jit(solution)/shard_map/gather_sketch/ppermute | solution.py:26
  35.9 1.8 %collective-permute-done.12.refs_4_ = bf16[1024,128]{1,0:T(8,128)(2,1)S(1)} collective-permute-done((bf16[1024,128]{1,0:T(8,128)(2,1)S(1)}, bf16[1024,128]{1,0:T(8,128)(2,1)S(1)}, u32[]{:S(2)}, u32[]{:S(2)}) %collective-permute-start.12) | collective-permute-done | bytes 262176 | tf_op jit(solution)/shard_map/gather_sketch/ppermute | solution.py:26
  37.7 2.5 %collective-permute-done.6.refs_1_ = bf16[1024,128]{1,0:T(8,128)(2,1)S(1)} collective-permute-done((bf16[1024,128]{1,0:T(8,128)(2,1)S(1)}, bf16[1024,128]{1,0:T(8,128)(2,1)S(1)}, u32[]{:S(2)}, u32[]{:S(2)}) %collective-permute-start.6) | collective-permute-done | bytes 262176 | tf_op jit(solution)/shard_map/gather_sketch/ppermute | solution.py:26
  40.2 1.5 %collective-permute-done.8.refs_2_ = bf16[1024,128]{1,0:T(8,128)(2,1)S(1)} collective-permute-done((bf16[1024,128]{1,0:T(8,128)(2,1)S(1)}, bf16[1024,128]{1,0:T(8,128)(2,1)S(1)}, u32[]{:S(2)}, u32[]{:S(2)}) %collective-permute-start.8) | collective-permute-done | bytes 262176 | tf_op jit(solution)/shard_map/gather_sketch/ppermute | solution.py:26
  41.7 1.3 %sketched.3 = f32[512,128]{1,0:T(8,128)S(1)} custom-call(s32[1]{0:T(128)} %bitcast.index_ref, bf16[256,16384]{1,0:T(8,128)(2,1)S(1)} %get-tuple-element.22.x_ref, bf16[256,8192]{1,0:T(8,128)(2,1)S(1)} %collective-permute-done.4.refs_0_, bf16[1024,128]{1,0:T(8,128)(2,1)S(1)} %collective-permute-done.6.refs_1_, ...), custom_call_target="tpu_custom_call" | custom-call | flops 536870912 | bytes 4194304 | tf_op jit(solution)/shard_map/sketched/pallas_call | solution.py:130
  43.1 1.5 %collective-permute-done.13 = f32[512,128]{1,0:T(8,128)S(1)} collective-permute-done((f32[512,128]{1,0:T(8,128)S(1)}, f32[512,128]{1,0:T(8,128)S(1)}, u32[]{:S(2)}, u32[]{:S(2)}) %collective-permute-start.13) | collective-permute-done | bytes 262176 | tf_op jit(solution)/shard_map/sketched/ppermute | solution.py:26
  44.6 0.9 range.3
  45.6 0.4 collective-permute-start.23
  46.0 0.5 collective-permute-start.14
  46.5 1.5 %collective-permute-start.17 = (bf16[1024,128]{1,0:T(8,128)(2,1)S(1)}, bf16[1024,128]{1,0:T(8,128)(2,1)S(1)}, u32[]{:S(2)}, u32[]{:S(2)}) collective-permute-start(bf16[1024,128]{1,0:T(8,128)(2,1)S(1)} %get-tuple-element.28), channel_id=1, source_target_pairs={{0,4},{1,5},{2,6},{3,7},{4,0},{5,1},{6,2},{7,3},{8,12},{9,13},{10,... | collective-permute-start | bytes 786440 | tf_op jit(solution)/shard_map/range/ppermute | solution.py:26
  48.0 1.7 %collective-permute-start.20 = (bf16[1024,128]{1,0:T(8,128)(2,1)S(1)}, bf16[1024,128]{1,0:T(8,128)(2,1)S(1)}, u32[]{:S(2)}, u32[]{:S(2)}) collective-permute-start(bf16[1024,128]{1,0:T(8,128)(2,1)S(1)} %get-tuple-element.30), channel_id=1, source_target_pairs={{0,2},{1,3},{2,0},{3,1},{4,6},{5,7},{6,4},{7,5},{8,10},{9,11},{10,... | collective-permute-start | bytes 786440 | tf_op jit(solution)/shard_map/range/ppermute | solution.py:26
  49.7 0.9 range.2
  50.6 4.2 %collective-permute-done.23 = bf16[1024,128]{1,0:T(8,128)(2,1)S(1)} collective-permute-done((bf16[1024,128]{1,0:T(8,128)(2,1)S(1)}, bf16[1024,128]{1,0:T(8,128)(2,1)S(1)}, u32[]{:S(2)}, u32[]{:S(2)}) %collective-permute-start.23) | collective-permute-done | bytes 262176 | tf_op jit(solution)/shard_map/range/ppermute | solution.py:26
  55.0 0.4 collective-permute-start.24
  55.7 1.5 %collective-permute-start.15 = (bf16[512,128]{1,0:T(8,128)(2,1)S(1)}, bf16[512,128]{1,0:T(8,128)(2,1)S(1)}, u32[]{:S(2)}, u32[]{:S(2)}) collective-permute-start(bf16[512,128]{1,0:T(8,128)(2,1)S(1)} %fusion.12), channel_id=1, source_target_pairs={{0,4},{1,5},{2,6},{3,7},{4,0},{5,1},{6,2},{7,3},{8,12},{9,13},{10,... | collective-permute-start | bytes 393224 | tf_op jit(solution)/shard_map/range/ppermute | solution.py:26
  57.2 3.2 %collective-permute-done.17 = bf16[1024,128]{1,0:T(8,128)(2,1)S(1)} collective-permute-done((bf16[1024,128]{1,0:T(8,128)(2,1)S(1)}, bf16[1024,128]{1,0:T(8,128)(2,1)S(1)}, u32[]{:S(2)}, u32[]{:S(2)}) %collective-permute-start.17) | collective-permute-done | bytes 262176 | tf_op jit(solution)/shard_map/range/ppermute | solution.py:26
  60.7 0.4 collective-permute-start.18
  61.3 1.5 %collective-permute-start.21 = (bf16[512,128]{1,0:T(8,128)(2,1)S(1)}, bf16[512,128]{1,0:T(8,128)(2,1)S(1)}, u32[]{:S(2)}, u32[]{:S(2)}) collective-permute-start(bf16[512,128]{1,0:T(8,128)(2,1)S(1)} %fusion.16), channel_id=1, source_target_pairs={{0,4},{1,5},{2,6},{3,7},{4,0},{5,1},{6,2},{7,3},{8,12},{9,13},{10,... | collective-permute-start | bytes 393224 | tf_op jit(solution)/shard_map/range/ppermute | solution.py:26
  63.2 4.0 %collective-permute-start.25 = (bf16[256,128]{1,0:T(8,128)(2,1)S(1)}, bf16[256,128]{1,0:T(8,128)(2,1)S(1)}, u32[]{:S(2)}, u32[]{:S(2)}) collective-permute-start(bf16[256,128]{1,0:T(8,128)(2,1)S(1)} %fusion.31), channel_id=1, source_target_pairs={{0,8},{1,9},{2,10},{3,11},{4,12},{5,13},{6,14},{7,15},{8,0},{9,1},... | collective-permute-start | bytes 196616 | tf_op jit(solution)/shard_map/range/ppermute | solution.py:26
  67.6 3.0 %collective-permute-start.19 = (bf16[256,128]{1,0:T(8,128)(2,1)S(1)}, bf16[256,128]{1,0:T(8,128)(2,1)S(1)}, u32[]{:S(2)}, u32[]{:S(2)}) collective-permute-start(bf16[256,128]{1,0:T(8,128)(2,1)S(1)} %fusion.27), channel_id=1, source_target_pairs={{0,8},{1,9},{2,10},{3,11},{4,12},{5,13},{6,14},{7,15},{8,0},{9,1},... | collective-permute-start | bytes 196616 | tf_op jit(solution)/shard_map/range/ppermute | solution.py:26
  70.8 4.8 %collective-permute-done.25 = bf16[256,128]{1,0:T(8,128)(2,1)S(1)} collective-permute-done((bf16[256,128]{1,0:T(8,128)(2,1)S(1)}, bf16[256,128]{1,0:T(8,128)(2,1)S(1)}, u32[]{:S(2)}, u32[]{:S(2)}) %collective-permute-start.25) | collective-permute-done | bytes 65568 | tf_op jit(solution)/shard_map/range/ppermute | solution.py:26
  75.8 1.3 %collective-permute-done.16 = bf16[256,128]{1,0:T(8,128)(2,1)S(1)} collective-permute-done((bf16[256,128]{1,0:T(8,128)(2,1)S(1)}, bf16[256,128]{1,0:T(8,128)(2,1)S(1)}, u32[]{:S(2)}, u32[]{:S(2)}) %collective-permute-start.16) | collective-permute-done | bytes 65568 | tf_op jit(solution)/shard_map/range/ppermute | solution.py:26
  77.1 1.3 %collective-permute-done.19 = bf16[256,128]{1,0:T(8,128)(2,1)S(1)} collective-permute-done((bf16[256,128]{1,0:T(8,128)(2,1)S(1)}, bf16[256,128]{1,0:T(8,128)(2,1)S(1)}, u32[]{:S(2)}, u32[]{:S(2)}) %collective-permute-start.19) | collective-permute-done | bytes 65568 | tf_op jit(solution)/shard_map/range/ppermute | solution.py:26
  78.5 1.9 %collective-permute-done.22 = bf16[256,128]{1,0:T(8,128)(2,1)S(1)} collective-permute-done((bf16[256,128]{1,0:T(8,128)(2,1)S(1)}, bf16[256,128]{1,0:T(8,128)(2,1)S(1)}, u32[]{:S(2)}, u32[]{:S(2)}) %collective-permute-start.22) | collective-permute-done | bytes 65568 | tf_op jit(solution)/shard_map/range/ppermute | solution.py:26
  80.5 1.0 fusion.33
  81.6 2.9 %collective-permute-start.34 = (bf16[256,128]{1,0:T(8,128)(2,1)S(1)}, bf16[256,128]{1,0:T(8,128)(2,1)S(1)}, u32[]{:S(2)}, u32[]{:S(2)}) collective-permute-start(bf16[256,128]{1,0:T(8,128)(2,1)S(1)} %get-tuple-element.45), channel_id=1, source_target_pairs={{0,8},{1,9},{2,10},{3,11},{4,12},{5,13},{6,14},{7,15},{8,0},{9,1},... | collective-permute-start | bytes 196616 | tf_op jit(solution)/shard_map/gather_range/ppermute | solution.py:26
  84.7 0.6 collective-permute-start.27
  85.3 4.9 %collective-permute-done.37 = bf16[256,128]{1,0:T(8,128)(2,1)S(1)} collective-permute-done((bf16[256,128]{1,0:T(8,128)(2,1)S(1)}, bf16[256,128]{1,0:T(8,128)(2,1)S(1)}, u32[]{:S(2)}, u32[]{:S(2)}) %collective-permute-start.37) | collective-permute-done | bytes 65568 | tf_op jit(solution)/shard_map/gather_range/ppermute | solution.py:26
  90.3 1.3 %collective-permute-done.34 = bf16[256,128]{1,0:T(8,128)(2,1)S(1)} collective-permute-done((bf16[256,128]{1,0:T(8,128)(2,1)S(1)}, bf16[256,128]{1,0:T(8,128)(2,1)S(1)}, u32[]{:S(2)}, u32[]{:S(2)}) %collective-permute-start.34) | collective-permute-done | bytes 65568 | tf_op jit(solution)/shard_map/gather_range/ppermute | solution.py:26
  91.6 0.6 collective-permute-start.35
  92.2 0.4 collective-permute-done.31
  92.7 1.2 %collective-permute-start.41 = (bf16[512,128]{1,0:T(8,128)(2,1)S(1)}, bf16[512,128]{1,0:T(8,128)(2,1)S(1)}, u32[]{:S(2)}, u32[]{:S(2)}) collective-permute-start(bf16[512,128]{1,0:T(8,128)(2,1)S(1)} %pad_maximum_fusion.14), channel_id=1, source_target_pairs={{0,2},{1,3},{2,0},{3,1},{4,6},{5,7},{6,4},{7,5},{8,10},{9,11},{10,... | collective-permute-start | bytes 393224 | tf_op jit(solution)/shard_map/gather_range/ppermute | solution.py:26
  93.9 0.8 collective-permute-start.32
  94.7 1.3 %collective-permute-start.28 = (f32[128,128]{1,0:T(8,128)S(1)}, f32[128,128]{1,0:T(8,128)S(1)}, u32[]{:S(2)}, u32[]{:S(2)}) collective-permute-start(f32[128,128]{1,0:T(8,128)S(1)} %add.68), channel_id=1, source_target_pairs={{0,4},{1,5},{2,6},{3,7},{4,0},{5,1},{6,2},{7,3},{8,12},{9,13},{10,... | collective-permute-start | bytes 196616 | tf_op jit(solution)/shard_map/gram/ppermute | solution.py:26
  96.0 1.5 %collective-permute-start.29 = (f32[128,128]{1,0:T(8,128)S(1)}, f32[128,128]{1,0:T(8,128)S(1)}, u32[]{:S(2)}, u32[]{:S(2)}) collective-permute-start(f32[128,128]{1,0:T(8,128)S(1)} %add.68), channel_id=1, source_target_pairs={{0,8},{1,9},{2,10},{3,11},{4,12},{5,13},{6,14},{7,15},{8,0},{9,1},... | collective-permute-start | bytes 196616 | tf_op jit(solution)/shard_map/gram/ppermute | solution.py:26
  97.5 0.3 collective-permute-done.35
  97.8 2.2 %collective-permute-start.30 = (f32[128,128]{1,0:T(8,128)S(1)}, f32[128,128]{1,0:T(8,128)S(1)}, u32[]{:S(2)}, u32[]{:S(2)}) collective-permute-start(f32[128,128]{1,0:T(8,128)S(1)} %add.68), channel_id=1, source_target_pairs={{0,12},{1,13},{2,14},{3,15},{4,8},{5,9},{6,10},{7,11},{8,4},{9,5},... | collective-permute-start | bytes 196616 | tf_op jit(solution)/shard_map/gram/ppermute | solution.py:26
  100.0 0.5 collective-permute-start.39
  100.7 1.3 %collective-permute-done.28 = f32[128,128]{1,0:T(8,128)S(1)} collective-permute-done((f32[128,128]{1,0:T(8,128)S(1)}, f32[128,128]{1,0:T(8,128)S(1)}, u32[]{:S(2)}, u32[]{:S(2)}) %collective-permute-start.28) | collective-permute-done | bytes 65568 | tf_op jit(solution)/shard_map/gram/ppermute | solution.py:26
  102.1 0.8 collective-permute-start.42
  102.8 1.5 %collective-permute-start.33 = (bf16[1024,128]{1,0:T(8,128)(2,1)S(1)}, bf16[1024,128]{1,0:T(8,128)(2,1)S(1)}, u32[]{:S(2)}, u32[]{:S(2)}) collective-permute-start(bf16[1024,128]{1,0:T(8,128)(2,1)S(1)} %constant_dynamic-update-slice_fusion.refs_1_), channel_id=1, source_target_pairs={{0,2},{1,3},{2,0},{3,1},{4,6},{5,7},{6,4},{7,5},{8,10},{9,11},{10,... | collective-permute-start | bytes 786440 | tf_op jit(solution)/shard_map/gather_range/ppermute | solution.py:26
  104.6 6.4 %factor.1 = (f32[128,128]{1,0:T(8,128)S(1)}, f32[1024,128]{1,0:T(8,128)}) custom-call(f32[128,128]{1,0:T(8,128)S(1)} %add_add_fusion.gram_ref, f32[1024,128]{1,0:T(8,128)S(1)} %pad_maximum_fusion.range_ref), custom_call_target="tpu_custom_call" | custom-call | flops 10000000 | bytes 20000000 | tf_op jit(solution)/shard_map/factor/pallas_call | solution.py:212
  111.1 1.3 %coords.3.refs_5_ = f32[512,128]{1,0:T(8,128)S(1)} custom-call(s32[1]{0:T(128)} %bitcast.index_ref, bf16[256,16384]{1,0:T(8,128)(2,1)S(1)} %get-tuple-element.22.x_ref, bf16[256,8192]{1,0:T(8,128)(2,1)S(1)} %collective-permute-done.4.refs_0_, bf16[1024,128]{1,0:T(8,128)(2,1)S(1)} %constant_dynamic-update-slice_fusion.refs_1_, ...), custom_call_target="tpu_custom_call" | custom-call | flops 536870912 | bytes 4194304 | tf_op jit(solution)/shard_map/coords/pallas_call | solution.py:130
  112.3 1.4 %collective-permute-done.42.refs_4_ = bf16[1024,128]{1,0:T(8,128)(2,1)S(1)} collective-permute-done((bf16[1024,128]{1,0:T(8,128)(2,1)S(1)}, bf16[1024,128]{1,0:T(8,128)(2,1)S(1)}, u32[]{:S(2)}, u32[]{:S(2)}) %collective-permute-start.42) | collective-permute-done | bytes 262176 | tf_op jit(solution)/shard_map/gather_range/ppermute | solution.py:26
  113.7 1.3 %coords.4.part_ref = f32[512,128]{1,0:T(8,128)S(1)} custom-call(s32[1]{0:T(128)} %bitcast.index_ref, bf16[256,16384]{1,0:T(8,128)(2,1)S(1)} %get-tuple-element.22.x_ref, bf16[256,8192]{1,0:T(8,128)(2,1)S(1)} %collective-permute-done.4.refs_0_, bf16[1024,128]{1,0:T(8,128)(2,1)S(1)} %collective-permute-done.33.refs_1_, ...), custom_call_target="tpu_custom_call" | custom-call | flops 536870912 | bytes 4194304 | tf_op jit(solution)/shard_map/coords/pallas_call | solution.py:130
  115.1 1.3 %collective-permute-done.43.theirs_ref = f32[256,128]{1,0:T(8,128)S(1)} collective-permute-done((f32[256,128]{1,0:T(8,128)S(1)}, f32[256,128]{1,0:T(8,128)S(1)}, u32[]{:S(2)}, u32[]{:S(2)}) %collective-permute-start.43) | collective-permute-done | bytes 131104 | tf_op jit(solution)/shard_map/coords/ppermute | solution.py:26
  116.4 1.0 coords.5
  (80 shorter events, 3.7 us)
Async XLA Ops:
  1.6 10.9 %collective-permute-start = (bf16[256,128]{1,0:T(8,128)(2,1)S(1)}, bf16[256,128]{1,0:T(8,128)(2,1)S(1)}, u32[]{:S(2)}, u32[]{:S(2)}) collective-permute-start(bf16[256,128]{1,0:T(8,128)(2,1)S(1)} %get-tuple-element.53), channel_id=1, source_target_pairs={{0,8},{1,9},{2,10},{3,11},{4,12},{5,13},{6,14},{7,15},{8,0},{9,1},... | collective-permute-start | bytes 196616 | tf_op jit(solution)/shard_map/gather_sketch/ppermute | solution.py:26
  5.7 9.8 %collective-permute-start.1 = (bf16[256,128]{1,0:T(8,128)(2,1)S(1)}, bf16[256,128]{1,0:T(8,128)(2,1)S(1)}, u32[]{:S(2)}, u32[]{:S(2)}) collective-permute-start(bf16[256,128]{1,0:T(8,128)(2,1)S(1)} %get-tuple-element.52), channel_id=1, source_target_pairs={{0,8},{1,9},{2,10},{3,11},{4,12},{5,13},{6,14},{7,15},{8,0},{9,1},... | collective-permute-start | bytes 196616 | tf_op jit(solution)/shard_map/gather_sketch/ppermute | solution.py:26
  5.8 11.2 %collective-permute-start.2 = (bf16[256,128]{1,0:T(8,128)(2,1)S(1)}, bf16[256,128]{1,0:T(8,128)(2,1)S(1)}, u32[]{:S(2)}, u32[]{:S(2)}) collective-permute-start(bf16[256,128]{1,0:T(8,128)(2,1)S(1)} %get-tuple-element.54), channel_id=1, source_target_pairs={{0,8},{1,9},{2,10},{3,11},{4,12},{5,13},{6,14},{7,15},{8,0},{9,1},... | collective-permute-start | bytes 196616 | tf_op jit(solution)/shard_map/gather_sketch/ppermute | solution.py:26
  8.6 9.2 %collective-permute-start.3 = (bf16[256,128]{1,0:T(8,128)(2,1)S(1)}, bf16[256,128]{1,0:T(8,128)(2,1)S(1)}, u32[]{:S(2)}, u32[]{:S(2)}) collective-permute-start(bf16[256,128]{1,0:T(8,128)(2,1)S(1)} %get-tuple-element.51), channel_id=1, source_target_pairs={{0,8},{1,9},{2,10},{3,11},{4,12},{5,13},{6,14},{7,15},{8,0},{9,1},... | collective-permute-start | bytes 196616 | tf_op jit(solution)/shard_map/gather_sketch/ppermute | solution.py:26
  17.8 13.2 %collective-permute-start.4 = (bf16[256,8192]{1,0:T(8,128)(2,1)S(1)}, bf16[256,8192]{1,0:T(8,128)(2,1)S(1)}, u32[]{:S(2)}, u32[]{:S(2)}) collective-permute-start(bf16[256,8192]{1,0:T(8,128)(2,1)S(1)} %get-tuple-element.24), channel_id=1, source_target_pairs={{0,1},{1,0},{2,3},{3,2},{4,5},{5,4},{6,7},{7,6},{8,9},{9,8},{10,11... | collective-permute-start | bytes 12582920 | tf_op jit(solution)/shard_map/split_features/ppermute | solution.py:26
  17.8 11.0 %collective-permute-start.5 = (bf16[512,128]{1,0:T(8,128)(2,1)S(1)}, bf16[512,128]{1,0:T(8,128)(2,1)S(1)}, u32[]{:S(2)}, u32[]{:S(2)}) collective-permute-start(bf16[512,128]{1,0:T(8,128)(2,1)S(1)} %pad_maximum_fusion.7), channel_id=1, source_target_pairs={{0,4},{1,5},{2,6},{3,7},{4,0},{5,1},{6,2},{7,3},{8,12},{9,13},{10,... | collective-permute-start | bytes 393224 | tf_op jit(solution)/shard_map/gather_sketch/ppermute | solution.py:26
  18.4 8.1 %collective-permute-start.9 = (bf16[512,128]{1,0:T(8,128)(2,1)S(1)}, bf16[512,128]{1,0:T(8,128)(2,1)S(1)}, u32[]{:S(2)}, u32[]{:S(2)}) collective-permute-start(bf16[512,128]{1,0:T(8,128)(2,1)S(1)} %pad_maximum_fusion.9), channel_id=1, source_target_pairs={{0,4},{1,5},{2,6},{3,7},{4,0},{5,1},{6,2},{7,3},{8,12},{9,13},{10,... | collective-permute-start | bytes 393224 | tf_op jit(solution)/shard_map/gather_sketch/ppermute | solution.py:26
  20.0 8.4 %collective-permute-start.11 = (bf16[512,128]{1,0:T(8,128)(2,1)S(1)}, bf16[512,128]{1,0:T(8,128)(2,1)S(1)}, u32[]{:S(2)}, u32[]{:S(2)}) collective-permute-start(bf16[512,128]{1,0:T(8,128)(2,1)S(1)} %pad_maximum_fusion.10), channel_id=1, source_target_pairs={{0,2},{1,3},{2,0},{3,1},{4,6},{5,7},{6,4},{7,5},{8,10},{9,11},{10,... | collective-permute-start | bytes 393224 | tf_op jit(solution)/shard_map/gather_sketch/ppermute | solution.py:26
  21.7 7.7 %collective-permute-start.7 = (bf16[512,128]{1,0:T(8,128)(2,1)S(1)}, bf16[512,128]{1,0:T(8,128)(2,1)S(1)}, u32[]{:S(2)}, u32[]{:S(2)}) collective-permute-start(bf16[512,128]{1,0:T(8,128)(2,1)S(1)} %pad_maximum_fusion.8), channel_id=1, source_target_pairs={{0,2},{1,3},{2,0},{3,1},{4,6},{5,7},{6,4},{7,5},{8,10},{9,11},{10,... | collective-permute-start | bytes 393224 | tf_op jit(solution)/shard_map/gather_sketch/ppermute | solution.py:26
  26.6 9.3 %collective-permute-start.10 = (bf16[1024,128]{1,0:T(8,128)(2,1)S(1)}, bf16[1024,128]{1,0:T(8,128)(2,1)S(1)}, u32[]{:S(2)}, u32[]{:S(2)}) collective-permute-start(bf16[1024,128]{1,0:T(8,128)(2,1)S(1)} %pad_maximum_fusion.3.refs_3_), channel_id=1, source_target_pairs={{0,2},{1,3},{2,0},{3,1},{4,6},{5,7},{6,4},{7,5},{8,10},{9,11},{10,... | collective-permute-start | bytes 786440 | tf_op jit(solution)/shard_map/gather_sketch/ppermute | solution.py:26
  28.4 9.3 %collective-permute-start.12 = (bf16[1024,128]{1,0:T(8,128)(2,1)S(1)}, bf16[1024,128]{1,0:T(8,128)(2,1)S(1)}, u32[]{:S(2)}, u32[]{:S(2)}) collective-permute-start(bf16[1024,128]{1,0:T(8,128)(2,1)S(1)} %pad_maximum_fusion.4.refs_4_), channel_id=1, source_target_pairs={{0,4},{1,5},{2,6},{3,7},{4,0},{5,1},{6,2},{7,3},{8,12},{9,13},{10,... | collective-permute-start | bytes 786440 | tf_op jit(solution)/shard_map/gather_sketch/ppermute | solution.py:26
  28.8 11.4 %collective-permute-start.6 = (bf16[1024,128]{1,0:T(8,128)(2,1)S(1)}, bf16[1024,128]{1,0:T(8,128)(2,1)S(1)}, u32[]{:S(2)}, u32[]{:S(2)}) collective-permute-start(bf16[1024,128]{1,0:T(8,128)(2,1)S(1)} %pad_maximum_fusion.1.refs_1_), channel_id=1, source_target_pairs={{0,2},{1,3},{2,0},{3,1},{4,6},{5,7},{6,4},{7,5},{8,10},{9,11},{10,... | collective-permute-start | bytes 786440 | tf_op jit(solution)/shard_map/gather_sketch/ppermute | solution.py:26
  29.5 12.3 %collective-permute-start.8 = (bf16[1024,128]{1,0:T(8,128)(2,1)S(1)}, bf16[1024,128]{1,0:T(8,128)(2,1)S(1)}, u32[]{:S(2)}, u32[]{:S(2)}) collective-permute-start(bf16[1024,128]{1,0:T(8,128)(2,1)S(1)} %pad_maximum_fusion.2.refs_2_), channel_id=1, source_target_pairs={{0,4},{1,5},{2,6},{3,7},{4,0},{5,1},{6,2},{7,3},{8,12},{9,13},{10,... | collective-permute-start | bytes 786440 | tf_op jit(solution)/shard_map/gather_sketch/ppermute | solution.py:26
  43.0 1.6 %collective-permute-start.13 = (f32[512,128]{1,0:T(8,128)S(1)}, f32[512,128]{1,0:T(8,128)S(1)}, u32[]{:S(2)}, u32[]{:S(2)}) collective-permute-start(f32[512,128]{1,0:T(8,128)S(1)} %sketched.3), channel_id=1, source_target_pairs={{0,1},{1,0},{2,3},{3,2},{4,5},{5,4},{6,7},{7,6},{8,9},{9,8},{10,11... | collective-permute-start | bytes 786440 | tf_op jit(solution)/shard_map/sketched/ppermute | solution.py:26
  45.6 9.2 %collective-permute-start.23 = (bf16[1024,128]{1,0:T(8,128)(2,1)S(1)}, bf16[1024,128]{1,0:T(8,128)(2,1)S(1)}, u32[]{:S(2)}, u32[]{:S(2)}) collective-permute-start(bf16[1024,128]{1,0:T(8,128)(2,1)S(1)} %get-tuple-element.32), channel_id=1, source_target_pairs={{0,4},{1,5},{2,6},{3,7},{4,0},{5,1},{6,2},{7,3},{8,12},{9,13},{10,... | collective-permute-start | bytes 786440 | tf_op jit(solution)/shard_map/range/ppermute | solution.py:26
  46.0 9.5 %collective-permute-start.14 = (bf16[1024,128]{1,0:T(8,128)(2,1)S(1)}, bf16[1024,128]{1,0:T(8,128)(2,1)S(1)}, u32[]{:S(2)}, u32[]{:S(2)}) collective-permute-start(bf16[1024,128]{1,0:T(8,128)(2,1)S(1)} %get-tuple-element.26), channel_id=1, source_target_pairs={{0,2},{1,3},{2,0},{3,1},{4,6},{5,7},{6,4},{7,5},{8,10},{9,11},{10,... | collective-permute-start | bytes 786440 | tf_op jit(solution)/shard_map/range/ppermute | solution.py:26
  46.5 13.9 %collective-permute-start.17 = (bf16[1024,128]{1,0:T(8,128)(2,1)S(1)}, bf16[1024,128]{1,0:T(8,128)(2,1)S(1)}, u32[]{:S(2)}, u32[]{:S(2)}) collective-permute-start(bf16[1024,128]{1,0:T(8,128)(2,1)S(1)} %get-tuple-element.28), channel_id=1, source_target_pairs={{0,4},{1,5},{2,6},{3,7},{4,0},{5,1},{6,2},{7,3},{8,12},{9,13},{10,... | collective-permute-start | bytes 786440 | tf_op jit(solution)/shard_map/range/ppermute | solution.py:26
  48.0 13.1 %collective-permute-start.20 = (bf16[1024,128]{1,0:T(8,128)(2,1)S(1)}, bf16[1024,128]{1,0:T(8,128)(2,1)S(1)}, u32[]{:S(2)}, u32[]{:S(2)}) collective-permute-start(bf16[1024,128]{1,0:T(8,128)(2,1)S(1)} %get-tuple-element.30), channel_id=1, source_target_pairs={{0,2},{1,3},{2,0},{3,1},{4,6},{5,7},{6,4},{7,5},{8,10},{9,11},{10,... | collective-permute-start | bytes 786440 | tf_op jit(solution)/shard_map/range/ppermute | solution.py:26
  55.0 8.0 %collective-permute-start.24 = (bf16[512,128]{1,0:T(8,128)(2,1)S(1)}, bf16[512,128]{1,0:T(8,128)(2,1)S(1)}, u32[]{:S(2)}, u32[]{:S(2)}) collective-permute-start(bf16[512,128]{1,0:T(8,128)(2,1)S(1)} %fusion.18), channel_id=1, source_target_pairs={{0,2},{1,3},{2,0},{3,1},{4,6},{5,7},{6,4},{7,5},{8,10},{9,11},{10,... | collective-permute-start | bytes 393224 | tf_op jit(solution)/shard_map/range/ppermute | solution.py:26
  55.7 11.5 %collective-permute-start.15 = (bf16[512,128]{1,0:T(8,128)(2,1)S(1)}, bf16[512,128]{1,0:T(8,128)(2,1)S(1)}, u32[]{:S(2)}, u32[]{:S(2)}) collective-permute-start(bf16[512,128]{1,0:T(8,128)(2,1)S(1)} %fusion.12), channel_id=1, source_target_pairs={{0,4},{1,5},{2,6},{3,7},{4,0},{5,1},{6,2},{7,3},{8,12},{9,13},{10,... | collective-permute-start | bytes 393224 | tf_op jit(solution)/shard_map/range/ppermute | solution.py:26
  60.7 6.8 %collective-permute-start.18 = (bf16[512,128]{1,0:T(8,128)(2,1)S(1)}, bf16[512,128]{1,0:T(8,128)(2,1)S(1)}, u32[]{:S(2)}, u32[]{:S(2)}) collective-permute-start(bf16[512,128]{1,0:T(8,128)(2,1)S(1)} %fusion.14), channel_id=1, source_target_pairs={{0,2},{1,3},{2,0},{3,1},{4,6},{5,7},{6,4},{7,5},{8,10},{9,11},{10,... | collective-permute-start | bytes 393224 | tf_op jit(solution)/shard_map/range/ppermute | solution.py:26
  61.3 9.3 %collective-permute-start.21 = (bf16[512,128]{1,0:T(8,128)(2,1)S(1)}, bf16[512,128]{1,0:T(8,128)(2,1)S(1)}, u32[]{:S(2)}, u32[]{:S(2)}) collective-permute-start(bf16[512,128]{1,0:T(8,128)(2,1)S(1)} %fusion.16), channel_id=1, source_target_pairs={{0,4},{1,5},{2,6},{3,7},{4,0},{5,1},{6,2},{7,3},{8,12},{9,13},{10,... | collective-permute-start | bytes 393224 | tf_op jit(solution)/shard_map/range/ppermute | solution.py:26
  63.2 12.4 %collective-permute-start.25 = (bf16[256,128]{1,0:T(8,128)(2,1)S(1)}, bf16[256,128]{1,0:T(8,128)(2,1)S(1)}, u32[]{:S(2)}, u32[]{:S(2)}) collective-permute-start(bf16[256,128]{1,0:T(8,128)(2,1)S(1)} %fusion.31), channel_id=1, source_target_pairs={{0,8},{1,9},{2,10},{3,11},{4,12},{5,13},{6,14},{7,15},{8,0},{9,1},... | collective-permute-start | bytes 196616 | tf_op jit(solution)/shard_map/range/ppermute | solution.py:26
  67.4 9.6 %collective-permute-start.16 = (bf16[256,128]{1,0:T(8,128)(2,1)S(1)}, bf16[256,128]{1,0:T(8,128)(2,1)S(1)}, u32[]{:S(2)}, u32[]{:S(2)}) collective-permute-start(bf16[256,128]{1,0:T(8,128)(2,1)S(1)} %fusion.25), channel_id=1, source_target_pairs={{0,8},{1,9},{2,10},{3,11},{4,12},{5,13},{6,14},{7,15},{8,0},{9,1},... | collective-permute-start | bytes 196616 | tf_op jit(solution)/shard_map/range/ppermute | solution.py:26
  67.6 10.8 %collective-permute-start.19 = (bf16[256,128]{1,0:T(8,128)(2,1)S(1)}, bf16[256,128]{1,0:T(8,128)(2,1)S(1)}, u32[]{:S(2)}, u32[]{:S(2)}) collective-permute-start(bf16[256,128]{1,0:T(8,128)(2,1)S(1)} %fusion.27), channel_id=1, source_target_pairs={{0,8},{1,9},{2,10},{3,11},{4,12},{5,13},{6,14},{7,15},{8,0},{9,1},... | collective-permute-start | bytes 196616 | tf_op jit(solution)/shard_map/range/ppermute | solution.py:26
  70.8 9.6 %collective-permute-start.22 = (bf16[256,128]{1,0:T(8,128)(2,1)S(1)}, bf16[256,128]{1,0:T(8,128)(2,1)S(1)}, u32[]{:S(2)}, u32[]{:S(2)}) collective-permute-start(bf16[256,128]{1,0:T(8,128)(2,1)S(1)} %fusion.29), channel_id=1, source_target_pairs={{0,8},{1,9},{2,10},{3,11},{4,12},{5,13},{6,14},{7,15},{8,0},{9,1},... | collective-permute-start | bytes 196616 | tf_op jit(solution)/shard_map/range/ppermute | solution.py:26
  75.7 16.6 %collective-permute-start.40 = (bf16[256,128]{1,0:T(8,128)(2,1)S(1)}, bf16[256,128]{1,0:T(8,128)(2,1)S(1)}, u32[]{:S(2)}, u32[]{:S(2)}) collective-permute-start(bf16[256,128]{1,0:T(8,128)(2,1)S(1)} %get-tuple-element.41), channel_id=1, source_target_pairs={{0,8},{1,9},{2,10},{3,11},{4,12},{5,13},{6,14},{7,15},{8,0},{9,1},... | collective-permute-start | bytes 196616 | tf_op jit(solution)/shard_map/gather_range/ppermute | solution.py:26
  81.5 3.2 %collective-permute-start.26 = (f32[128,128]{1,0:T(8,128)S(1)}, f32[128,128]{1,0:T(8,128)S(1)}, u32[]{:S(2)}, u32[]{:S(2)}) collective-permute-start(f32[128,128]{1,0:T(8,128)S(1)} %fusion.33), channel_id=1, source_target_pairs={{0,1},{1,0},{2,3},{3,2},{4,5},{5,4},{6,7},{7,6},{8,9},{9,8},{10,11... | collective-permute-start | bytes 196616 | tf_op jit(solution)/shard_map/gram/ppermute | solution.py:26
  81.6 8.7 %collective-permute-start.37 = (bf16[256,128]{1,0:T(8,128)(2,1)S(1)}, bf16[256,128]{1,0:T(8,128)(2,1)S(1)}, u32[]{:S(2)}, u32[]{:S(2)}) collective-permute-start(bf16[256,128]{1,0:T(8,128)(2,1)S(1)} %get-tuple-element.43), channel_id=1, source_target_pairs={{0,8},{1,9},{2,10},{3,11},{4,12},{5,13},{6,14},{7,15},{8,0},{9,1},... | collective-permute-start | bytes 196616 | tf_op jit(solution)/shard_map/gather_range/ppermute | solution.py:26
  81.6 10.0 %collective-permute-start.34 = (bf16[256,128]{1,0:T(8,128)(2,1)S(1)}, bf16[256,128]{1,0:T(8,128)(2,1)S(1)}, u32[]{:S(2)}, u32[]{:S(2)}) collective-permute-start(bf16[256,128]{1,0:T(8,128)(2,1)S(1)} %get-tuple-element.45), channel_id=1, source_target_pairs={{0,8},{1,9},{2,10},{3,11},{4,12},{5,13},{6,14},{7,15},{8,0},{9,1},... | collective-permute-start | bytes 196616 | tf_op jit(solution)/shard_map/gather_range/ppermute | solution.py:26
  84.6 8.1 %collective-permute-start.31 = (bf16[256,128]{1,0:T(8,128)(2,1)S(1)}, bf16[256,128]{1,0:T(8,128)(2,1)S(1)}, u32[]{:S(2)}, u32[]{:S(2)}) collective-permute-start(bf16[256,128]{1,0:T(8,128)(2,1)S(1)} %get-tuple-element.47), channel_id=1, source_target_pairs={{0,8},{1,9},{2,10},{3,11},{4,12},{5,13},{6,14},{7,15},{8,0},{9,1},... | collective-permute-start | bytes 196616 | tf_op jit(solution)/shard_map/gather_range/ppermute | solution.py:26
  84.7 7.9 %collective-permute-start.27 = (f32[128,128]{1,0:T(8,128)S(1)}, f32[128,128]{1,0:T(8,128)S(1)}, u32[]{:S(2)}, u32[]{:S(2)}) collective-permute-start(f32[128,128]{1,0:T(8,128)S(1)} %add.67), channel_id=1, source_target_pairs={{0,2},{1,3},{2,0},{3,1},{4,6},{5,7},{6,4},{7,5},{8,10},{9,11},{10,... | collective-permute-start | bytes 196616 | tf_op jit(solution)/shard_map/gram/ppermute | solution.py:26
  90.2 5.8 %collective-permute-start.38 = (bf16[512,128]{1,0:T(8,128)(2,1)S(1)}, bf16[512,128]{1,0:T(8,128)(2,1)S(1)}, u32[]{:S(2)}, u32[]{:S(2)}) collective-permute-start(bf16[512,128]{1,0:T(8,128)(2,1)S(1)} %pad_maximum_fusion.13), channel_id=1, source_target_pairs={{0,4},{1,5},{2,6},{3,7},{4,0},{5,1},{6,2},{7,3},{8,12},{9,13},{10,... | collective-permute-start | bytes 393224 | tf_op jit(solution)/shard_map/gather_range/ppermute | solution.py:26
  91.6 6.2 %collective-permute-start.35 = (bf16[512,128]{1,0:T(8,128)(2,1)S(1)}, bf16[512,128]{1,0:T(8,128)(2,1)S(1)}, u32[]{:S(2)}, u32[]{:S(2)}) collective-permute-start(bf16[512,128]{1,0:T(8,128)(2,1)S(1)} %pad_maximum_fusion.12), channel_id=1, source_target_pairs={{0,2},{1,3},{2,0},{3,1},{4,6},{5,7},{6,4},{7,5},{8,10},{9,11},{10,... | collective-permute-start | bytes 393224 | tf_op jit(solution)/shard_map/gather_range/ppermute | solution.py:26
  92.7 7.3 %collective-permute-start.41 = (bf16[512,128]{1,0:T(8,128)(2,1)S(1)}, bf16[512,128]{1,0:T(8,128)(2,1)S(1)}, u32[]{:S(2)}, u32[]{:S(2)}) collective-permute-start(bf16[512,128]{1,0:T(8,128)(2,1)S(1)} %pad_maximum_fusion.14), channel_id=1, source_target_pairs={{0,2},{1,3},{2,0},{3,1},{4,6},{5,7},{6,4},{7,5},{8,10},{9,11},{10,... | collective-permute-start | bytes 393224 | tf_op jit(solution)/shard_map/gather_range/ppermute | solution.py:26
  93.9 6.7 %collective-permute-start.32 = (bf16[512,128]{1,0:T(8,128)(2,1)S(1)}, bf16[512,128]{1,0:T(8,128)(2,1)S(1)}, u32[]{:S(2)}, u32[]{:S(2)}) collective-permute-start(bf16[512,128]{1,0:T(8,128)(2,1)S(1)} %pad_maximum_fusion.11), channel_id=1, source_target_pairs={{0,4},{1,5},{2,6},{3,7},{4,0},{5,1},{6,2},{7,3},{8,12},{9,13},{10,... | collective-permute-start | bytes 393224 | tf_op jit(solution)/shard_map/gather_range/ppermute | solution.py:26
  94.7 7.4 %collective-permute-start.28 = (f32[128,128]{1,0:T(8,128)S(1)}, f32[128,128]{1,0:T(8,128)S(1)}, u32[]{:S(2)}, u32[]{:S(2)}) collective-permute-start(f32[128,128]{1,0:T(8,128)S(1)} %add.68), channel_id=1, source_target_pairs={{0,4},{1,5},{2,6},{3,7},{4,0},{5,1},{6,2},{7,3},{8,12},{9,13},{10,... | collective-permute-start | bytes 196616 | tf_op jit(solution)/shard_map/gram/ppermute | solution.py:26
  96.0 6.8 %collective-permute-start.29 = (f32[128,128]{1,0:T(8,128)S(1)}, f32[128,128]{1,0:T(8,128)S(1)}, u32[]{:S(2)}, u32[]{:S(2)}) collective-permute-start(f32[128,128]{1,0:T(8,128)S(1)} %add.68), channel_id=1, source_target_pairs={{0,8},{1,9},{2,10},{3,11},{4,12},{5,13},{6,14},{7,15},{8,0},{9,1},... | collective-permute-start | bytes 196616 | tf_op jit(solution)/shard_map/gram/ppermute | solution.py:26
  97.8 6.8 %collective-permute-start.30 = (f32[128,128]{1,0:T(8,128)S(1)}, f32[128,128]{1,0:T(8,128)S(1)}, u32[]{:S(2)}, u32[]{:S(2)}) collective-permute-start(f32[128,128]{1,0:T(8,128)S(1)} %add.68), channel_id=1, source_target_pairs={{0,12},{1,13},{2,14},{3,15},{4,8},{5,9},{6,10},{7,11},{8,4},{9,5},... | collective-permute-start | bytes 196616 | tf_op jit(solution)/shard_map/gram/ppermute | solution.py:26
  100.0 12.3 %collective-permute-start.39 = (bf16[1024,128]{1,0:T(8,128)(2,1)S(1)}, bf16[1024,128]{1,0:T(8,128)(2,1)S(1)}, u32[]{:S(2)}, u32[]{:S(2)}) collective-permute-start(bf16[1024,128]{1,0:T(8,128)(2,1)S(1)} %pad_maximum_fusion.6.refs_3_), channel_id=1, source_target_pairs={{0,2},{1,3},{2,0},{3,1},{4,6},{5,7},{6,4},{7,5},{8,10},{9,11},{10,... | collective-permute-start | bytes 786440 | tf_op jit(solution)/shard_map/gather_range/ppermute | solution.py:26
  100.6 11.7 %collective-permute-start.36 = (bf16[1024,128]{1,0:T(8,128)(2,1)S(1)}, bf16[1024,128]{1,0:T(8,128)(2,1)S(1)}, u32[]{:S(2)}, u32[]{:S(2)}) collective-permute-start(bf16[1024,128]{1,0:T(8,128)(2,1)S(1)} %pad_maximum_fusion.5.refs_2_), channel_id=1, source_target_pairs={{0,4},{1,5},{2,6},{3,7},{4,0},{5,1},{6,2},{7,3},{8,12},{9,13},{10,... | collective-permute-start | bytes 786440 | tf_op jit(solution)/shard_map/gather_range/ppermute | solution.py:26
  102.1 11.6 %collective-permute-start.42 = (bf16[1024,128]{1,0:T(8,128)(2,1)S(1)}, bf16[1024,128]{1,0:T(8,128)(2,1)S(1)}, u32[]{:S(2)}, u32[]{:S(2)}) collective-permute-start(bf16[1024,128]{1,0:T(8,128)(2,1)S(1)} %constant_dynamic-update-slice_fusion.2.refs_4_), channel_id=1, source_target_pairs={{0,4},{1,5},{2,6},{3,7},{4,0},{5,1},{6,2},{7,3},{8,12},{9,13},{10,... | collective-permute-start | bytes 786440 | tf_op jit(solution)/shard_map/gather_range/ppermute | solution.py:26
  102.8 10.9 %collective-permute-start.33 = (bf16[1024,128]{1,0:T(8,128)(2,1)S(1)}, bf16[1024,128]{1,0:T(8,128)(2,1)S(1)}, u32[]{:S(2)}, u32[]{:S(2)}) collective-permute-start(bf16[1024,128]{1,0:T(8,128)(2,1)S(1)} %constant_dynamic-update-slice_fusion.refs_1_), channel_id=1, source_target_pairs={{0,2},{1,3},{2,0},{3,1},{4,6},{5,7},{6,4},{7,5},{8,10},{9,11},{10,... | collective-permute-start | bytes 786440 | tf_op jit(solution)/shard_map/gather_range/ppermute | solution.py:26
  115.0 1.4 %collective-permute-start.43 = (f32[256,128]{1,0:T(8,128)S(1)}, f32[256,128]{1,0:T(8,128)S(1)}, u32[]{:S(2)}, u32[]{:S(2)}) collective-permute-start(f32[256,128]{1,0:T(8,128)S(1)} %slice.110), channel_id=1, source_target_pairs={{0,1},{1,0},{2,3},{3,2},{4,5},{5,4},{6,7},{7,6},{8,9},{9,8},{10,11... | collective-permute-start | bytes 393224 | tf_op jit(solution)/shard_map/coords/ppermute | solution.py:26

commit v4 on v3

--- a/solution.py
+++ b/solution.py
@@ -17,9 +17,10 @@
 
 X_BIT, ZLO, ZHI = 1, 2, 4
 HLX, HXL, LHX = (ZHI, ZLO, X_BIT), (ZHI, X_BIT, ZLO), (ZLO, ZHI, X_BIT)
-PIECES = ((2, HLX), (2, HXL), (2, HLX), (2, HXL))
+SKETCH_PIECES = ((2, HXL, True), (2, HLX, False), (2, HXL, False))
+RANGE_PIECES = ((2, HLX, False), (2, HXL, False), (2, LHX, False), (2, HXL, False))
 LOADS, PARTS = 8, 1
-NEAR, FAR = 0, 1
+TIED = 2
 
 
 def swap(value, bit, n):
@@ -33,11 +34,12 @@
     return near, [owner ^ bits[-1] for owner in near]
 
 
-def layout(width):
+def layout(width, pieces):
     place, out = 0, []
-    for share, order in PIECES:
-        out.append((place, width * share // 8, owners(order)))
-        place += width * share // 8
+    for share, order, shared in pieces:
+        size = width * share // 8
+        out.append((place, size, owners(order)))
+        place += size * (2 if shared else 1)
     return out
 
 
@@ -100,68 +102,71 @@
     )(index, pltpu.with_memory_space_constraint(x, pltpu.HBM))
 
 
-def tokens(place, owner, start, size, x_ref, other_refs):
-    index_ref, width = place
-    block = jnp.bitwise_xor(index_ref[0], 2 * owner)
+def tokens(index_ref, group_ref, width, entry, j, x_ref, other_refs):
+    owner, start, size, flip = entry
+    block = jnp.bitwise_xor(index_ref[0], 2 * owner[j])
+    if flip is not None:
+        start = start + jnp.bitwise_xor(group_ref[0], flip) * size
     mine = x_ref[:, pl.ds(pl.multiple_of(block * width + start, 128), size)]
     where = pl.ds(pl.multiple_of(block // 2 * width + start, 128), size)
     return jnp.concatenate([mine] + [ref[:, where] for ref in other_refs], axis=0)
 
 
-def project_kernel(width, which, has_init, index_ref, x_ref, *refs):
+def project_kernel(width, entries, has_init, index_ref, group_ref, x_ref, *refs):
     others, refs, out_ref = refs[:PARTS], refs[PARTS:-1], refs[-1]
-    count = len(PIECES)
-    total = refs[count][...] if has_init else None
+    total = refs[len(entries)][...] if has_init else None
     for j in range(4):
-        left, block = [], []
-        for ref, (start, size, lists) in zip(refs, layout(width)):
-            left.append(tokens((index_ref, width), lists[which][j], start, size, x_ref, others))
-            block.append(ref[j * size : (j + 1) * size, :])
-        left, block = jnp.concatenate(left, axis=1), jnp.concatenate(block, axis=0)
-        term = jnp.dot(left, block, preferred_element_type=F32)
+        left = [tokens(index_ref, group_ref, width, entry, j, x_ref, others) for entry in entries]
+        block = [ref[j * entry[2] : (j + 1) * entry[2], :] for ref, entry in zip(refs, entries)]
+        term = jnp.dot(
+            jnp.concatenate(left, axis=1), jnp.concatenate(block, axis=0), preferred_element_type=F32
+        )
         total = term if total is None else total + term
     out_ref[...] = total
 
 
-def project(place, which, x, others, pieces, init=None):
-    rows, rank = x.shape[0], pieces[0].shape[1]
-    depth = sum(piece.shape[0] for piece in pieces)
+def project(place, entries, x, others, arrays, init=None):
+    index, group, width = place
+    rows, rank = x.shape[0], arrays[0].shape[1]
+    depth = sum(array.shape[0] for array in arrays)
     extra = [] if init is None else [init]
     return pl.pallas_call(
-        functools.partial(project_kernel, place[1], which, init is not None),
-        in_specs=[SMEM] + [VMEM] * (1 + PARTS + len(pieces) + len(extra)),
+        functools.partial(project_kernel, width, entries, init is not None),
+        in_specs=[SMEM] * 2 + [VMEM] * (1 + PARTS + len(arrays) + len(extra)),
         out_specs=VMEM,
         out_shape=jax.ShapeDtypeStruct((2 * rows, rank), F32),
         compiler_params=PARAMS,
         cost_estimate=pl.CostEstimate(
             flops=4 * rows * depth * rank, bytes_accessed=4 * rows * depth, transcendentals=0
         ),
-    )(place[0], pinned(x), *map(pinned, others), *pieces, *extra)
-
-
-def spread_kernel(width, which, index_ref, x_ref, *refs):
+    )(index, group, pinned(x), *map(pinned, others), *arrays, *extra)
+
+
+def spread_kernel(width, entries, coded, index_ref, group_ref, x_ref, *refs):
     others, y_ref, outs = refs[:PARTS], refs[PARTS], refs[PARTS + 1 :]
     turned = y_ref[...].astype(F32).T.astype(BF16)
-    for out, (start, size, lists) in zip(outs, layout(width)):
+    for out, entry in zip(outs, entries):
+        size = entry[2]
         for j in range(4):
-            right = tokens((index_ref, width), lists[which][j], start, size, x_ref, others)
+            right = tokens(index_ref, group_ref, width, entry, j, x_ref, others)
             term = jnp.dot(turned, right, preferred_element_type=F32).T
-            out[j * size : (j + 1) * size, :] = encode(term) if which == FAR else term
-
-
-def spread(place, which, x, others, y):
+            out[j * size : (j + 1) * size, :] = encode(term) if coded else term
+
+
+def spread(place, entries, coded, x, others, y):
+    index, group, width = place
     rows, rank = x.shape[0], y.shape[1]
-    sizes = [size for _, size, _ in layout(place[1])]
-    return pl.pallas_call(
-        functools.partial(spread_kernel, place[1], which),
-        in_specs=[SMEM] + [VMEM] * (2 + PARTS),
+    sizes = [entry[2] for entry in entries]
+    return pl.pallas_call(
+        functools.partial(spread_kernel, width, entries, coded),
+        in_specs=[SMEM] * 2 + [VMEM] * (2 + PARTS),
         out_specs=[VMEM] * len(sizes),
-        out_shape=[jax.ShapeDtypeStruct((4 * size, rank), BF16 if which == FAR else F32) for size in sizes],
+        out_shape=[jax.ShapeDtypeStruct((4 * size, rank), BF16 if coded else F32) for size in sizes],
         compiler_params=PARAMS,
         cost_estimate=pl.CostEstimate(
             flops=16 * rows * sum(sizes) * rank, bytes_accessed=16 * rows * sum(sizes), transcendentals=0
         ),
-    )(place[0], pinned(x), *map(pinned, others), y)
+    )(index, group, pinned(x), *map(pinned, others), y)
 
 
 def factor_kernel(scale, gram_ref, range_ref, out_ref, basis_ref):
@@ -243,62 +248,79 @@
 
 def shards(n, activations, sketch):
     x, rows = activations, activations.shape[0]
-    width = sketch.shape[1]
+    width, rank = sketch.shape[1:]
     depth = n * width
-    index = lax.axis_index("tok").astype(jnp.int32).reshape(1)
-    place = (index, width)
-    orders = [order for _, order in PIECES]
-    every = range(len(PIECES))
+    index, group = (lax.axis_index(axis).astype(jnp.int32).reshape(1) for axis in ("tok", "groups"))
+    place = (index, group, width)
+
+    def across(value):
+        return lax.ppermute(value, "groups", [(0, 1), (1, 0)])
 
     with jax.named_scope("gather_sketch"):
-        held = [sketch[0, start : start + size] for start, size, _ in layout(width)]
-        came = [swap(held[p], 2 * orders[p][0], n) for p in every]
+        pieces = layout(width, SKETCH_PIECES)
+        held = []
+        for (start, size, _), (_, _, shared) in zip(pieces, SKETCH_PIECES):
+            first = start + (group[0] * size if shared else 0)
+            held.append(lax.dynamic_slice(sketch[0], (first, 0), (size, rank)))
+        came = [swap(held[p], 2 * order[0], n) for p, (_, order, _) in enumerate(SKETCH_PIECES)]
     with jax.named_scope("split_features"):
         x, norm, *others = load(index, x, width)
-        others = lax.optimization_barrier((*others, *came))[:PARTS]
+        others = lax.optimization_barrier((*others, *came[:TIED]))[:PARTS]
         others = [swap(part, 1, n) for part in others]
     with jax.named_scope("gather_sketch"):
-        held = [jnp.concatenate([held[p], came[p]]) for p in every]
-        held = [jnp.concatenate([held[p], swap(held[p], 2 * orders[p][1], n)]) for p in every]
-        came = [swap(held[p], 2 * orders[p][2], n) for p in every]
+        near, near_rows, far, far_rows = [], [], [], []
+        for p, (share, order, shared) in enumerate(SKETCH_PIECES):
+            start, size, (near_owners, far_owners) = pieces[p]
+            own = 0 if shared else None
+            first = jnp.concatenate([held[p], came[p]])
+            array = jnp.concatenate([first, swap(first, 2 * order[1], n)])
+            last = swap(array, 2 * order[2], n)
+            near.append(array)
+            near_rows.append((near_owners, start, size, own))
+            far.append(last)
+            far_rows.append((far_owners, start, size, own))
+            if shared:
+                far += [across(array), across(last)]
+                far_rows += [(near_owners, start, size, 1), (far_owners, start, size, 1)]
     with jax.named_scope("sketched"):
-        part = project(place, NEAR, x, others, held)
-        part = project(place, FAR, x, others, came, part)
+        part = project(place, near_rows, x, others, near)
+        part = project(place, far_rows, x, others, far, part)
         theirs = swap(part, 1, n)
         sketched = (part + jnp.concatenate([theirs[rows:], theirs[:rows]])).astype(BF16)
     with jax.named_scope("range"):
-        sent = spread(place, FAR, x, others, sketched)
-        kept = spread(place, NEAR, x, others, sketched)
-        sums = []
+        orders = [order for _, order, _ in RANGE_PIECES]
+        every = range(len(orders))
+        pieces = layout(width, RANGE_PIECES)
+        near_rows = [(near_owners, start, size, None) for start, size, (near_owners, _) in pieces]
+        far_rows = [(far_owners, start, size, None) for start, size, (_, far_owners) in pieces]
+        sent = spread(place, far_rows, True, x, others, sketched)
+        kept = spread(place, near_rows, False, x, others, sketched)
+        sums, held = [], []
         for p in every:
             mine, coded = kept[p], sent[p]
-            for bit in orders[p][::-1]:
+            for bit in orders[p][:0:-1]:
                 total = mine + decode(swap(coded, 2 * bit, n))
                 cut = total.shape[0] // 2
                 mine, coded = total[:cut], encode(total[cut:])
-            sums.append(total)
+            theirs = decode(swap(encode(total), 2 * orders[p][0], n))
+            own = total[:cut] + theirs[cut:]
+            sums.append(own)
+            held.append(jnp.concatenate([own, total[cut:] + theirs[:cut]]).astype(BF16))
         range_rows = jnp.concatenate(sums, axis=0)
     with jax.named_scope("gram"):
         gram = jnp.dot(range_rows.T, range_rows, preferred_element_type=F32, precision=HIGH)
-        grams = [gram]
         for bit in (1, 2):
             gram = gram + swap(gram, bit, n)
-            grams.append(gram)
-        far = [swap(gram, bit, n) for bit in (4, 8, 12)]
-        gram = (gram + far[0]) + (far[1] + far[2])
-        grams += [gram, gram]
+        apart = [swap(gram, bit, n) for bit in (4, 8, 12)]
+        gram = (gram + apart[0]) + (apart[1] + apart[2])
     with jax.named_scope("gather_range"):
-        held = [total.astype(BF16) for total in sums]
-        held = [jnp.concatenate([held[p], swap(held[p], 2 * orders[p][0], n)]) for p in every]
-        held[0] = after(held[0], grams[2])
-        held[-1] = after(held[-1], grams[2])
         held = [jnp.concatenate([held[p], swap(held[p], 2 * orders[p][1], n)]) for p in every]
         came = [swap(held[p], 2 * orders[p][2], n) for p in every]
     with jax.named_scope("factor"):
         inverse, basis = factored(math.sqrt(depth), gram, range_rows)
     with jax.named_scope("coords"):
-        part = project(place, NEAR, x, others, held)
-        part = project(place, FAR, x, others, came, after(part, inverse))
+        part = project(place, near_rows, x, others, held)
+        part = project(place, far_rows, x, others, came, after(part, inverse))
         coords, resid_rms = close(depth, part, swap(part[rows:], 1, n), inverse, norm)
     return basis[None], coords, resid_rms.reshape(rows)
 

time: 118 us -> 110 us (0.932)
  waiting for transfers between devices: 48.9 us -> 44.3 us
  starting transfers between devices: 45.3 us -> 41.6 us
    ppermute x44 -> x37, starting transfers between devices: 45.3 us -> 38.4 us  [swap(): return lax.ppermute(value, 'tok', [(i, i ^ bit) for i in range(n)])]
    ppermute x44 -> x37, waiting for transfers between devices: 48.9 us -> 42.4 us  [swap(): return lax.ppermute(value, 'tok', [(i, i ^ bit) for i in range(n)])]
    ppermute x0 -> x2, starting transfers between devices: none -> 3.2 us  [across(): return lax.ppermute(value, 'groups', [(0, 1), (1, 0)])]
    ppermute x0 -> x2, waiting for transfers between devices: none -> 1.88 us  [across(): return lax.ppermute(value, 'groups', [(0, 1), (1, 0)])]
  transfers between devices with their start and end apart: 44 -> 39, of which waited for: 24 -> 24; matrix products, arithmetic and copies ran while one was open for 3% -> 2% of each run, Pallas kernels for 12% -> 12%
where the time goes in v4:
time: 110 us; the launch traced here: 109 us
  waiting for transfers between devices  44.3 us (40%)
  starting transfers between devices  41.6 us (38%)
  Pallas kernels  18 us (16%)
  other arithmetic  2.52 us (2%)
    ppermute x37, waiting for transfers between devices, swap(): return lax.ppermute(value, 'tok', [(i, i ^ bit) for i in range(n)])  42.4 us
    ppermute x37, starting transfers between devices, swap(): return lax.ppermute(value, 'tok', [(i, i ^ bit) for i in range(n)])  38.4 us
    pallas_call x1, Pallas kernels, factored(): pl.pallas_call(functools.partial(factor_kernel, scale), in_specs=[VMEM] *...  6.41 us
    pallas_call x4, Pallas kernels, project(): pl.pallas_call(functools.partial(project_kernel, width, entries, init is...  5.02 us
    pallas_call x1, Pallas kernels, load(): pl.pallas_call(functools.partial(load_kernel, width), in_specs=[SMEM, ANY...  3.78 us
    ppermute x2, starting transfers between devices, across(): return lax.ppermute(value, 'groups', [(0, 1), (1, 0)])  3.2 us
  transfers between devices with their start and end apart: 39, of which 24 were waited for; matrix products, arithmetic and copies ran while one was open for 2% of the time, Pallas kernels for 12%

profile of v4, /device:TPU:0, one launch (start us, length us, event | category | flops | bytes accessed | tf_op | source)
XLA Modules:
  0.0 109.4 jit_solution(7151793499446396624)
XLA Ops:
  0.6 0.9 slice_bitcast_fusion
  1.6 4.1 %collective-permute-start = (bf16[256,128]{1,0:T(8,128)(2,1)S(1)}, bf16[256,128]{1,0:T(8,128)(2,1)S(1)}, u32[]{:S(2)}, u32[]{:S(2)}) collective-permute-start(bf16[256,128]{1,0:T(8,128)(2,1)S(1)} %get-tuple-element.60), channel_id=1, source_target_pairs={{0,8},{1,9},{2,10},{3,11},{4,12},{5,13},{6,14},{7,15},{8,0},{9,1},... | collective-permute-start | bytes 196616 | tf_op jit(solution)/shard_map/gather_sketch/ppermute | solution.py:27
  5.7 3.8 %split_features.1 = (bf16[256,16384]{1,0:T(8,128)(2,1)S(1)}, f32[256,128]{1,0:T(8,128)S(1)}, bf16[256,8192]{1,0:T(8,128)(2,1)S(1)}) custom-call(s32[1]{0:T(128)} %bitcast.index_ref, bf16[256,16384]{1,0:T(8,128)(2,1)} %x_ref.1), custom_call_target="tpu_custom_call" | custom-call | flops 8388608 | bytes 16777216 | tf_op jit(solution)/shard_map/split_features/pallas_call | solution.py:94
  9.5 2.6 %collective-permute-done.1 = bf16[256,128]{1,0:T(8,128)(2,1)S(1)} collective-permute-done((bf16[256,128]{1,0:T(8,128)(2,1)S(1)}, bf16[256,128]{1,0:T(8,128)(2,1)S(1)}, u32[]{:S(2)}, u32[]{:S(2)}) %collective-permute-start.1) | collective-permute-done | bytes 65568 | tf_op jit(solution)/shard_map/gather_sketch/ppermute | solution.py:27
  12.1 1.8 %collective-permute-start.3 = (bf16[512,128]{1,0:T(8,128)(2,1)S(1)}, bf16[512,128]{1,0:T(8,128)(2,1)S(1)}, u32[]{:S(2)}, u32[]{:S(2)}) collective-permute-start(bf16[512,128]{1,0:T(8,128)(2,1)S(1)} %pad_maximum_fusion.8), channel_id=1, source_target_pairs={{0,2},{1,3},{2,0},{3,1},{4,6},{5,7},{6,4},{7,5},{8,10},{9,11},{10,... | collective-permute-start | bytes 393224 | tf_op jit(solution)/shard_map/gather_sketch/ppermute | solution.py:27
  14.1 3.7 %collective-permute-start.7 = (bf16[512,128]{1,0:T(8,128)(2,1)S(1)}, bf16[512,128]{1,0:T(8,128)(2,1)S(1)}, u32[]{:S(2)}, u32[]{:S(2)}) collective-permute-start(bf16[512,128]{1,0:T(8,128)(2,1)S(1)} %pad_maximum_fusion.9), channel_id=1, source_target_pairs={{0,4},{1,5},{2,6},{3,7},{4,0},{5,1},{6,2},{7,3},{8,12},{9,13},{10,... | collective-permute-start | bytes 393224 | tf_op jit(solution)/shard_map/gather_sketch/ppermute | solution.py:27
  17.7 0.4 collective-permute-done.3
  18.1 0.6 collective-permute-start.4
  18.8 1.8 %collective-permute-done.9 = bf16[256,128]{1,0:T(8,128)(2,1)S(1)} collective-permute-done((bf16[256,128]{1,0:T(8,128)(2,1)S(1)}, bf16[256,128]{1,0:T(8,128)(2,1)S(1)}, u32[]{:S(2)}, u32[]{:S(2)}) %collective-permute-start.9) | collective-permute-done | bytes 65568 | tf_op jit(solution)/shard_map/gather_sketch/ppermute | solution.py:27
  20.5 0.4 collective-permute-start.10
  21.0 1.7 %collective-permute-start.5 = (bf16[1024,128]{1,0:T(8,128)(2,1)S(1)}, bf16[1024,128]{1,0:T(8,128)(2,1)S(1)}, u32[]{:S(2)}, u32[]{:S(2)}) collective-permute-start(bf16[1024,128]{1,0:T(8,128)(2,1)S(1)} %pad_maximum_fusion.1.refs_1_), channel_id=1, source_target_pairs={{0,16},{16,0},{1,17},{17,1},{2,18},{18,2},{3,19},{19,3},{4,20},{20... | collective-permute-start | bytes 786440 | tf_op jit(solution)/shard_map/gather_sketch/ppermute | solution.py:257
  22.8 1.4 %collective-permute-start.8 = (bf16[1024,128]{1,0:T(8,128)(2,1)S(1)}, bf16[1024,128]{1,0:T(8,128)(2,1)S(1)}, u32[]{:S(2)}, u32[]{:S(2)}) collective-permute-start(bf16[1024,128]{1,0:T(8,128)(2,1)S(1)} %pad_maximum_fusion.2.refs_2_), channel_id=1, source_target_pairs={{0,2},{1,3},{2,0},{3,1},{4,6},{5,7},{6,4},{7,5},{8,10},{9,11},{10,... | collective-permute-start | bytes 786440 | tf_op jit(solution)/shard_map/gather_sketch/ppermute | solution.py:27
  24.3 2.7 %collective-permute-done.10 = bf16[512,128]{1,0:T(8,128)(2,1)S(1)} collective-permute-done((bf16[512,128]{1,0:T(8,128)(2,1)S(1)}, bf16[512,128]{1,0:T(8,128)(2,1)S(1)}, u32[]{:S(2)}, u32[]{:S(2)}) %collective-permute-start.10) | collective-permute-done | bytes 131104 | tf_op jit(solution)/shard_map/gather_sketch/ppermute | solution.py:27
  27.1 1.3 %collective-permute-done.4.refs_1_ = bf16[1024,128]{1,0:T(8,128)(2,1)S(1)} collective-permute-done((bf16[1024,128]{1,0:T(8,128)(2,1)S(1)}, bf16[1024,128]{1,0:T(8,128)(2,1)S(1)}, u32[]{:S(2)}, u32[]{:S(2)}) %collective-permute-start.4) | collective-permute-done | bytes 262176 | tf_op jit(solution)/shard_map/gather_sketch/ppermute | solution.py:27
  28.4 1.5 %collective-permute-start.6 = (bf16[1024,128]{1,0:T(8,128)(2,1)S(1)}, bf16[1024,128]{1,0:T(8,128)(2,1)S(1)}, u32[]{:S(2)}, u32[]{:S(2)}) collective-permute-start(bf16[1024,128]{1,0:T(8,128)(2,1)S(1)} %collective-permute-done.4.refs_1_), channel_id=1, source_target_pairs={{0,16},{16,0},{1,17},{17,1},{2,18},{18,2},{3,19},{19,3},{4,20},{20... | collective-permute-start | bytes 786440 | tf_op jit(solution)/shard_map/gather_sketch/ppermute | solution.py:257
  30.0 1.0 sketched.2.refs_6_
  31.0 0.2 collective-permute-done.8.refs_4_
  31.2 2.2 %collective-permute-done.11.refs_5_ = bf16[1024,128]{1,0:T(8,128)(2,1)S(1)} collective-permute-done((bf16[1024,128]{1,0:T(8,128)(2,1)S(1)}, bf16[1024,128]{1,0:T(8,128)(2,1)S(1)}, u32[]{:S(2)}, u32[]{:S(2)}) %collective-permute-start.11) | collective-permute-done | bytes 262176 | tf_op jit(solution)/shard_map/gather_sketch/ppermute | solution.py:27
  33.4 1.9 %collective-permute-done.6.refs_3_ = bf16[1024,128]{1,0:T(8,128)(2,1)S(1)} collective-permute-done((bf16[1024,128]{1,0:T(8,128)(2,1)S(1)}, bf16[1024,128]{1,0:T(8,128)(2,1)S(1)}, u32[]{:S(2)}, u32[]{:S(2)}) %collective-permute-start.6) | collective-permute-done | bytes 262176 | tf_op jit(solution)/shard_map/gather_sketch/ppermute | solution.py:257
  35.3 1.5 %sketched.3 = f32[512,128]{1,0:T(8,128)S(1)} custom-call(s32[1]{0:T(128)} %bitcast.index_ref, s32[1]{0:T(128)} %bitcast.1.group_ref, bf16[256,16384]{1,0:T(8,128)(2,1)S(1)} %get-tuple-element.20.x_ref, bf16[256,8192]{1,0:T(8,128)(2,1)S(1)} %collective-permute-done.2.refs_0_, bf16[1024,128]{1,0:T(8,128)(2,1)S(1)} %collective-permute-done.4.refs_1_, ...), custom_call_target="tpu_custom_call" | custom-call | flops 671088640 | bytes 5242880 | tf_op jit(solution)/shard_map/sketched/pallas_call | solution.py:133
  36.9 1.5 %collective-permute-done.12 = f32[512,128]{1,0:T(8,128)S(1)} collective-permute-done((f32[512,128]{1,0:T(8,128)S(1)}, f32[512,128]{1,0:T(8,128)S(1)}, u32[]{:S(2)}, u32[]{:S(2)}) %collective-permute-start.12) | collective-permute-done | bytes 262176 | tf_op jit(solution)/shard_map/sketched/ppermute | solution.py:27
  38.5 0.9 range.3
  39.4 0.8 collective-permute-start.22
  40.3 0.4 collective-permute-start.19
  40.7 1.0 collective-permute-start.16
  41.7 1.8 %collective-permute-start.13 = (bf16[1024,128]{1,0:T(8,128)(2,1)S(1)}, bf16[1024,128]{1,0:T(8,128)(2,1)S(1)}, u32[]{:S(2)}, u32[]{:S(2)}) collective-permute-start(bf16[1024,128]{1,0:T(8,128)(2,1)S(1)} %get-tuple-element.24), channel_id=1, source_target_pairs={{0,2},{1,3},{2,0},{3,1},{4,6},{5,7},{6,4},{7,5},{8,10},{9,11},{10,... | collective-permute-start | bytes 786440 | tf_op jit(solution)/shard_map/range/ppermute | solution.py:27
  43.6 0.9 range.2
  44.5 4.2 %collective-permute-done.22 = bf16[1024,128]{1,0:T(8,128)(2,1)S(1)} collective-permute-done((bf16[1024,128]{1,0:T(8,128)(2,1)S(1)}, bf16[1024,128]{1,0:T(8,128)(2,1)S(1)}, u32[]{:S(2)}, u32[]{:S(2)}) %collective-permute-start.22) | collective-permute-done | bytes 262176 | tf_op jit(solution)/shard_map/range/ppermute | solution.py:27
  48.7 0.2 fusion.7
  48.9 0.3 collective-permute-start.23
  49.2 0.3 collective-permute-done.19
  49.5 0.2 fusion.6
  49.7 1.7 %collective-permute-start.20 = (bf16[512,128]{1,0:T(8,128)(2,1)S(1)}, bf16[512,128]{1,0:T(8,128)(2,1)S(1)}, u32[]{:S(2)}, u32[]{:S(2)}) collective-permute-start(bf16[512,128]{1,0:T(8,128)(2,1)S(1)} %fusion.22), channel_id=1, source_target_pairs={{0,8},{1,9},{2,10},{3,11},{4,12},{5,13},{6,14},{7,15},{8,0},{9,1},... | collective-permute-start | bytes 393224 | tf_op jit(solution)/shard_map/range/ppermute | solution.py:27
  51.4 3.9 %collective-permute-done.16 = bf16[1024,128]{1,0:T(8,128)(2,1)S(1)} collective-permute-done((bf16[1024,128]{1,0:T(8,128)(2,1)S(1)}, bf16[1024,128]{1,0:T(8,128)(2,1)S(1)}, u32[]{:S(2)}, u32[]{:S(2)}) %collective-permute-start.16) | collective-permute-done | bytes 262176 | tf_op jit(solution)/shard_map/range/ppermute | solution.py:27
  55.4 0.2 fusion.5
  55.7 0.2 fusion.4
  56.0 0.7 collective-permute-start.14
  56.9 2.9 %collective-permute-start.24 = (bf16[512,128]{1,0:T(8,128)(2,1)S(1)}, bf16[512,128]{1,0:T(8,128)(2,1)S(1)}, u32[]{:S(2)}, u32[]{:S(2)}) collective-permute-start(bf16[512,128]{1,0:T(8,128)(2,1)S(1)} %get-tuple-element.51), channel_id=1, source_target_pairs={{0,8},{1,9},{2,10},{3,11},{4,12},{5,13},{6,14},{7,15},{8,0},{9,1},... | collective-permute-start | bytes 393224 | tf_op jit(solution)/shard_map/range/ppermute | solution.py:27
  60.0 0.7 collective-permute-done.17
  60.8 1.9 %collective-permute-start.18 = (bf16[512,128]{1,0:T(8,128)(2,1)S(1)}, bf16[512,128]{1,0:T(8,128)(2,1)S(1)}, u32[]{:S(2)}, u32[]{:S(2)}) collective-permute-start(bf16[512,128]{1,0:T(8,128)(2,1)S(1)} %get-tuple-element.47), channel_id=1, source_target_pairs={{0,8},{1,9},{2,10},{3,11},{4,12},{5,13},{6,14},{7,15},{8,0},{9,1},... | collective-permute-start | bytes 393224 | tf_op jit(solution)/shard_map/range/ppermute | solution.py:27
  62.7 2.5 %collective-permute-done.14 = bf16[512,128]{1,0:T(8,128)(2,1)S(1)} collective-permute-done((bf16[512,128]{1,0:T(8,128)(2,1)S(1)}, bf16[512,128]{1,0:T(8,128)(2,1)S(1)}, u32[]{:S(2)}, u32[]{:S(2)}) %collective-permute-start.14) | collective-permute-done | bytes 131104 | tf_op jit(solution)/shard_map/range/ppermute | solution.py:27
  65.4 0.3 collective-permute-start.15
  65.7 1.5 %collective-permute-done.24 = bf16[512,128]{1,0:T(8,128)(2,1)S(1)} collective-permute-done((bf16[512,128]{1,0:T(8,128)(2,1)S(1)}, bf16[512,128]{1,0:T(8,128)(2,1)S(1)}, u32[]{:S(2)}, u32[]{:S(2)}) %collective-permute-start.24) | collective-permute-done | bytes 131104 | tf_op jit(solution)/shard_map/range/ppermute | solution.py:27
  67.3 1.0 collective-permute-done.21
  68.5 6.3 %collective-permute-done.18 = bf16[512,128]{1,0:T(8,128)(2,1)S(1)} collective-permute-done((bf16[512,128]{1,0:T(8,128)(2,1)S(1)}, bf16[512,128]{1,0:T(8,128)(2,1)S(1)}, u32[]{:S(2)}, u32[]{:S(2)}) %collective-permute-start.18) | collective-permute-done | bytes 131104 | tf_op jit(solution)/shard_map/range/ppermute | solution.py:27
  74.9 1.4 %collective-permute-done.15 = bf16[512,128]{1,0:T(8,128)(2,1)S(1)} collective-permute-done((bf16[512,128]{1,0:T(8,128)(2,1)S(1)}, bf16[512,128]{1,0:T(8,128)(2,1)S(1)}, u32[]{:S(2)}, u32[]{:S(2)}) %collective-permute-start.15) | collective-permute-done | bytes 131104 | tf_op jit(solution)/shard_map/range/ppermute | solution.py:27
  76.5 1.0 fusion.33
  77.7 1.3 %collective-permute-start.32 = (bf16[512,128]{1,0:T(8,128)(2,1)S(1)}, bf16[512,128]{1,0:T(8,128)(2,1)S(1)}, u32[]{:S(2)}, u32[]{:S(2)}) collective-permute-start(bf16[512,128]{1,0:T(8,128)(2,1)S(1)} %pad_maximum_fusion.12), channel_id=1, source_target_pairs={{0,2},{1,3},{2,0},{3,1},{4,6},{5,7},{6,4},{7,5},{8,10},{9,11},{10,... | collective-permute-start | bytes 393224 | tf_op jit(solution)/shard_map/gather_range/ppermute | solution.py:27
  79.1 2.3 %collective-permute-start.34 = (bf16[512,128]{1,0:T(8,128)(2,1)S(1)}, bf16[512,128]{1,0:T(8,128)(2,1)S(1)}, u32[]{:S(2)}, u32[]{:S(2)}) collective-permute-start(bf16[512,128]{1,0:T(8,128)(2,1)S(1)} %pad_maximum_fusion.13), channel_id=1, source_target_pairs={{0,8},{1,9},{2,10},{3,11},{4,12},{5,13},{6,14},{7,15},{8,0},{9,1},... | collective-permute-start | bytes 393224 | tf_op jit(solution)/shard_map/gather_range/ppermute | solution.py:27
  81.4 1.4 %collective-permute-start.26 = (f32[128,128]{1,0:T(8,128)S(1)}, f32[128,128]{1,0:T(8,128)S(1)}, u32[]{:S(2)}, u32[]{:S(2)}) collective-permute-start(f32[128,128]{1,0:T(8,128)S(1)} %add.83), channel_id=1, source_target_pairs={{0,2},{1,3},{2,0},{3,1},{4,6},{5,7},{6,4},{7,5},{8,10},{9,11},{10,... | collective-permute-start | bytes 196616 | tf_op jit(solution)/shard_map/gram/ppermute | solution.py:27
  82.8 0.8 collective-permute-start.36
  83.6 2.9 %collective-permute-done.26 = f32[128,128]{1,0:T(8,128)S(1)} collective-permute-done((f32[128,128]{1,0:T(8,128)S(1)}, f32[128,128]{1,0:T(8,128)S(1)}, u32[]{:S(2)}, u32[]{:S(2)}) %collective-permute-start.26) | collective-permute-done | bytes 65568 | tf_op jit(solution)/shard_map/gram/ppermute | solution.py:27
  86.5 2.1 %collective-permute-start.28 = (f32[128,128]{1,0:T(8,128)S(1)}, f32[128,128]{1,0:T(8,128)S(1)}, u32[]{:S(2)}, u32[]{:S(2)}) collective-permute-start(f32[128,128]{1,0:T(8,128)S(1)} %add.84), channel_id=1, source_target_pairs={{0,8},{1,9},{2,10},{3,11},{4,12},{5,13},{6,14},{7,15},{8,0},{9,1},... | collective-permute-start | bytes 196616 | tf_op jit(solution)/shard_map/gram/ppermute | solution.py:27
  88.6 1.5 %collective-permute-start.29 = (f32[128,128]{1,0:T(8,128)S(1)}, f32[128,128]{1,0:T(8,128)S(1)}, u32[]{:S(2)}, u32[]{:S(2)}) collective-permute-start(f32[128,128]{1,0:T(8,128)S(1)} %add.84), channel_id=1, source_target_pairs={{0,12},{1,13},{2,14},{3,15},{4,8},{5,9},{6,10},{7,11},{8,4},{9,5},... | collective-permute-start | bytes 196616 | tf_op jit(solution)/shard_map/gram/ppermute | solution.py:27
  90.3 1.5 %collective-permute-start.31 = (bf16[1024,128]{1,0:T(8,128)(2,1)S(1)}, bf16[1024,128]{1,0:T(8,128)(2,1)S(1)}, u32[]{:S(2)}, u32[]{:S(2)}) collective-permute-start(bf16[1024,128]{1,0:T(8,128)(2,1)S(1)} %pad_maximum_fusion.4.refs_1_), channel_id=1, source_target_pairs={{0,2},{1,3},{2,0},{3,1},{4,6},{5,7},{6,4},{7,5},{8,10},{9,11},{10,... | collective-permute-start | bytes 786440 | tf_op jit(solution)/shard_map/gather_range/ppermute | solution.py:27
  91.8 1.9 %collective-permute-start.33 = (bf16[1024,128]{1,0:T(8,128)(2,1)S(1)}, bf16[1024,128]{1,0:T(8,128)(2,1)S(1)}, u32[]{:S(2)}, u32[]{:S(2)}) collective-permute-start(bf16[1024,128]{1,0:T(8,128)(2,1)S(1)} %pad_maximum_fusion.5.refs_2_), channel_id=1, source_target_pairs={{0,4},{1,5},{2,6},{3,7},{4,0},{5,1},{6,2},{7,3},{8,12},{9,13},{10,... | collective-permute-start | bytes 786440 | tf_op jit(solution)/shard_map/gather_range/ppermute | solution.py:27
  93.8 0.8 collective-permute-start.35
  94.6 0.7 collective-permute-done.29
  95.3 1.3 %coords.3.refs_5_ = f32[512,128]{1,0:T(8,128)S(1)} custom-call(s32[1]{0:T(128)} %bitcast.index_ref, s32[1]{0:T(128)} %bitcast.1.group_ref, bf16[256,16384]{1,0:T(8,128)(2,1)S(1)} %get-tuple-element.20.x_ref, bf16[256,8192]{1,0:T(8,128)(2,1)S(1)} %collective-permute-done.2.refs_0_, bf16[1024,128]{1,0:T(8,128)(2,1)S(1)} %pad_maximum_fusion.4.refs_1_, ...), custom_call_target="tpu_custom_call" | custom-call | flops 536870912 | bytes 4194304 | tf_op jit(solution)/shard_map/coords/pallas_call | solution.py:133
  96.6 6.4 %factor.1 = (f32[128,128]{1,0:T(8,128)S(1)}, f32[1024,128]{1,0:T(8,128)}) custom-call(f32[128,128]{1,0:T(8,128)S(1)} %add_add_fusion.gram_ref, f32[1024,128]{1,0:T(8,128)S(1)} %pad_maximum_fusion.range_ref), custom_call_target="tpu_custom_call" | custom-call | flops 10000000 | bytes 20000000 | tf_op jit(solution)/shard_map/factor/pallas_call | solution.py:217
  103.0 2.7 %collective-permute-done.37.refs_4_ = bf16[1024,128]{1,0:T(8,128)(2,1)S(1)} collective-permute-done((bf16[1024,128]{1,0:T(8,128)(2,1)S(1)}, bf16[1024,128]{1,0:T(8,128)(2,1)S(1)}, u32[]{:S(2)}, u32[]{:S(2)}) %collective-permute-start.37) | collective-permute-done | bytes 262176 | tf_op jit(solution)/shard_map/gather_range/ppermute | solution.py:27
  105.7 1.3 %coords.4.part_ref = f32[512,128]{1,0:T(8,128)S(1)} custom-call(s32[1]{0:T(128)} %bitcast.index_ref, s32[1]{0:T(128)} %bitcast.1.group_ref, bf16[256,16384]{1,0:T(8,128)(2,1)S(1)} %get-tuple-element.20.x_ref, bf16[256,8192]{1,0:T(8,128)(2,1)S(1)} %collective-permute-done.2.refs_0_, bf16[1024,128]{1,0:T(8,128)(2,1)S(1)} %collective-permute-done.31.refs_1_, ...), custom_call_target="tpu_custom_call" | custom-call | flops 536870912 | bytes 4194304 | tf_op jit(solution)/shard_map/coords/pallas_call | solution.py:133
  107.1 1.3 %collective-permute-done.38.theirs_ref = f32[256,128]{1,0:T(8,128)S(1)} collective-permute-done((f32[256,128]{1,0:T(8,128)S(1)}, f32[256,128]{1,0:T(8,128)S(1)}, u32[]{:S(2)}, u32[]{:S(2)}) %collective-permute-start.38) | collective-permute-done | bytes 131104 | tf_op jit(solution)/shard_map/coords/ppermute | solution.py:27
  108.4 0.9 coords.5
  (66 shorter events, 2.8 us)
Async XLA Ops:
  1.6 8.0 %collective-permute-start = (bf16[256,128]{1,0:T(8,128)(2,1)S(1)}, bf16[256,128]{1,0:T(8,128)(2,1)S(1)}, u32[]{:S(2)}, u32[]{:S(2)}) collective-permute-start(bf16[256,128]{1,0:T(8,128)(2,1)S(1)} %get-tuple-element.60), channel_id=1, source_target_pairs={{0,8},{1,9},{2,10},{3,11},{4,12},{5,13},{6,14},{7,15},{8,0},{9,1},... | collective-permute-start | bytes 196616 | tf_op jit(solution)/shard_map/gather_sketch/ppermute | solution.py:27
  5.7 6.5 %collective-permute-start.1 = (bf16[256,128]{1,0:T(8,128)(2,1)S(1)}, bf16[256,128]{1,0:T(8,128)(2,1)S(1)}, u32[]{:S(2)}, u32[]{:S(2)}) collective-permute-start(bf16[256,128]{1,0:T(8,128)(2,1)S(1)} %get-tuple-element.61), channel_id=1, source_target_pairs={{0,8},{1,9},{2,10},{3,11},{4,12},{5,13},{6,14},{7,15},{8,0},{9,1},... | collective-permute-start | bytes 196616 | tf_op jit(solution)/shard_map/gather_sketch/ppermute | solution.py:27
  12.1 17.8 %collective-permute-start.2 = (bf16[256,8192]{1,0:T(8,128)(2,1)S(1)}, bf16[256,8192]{1,0:T(8,128)(2,1)S(1)}, u32[]{:S(2)}, u32[]{:S(2)}) collective-permute-start(bf16[256,8192]{1,0:T(8,128)(2,1)S(1)} %get-tuple-element.22), channel_id=1, source_target_pairs={{0,1},{1,0},{2,3},{3,2},{4,5},{5,4},{6,7},{7,6},{8,9},{9,8},{10,11... | collective-permute-start | bytes 12582920 | tf_op jit(solution)/shard_map/split_features/ppermute | solution.py:27
  12.1 6.0 %collective-permute-start.3 = (bf16[512,128]{1,0:T(8,128)(2,1)S(1)}, bf16[512,128]{1,0:T(8,128)(2,1)S(1)}, u32[]{:S(2)}, u32[]{:S(2)}) collective-permute-start(bf16[512,128]{1,0:T(8,128)(2,1)S(1)} %pad_maximum_fusion.8), channel_id=1, source_target_pairs={{0,2},{1,3},{2,0},{3,1},{4,6},{5,7},{6,4},{7,5},{8,10},{9,11},{10,... | collective-permute-start | bytes 393224 | tf_op jit(solution)/shard_map/gather_sketch/ppermute | solution.py:27
  13.9 6.6 %collective-permute-start.9 = (bf16[256,128]{1,0:T(8,128)(2,1)S(1)}, bf16[256,128]{1,0:T(8,128)(2,1)S(1)}, u32[]{:S(2)}, u32[]{:S(2)}) collective-permute-start(bf16[256,128]{1,0:T(8,128)(2,1)S(1)} %get-tuple-element.59), channel_id=1, source_target_pairs={{0,8},{1,9},{2,10},{3,11},{4,12},{5,13},{6,14},{7,15},{8,0},{9,1},... | collective-permute-start | bytes 196616 | tf_op jit(solution)/shard_map/gather_sketch/ppermute | solution.py:27
  14.1 8.7 %collective-permute-start.7 = (bf16[512,128]{1,0:T(8,128)(2,1)S(1)}, bf16[512,128]{1,0:T(8,128)(2,1)S(1)}, u32[]{:S(2)}, u32[]{:S(2)}) collective-permute-start(bf16[512,128]{1,0:T(8,128)(2,1)S(1)} %pad_maximum_fusion.9), channel_id=1, source_target_pairs={{0,4},{1,5},{2,6},{3,7},{4,0},{5,1},{6,2},{7,3},{8,12},{9,13},{10,... | collective-permute-start | bytes 393224 | tf_op jit(solution)/shard_map/gather_sketch/ppermute | solution.py:27
  18.1 10.3 %collective-permute-start.4 = (bf16[1024,128]{1,0:T(8,128)(2,1)S(1)}, bf16[1024,128]{1,0:T(8,128)(2,1)S(1)}, u32[]{:S(2)}, u32[]{:S(2)}) collective-permute-start(bf16[1024,128]{1,0:T(8,128)(2,1)S(1)} %pad_maximum_fusion.1.refs_1_), channel_id=1, source_target_pairs={{0,4},{1,5},{2,6},{3,7},{4,0},{5,1},{6,2},{7,3},{8,12},{9,13},{10,... | collective-permute-start | bytes 786440 | tf_op jit(solution)/shard_map/gather_sketch/ppermute | solution.py:27
  20.5 6.4 %collective-permute-start.10 = (bf16[512,128]{1,0:T(8,128)(2,1)S(1)}, bf16[512,128]{1,0:T(8,128)(2,1)S(1)}, u32[]{:S(2)}, u32[]{:S(2)}) collective-permute-start(bf16[512,128]{1,0:T(8,128)(2,1)S(1)} %pad_maximum_fusion.10), channel_id=1, source_target_pairs={{0,2},{1,3},{2,0},{3,1},{4,6},{5,7},{6,4},{7,5},{8,10},{9,11},{10,... | collective-permute-start | bytes 393224 | tf_op jit(solution)/shard_map/gather_sketch/ppermute | solution.py:27
  21.0 10.0 %collective-permute-start.5 = (bf16[1024,128]{1,0:T(8,128)(2,1)S(1)}, bf16[1024,128]{1,0:T(8,128)(2,1)S(1)}, u32[]{:S(2)}, u32[]{:S(2)}) collective-permute-start(bf16[1024,128]{1,0:T(8,128)(2,1)S(1)} %pad_maximum_fusion.1.refs_1_), channel_id=1, source_target_pairs={{0,16},{16,0},{1,17},{17,1},{2,18},{18,2},{3,19},{19,3},{4,20},{20... | collective-permute-start | bytes 786440 | tf_op jit(solution)/shard_map/gather_sketch/ppermute | solution.py:257
  22.8 8.4 %collective-permute-start.8 = (bf16[1024,128]{1,0:T(8,128)(2,1)S(1)}, bf16[1024,128]{1,0:T(8,128)(2,1)S(1)}, u32[]{:S(2)}, u32[]{:S(2)}) collective-permute-start(bf16[1024,128]{1,0:T(8,128)(2,1)S(1)} %pad_maximum_fusion.2.refs_2_), channel_id=1, source_target_pairs={{0,2},{1,3},{2,0},{3,1},{4,6},{5,7},{6,4},{7,5},{8,10},{9,11},{10,... | collective-permute-start | bytes 786440 | tf_op jit(solution)/shard_map/gather_sketch/ppermute | solution.py:27
  27.0 6.4 %collective-permute-start.11 = (bf16[1024,128]{1,0:T(8,128)(2,1)S(1)}, bf16[1024,128]{1,0:T(8,128)(2,1)S(1)}, u32[]{:S(2)}, u32[]{:S(2)}) collective-permute-start(bf16[1024,128]{1,0:T(8,128)(2,1)S(1)} %pad_maximum_fusion.3.refs_3_), channel_id=1, source_target_pairs={{0,4},{1,5},{2,6},{3,7},{4,0},{5,1},{6,2},{7,3},{8,12},{9,13},{10,... | collective-permute-start | bytes 786440 | tf_op jit(solution)/shard_map/gather_sketch/ppermute | solution.py:27
  28.4 6.9 %collective-permute-start.6 = (bf16[1024,128]{1,0:T(8,128)(2,1)S(1)}, bf16[1024,128]{1,0:T(8,128)(2,1)S(1)}, u32[]{:S(2)}, u32[]{:S(2)}) collective-permute-start(bf16[1024,128]{1,0:T(8,128)(2,1)S(1)} %collective-permute-done.4.refs_1_), channel_id=1, source_target_pairs={{0,16},{16,0},{1,17},{17,1},{2,18},{18,2},{3,19},{19,3},{4,20},{20... | collective-permute-start | bytes 786440 | tf_op jit(solution)/shard_map/gather_sketch/ppermute | solution.py:257
  36.9 1.6 %collective-permute-start.12 = (f32[512,128]{1,0:T(8,128)S(1)}, f32[512,128]{1,0:T(8,128)S(1)}, u32[]{:S(2)}, u32[]{:S(2)}) collective-permute-start(f32[512,128]{1,0:T(8,128)S(1)} %sketched.3), channel_id=1, source_target_pairs={{0,1},{1,0},{2,3},{3,2},{4,5},{5,4},{6,7},{7,6},{8,9},{9,8},{10,11... | collective-permute-start | bytes 786440 | tf_op jit(solution)/shard_map/sketched/ppermute | solution.py:27
  39.4 9.2 %collective-permute-start.22 = (bf16[1024,128]{1,0:T(8,128)(2,1)S(1)}, bf16[1024,128]{1,0:T(8,128)(2,1)S(1)}, u32[]{:S(2)}, u32[]{:S(2)}) collective-permute-start(bf16[1024,128]{1,0:T(8,128)(2,1)S(1)} %get-tuple-element.30), channel_id=1, source_target_pairs={{0,4},{1,5},{2,6},{3,7},{4,0},{5,1},{6,2},{7,3},{8,12},{9,13},{10,... | collective-permute-start | bytes 786440 | tf_op jit(solution)/shard_map/range/ppermute | solution.py:27
  40.3 9.2 %collective-permute-start.19 = (bf16[1024,128]{1,0:T(8,128)(2,1)S(1)}, bf16[1024,128]{1,0:T(8,128)(2,1)S(1)}, u32[]{:S(2)}, u32[]{:S(2)}) collective-permute-start(bf16[1024,128]{1,0:T(8,128)(2,1)S(1)} %get-tuple-element.28), channel_id=1, source_target_pairs={{0,2},{1,3},{2,0},{3,1},{4,6},{5,7},{6,4},{7,5},{8,10},{9,11},{10,... | collective-permute-start | bytes 786440 | tf_op jit(solution)/shard_map/range/ppermute | solution.py:27
  40.7 14.7 %collective-permute-start.16 = (bf16[1024,128]{1,0:T(8,128)(2,1)S(1)}, bf16[1024,128]{1,0:T(8,128)(2,1)S(1)}, u32[]{:S(2)}, u32[]{:S(2)}) collective-permute-start(bf16[1024,128]{1,0:T(8,128)(2,1)S(1)} %get-tuple-element.26), channel_id=1, source_target_pairs={{0,4},{1,5},{2,6},{3,7},{4,0},{5,1},{6,2},{7,3},{8,12},{9,13},{10,... | collective-permute-start | bytes 786440 | tf_op jit(solution)/shard_map/range/ppermute | solution.py:27
  41.7 14.0 %collective-permute-start.13 = (bf16[1024,128]{1,0:T(8,128)(2,1)S(1)}, bf16[1024,128]{1,0:T(8,128)(2,1)S(1)}, u32[]{:S(2)}, u32[]{:S(2)}) collective-permute-start(bf16[1024,128]{1,0:T(8,128)(2,1)S(1)} %get-tuple-element.24), channel_id=1, source_target_pairs={{0,2},{1,3},{2,0},{3,1},{4,6},{5,7},{6,4},{7,5},{8,10},{9,11},{10,... | collective-permute-start | bytes 786440 | tf_op jit(solution)/shard_map/range/ppermute | solution.py:27
  48.9 7.9 %collective-permute-start.23 = (bf16[512,128]{1,0:T(8,128)(2,1)S(1)}, bf16[512,128]{1,0:T(8,128)(2,1)S(1)}, u32[]{:S(2)}, u32[]{:S(2)}) collective-permute-start(bf16[512,128]{1,0:T(8,128)(2,1)S(1)} %fusion.25), channel_id=1, source_target_pairs={{0,2},{1,3},{2,0},{3,1},{4,6},{5,7},{6,4},{7,5},{8,10},{9,11},{10,... | collective-permute-start | bytes 393224 | tf_op jit(solution)/shard_map/range/ppermute | solution.py:27
  49.7 10.0 %collective-permute-start.20 = (bf16[512,128]{1,0:T(8,128)(2,1)S(1)}, bf16[512,128]{1,0:T(8,128)(2,1)S(1)}, u32[]{:S(2)}, u32[]{:S(2)}) collective-permute-start(bf16[512,128]{1,0:T(8,128)(2,1)S(1)} %fusion.22), channel_id=1, source_target_pairs={{0,8},{1,9},{2,10},{3,11},{4,12},{5,13},{6,14},{7,15},{8,0},{9,1},... | collective-permute-start | bytes 393224 | tf_op jit(solution)/shard_map/range/ppermute | solution.py:27
  55.7 5.0 %collective-permute-start.17 = (bf16[512,128]{1,0:T(8,128)(2,1)S(1)}, bf16[512,128]{1,0:T(8,128)(2,1)S(1)}, u32[]{:S(2)}, u32[]{:S(2)}) collective-permute-start(bf16[512,128]{1,0:T(8,128)(2,1)S(1)} %fusion.19), channel_id=1, source_target_pairs={{0,2},{1,3},{2,0},{3,1},{4,6},{5,7},{6,4},{7,5},{8,10},{9,11},{10,... | collective-permute-start | bytes 393224 | tf_op jit(solution)/shard_map/range/ppermute | solution.py:27
  56.0 9.2 %collective-permute-start.14 = (bf16[512,128]{1,0:T(8,128)(2,1)S(1)}, bf16[512,128]{1,0:T(8,128)(2,1)S(1)}, u32[]{:S(2)}, u32[]{:S(2)}) collective-permute-start(bf16[512,128]{1,0:T(8,128)(2,1)S(1)} %fusion.16), channel_id=1, source_target_pairs={{0,4},{1,5},{2,6},{3,7},{4,0},{5,1},{6,2},{7,3},{8,12},{9,13},{10,... | collective-permute-start | bytes 393224 | tf_op jit(solution)/shard_map/range/ppermute | solution.py:27
  56.9 10.3 %collective-permute-start.24 = (bf16[512,128]{1,0:T(8,128)(2,1)S(1)}, bf16[512,128]{1,0:T(8,128)(2,1)S(1)}, u32[]{:S(2)}, u32[]{:S(2)}) collective-permute-start(bf16[512,128]{1,0:T(8,128)(2,1)S(1)} %get-tuple-element.51), channel_id=1, source_target_pairs={{0,8},{1,9},{2,10},{3,11},{4,12},{5,13},{6,14},{7,15},{8,0},{9,1},... | collective-permute-start | bytes 393224 | tf_op jit(solution)/shard_map/range/ppermute | solution.py:27
  59.9 8.4 %collective-permute-start.21 = (bf16[512,128]{1,0:T(8,128)(2,1)S(1)}, bf16[512,128]{1,0:T(8,128)(2,1)S(1)}, u32[]{:S(2)}, u32[]{:S(2)}) collective-permute-start(bf16[512,128]{1,0:T(8,128)(2,1)S(1)} %get-tuple-element.49), channel_id=1, source_target_pairs={{0,4},{1,5},{2,6},{3,7},{4,0},{5,1},{6,2},{7,3},{8,12},{9,13},{10,... | collective-permute-start | bytes 393224 | tf_op jit(solution)/shard_map/range/ppermute | solution.py:27
  60.8 13.9 %collective-permute-start.18 = (bf16[512,128]{1,0:T(8,128)(2,1)S(1)}, bf16[512,128]{1,0:T(8,128)(2,1)S(1)}, u32[]{:S(2)}, u32[]{:S(2)}) collective-permute-start(bf16[512,128]{1,0:T(8,128)(2,1)S(1)} %get-tuple-element.47), channel_id=1, source_target_pairs={{0,8},{1,9},{2,10},{3,11},{4,12},{5,13},{6,14},{7,15},{8,0},{9,1},... | collective-permute-start | bytes 393224 | tf_op jit(solution)/shard_map/range/ppermute | solution.py:27
  65.4 10.9 %collective-permute-start.15 = (bf16[512,128]{1,0:T(8,128)(2,1)S(1)}, bf16[512,128]{1,0:T(8,128)(2,1)S(1)}, u32[]{:S(2)}, u32[]{:S(2)}) collective-permute-start(bf16[512,128]{1,0:T(8,128)(2,1)S(1)} %get-tuple-element.45), channel_id=1, source_target_pairs={{0,8},{1,9},{2,10},{3,11},{4,12},{5,13},{6,14},{7,15},{8,0},{9,1},... | collective-permute-start | bytes 393224 | tf_op jit(solution)/shard_map/range/ppermute | solution.py:27
  77.5 3.9 %collective-permute-start.25 = (f32[128,128]{1,0:T(8,128)S(1)}, f32[128,128]{1,0:T(8,128)S(1)}, u32[]{:S(2)}, u32[]{:S(2)}) collective-permute-start(f32[128,128]{1,0:T(8,128)S(1)} %fusion.33), channel_id=1, source_target_pairs={{0,1},{1,0},{2,3},{3,2},{4,5},{5,4},{6,7},{7,6},{8,9},{9,8},{10,11... | collective-permute-start | bytes 196616 | tf_op jit(solution)/shard_map/gram/ppermute | solution.py:27
  77.6 11.0 %collective-permute-start.30 = (bf16[512,128]{1,0:T(8,128)(2,1)S(1)}, bf16[512,128]{1,0:T(8,128)(2,1)S(1)}, u32[]{:S(2)}, u32[]{:S(2)}) collective-permute-start(bf16[512,128]{1,0:T(8,128)(2,1)S(1)} %pad_maximum_fusion.11), channel_id=1, source_target_pairs={{0,4},{1,5},{2,6},{3,7},{4,0},{5,1},{6,2},{7,3},{8,12},{9,13},{10,... | collective-permute-start | bytes 393224 | tf_op jit(solution)/shard_map/gather_range/ppermute | solution.py:27
  77.7 12.5 %collective-permute-start.32 = (bf16[512,128]{1,0:T(8,128)(2,1)S(1)}, bf16[512,128]{1,0:T(8,128)(2,1)S(1)}, u32[]{:S(2)}, u32[]{:S(2)}) collective-permute-start(bf16[512,128]{1,0:T(8,128)(2,1)S(1)} %pad_maximum_fusion.12), channel_id=1, source_target_pairs={{0,2},{1,3},{2,0},{3,1},{4,6},{5,7},{6,4},{7,5},{8,10},{9,11},{10,... | collective-permute-start | bytes 393224 | tf_op jit(solution)/shard_map/gather_range/ppermute | solution.py:27
  79.1 11.2 %collective-permute-start.34 = (bf16[512,128]{1,0:T(8,128)(2,1)S(1)}, bf16[512,128]{1,0:T(8,128)(2,1)S(1)}, u32[]{:S(2)}, u32[]{:S(2)}) collective-permute-start(bf16[512,128]{1,0:T(8,128)(2,1)S(1)} %pad_maximum_fusion.13), channel_id=1, source_target_pairs={{0,8},{1,9},{2,10},{3,11},{4,12},{5,13},{6,14},{7,15},{8,0},{9,1},... | collective-permute-start | bytes 393224 | tf_op jit(solution)/shard_map/gather_range/ppermute | solution.py:27
  81.4 5.0 %collective-permute-start.26 = (f32[128,128]{1,0:T(8,128)S(1)}, f32[128,128]{1,0:T(8,128)S(1)}, u32[]{:S(2)}, u32[]{:S(2)}) collective-permute-start(f32[128,128]{1,0:T(8,128)S(1)} %add.83), channel_id=1, source_target_pairs={{0,2},{1,3},{2,0},{3,1},{4,6},{5,7},{6,4},{7,5},{8,10},{9,11},{10,... | collective-permute-start | bytes 196616 | tf_op jit(solution)/shard_map/gram/ppermute | solution.py:27
  82.8 9.0 %collective-permute-start.36 = (bf16[512,128]{1,0:T(8,128)(2,1)S(1)}, bf16[512,128]{1,0:T(8,128)(2,1)S(1)}, u32[]{:S(2)}, u32[]{:S(2)}) collective-permute-start(bf16[512,128]{1,0:T(8,128)(2,1)S(1)} %pad_maximum_fusion.14), channel_id=1, source_target_pairs={{0,2},{1,3},{2,0},{3,1},{4,6},{5,7},{6,4},{7,5},{8,10},{9,11},{10,... | collective-permute-start | bytes 393224 | tf_op jit(solution)/shard_map/gather_range/ppermute | solution.py:27
  86.5 7.3 %collective-permute-start.28 = (f32[128,128]{1,0:T(8,128)S(1)}, f32[128,128]{1,0:T(8,128)S(1)}, u32[]{:S(2)}, u32[]{:S(2)}) collective-permute-start(f32[128,128]{1,0:T(8,128)S(1)} %add.84), channel_id=1, source_target_pairs={{0,8},{1,9},{2,10},{3,11},{4,12},{5,13},{6,14},{7,15},{8,0},{9,1},... | collective-permute-start | bytes 196616 | tf_op jit(solution)/shard_map/gram/ppermute | solution.py:27
  88.6 6.7 %collective-permute-start.29 = (f32[128,128]{1,0:T(8,128)S(1)}, f32[128,128]{1,0:T(8,128)S(1)}, u32[]{:S(2)}, u32[]{:S(2)}) collective-permute-start(f32[128,128]{1,0:T(8,128)S(1)} %add.84), channel_id=1, source_target_pairs={{0,12},{1,13},{2,14},{3,15},{4,8},{5,9},{6,10},{7,11},{8,4},{9,5},... | collective-permute-start | bytes 196616 | tf_op jit(solution)/shard_map/gram/ppermute | solution.py:27
  90.2 6.4 %collective-permute-start.27 = (f32[128,128]{1,0:T(8,128)S(1)}, f32[128,128]{1,0:T(8,128)S(1)}, u32[]{:S(2)}, u32[]{:S(2)}) collective-permute-start(f32[128,128]{1,0:T(8,128)S(1)} %add.84), channel_id=1, source_target_pairs={{0,4},{1,5},{2,6},{3,7},{4,0},{5,1},{6,2},{7,3},{8,12},{9,13},{10,... | collective-permute-start | bytes 196616 | tf_op jit(solution)/shard_map/gram/ppermute | solution.py:27
  90.3 12.7 %collective-permute-start.31 = (bf16[1024,128]{1,0:T(8,128)(2,1)S(1)}, bf16[1024,128]{1,0:T(8,128)(2,1)S(1)}, u32[]{:S(2)}, u32[]{:S(2)}) collective-permute-start(bf16[1024,128]{1,0:T(8,128)(2,1)S(1)} %pad_maximum_fusion.4.refs_1_), channel_id=1, source_target_pairs={{0,2},{1,3},{2,0},{3,1},{4,6},{5,7},{6,4},{7,5},{8,10},{9,11},{10,... | collective-permute-start | bytes 786440 | tf_op jit(solution)/shard_map/gather_range/ppermute | solution.py:27
  91.8 11.2 %collective-permute-start.33 = (bf16[1024,128]{1,0:T(8,128)(2,1)S(1)}, bf16[1024,128]{1,0:T(8,128)(2,1)S(1)}, u32[]{:S(2)}, u32[]{:S(2)}) collective-permute-start(bf16[1024,128]{1,0:T(8,128)(2,1)S(1)} %pad_maximum_fusion.5.refs_2_), channel_id=1, source_target_pairs={{0,4},{1,5},{2,6},{3,7},{4,0},{5,1},{6,2},{7,3},{8,12},{9,13},{10,... | collective-permute-start | bytes 786440 | tf_op jit(solution)/shard_map/gather_range/ppermute | solution.py:27
  93.8 9.2 %collective-permute-start.35 = (bf16[1024,128]{1,0:T(8,128)(2,1)S(1)}, bf16[1024,128]{1,0:T(8,128)(2,1)S(1)}, u32[]{:S(2)}, u32[]{:S(2)}) collective-permute-start(bf16[1024,128]{1,0:T(8,128)(2,1)S(1)} %pad_maximum_fusion.6.refs_3_), channel_id=1, source_target_pairs={{0,2},{1,3},{2,0},{3,1},{4,6},{5,7},{6,4},{7,5},{8,10},{9,11},{10,... | collective-permute-start | bytes 786440 | tf_op jit(solution)/shard_map/gather_range/ppermute | solution.py:27
  95.3 10.4 %collective-permute-start.37 = (bf16[1024,128]{1,0:T(8,128)(2,1)S(1)}, bf16[1024,128]{1,0:T(8,128)(2,1)S(1)}, u32[]{:S(2)}, u32[]{:S(2)}) collective-permute-start(bf16[1024,128]{1,0:T(8,128)(2,1)S(1)} %pad_maximum_fusion.7.refs_4_), channel_id=1, source_target_pairs={{0,4},{1,5},{2,6},{3,7},{4,0},{5,1},{6,2},{7,3},{8,12},{9,13},{10,... | collective-permute-start | bytes 786440 | tf_op jit(solution)/shard_map/gather_range/ppermute | solution.py:27
  107.0 1.4 %collective-permute-start.38 = (f32[256,128]{1,0:T(8,128)S(1)}, f32[256,128]{1,0:T(8,128)S(1)}, u32[]{:S(2)}, u32[]{:S(2)}) collective-permute-start(f32[256,128]{1,0:T(8,128)S(1)} %slice.136), channel_id=1, source_target_pairs={{0,1},{1,0},{2,3},{3,2},{4,5},{5,4},{6,7},{7,6},{8,9},{9,8},{10,11... | collective-permute-start | bytes 393224 | tf_op jit(solution)/shard_map/coords/ppermute | solution.py:27

commit v5 on v4

--- a/solution.py
+++ b/solution.py
@@ -307,14 +307,17 @@
             sums.append(own)
             held.append(jnp.concatenate([own, total[cut:] + theirs[:cut]]).astype(BF16))
         range_rows = jnp.concatenate(sums, axis=0)
+    with jax.named_scope("gather_range"):
+        came = [swap(held[p], 2 * orders[p][1], n) for p in every]
     with jax.named_scope("gram"):
         gram = jnp.dot(range_rows.T, range_rows, preferred_element_type=F32, precision=HIGH)
         for bit in (1, 2):
             gram = gram + swap(gram, bit, n)
+        gram = after(gram, came[1])
         apart = [swap(gram, bit, n) for bit in (4, 8, 12)]
         gram = (gram + apart[0]) + (apart[1] + apart[2])
     with jax.named_scope("gather_range"):
-        held = [jnp.concatenate([held[p], swap(held[p], 2 * orders[p][1], n)]) for p in every]
+        held = [jnp.concatenate([held[p], came[p]]) for p in every]
         came = [swap(held[p], 2 * orders[p][2], n) for p in every]
     with jax.named_scope("factor"):
         inverse, basis = factored(math.sqrt(depth), gram, range_rows)

time: 110 us -> 109 us (level)
  transfers between devices with their start and end apart: 39 -> 39, of which waited for: 24 -> 25; matrix products, arithmetic and copies ran while one was open for 2% -> 2% of each run, Pallas kernels for 12% -> 12%
where the time goes in v5:
time: 109 us; the launch traced here: 108 us
  waiting for transfers between devices  43.6 us (40%)
  starting transfers between devices  41.3 us (38%)
  Pallas kernels  18 us (17%)
  other arithmetic  2.51 us (2%)
    ppermute x37, waiting for transfers between devices, swap(): return lax.ppermute(value, 'tok', [(i, i ^ bit) for i in range(n)])  41.7 us
    ppermute x37, starting transfers between devices, swap(): return lax.ppermute(value, 'tok', [(i, i ^ bit) for i in range(n)])  38.1 us
    pallas_call x1, Pallas kernels, factored(): pl.pallas_call(functools.partial(factor_kernel, scale), in_specs=[VMEM] *...  6.41 us
    pallas_call x4, Pallas kernels, project(): pl.pallas_call(functools.partial(project_kernel, width, entries, init is...  5.02 us
    pallas_call x1, Pallas kernels, load(): pl.pallas_call(functools.partial(load_kernel, width), in_specs=[SMEM, ANY...  3.78 us
    ppermute x2, starting transfers between devices, across(): return lax.ppermute(value, 'groups', [(0, 1), (1, 0)])  3.2 us
  transfers between devices with their start and end apart: 39, of which 25 were waited for; matrix products, arithmetic and copies ran while one was open for 2% of the time, Pallas kernels for 12%

profile of v5, /device:TPU:0, one launch (start us, length us, event | category | flops | bytes accessed | tf_op | source)
XLA Modules:
  0.0 108.4 jit_solution(16872703577048134891)
XLA Ops:
  0.6 0.9 slice_bitcast_fusion
  1.6 4.1 %collective-permute-start = (bf16[256,128]{1,0:T(8,128)(2,1)S(1)}, bf16[256,128]{1,0:T(8,128)(2,1)S(1)}, u32[]{:S(2)}, u32[]{:S(2)}) collective-permute-start(bf16[256,128]{1,0:T(8,128)(2,1)S(1)} %get-tuple-element.62), channel_id=1, source_target_pairs={{0,8},{1,9},{2,10},{3,11},{4,12},{5,13},{6,14},{7,15},{8,0},{9,1},... | collective-permute-start | bytes 196616 | tf_op jit(solution)/shard_map/gather_sketch/ppermute | solution.py:27
  5.7 3.8 %split_features.1 = (bf16[256,16384]{1,0:T(8,128)(2,1)S(1)}, f32[256,128]{1,0:T(8,128)S(1)}, bf16[256,8192]{1,0:T(8,128)(2,1)S(1)}) custom-call(s32[1]{0:T(128)} %bitcast.index_ref, bf16[256,16384]{1,0:T(8,128)(2,1)} %x_ref.1), custom_call_target="tpu_custom_call" | custom-call | flops 8388608 | bytes 16777216 | tf_op jit(solution)/shard_map/split_features/pallas_call | solution.py:94
  9.5 2.6 %collective-permute-done.1 = bf16[256,128]{1,0:T(8,128)(2,1)S(1)} collective-permute-done((bf16[256,128]{1,0:T(8,128)(2,1)S(1)}, bf16[256,128]{1,0:T(8,128)(2,1)S(1)}, u32[]{:S(2)}, u32[]{:S(2)}) %collective-permute-start.1) | collective-permute-done | bytes 65568 | tf_op jit(solution)/shard_map/gather_sketch/ppermute | solution.py:27
  12.1 1.8 %collective-permute-start.3 = (bf16[512,128]{1,0:T(8,128)(2,1)S(1)}, bf16[512,128]{1,0:T(8,128)(2,1)S(1)}, u32[]{:S(2)}, u32[]{:S(2)}) collective-permute-start(bf16[512,128]{1,0:T(8,128)(2,1)S(1)} %pad_maximum_fusion.8), channel_id=1, source_target_pairs={{0,2},{1,3},{2,0},{3,1},{4,6},{5,7},{6,4},{7,5},{8,10},{9,11},{10,... | collective-permute-start | bytes 393224 | tf_op jit(solution)/shard_map/gather_sketch/ppermute | solution.py:27
  14.1 3.7 %collective-permute-start.7 = (bf16[512,128]{1,0:T(8,128)(2,1)S(1)}, bf16[512,128]{1,0:T(8,128)(2,1)S(1)}, u32[]{:S(2)}, u32[]{:S(2)}) collective-permute-start(bf16[512,128]{1,0:T(8,128)(2,1)S(1)} %pad_maximum_fusion.9), channel_id=1, source_target_pairs={{0,4},{1,5},{2,6},{3,7},{4,0},{5,1},{6,2},{7,3},{8,12},{9,13},{10,... | collective-permute-start | bytes 393224 | tf_op jit(solution)/shard_map/gather_sketch/ppermute | solution.py:27
  17.7 0.4 collective-permute-done.3
  18.1 0.6 collective-permute-start.4
  18.8 1.8 %collective-permute-done.9 = bf16[256,128]{1,0:T(8,128)(2,1)S(1)} collective-permute-done((bf16[256,128]{1,0:T(8,128)(2,1)S(1)}, bf16[256,128]{1,0:T(8,128)(2,1)S(1)}, u32[]{:S(2)}, u32[]{:S(2)}) %collective-permute-start.9) | collective-permute-done | bytes 65568 | tf_op jit(solution)/shard_map/gather_sketch/ppermute | solution.py:27
  20.5 0.4 collective-permute-start.10
  21.0 1.7 %collective-permute-start.5 = (bf16[1024,128]{1,0:T(8,128)(2,1)S(1)}, bf16[1024,128]{1,0:T(8,128)(2,1)S(1)}, u32[]{:S(2)}, u32[]{:S(2)}) collective-permute-start(bf16[1024,128]{1,0:T(8,128)(2,1)S(1)} %pad_maximum_fusion.1.refs_1_), channel_id=1, source_target_pairs={{0,16},{16,0},{1,17},{17,1},{2,18},{18,2},{3,19},{19,3},{4,20},{20... | collective-permute-start | bytes 786440 | tf_op jit(solution)/shard_map/gather_sketch/ppermute | solution.py:257
  22.8 1.4 %collective-permute-start.8 = (bf16[1024,128]{1,0:T(8,128)(2,1)S(1)}, bf16[1024,128]{1,0:T(8,128)(2,1)S(1)}, u32[]{:S(2)}, u32[]{:S(2)}) collective-permute-start(bf16[1024,128]{1,0:T(8,128)(2,1)S(1)} %pad_maximum_fusion.2.refs_2_), channel_id=1, source_target_pairs={{0,2},{1,3},{2,0},{3,1},{4,6},{5,7},{6,4},{7,5},{8,10},{9,11},{10,... | collective-permute-start | bytes 786440 | tf_op jit(solution)/shard_map/gather_sketch/ppermute | solution.py:27
  24.3 2.7 %collective-permute-done.10 = bf16[512,128]{1,0:T(8,128)(2,1)S(1)} collective-permute-done((bf16[512,128]{1,0:T(8,128)(2,1)S(1)}, bf16[512,128]{1,0:T(8,128)(2,1)S(1)}, u32[]{:S(2)}, u32[]{:S(2)}) %collective-permute-start.10) | collective-permute-done | bytes 131104 | tf_op jit(solution)/shard_map/gather_sketch/ppermute | solution.py:27
  27.1 1.3 %collective-permute-done.4.refs_1_ = bf16[1024,128]{1,0:T(8,128)(2,1)S(1)} collective-permute-done((bf16[1024,128]{1,0:T(8,128)(2,1)S(1)}, bf16[1024,128]{1,0:T(8,128)(2,1)S(1)}, u32[]{:S(2)}, u32[]{:S(2)}) %collective-permute-start.4) | collective-permute-done | bytes 262176 | tf_op jit(solution)/shard_map/gather_sketch/ppermute | solution.py:27
  28.4 1.5 %collective-permute-start.6 = (bf16[1024,128]{1,0:T(8,128)(2,1)S(1)}, bf16[1024,128]{1,0:T(8,128)(2,1)S(1)}, u32[]{:S(2)}, u32[]{:S(2)}) collective-permute-start(bf16[1024,128]{1,0:T(8,128)(2,1)S(1)} %collective-permute-done.4.refs_1_), channel_id=1, source_target_pairs={{0,16},{16,0},{1,17},{17,1},{2,18},{18,2},{3,19},{19,3},{4,20},{20... | collective-permute-start | bytes 786440 | tf_op jit(solution)/shard_map/gather_sketch/ppermute | solution.py:257
  30.0 1.0 sketched.2.refs_6_
  31.0 0.2 collective-permute-done.8.refs_4_
  31.2 2.2 %collective-permute-done.11.refs_5_ = bf16[1024,128]{1,0:T(8,128)(2,1)S(1)} collective-permute-done((bf16[1024,128]{1,0:T(8,128)(2,1)S(1)}, bf16[1024,128]{1,0:T(8,128)(2,1)S(1)}, u32[]{:S(2)}, u32[]{:S(2)}) %collective-permute-start.11) | collective-permute-done | bytes 262176 | tf_op jit(solution)/shard_map/gather_sketch/ppermute | solution.py:27
  33.4 1.9 %collective-permute-done.6.refs_3_ = bf16[1024,128]{1,0:T(8,128)(2,1)S(1)} collective-permute-done((bf16[1024,128]{1,0:T(8,128)(2,1)S(1)}, bf16[1024,128]{1,0:T(8,128)(2,1)S(1)}, u32[]{:S(2)}, u32[]{:S(2)}) %collective-permute-start.6) | collective-permute-done | bytes 262176 | tf_op jit(solution)/shard_map/gather_sketch/ppermute | solution.py:257
  35.3 1.5 %sketched.3 = f32[512,128]{1,0:T(8,128)S(1)} custom-call(s32[1]{0:T(128)} %bitcast.index_ref, s32[1]{0:T(128)} %bitcast.1.group_ref, bf16[256,16384]{1,0:T(8,128)(2,1)S(1)} %get-tuple-element.21.x_ref, bf16[256,8192]{1,0:T(8,128)(2,1)S(1)} %collective-permute-done.2.refs_0_, bf16[1024,128]{1,0:T(8,128)(2,1)S(1)} %collective-permute-done.4.refs_1_, ...), custom_call_target="tpu_custom_call" | custom-call | flops 671088640 | bytes 5242880 | tf_op jit(solution)/shard_map/sketched/pallas_call | solution.py:133
  36.9 1.5 %collective-permute-done.12 = f32[512,128]{1,0:T(8,128)S(1)} collective-permute-done((f32[512,128]{1,0:T(8,128)S(1)}, f32[512,128]{1,0:T(8,128)S(1)}, u32[]{:S(2)}, u32[]{:S(2)}) %collective-permute-start.12) | collective-permute-done | bytes 262176 | tf_op jit(solution)/shard_map/sketched/ppermute | solution.py:27
  38.5 0.9 range.3
  39.4 0.8 collective-permute-start.22
  40.3 0.4 collective-permute-start.19
  40.7 1.0 collective-permute-start.16
  41.7 1.8 %collective-permute-start.13 = (bf16[1024,128]{1,0:T(8,128)(2,1)S(1)}, bf16[1024,128]{1,0:T(8,128)(2,1)S(1)}, u32[]{:S(2)}, u32[]{:S(2)}) collective-permute-start(bf16[1024,128]{1,0:T(8,128)(2,1)S(1)} %get-tuple-element.25), channel_id=1, source_target_pairs={{0,2},{1,3},{2,0},{3,1},{4,6},{5,7},{6,4},{7,5},{8,10},{9,11},{10,... | collective-permute-start | bytes 786440 | tf_op jit(solution)/shard_map/range/ppermute | solution.py:27
  43.6 0.9 range.2
  44.5 4.2 %collective-permute-done.22 = bf16[1024,128]{1,0:T(8,128)(2,1)S(1)} collective-permute-done((bf16[1024,128]{1,0:T(8,128)(2,1)S(1)}, bf16[1024,128]{1,0:T(8,128)(2,1)S(1)}, u32[]{:S(2)}, u32[]{:S(2)}) %collective-permute-start.22) | collective-permute-done | bytes 262176 | tf_op jit(solution)/shard_map/range/ppermute | solution.py:27
  48.9 0.3 collective-permute-start.23
  49.2 0.3 collective-permute-done.19
  49.5 0.2 fusion.6
  49.7 1.7 %collective-permute-start.20 = (bf16[512,128]{1,0:T(8,128)(2,1)S(1)}, bf16[512,128]{1,0:T(8,128)(2,1)S(1)}, u32[]{:S(2)}, u32[]{:S(2)}) collective-permute-start(bf16[512,128]{1,0:T(8,128)(2,1)S(1)} %fusion.22), channel_id=1, source_target_pairs={{0,8},{1,9},{2,10},{3,11},{4,12},{5,13},{6,14},{7,15},{8,0},{9,1},... | collective-permute-start | bytes 393224 | tf_op jit(solution)/shard_map/range/ppermute | solution.py:27
  51.4 3.9 %collective-permute-done.16 = bf16[1024,128]{1,0:T(8,128)(2,1)S(1)} collective-permute-done((bf16[1024,128]{1,0:T(8,128)(2,1)S(1)}, bf16[1024,128]{1,0:T(8,128)(2,1)S(1)}, u32[]{:S(2)}, u32[]{:S(2)}) %collective-permute-start.16) | collective-permute-done | bytes 262176 | tf_op jit(solution)/shard_map/range/ppermute | solution.py:27
  55.7 0.2 fusion.4
  56.0 0.7 collective-permute-start.14
  56.9 2.9 %collective-permute-start.24 = (bf16[512,128]{1,0:T(8,128)(2,1)S(1)}, bf16[512,128]{1,0:T(8,128)(2,1)S(1)}, u32[]{:S(2)}, u32[]{:S(2)}) collective-permute-start(bf16[512,128]{1,0:T(8,128)(2,1)S(1)} %get-tuple-element.53), channel_id=1, source_target_pairs={{0,8},{1,9},{2,10},{3,11},{4,12},{5,13},{6,14},{7,15},{8,0},{9,1},... | collective-permute-start | bytes 393224 | tf_op jit(solution)/shard_map/range/ppermute | solution.py:27
  60.0 0.7 collective-permute-done.17
  60.8 1.9 %collective-permute-start.18 = (bf16[512,128]{1,0:T(8,128)(2,1)S(1)}, bf16[512,128]{1,0:T(8,128)(2,1)S(1)}, u32[]{:S(2)}, u32[]{:S(2)}) collective-permute-start(bf16[512,128]{1,0:T(8,128)(2,1)S(1)} %get-tuple-element.49), channel_id=1, source_target_pairs={{0,8},{1,9},{2,10},{3,11},{4,12},{5,13},{6,14},{7,15},{8,0},{9,1},... | collective-permute-start | bytes 393224 | tf_op jit(solution)/shard_map/range/ppermute | solution.py:27
  62.7 2.5 %collective-permute-done.14 = bf16[512,128]{1,0:T(8,128)(2,1)S(1)} collective-permute-done((bf16[512,128]{1,0:T(8,128)(2,1)S(1)}, bf16[512,128]{1,0:T(8,128)(2,1)S(1)}, u32[]{:S(2)}, u32[]{:S(2)}) %collective-permute-start.14) | collective-permute-done | bytes 131104 | tf_op jit(solution)/shard_map/range/ppermute | solution.py:27
  65.4 0.3 collective-permute-start.15
  65.7 1.4 %collective-permute-done.24 = bf16[512,128]{1,0:T(8,128)(2,1)S(1)} collective-permute-done((bf16[512,128]{1,0:T(8,128)(2,1)S(1)}, bf16[512,128]{1,0:T(8,128)(2,1)S(1)}, u32[]{:S(2)}, u32[]{:S(2)}) %collective-permute-start.24) | collective-permute-done | bytes 131104 | tf_op jit(solution)/shard_map/range/ppermute | solution.py:27
  67.3 1.0 collective-permute-done.21
  68.5 6.3 %collective-permute-done.18 = bf16[512,128]{1,0:T(8,128)(2,1)S(1)} collective-permute-done((bf16[512,128]{1,0:T(8,128)(2,1)S(1)}, bf16[512,128]{1,0:T(8,128)(2,1)S(1)}, u32[]{:S(2)}, u32[]{:S(2)}) %collective-permute-start.18) | collective-permute-done | bytes 131104 | tf_op jit(solution)/shard_map/range/ppermute | solution.py:27
  74.9 1.4 %collective-permute-done.15 = bf16[512,128]{1,0:T(8,128)(2,1)S(1)} collective-permute-done((bf16[512,128]{1,0:T(8,128)(2,1)S(1)}, bf16[512,128]{1,0:T(8,128)(2,1)S(1)}, u32[]{:S(2)}, u32[]{:S(2)}) %collective-permute-start.15) | collective-permute-done | bytes 131104 | tf_op jit(solution)/shard_map/range/ppermute | solution.py:27
  76.5 1.0 fusion.33
  77.7 1.3 %collective-permute-start.27 = (bf16[512,128]{1,0:T(8,128)(2,1)S(1)}, bf16[512,128]{1,0:T(8,128)(2,1)S(1)}, u32[]{:S(2)}, u32[]{:S(2)}) collective-permute-start(bf16[512,128]{1,0:T(8,128)(2,1)S(1)} %pad_maximum_fusion.11), channel_id=1, source_target_pairs={{0,2},{1,3},{2,0},{3,1},{4,6},{5,7},{6,4},{7,5},{8,10},{9,11},{10,... | collective-permute-start | bytes 393224 | tf_op jit(solution)/shard_map/gather_range/ppermute | solution.py:27
  79.1 2.3 %collective-permute-start.34 = (bf16[512,128]{1,0:T(8,128)(2,1)S(1)}, bf16[512,128]{1,0:T(8,128)(2,1)S(1)}, u32[]{:S(2)}, u32[]{:S(2)}) collective-permute-start(bf16[512,128]{1,0:T(8,128)(2,1)S(1)} %pad_maximum_fusion.13), channel_id=1, source_target_pairs={{0,8},{1,9},{2,10},{3,11},{4,12},{5,13},{6,14},{7,15},{8,0},{9,1},... | collective-permute-start | bytes 393224 | tf_op jit(solution)/shard_map/gather_range/ppermute | solution.py:27
  81.4 1.4 %collective-permute-start.26 = (f32[128,128]{1,0:T(8,128)S(1)}, f32[128,128]{1,0:T(8,128)S(1)}, u32[]{:S(2)}, u32[]{:S(2)}) collective-permute-start(f32[128,128]{1,0:T(8,128)S(1)} %add.83), channel_id=1, source_target_pairs={{0,2},{1,3},{2,0},{3,1},{4,6},{5,7},{6,4},{7,5},{8,10},{9,11},{10,... | collective-permute-start | bytes 196616 | tf_op jit(solution)/shard_map/gram/ppermute | solution.py:27
  82.8 0.8 collective-permute-start.36
  83.6 2.9 %collective-permute-done.26 = f32[128,128]{1,0:T(8,128)S(1)} collective-permute-done((f32[128,128]{1,0:T(8,128)S(1)}, f32[128,128]{1,0:T(8,128)S(1)}, u32[]{:S(2)}, u32[]{:S(2)}) %collective-permute-start.26) | collective-permute-done | bytes 65568 | tf_op jit(solution)/shard_map/gram/ppermute | solution.py:27
  86.5 0.9 collective-permute-start.29
  87.4 1.6 %collective-permute-start.30 = (f32[128,128]{1,0:T(8,128)S(1)}, f32[128,128]{1,0:T(8,128)S(1)}, u32[]{:S(2)}, u32[]{:S(2)}) collective-permute-start(f32[128,128]{1,0:T(8,128)S(1)} %add.84), channel_id=1, source_target_pairs={{0,12},{1,13},{2,14},{3,15},{4,8},{5,9},{6,10},{7,11},{8,4},{9,5},... | collective-permute-start | bytes 196616 | tf_op jit(solution)/shard_map/gram/ppermute | solution.py:27
  89.1 1.2 %collective-permute-start.28 = (f32[128,128]{1,0:T(8,128)S(1)}, f32[128,128]{1,0:T(8,128)S(1)}, u32[]{:S(2)}, u32[]{:S(2)}) collective-permute-start(f32[128,128]{1,0:T(8,128)S(1)} %add.84), channel_id=1, source_target_pairs={{0,4},{1,5},{2,6},{3,7},{4,0},{5,1},{6,2},{7,3},{8,12},{9,13},{10,... | collective-permute-start | bytes 196616 | tf_op jit(solution)/shard_map/gram/ppermute | solution.py:27
  90.4 1.4 %collective-permute-start.32 = (bf16[1024,128]{1,0:T(8,128)(2,1)S(1)}, bf16[1024,128]{1,0:T(8,128)(2,1)S(1)}, u32[]{:S(2)}, u32[]{:S(2)}) collective-permute-start(bf16[1024,128]{1,0:T(8,128)(2,1)S(1)} %pad_maximum_fusion.4.refs_1_), channel_id=1, source_target_pairs={{0,2},{1,3},{2,0},{3,1},{4,6},{5,7},{6,4},{7,5},{8,10},{9,11},{10,... | collective-permute-start | bytes 786440 | tf_op jit(solution)/shard_map/gather_range/ppermute | solution.py:27
  91.8 0.9 collective-permute-start.33
  92.9 0.9 collective-permute-start.35
  93.8 0.4 collective-permute-done.30
  94.1 0.6 collective-permute-start.37
  94.7 1.2 %coords.3.refs_5_ = f32[512,128]{1,0:T(8,128)S(1)} custom-call(s32[1]{0:T(128)} %bitcast.index_ref, s32[1]{0:T(128)} %bitcast.1.group_ref, bf16[256,16384]{1,0:T(8,128)(2,1)S(1)} %get-tuple-element.21.x_ref, bf16[256,8192]{1,0:T(8,128)(2,1)S(1)} %collective-permute-done.2.refs_0_, bf16[1024,128]{1,0:T(8,128)(2,1)S(1)} %pad_maximum_fusion.4.refs_1_, ...), custom_call_target="tpu_custom_call" | custom-call | flops 536870912 | bytes 4194304 | tf_op jit(solution)/shard_map/coords/pallas_call | solution.py:133
  96.0 6.4 %factor.1 = (f32[128,128]{1,0:T(8,128)S(1)}, f32[1024,128]{1,0:T(8,128)}) custom-call(f32[128,128]{1,0:T(8,128)S(1)} %add_add_fusion.gram_ref, f32[1024,128]{1,0:T(8,128)S(1)} %pad_maximum_fusion.range_ref), custom_call_target="tpu_custom_call" | custom-call | flops 10000000 | bytes 20000000 | tf_op jit(solution)/shard_map/factor/pallas_call | solution.py:217
  102.4 2.3 %collective-permute-done.37.refs_4_ = bf16[1024,128]{1,0:T(8,128)(2,1)S(1)} collective-permute-done((bf16[1024,128]{1,0:T(8,128)(2,1)S(1)}, bf16[1024,128]{1,0:T(8,128)(2,1)S(1)}, u32[]{:S(2)}, u32[]{:S(2)}) %collective-permute-start.37) | collective-permute-done | bytes 262176 | tf_op jit(solution)/shard_map/gather_range/ppermute | solution.py:27
  104.7 1.3 %coords.4.part_ref = f32[512,128]{1,0:T(8,128)S(1)} custom-call(s32[1]{0:T(128)} %bitcast.index_ref, s32[1]{0:T(128)} %bitcast.1.group_ref, bf16[256,16384]{1,0:T(8,128)(2,1)S(1)} %get-tuple-element.21.x_ref, bf16[256,8192]{1,0:T(8,128)(2,1)S(1)} %collective-permute-done.2.refs_0_, bf16[1024,128]{1,0:T(8,128)(2,1)S(1)} %collective-permute-done.32.refs_1_, ...), custom_call_target="tpu_custom_call" | custom-call | flops 536870912 | bytes 4194304 | tf_op jit(solution)/shard_map/coords/pallas_call | solution.py:133
  106.1 1.3 %collective-permute-done.38.theirs_ref = f32[256,128]{1,0:T(8,128)S(1)} collective-permute-done((f32[256,128]{1,0:T(8,128)S(1)}, f32[256,128]{1,0:T(8,128)S(1)}, u32[]{:S(2)}, u32[]{:S(2)}) %collective-permute-start.38) | collective-permute-done | bytes 131104 | tf_op jit(solution)/shard_map/coords/ppermute | solution.py:27
  107.4 1.0 coords.5
  (66 shorter events, 3.2 us)
Async XLA Ops:
  1.6 8.0 %collective-permute-start = (bf16[256,128]{1,0:T(8,128)(2,1)S(1)}, bf16[256,128]{1,0:T(8,128)(2,1)S(1)}, u32[]{:S(2)}, u32[]{:S(2)}) collective-permute-start(bf16[256,128]{1,0:T(8,128)(2,1)S(1)} %get-tuple-element.62), channel_id=1, source_target_pairs={{0,8},{1,9},{2,10},{3,11},{4,12},{5,13},{6,14},{7,15},{8,0},{9,1},... | collective-permute-start | bytes 196616 | tf_op jit(solution)/shard_map/gather_sketch/ppermute | solution.py:27
  5.7 6.5 %collective-permute-start.1 = (bf16[256,128]{1,0:T(8,128)(2,1)S(1)}, bf16[256,128]{1,0:T(8,128)(2,1)S(1)}, u32[]{:S(2)}, u32[]{:S(2)}) collective-permute-start(bf16[256,128]{1,0:T(8,128)(2,1)S(1)} %get-tuple-element.63), channel_id=1, source_target_pairs={{0,8},{1,9},{2,10},{3,11},{4,12},{5,13},{6,14},{7,15},{8,0},{9,1},... | collective-permute-start | bytes 196616 | tf_op jit(solution)/shard_map/gather_sketch/ppermute | solution.py:27
  12.1 17.8 %collective-permute-start.2 = (bf16[256,8192]{1,0:T(8,128)(2,1)S(1)}, bf16[256,8192]{1,0:T(8,128)(2,1)S(1)}, u32[]{:S(2)}, u32[]{:S(2)}) collective-permute-start(bf16[256,8192]{1,0:T(8,128)(2,1)S(1)} %get-tuple-element.23), channel_id=1, source_target_pairs={{0,1},{1,0},{2,3},{3,2},{4,5},{5,4},{6,7},{7,6},{8,9},{9,8},{10,11... | collective-permute-start | bytes 12582920 | tf_op jit(solution)/shard_map/split_features/ppermute | solution.py:27
  12.1 6.0 %collective-permute-start.3 = (bf16[512,128]{1,0:T(8,128)(2,1)S(1)}, bf16[512,128]{1,0:T(8,128)(2,1)S(1)}, u32[]{:S(2)}, u32[]{:S(2)}) collective-permute-start(bf16[512,128]{1,0:T(8,128)(2,1)S(1)} %pad_maximum_fusion.8), channel_id=1, source_target_pairs={{0,2},{1,3},{2,0},{3,1},{4,6},{5,7},{6,4},{7,5},{8,10},{9,11},{10,... | collective-permute-start | bytes 393224 | tf_op jit(solution)/shard_map/gather_sketch/ppermute | solution.py:27
  13.9 6.6 %collective-permute-start.9 = (bf16[256,128]{1,0:T(8,128)(2,1)S(1)}, bf16[256,128]{1,0:T(8,128)(2,1)S(1)}, u32[]{:S(2)}, u32[]{:S(2)}) collective-permute-start(bf16[256,128]{1,0:T(8,128)(2,1)S(1)} %get-tuple-element.61), channel_id=1, source_target_pairs={{0,8},{1,9},{2,10},{3,11},{4,12},{5,13},{6,14},{7,15},{8,0},{9,1},... | collective-permute-start | bytes 196616 | tf_op jit(solution)/shard_map/gather_sketch/ppermute | solution.py:27
  14.1 8.7 %collective-permute-start.7 = (bf16[512,128]{1,0:T(8,128)(2,1)S(1)}, bf16[512,128]{1,0:T(8,128)(2,1)S(1)}, u32[]{:S(2)}, u32[]{:S(2)}) collective-permute-start(bf16[512,128]{1,0:T(8,128)(2,1)S(1)} %pad_maximum_fusion.9), channel_id=1, source_target_pairs={{0,4},{1,5},{2,6},{3,7},{4,0},{5,1},{6,2},{7,3},{8,12},{9,13},{10,... | collective-permute-start | bytes 393224 | tf_op jit(solution)/shard_map/gather_sketch/ppermute | solution.py:27
  18.1 10.3 %collective-permute-start.4 = (bf16[1024,128]{1,0:T(8,128)(2,1)S(1)}, bf16[1024,128]{1,0:T(8,128)(2,1)S(1)}, u32[]{:S(2)}, u32[]{:S(2)}) collective-permute-start(bf16[1024,128]{1,0:T(8,128)(2,1)S(1)} %pad_maximum_fusion.1.refs_1_), channel_id=1, source_target_pairs={{0,4},{1,5},{2,6},{3,7},{4,0},{5,1},{6,2},{7,3},{8,12},{9,13},{10,... | collective-permute-start | bytes 786440 | tf_op jit(solution)/shard_map/gather_sketch/ppermute | solution.py:27
  20.5 6.4 %collective-permute-start.10 = (bf16[512,128]{1,0:T(8,128)(2,1)S(1)}, bf16[512,128]{1,0:T(8,128)(2,1)S(1)}, u32[]{:S(2)}, u32[]{:S(2)}) collective-permute-start(bf16[512,128]{1,0:T(8,128)(2,1)S(1)} %pad_maximum_fusion.10), channel_id=1, source_target_pairs={{0,2},{1,3},{2,0},{3,1},{4,6},{5,7},{6,4},{7,5},{8,10},{9,11},{10,... | collective-permute-start | bytes 393224 | tf_op jit(solution)/shard_map/gather_sketch/ppermute | solution.py:27
  21.0 10.0 %collective-permute-start.5 = (bf16[1024,128]{1,0:T(8,128)(2,1)S(1)}, bf16[1024,128]{1,0:T(8,128)(2,1)S(1)}, u32[]{:S(2)}, u32[]{:S(2)}) collective-permute-start(bf16[1024,128]{1,0:T(8,128)(2,1)S(1)} %pad_maximum_fusion.1.refs_1_), channel_id=1, source_target_pairs={{0,16},{16,0},{1,17},{17,1},{2,18},{18,2},{3,19},{19,3},{4,20},{20... | collective-permute-start | bytes 786440 | tf_op jit(solution)/shard_map/gather_sketch/ppermute | solution.py:257
  22.8 8.4 %collective-permute-start.8 = (bf16[1024,128]{1,0:T(8,128)(2,1)S(1)}, bf16[1024,128]{1,0:T(8,128)(2,1)S(1)}, u32[]{:S(2)}, u32[]{:S(2)}) collective-permute-start(bf16[1024,128]{1,0:T(8,128)(2,1)S(1)} %pad_maximum_fusion.2.refs_2_), channel_id=1, source_target_pairs={{0,2},{1,3},{2,0},{3,1},{4,6},{5,7},{6,4},{7,5},{8,10},{9,11},{10,... | collective-permute-start | bytes 786440 | tf_op jit(solution)/shard_map/gather_sketch/ppermute | solution.py:27
  27.0 6.4 %collective-permute-start.11 = (bf16[1024,128]{1,0:T(8,128)(2,1)S(1)}, bf16[1024,128]{1,0:T(8,128)(2,1)S(1)}, u32[]{:S(2)}, u32[]{:S(2)}) collective-permute-start(bf16[1024,128]{1,0:T(8,128)(2,1)S(1)} %pad_maximum_fusion.3.refs_3_), channel_id=1, source_target_pairs={{0,4},{1,5},{2,6},{3,7},{4,0},{5,1},{6,2},{7,3},{8,12},{9,13},{10,... | collective-permute-start | bytes 786440 | tf_op jit(solution)/shard_map/gather_sketch/ppermute | solution.py:27
  28.4 6.9 %collective-permute-start.6 = (bf16[1024,128]{1,0:T(8,128)(2,1)S(1)}, bf16[1024,128]{1,0:T(8,128)(2,1)S(1)}, u32[]{:S(2)}, u32[]{:S(2)}) collective-permute-start(bf16[1024,128]{1,0:T(8,128)(2,1)S(1)} %collective-permute-done.4.refs_1_), channel_id=1, source_target_pairs={{0,16},{16,0},{1,17},{17,1},{2,18},{18,2},{3,19},{19,3},{4,20},{20... | collective-permute-start | bytes 786440 | tf_op jit(solution)/shard_map/gather_sketch/ppermute | solution.py:257
  36.9 1.6 %collective-permute-start.12 = (f32[512,128]{1,0:T(8,128)S(1)}, f32[512,128]{1,0:T(8,128)S(1)}, u32[]{:S(2)}, u32[]{:S(2)}) collective-permute-start(f32[512,128]{1,0:T(8,128)S(1)} %sketched.3), channel_id=1, source_target_pairs={{0,1},{1,0},{2,3},{3,2},{4,5},{5,4},{6,7},{7,6},{8,9},{9,8},{10,11... | collective-permute-start | bytes 786440 | tf_op jit(solution)/shard_map/sketched/ppermute | solution.py:27
  39.4 9.2 %collective-permute-start.22 = (bf16[1024,128]{1,0:T(8,128)(2,1)S(1)}, bf16[1024,128]{1,0:T(8,128)(2,1)S(1)}, u32[]{:S(2)}, u32[]{:S(2)}) collective-permute-start(bf16[1024,128]{1,0:T(8,128)(2,1)S(1)} %get-tuple-element.31), channel_id=1, source_target_pairs={{0,4},{1,5},{2,6},{3,7},{4,0},{5,1},{6,2},{7,3},{8,12},{9,13},{10,... | collective-permute-start | bytes 786440 | tf_op jit(solution)/shard_map/range/ppermute | solution.py:27
  40.3 9.2 %collective-permute-start.19 = (bf16[1024,128]{1,0:T(8,128)(2,1)S(1)}, bf16[1024,128]{1,0:T(8,128)(2,1)S(1)}, u32[]{:S(2)}, u32[]{:S(2)}) collective-permute-start(bf16[1024,128]{1,0:T(8,128)(2,1)S(1)} %get-tuple-element.29), channel_id=1, source_target_pairs={{0,2},{1,3},{2,0},{3,1},{4,6},{5,7},{6,4},{7,5},{8,10},{9,11},{10,... | collective-permute-start | bytes 786440 | tf_op jit(solution)/shard_map/range/ppermute | solution.py:27
  40.7 14.7 %collective-permute-start.16 = (bf16[1024,128]{1,0:T(8,128)(2,1)S(1)}, bf16[1024,128]{1,0:T(8,128)(2,1)S(1)}, u32[]{:S(2)}, u32[]{:S(2)}) collective-permute-start(bf16[1024,128]{1,0:T(8,128)(2,1)S(1)} %get-tuple-element.27), channel_id=1, source_target_pairs={{0,4},{1,5},{2,6},{3,7},{4,0},{5,1},{6,2},{7,3},{8,12},{9,13},{10,... | collective-permute-start | bytes 786440 | tf_op jit(solution)/shard_map/range/ppermute | solution.py:27
  41.7 14.0 %collective-permute-start.13 = (bf16[1024,128]{1,0:T(8,128)(2,1)S(1)}, bf16[1024,128]{1,0:T(8,128)(2,1)S(1)}, u32[]{:S(2)}, u32[]{:S(2)}) collective-permute-start(bf16[1024,128]{1,0:T(8,128)(2,1)S(1)} %get-tuple-element.25), channel_id=1, source_target_pairs={{0,2},{1,3},{2,0},{3,1},{4,6},{5,7},{6,4},{7,5},{8,10},{9,11},{10,... | collective-permute-start | bytes 786440 | tf_op jit(solution)/shard_map/range/ppermute | solution.py:27
  48.9 7.9 %collective-permute-start.23 = (bf16[512,128]{1,0:T(8,128)(2,1)S(1)}, bf16[512,128]{1,0:T(8,128)(2,1)S(1)}, u32[]{:S(2)}, u32[]{:S(2)}) collective-permute-start(bf16[512,128]{1,0:T(8,128)(2,1)S(1)} %fusion.25), channel_id=1, source_target_pairs={{0,2},{1,3},{2,0},{3,1},{4,6},{5,7},{6,4},{7,5},{8,10},{9,11},{10,... | collective-permute-start | bytes 393224 | tf_op jit(solution)/shard_map/range/ppermute | solution.py:27
  49.7 10.0 %collective-permute-start.20 = (bf16[512,128]{1,0:T(8,128)(2,1)S(1)}, bf16[512,128]{1,0:T(8,128)(2,1)S(1)}, u32[]{:S(2)}, u32[]{:S(2)}) collective-permute-start(bf16[512,128]{1,0:T(8,128)(2,1)S(1)} %fusion.22), channel_id=1, source_target_pairs={{0,8},{1,9},{2,10},{3,11},{4,12},{5,13},{6,14},{7,15},{8,0},{9,1},... | collective-permute-start | bytes 393224 | tf_op jit(solution)/shard_map/range/ppermute | solution.py:27
  55.7 5.0 %collective-permute-start.17 = (bf16[512,128]{1,0:T(8,128)(2,1)S(1)}, bf16[512,128]{1,0:T(8,128)(2,1)S(1)}, u32[]{:S(2)}, u32[]{:S(2)}) collective-permute-start(bf16[512,128]{1,0:T(8,128)(2,1)S(1)} %fusion.19), channel_id=1, source_target_pairs={{0,2},{1,3},{2,0},{3,1},{4,6},{5,7},{6,4},{7,5},{8,10},{9,11},{10,... | collective-permute-start | bytes 393224 | tf_op jit(solution)/shard_map/range/ppermute | solution.py:27
  56.0 9.2 %collective-permute-start.14 = (bf16[512,128]{1,0:T(8,128)(2,1)S(1)}, bf16[512,128]{1,0:T(8,128)(2,1)S(1)}, u32[]{:S(2)}, u32[]{:S(2)}) collective-permute-start(bf16[512,128]{1,0:T(8,128)(2,1)S(1)} %fusion.16), channel_id=1, source_target_pairs={{0,4},{1,5},{2,6},{3,7},{4,0},{5,1},{6,2},{7,3},{8,12},{9,13},{10,... | collective-permute-start | bytes 393224 | tf_op jit(solution)/shard_map/range/ppermute | solution.py:27
  56.9 10.3 %collective-permute-start.24 = (bf16[512,128]{1,0:T(8,128)(2,1)S(1)}, bf16[512,128]{1,0:T(8,128)(2,1)S(1)}, u32[]{:S(2)}, u32[]{:S(2)}) collective-permute-start(bf16[512,128]{1,0:T(8,128)(2,1)S(1)} %get-tuple-element.53), channel_id=1, source_target_pairs={{0,8},{1,9},{2,10},{3,11},{4,12},{5,13},{6,14},{7,15},{8,0},{9,1},... | collective-permute-start | bytes 393224 | tf_op jit(solution)/shard_map/range/ppermute | solution.py:27
  59.9 8.4 %collective-permute-start.21 = (bf16[512,128]{1,0:T(8,128)(2,1)S(1)}, bf16[512,128]{1,0:T(8,128)(2,1)S(1)}, u32[]{:S(2)}, u32[]{:S(2)}) collective-permute-start(bf16[512,128]{1,0:T(8,128)(2,1)S(1)} %get-tuple-element.51), channel_id=1, source_target_pairs={{0,4},{1,5},{2,6},{3,7},{4,0},{5,1},{6,2},{7,3},{8,12},{9,13},{10,... | collective-permute-start | bytes 393224 | tf_op jit(solution)/shard_map/range/ppermute | solution.py:27
  60.8 13.9 %collective-permute-start.18 = (bf16[512,128]{1,0:T(8,128)(2,1)S(1)}, bf16[512,128]{1,0:T(8,128)(2,1)S(1)}, u32[]{:S(2)}, u32[]{:S(2)}) collective-permute-start(bf16[512,128]{1,0:T(8,128)(2,1)S(1)} %get-tuple-element.49), channel_id=1, source_target_pairs={{0,8},{1,9},{2,10},{3,11},{4,12},{5,13},{6,14},{7,15},{8,0},{9,1},... | collective-permute-start | bytes 393224 | tf_op jit(solution)/shard_map/range/ppermute | solution.py:27
  65.4 10.9 %collective-permute-start.15 = (bf16[512,128]{1,0:T(8,128)(2,1)S(1)}, bf16[512,128]{1,0:T(8,128)(2,1)S(1)}, u32[]{:S(2)}, u32[]{:S(2)}) collective-permute-start(bf16[512,128]{1,0:T(8,128)(2,1)S(1)} %get-tuple-element.47), channel_id=1, source_target_pairs={{0,8},{1,9},{2,10},{3,11},{4,12},{5,13},{6,14},{7,15},{8,0},{9,1},... | collective-permute-start | bytes 393224 | tf_op jit(solution)/shard_map/range/ppermute | solution.py:27
  77.6 3.9 %collective-permute-start.25 = (f32[128,128]{1,0:T(8,128)S(1)}, f32[128,128]{1,0:T(8,128)S(1)}, u32[]{:S(2)}, u32[]{:S(2)}) collective-permute-start(f32[128,128]{1,0:T(8,128)S(1)} %fusion.33), channel_id=1, source_target_pairs={{0,1},{1,0},{2,3},{3,2},{4,5},{5,4},{6,7},{7,6},{8,9},{9,8},{10,11... | collective-permute-start | bytes 196616 | tf_op jit(solution)/shard_map/gram/ppermute | solution.py:27
  77.7 8.8 %collective-permute-start.27 = (bf16[512,128]{1,0:T(8,128)(2,1)S(1)}, bf16[512,128]{1,0:T(8,128)(2,1)S(1)}, u32[]{:S(2)}, u32[]{:S(2)}) collective-permute-start(bf16[512,128]{1,0:T(8,128)(2,1)S(1)} %pad_maximum_fusion.11), channel_id=1, source_target_pairs={{0,2},{1,3},{2,0},{3,1},{4,6},{5,7},{6,4},{7,5},{8,10},{9,11},{10,... | collective-permute-start | bytes 393224 | tf_op jit(solution)/shard_map/gather_range/ppermute | solution.py:27
  79.0 10.1 %collective-permute-start.31 = (bf16[512,128]{1,0:T(8,128)(2,1)S(1)}, bf16[512,128]{1,0:T(8,128)(2,1)S(1)}, u32[]{:S(2)}, u32[]{:S(2)}) collective-permute-start(bf16[512,128]{1,0:T(8,128)(2,1)S(1)} %pad_maximum_fusion.12), channel_id=1, source_target_pairs={{0,4},{1,5},{2,6},{3,7},{4,0},{5,1},{6,2},{7,3},{8,12},{9,13},{10,... | collective-permute-start | bytes 393224 | tf_op jit(solution)/shard_map/gather_range/ppermute | solution.py:27
  79.1 11.3 %collective-permute-start.34 = (bf16[512,128]{1,0:T(8,128)(2,1)S(1)}, bf16[512,128]{1,0:T(8,128)(2,1)S(1)}, u32[]{:S(2)}, u32[]{:S(2)}) collective-permute-start(bf16[512,128]{1,0:T(8,128)(2,1)S(1)} %pad_maximum_fusion.13), channel_id=1, source_target_pairs={{0,8},{1,9},{2,10},{3,11},{4,12},{5,13},{6,14},{7,15},{8,0},{9,1},... | collective-permute-start | bytes 393224 | tf_op jit(solution)/shard_map/gather_range/ppermute | solution.py:27
  81.4 5.0 %collective-permute-start.26 = (f32[128,128]{1,0:T(8,128)S(1)}, f32[128,128]{1,0:T(8,128)S(1)}, u32[]{:S(2)}, u32[]{:S(2)}) collective-permute-start(f32[128,128]{1,0:T(8,128)S(1)} %add.83), channel_id=1, source_target_pairs={{0,2},{1,3},{2,0},{3,1},{4,6},{5,7},{6,4},{7,5},{8,10},{9,11},{10,... | collective-permute-start | bytes 196616 | tf_op jit(solution)/shard_map/gram/ppermute | solution.py:27
  82.8 9.0 %collective-permute-start.36 = (bf16[512,128]{1,0:T(8,128)(2,1)S(1)}, bf16[512,128]{1,0:T(8,128)(2,1)S(1)}, u32[]{:S(2)}, u32[]{:S(2)}) collective-permute-start(bf16[512,128]{1,0:T(8,128)(2,1)S(1)} %pad_maximum_fusion.14), channel_id=1, source_target_pairs={{0,2},{1,3},{2,0},{3,1},{4,6},{5,7},{6,4},{7,5},{8,10},{9,11},{10,... | collective-permute-start | bytes 393224 | tf_op jit(solution)/shard_map/gather_range/ppermute | solution.py:27
  86.5 6.3 %collective-permute-start.29 = (f32[128,128]{1,0:T(8,128)S(1)}, f32[128,128]{1,0:T(8,128)S(1)}, u32[]{:S(2)}, u32[]{:S(2)}) collective-permute-start(f32[128,128]{1,0:T(8,128)S(1)} %add.84), channel_id=1, source_target_pairs={{0,8},{1,9},{2,10},{3,11},{4,12},{5,13},{6,14},{7,15},{8,0},{9,1},... | collective-permute-start | bytes 196616 | tf_op jit(solution)/shard_map/gram/ppermute | solution.py:27
  87.4 6.7 %collective-permute-start.30 = (f32[128,128]{1,0:T(8,128)S(1)}, f32[128,128]{1,0:T(8,128)S(1)}, u32[]{:S(2)}, u32[]{:S(2)}) collective-permute-start(f32[128,128]{1,0:T(8,128)S(1)} %add.84), channel_id=1, source_target_pairs={{0,12},{1,13},{2,14},{3,15},{4,8},{5,9},{6,10},{7,11},{8,4},{9,5},... | collective-permute-start | bytes 196616 | tf_op jit(solution)/shard_map/gram/ppermute | solution.py:27
  89.1 6.9 %collective-permute-start.28 = (f32[128,128]{1,0:T(8,128)S(1)}, f32[128,128]{1,0:T(8,128)S(1)}, u32[]{:S(2)}, u32[]{:S(2)}) collective-permute-start(f32[128,128]{1,0:T(8,128)S(1)} %add.84), channel_id=1, source_target_pairs={{0,4},{1,5},{2,6},{3,7},{4,0},{5,1},{6,2},{7,3},{8,12},{9,13},{10,... | collective-permute-start | bytes 196616 | tf_op jit(solution)/shard_map/gram/ppermute | solution.py:27
  90.4 12.1 %collective-permute-start.32 = (bf16[1024,128]{1,0:T(8,128)(2,1)S(1)}, bf16[1024,128]{1,0:T(8,128)(2,1)S(1)}, u32[]{:S(2)}, u32[]{:S(2)}) collective-permute-start(bf16[1024,128]{1,0:T(8,128)(2,1)S(1)} %pad_maximum_fusion.4.refs_1_), channel_id=1, source_target_pairs={{0,2},{1,3},{2,0},{3,1},{4,6},{5,7},{6,4},{7,5},{8,10},{9,11},{10,... | collective-permute-start | bytes 786440 | tf_op jit(solution)/shard_map/gather_range/ppermute | solution.py:27
  91.8 10.6 %collective-permute-start.33 = (bf16[1024,128]{1,0:T(8,128)(2,1)S(1)}, bf16[1024,128]{1,0:T(8,128)(2,1)S(1)}, u32[]{:S(2)}, u32[]{:S(2)}) collective-permute-start(bf16[1024,128]{1,0:T(8,128)(2,1)S(1)} %pad_maximum_fusion.5.refs_2_), channel_id=1, source_target_pairs={{0,4},{1,5},{2,6},{3,7},{4,0},{5,1},{6,2},{7,3},{8,12},{9,13},{10,... | collective-permute-start | bytes 786440 | tf_op jit(solution)/shard_map/gather_range/ppermute | solution.py:27
  92.9 9.6 %collective-permute-start.35 = (bf16[1024,128]{1,0:T(8,128)(2,1)S(1)}, bf16[1024,128]{1,0:T(8,128)(2,1)S(1)}, u32[]{:S(2)}, u32[]{:S(2)}) collective-permute-start(bf16[1024,128]{1,0:T(8,128)(2,1)S(1)} %pad_maximum_fusion.6.refs_3_), channel_id=1, source_target_pairs={{0,2},{1,3},{2,0},{3,1},{4,6},{5,7},{6,4},{7,5},{8,10},{9,11},{10,... | collective-permute-start | bytes 786440 | tf_op jit(solution)/shard_map/gather_range/ppermute | solution.py:27
  94.1 10.6 %collective-permute-start.37 = (bf16[1024,128]{1,0:T(8,128)(2,1)S(1)}, bf16[1024,128]{1,0:T(8,128)(2,1)S(1)}, u32[]{:S(2)}, u32[]{:S(2)}) collective-permute-start(bf16[1024,128]{1,0:T(8,128)(2,1)S(1)} %pad_maximum_fusion.7.refs_4_), channel_id=1, source_target_pairs={{0,4},{1,5},{2,6},{3,7},{4,0},{5,1},{6,2},{7,3},{8,12},{9,13},{10,... | collective-permute-start | bytes 786440 | tf_op jit(solution)/shard_map/gather_range/ppermute | solution.py:27
  106.0 1.4 %collective-permute-start.38 = (f32[256,128]{1,0:T(8,128)S(1)}, f32[256,128]{1,0:T(8,128)S(1)}, u32[]{:S(2)}, u32[]{:S(2)}) collective-permute-start(f32[256,128]{1,0:T(8,128)S(1)} %slice.136), channel_id=1, source_target_pairs={{0,1},{1,0},{2,3},{3,2},{4,5},{5,4},{6,7},{7,6},{8,9},{9,8},{10,11... | collective-permute-start | bytes 393224 | tf_op jit(solution)/shard_map/coords/ppermute | solution.py:27

commit v6 on v5

--- a/solution.py
+++ b/solution.py
@@ -18,7 +18,7 @@
 X_BIT, ZLO, ZHI = 1, 2, 4
 HLX, HXL, LHX = (ZHI, ZLO, X_BIT), (ZHI, X_BIT, ZLO), (ZLO, ZHI, X_BIT)
 SKETCH_PIECES = ((2, HXL, True), (2, HLX, False), (2, HXL, False))
-RANGE_PIECES = ((2, HLX, False), (2, HXL, False), (2, LHX, False), (2, HXL, False))
+RANGE_PIECES = ((2, HXL, False), (2, HLX, False), (2, LHX, False), (2, HXL, False))
 LOADS, PARTS = 8, 1
 TIED = 2
 
@@ -313,7 +313,7 @@
         gram = jnp.dot(range_rows.T, range_rows, preferred_element_type=F32, precision=HIGH)
         for bit in (1, 2):
             gram = gram + swap(gram, bit, n)
-        gram = after(gram, came[1])
+        gram = after(gram, came[0])
         apart = [swap(gram, bit, n) for bit in (4, 8, 12)]
         gram = (gram + apart[0]) + (apart[1] + apart[2])
     with jax.named_scope("gather_range"):

time: 109 us -> 108 us (level)
  waiting for transfers between devices: 43.6 us -> 40.4 us
  starting transfers between devices: 41.3 us -> 43.9 us
    ppermute x37, waiting for transfers between devices: 41.7 us -> 38.5 us  [swap(): return lax.ppermute(value, 'tok', [(i, i ^ bit) for i in range(n)])]
    ppermute x37, starting transfers between devices: 38.1 us -> 40.7 us  [swap(): return lax.ppermute(value, 'tok', [(i, i ^ bit) for i in range(n)])]
  transfers between devices with their start and end apart: 39 -> 39, of which waited for: 25 -> 20; matrix products, arithmetic and copies ran while one was open for 2% -> 2% of each run, Pallas kernels for 12% -> 12%
where the time goes in v6:
time: 108 us
  starting transfers between devices  43.9 us (41%)
  waiting for transfers between devices  40.4 us (37%)
  Pallas kernels  18 us (17%)
  other arithmetic  2.52 us (2%)
    ppermute x37, starting transfers between devices, swap(): return lax.ppermute(value, 'tok', [(i, i ^ bit) for i in range(n)])  40.7 us
    ppermute x37, waiting for transfers between devices, swap(): return lax.ppermute(value, 'tok', [(i, i ^ bit) for i in range(n)])  38.5 us
    pallas_call x1, Pallas kernels, factored(): pl.pallas_call(functools.partial(factor_kernel, scale), in_specs=[VMEM] *...  6.41 us
    pallas_call x4, Pallas kernels, project(): pl.pallas_call(functools.partial(project_kernel, width, entries, init is...  5.02 us
    pallas_call x1, Pallas kernels, load(): pl.pallas_call(functools.partial(load_kernel, width), in_specs=[SMEM, ANY...  3.78 us
    ppermute x2, starting transfers between devices, across(): return lax.ppermute(value, 'groups', [(0, 1), (1, 0)])  3.2 us
  transfers between devices with their start and end apart: 39, of which 20 were waited for; matrix products, arithmetic and copies ran while one was open for 2% of the time, Pallas kernels for 12%

profile of v6, /device:TPU:0, one launch (start us, length us, event | category | flops | bytes accessed | tf_op | source)
XLA Modules:
  0.0 107.8 jit_solution(2484833748116919532)
XLA Ops:
  0.6 0.9 slice_bitcast_fusion
  1.6 4.1 %collective-permute-start = (bf16[256,128]{1,0:T(8,128)(2,1)S(1)}, bf16[256,128]{1,0:T(8,128)(2,1)S(1)}, u32[]{:S(2)}, u32[]{:S(2)}) collective-permute-start(bf16[256,128]{1,0:T(8,128)(2,1)S(1)} %get-tuple-element.62), channel_id=1, source_target_pairs={{0,8},{1,9},{2,10},{3,11},{4,12},{5,13},{6,14},{7,15},{8,0},{9,1},... | collective-permute-start | bytes 196616 | tf_op jit(solution)/shard_map/gather_sketch/ppermute | solution.py:27
  5.7 3.8 %split_features.1 = (bf16[256,16384]{1,0:T(8,128)(2,1)S(1)}, f32[256,128]{1,0:T(8,128)S(1)}, bf16[256,8192]{1,0:T(8,128)(2,1)S(1)}) custom-call(s32[1]{0:T(128)} %bitcast.index_ref, bf16[256,16384]{1,0:T(8,128)(2,1)} %x_ref.1), custom_call_target="tpu_custom_call" | custom-call | flops 8388608 | bytes 16777216 | tf_op jit(solution)/shard_map/split_features/pallas_call | solution.py:94
  9.5 2.6 %collective-permute-done.1 = bf16[256,128]{1,0:T(8,128)(2,1)S(1)} collective-permute-done((bf16[256,128]{1,0:T(8,128)(2,1)S(1)}, bf16[256,128]{1,0:T(8,128)(2,1)S(1)}, u32[]{:S(2)}, u32[]{:S(2)}) %collective-permute-start.1) | collective-permute-done | bytes 65568 | tf_op jit(solution)/shard_map/gather_sketch/ppermute | solution.py:27
  12.1 1.8 %collective-permute-start.3 = (bf16[512,128]{1,0:T(8,128)(2,1)S(1)}, bf16[512,128]{1,0:T(8,128)(2,1)S(1)}, u32[]{:S(2)}, u32[]{:S(2)}) collective-permute-start(bf16[512,128]{1,0:T(8,128)(2,1)S(1)} %pad_maximum_fusion.8), channel_id=1, source_target_pairs={{0,2},{1,3},{2,0},{3,1},{4,6},{5,7},{6,4},{7,5},{8,10},{9,11},{10,... | collective-permute-start | bytes 393224 | tf_op jit(solution)/shard_map/gather_sketch/ppermute | solution.py:27
  14.1 3.7 %collective-permute-start.7 = (bf16[512,128]{1,0:T(8,128)(2,1)S(1)}, bf16[512,128]{1,0:T(8,128)(2,1)S(1)}, u32[]{:S(2)}, u32[]{:S(2)}) collective-permute-start(bf16[512,128]{1,0:T(8,128)(2,1)S(1)} %pad_maximum_fusion.9), channel_id=1, source_target_pairs={{0,4},{1,5},{2,6},{3,7},{4,0},{5,1},{6,2},{7,3},{8,12},{9,13},{10,... | collective-permute-start | bytes 393224 | tf_op jit(solution)/shard_map/gather_sketch/ppermute | solution.py:27
  17.7 0.4 collective-permute-done.3
  18.1 0.6 collective-permute-start.4
  18.8 1.8 %collective-permute-done.9 = bf16[256,128]{1,0:T(8,128)(2,1)S(1)} collective-permute-done((bf16[256,128]{1,0:T(8,128)(2,1)S(1)}, bf16[256,128]{1,0:T(8,128)(2,1)S(1)}, u32[]{:S(2)}, u32[]{:S(2)}) %collective-permute-start.9) | collective-permute-done | bytes 65568 | tf_op jit(solution)/shard_map/gather_sketch/ppermute | solution.py:27
  20.5 0.4 collective-permute-start.10
  21.0 1.7 %collective-permute-start.5 = (bf16[1024,128]{1,0:T(8,128)(2,1)S(1)}, bf16[1024,128]{1,0:T(8,128)(2,1)S(1)}, u32[]{:S(2)}, u32[]{:S(2)}) collective-permute-start(bf16[1024,128]{1,0:T(8,128)(2,1)S(1)} %pad_maximum_fusion.1.refs_1_), channel_id=1, source_target_pairs={{0,16},{16,0},{1,17},{17,1},{2,18},{18,2},{3,19},{19,3},{4,20},{20... | collective-permute-start | bytes 786440 | tf_op jit(solution)/shard_map/gather_sketch/ppermute | solution.py:257
  22.8 1.4 %collective-permute-start.8 = (bf16[1024,128]{1,0:T(8,128)(2,1)S(1)}, bf16[1024,128]{1,0:T(8,128)(2,1)S(1)}, u32[]{:S(2)}, u32[]{:S(2)}) collective-permute-start(bf16[1024,128]{1,0:T(8,128)(2,1)S(1)} %pad_maximum_fusion.2.refs_2_), channel_id=1, source_target_pairs={{0,2},{1,3},{2,0},{3,1},{4,6},{5,7},{6,4},{7,5},{8,10},{9,11},{10,... | collective-permute-start | bytes 786440 | tf_op jit(solution)/shard_map/gather_sketch/ppermute | solution.py:27
  24.3 2.7 %collective-permute-done.10 = bf16[512,128]{1,0:T(8,128)(2,1)S(1)} collective-permute-done((bf16[512,128]{1,0:T(8,128)(2,1)S(1)}, bf16[512,128]{1,0:T(8,128)(2,1)S(1)}, u32[]{:S(2)}, u32[]{:S(2)}) %collective-permute-start.10) | collective-permute-done | bytes 131104 | tf_op jit(solution)/shard_map/gather_sketch/ppermute | solution.py:27
  27.1 1.3 %collective-permute-done.4.refs_1_ = bf16[1024,128]{1,0:T(8,128)(2,1)S(1)} collective-permute-done((bf16[1024,128]{1,0:T(8,128)(2,1)S(1)}, bf16[1024,128]{1,0:T(8,128)(2,1)S(1)}, u32[]{:S(2)}, u32[]{:S(2)}) %collective-permute-start.4) | collective-permute-done | bytes 262176 | tf_op jit(solution)/shard_map/gather_sketch/ppermute | solution.py:27
  28.4 1.5 %collective-permute-start.6 = (bf16[1024,128]{1,0:T(8,128)(2,1)S(1)}, bf16[1024,128]{1,0:T(8,128)(2,1)S(1)}, u32[]{:S(2)}, u32[]{:S(2)}) collective-permute-start(bf16[1024,128]{1,0:T(8,128)(2,1)S(1)} %collective-permute-done.4.refs_1_), channel_id=1, source_target_pairs={{0,16},{16,0},{1,17},{17,1},{2,18},{18,2},{3,19},{19,3},{4,20},{20... | collective-permute-start | bytes 786440 | tf_op jit(solution)/shard_map/gather_sketch/ppermute | solution.py:257
  30.0 1.0 sketched.2.refs_6_
  31.0 0.2 collective-permute-done.8.refs_4_
  31.2 2.2 %collective-permute-done.11.refs_5_ = bf16[1024,128]{1,0:T(8,128)(2,1)S(1)} collective-permute-done((bf16[1024,128]{1,0:T(8,128)(2,1)S(1)}, bf16[1024,128]{1,0:T(8,128)(2,1)S(1)}, u32[]{:S(2)}, u32[]{:S(2)}) %collective-permute-start.11) | collective-permute-done | bytes 262176 | tf_op jit(solution)/shard_map/gather_sketch/ppermute | solution.py:27
  33.4 1.9 %collective-permute-done.6.refs_3_ = bf16[1024,128]{1,0:T(8,128)(2,1)S(1)} collective-permute-done((bf16[1024,128]{1,0:T(8,128)(2,1)S(1)}, bf16[1024,128]{1,0:T(8,128)(2,1)S(1)}, u32[]{:S(2)}, u32[]{:S(2)}) %collective-permute-start.6) | collective-permute-done | bytes 262176 | tf_op jit(solution)/shard_map/gather_sketch/ppermute | solution.py:257
  35.3 1.5 %sketched.3 = f32[512,128]{1,0:T(8,128)S(1)} custom-call(s32[1]{0:T(128)} %bitcast.index_ref, s32[1]{0:T(128)} %bitcast.1.group_ref, bf16[256,16384]{1,0:T(8,128)(2,1)S(1)} %get-tuple-element.21.x_ref, bf16[256,8192]{1,0:T(8,128)(2,1)S(1)} %collective-permute-done.2.refs_0_, bf16[1024,128]{1,0:T(8,128)(2,1)S(1)} %collective-permute-done.4.refs_1_, ...), custom_call_target="tpu_custom_call" | custom-call | flops 671088640 | bytes 5242880 | tf_op jit(solution)/shard_map/sketched/pallas_call | solution.py:133
  36.9 1.5 %collective-permute-done.12 = f32[512,128]{1,0:T(8,128)S(1)} collective-permute-done((f32[512,128]{1,0:T(8,128)S(1)}, f32[512,128]{1,0:T(8,128)S(1)}, u32[]{:S(2)}, u32[]{:S(2)}) %collective-permute-start.12) | collective-permute-done | bytes 262176 | tf_op jit(solution)/shard_map/sketched/ppermute | solution.py:27
  38.5 0.9 range.3
  39.4 0.8 collective-permute-start.22
  40.3 0.4 collective-permute-start.19
  40.7 1.6 %collective-permute-start.16 = (bf16[1024,128]{1,0:T(8,128)(2,1)S(1)}, bf16[1024,128]{1,0:T(8,128)(2,1)S(1)}, u32[]{:S(2)}, u32[]{:S(2)}) collective-permute-start(bf16[1024,128]{1,0:T(8,128)(2,1)S(1)} %get-tuple-element.27), channel_id=1, source_target_pairs={{0,2},{1,3},{2,0},{3,1},{4,6},{5,7},{6,4},{7,5},{8,10},{9,11},{10,... | collective-permute-start | bytes 786440 | tf_op jit(solution)/shard_map/range/ppermute | solution.py:27
  42.3 1.2 %collective-permute-start.13 = (bf16[1024,128]{1,0:T(8,128)(2,1)S(1)}, bf16[1024,128]{1,0:T(8,128)(2,1)S(1)}, u32[]{:S(2)}, u32[]{:S(2)}) collective-permute-start(bf16[1024,128]{1,0:T(8,128)(2,1)S(1)} %get-tuple-element.25), channel_id=1, source_target_pairs={{0,4},{1,5},{2,6},{3,7},{4,0},{5,1},{6,2},{7,3},{8,12},{9,13},{10,... | collective-permute-start | bytes 786440 | tf_op jit(solution)/shard_map/range/ppermute | solution.py:27
  43.6 0.9 range.2
  44.5 4.2 %collective-permute-done.22 = bf16[1024,128]{1,0:T(8,128)(2,1)S(1)} collective-permute-done((bf16[1024,128]{1,0:T(8,128)(2,1)S(1)}, bf16[1024,128]{1,0:T(8,128)(2,1)S(1)}, u32[]{:S(2)}, u32[]{:S(2)}) %collective-permute-start.22) | collective-permute-done | bytes 262176 | tf_op jit(solution)/shard_map/range/ppermute | solution.py:27
  48.9 0.3 collective-permute-start.23
  49.2 0.3 collective-permute-done.19
  49.5 0.2 fusion.6
  49.7 1.7 %collective-permute-start.20 = (bf16[512,128]{1,0:T(8,128)(2,1)S(1)}, bf16[512,128]{1,0:T(8,128)(2,1)S(1)}, u32[]{:S(2)}, u32[]{:S(2)}) collective-permute-start(bf16[512,128]{1,0:T(8,128)(2,1)S(1)} %fusion.22), channel_id=1, source_target_pairs={{0,8},{1,9},{2,10},{3,11},{4,12},{5,13},{6,14},{7,15},{8,0},{9,1},... | collective-permute-start | bytes 393224 | tf_op jit(solution)/shard_map/range/ppermute | solution.py:27
  51.4 3.6 %collective-permute-done.16 = bf16[1024,128]{1,0:T(8,128)(2,1)S(1)} collective-permute-done((bf16[1024,128]{1,0:T(8,128)(2,1)S(1)}, bf16[1024,128]{1,0:T(8,128)(2,1)S(1)}, u32[]{:S(2)}, u32[]{:S(2)}) %collective-permute-start.16) | collective-permute-done | bytes 262176 | tf_op jit(solution)/shard_map/range/ppermute | solution.py:27
  55.1 0.2 fusion.5
  55.4 1.3 %collective-permute-start.17 = (bf16[512,128]{1,0:T(8,128)(2,1)S(1)}, bf16[512,128]{1,0:T(8,128)(2,1)S(1)}, u32[]{:S(2)}, u32[]{:S(2)}) collective-permute-start(bf16[512,128]{1,0:T(8,128)(2,1)S(1)} %fusion.19), channel_id=1, source_target_pairs={{0,4},{1,5},{2,6},{3,7},{4,0},{5,1},{6,2},{7,3},{8,12},{9,13},{10,... | collective-permute-start | bytes 393224 | tf_op jit(solution)/shard_map/range/ppermute | solution.py:27
  56.7 0.2 fusion.4
  57.0 0.2 collective-permute-start.14
  57.4 1.8 %collective-permute-start.24 = (bf16[512,128]{1,0:T(8,128)(2,1)S(1)}, bf16[512,128]{1,0:T(8,128)(2,1)S(1)}, u32[]{:S(2)}, u32[]{:S(2)}) collective-permute-start(bf16[512,128]{1,0:T(8,128)(2,1)S(1)} %get-tuple-element.53), channel_id=1, source_target_pairs={{0,8},{1,9},{2,10},{3,11},{4,12},{5,13},{6,14},{7,15},{8,0},{9,1},... | collective-permute-start | bytes 393224 | tf_op jit(solution)/shard_map/range/ppermute | solution.py:27
  59.3 1.9 %collective-permute-start.21 = (bf16[512,128]{1,0:T(8,128)(2,1)S(1)}, bf16[512,128]{1,0:T(8,128)(2,1)S(1)}, u32[]{:S(2)}, u32[]{:S(2)}) collective-permute-start(bf16[512,128]{1,0:T(8,128)(2,1)S(1)} %get-tuple-element.51), channel_id=1, source_target_pairs={{0,4},{1,5},{2,6},{3,7},{4,0},{5,1},{6,2},{7,3},{8,12},{9,13},{10,... | collective-permute-start | bytes 393224 | tf_op jit(solution)/shard_map/range/ppermute | solution.py:27
  61.2 2.0 %collective-permute-done.17 = bf16[512,128]{1,0:T(8,128)(2,1)S(1)} collective-permute-done((bf16[512,128]{1,0:T(8,128)(2,1)S(1)}, bf16[512,128]{1,0:T(8,128)(2,1)S(1)}, u32[]{:S(2)}, u32[]{:S(2)}) %collective-permute-start.17) | collective-permute-done | bytes 131104 | tf_op jit(solution)/shard_map/range/ppermute | solution.py:27
  63.3 0.2 collective-permute-start.18
  63.7 2.8 %collective-permute-start.15 = (bf16[512,128]{1,0:T(8,128)(2,1)S(1)}, bf16[512,128]{1,0:T(8,128)(2,1)S(1)}, u32[]{:S(2)}, u32[]{:S(2)}) collective-permute-start(bf16[512,128]{1,0:T(8,128)(2,1)S(1)} %get-tuple-element.47), channel_id=1, source_target_pairs={{0,8},{1,9},{2,10},{3,11},{4,12},{5,13},{6,14},{7,15},{8,0},{9,1},... | collective-permute-start | bytes 393224 | tf_op jit(solution)/shard_map/range/ppermute | solution.py:27
  66.5 0.9 collective-permute-done.24
  67.7 7.3 %collective-permute-done.18 = bf16[512,128]{1,0:T(8,128)(2,1)S(1)} collective-permute-done((bf16[512,128]{1,0:T(8,128)(2,1)S(1)}, bf16[512,128]{1,0:T(8,128)(2,1)S(1)}, u32[]{:S(2)}, u32[]{:S(2)}) %collective-permute-start.18) | collective-permute-done | bytes 131104 | tf_op jit(solution)/shard_map/range/ppermute | solution.py:27
  75.2 1.3 %collective-permute-done.15 = bf16[512,128]{1,0:T(8,128)(2,1)S(1)} collective-permute-done((bf16[512,128]{1,0:T(8,128)(2,1)S(1)}, bf16[512,128]{1,0:T(8,128)(2,1)S(1)}, u32[]{:S(2)}, u32[]{:S(2)}) %collective-permute-start.15) | collective-permute-done | bytes 131104 | tf_op jit(solution)/shard_map/range/ppermute | solution.py:27
  76.6 1.0 fusion.33
  77.8 0.6 collective-permute-start.27
  78.4 3.0 %collective-permute-start.34 = (bf16[512,128]{1,0:T(8,128)(2,1)S(1)}, bf16[512,128]{1,0:T(8,128)(2,1)S(1)}, u32[]{:S(2)}, u32[]{:S(2)}) collective-permute-start(bf16[512,128]{1,0:T(8,128)(2,1)S(1)} %pad_maximum_fusion.13), channel_id=1, source_target_pairs={{0,8},{1,9},{2,10},{3,11},{4,12},{5,13},{6,14},{7,15},{8,0},{9,1},... | collective-permute-start | bytes 393224 | tf_op jit(solution)/shard_map/gather_range/ppermute | solution.py:27
  81.4 1.3 %collective-permute-start.26 = (f32[128,128]{1,0:T(8,128)S(1)}, f32[128,128]{1,0:T(8,128)S(1)}, u32[]{:S(2)}, u32[]{:S(2)}) collective-permute-start(f32[128,128]{1,0:T(8,128)S(1)} %add.83), channel_id=1, source_target_pairs={{0,2},{1,3},{2,0},{3,1},{4,6},{5,7},{6,4},{7,5},{8,10},{9,11},{10,... | collective-permute-start | bytes 196616 | tf_op jit(solution)/shard_map/gram/ppermute | solution.py:27
  82.7 0.8 collective-permute-start.36
  83.6 2.9 %collective-permute-done.26 = f32[128,128]{1,0:T(8,128)S(1)} collective-permute-done((f32[128,128]{1,0:T(8,128)S(1)}, f32[128,128]{1,0:T(8,128)S(1)}, u32[]{:S(2)}, u32[]{:S(2)}) %collective-permute-start.26) | collective-permute-done | bytes 65568 | tf_op jit(solution)/shard_map/gram/ppermute | solution.py:27
  86.5 0.3 collective-permute-start.29
  86.7 2.4 %collective-permute-start.30 = (f32[128,128]{1,0:T(8,128)S(1)}, f32[128,128]{1,0:T(8,128)S(1)}, u32[]{:S(2)}, u32[]{:S(2)}) collective-permute-start(f32[128,128]{1,0:T(8,128)S(1)} %add.84), channel_id=1, source_target_pairs={{0,12},{1,13},{2,14},{3,15},{4,8},{5,9},{6,10},{7,11},{8,4},{9,5},... | collective-permute-start | bytes 196616 | tf_op jit(solution)/shard_map/gram/ppermute | solution.py:27
  89.1 1.2 %collective-permute-start.28 = (f32[128,128]{1,0:T(8,128)S(1)}, f32[128,128]{1,0:T(8,128)S(1)}, u32[]{:S(2)}, u32[]{:S(2)}) collective-permute-start(f32[128,128]{1,0:T(8,128)S(1)} %add.84), channel_id=1, source_target_pairs={{0,4},{1,5},{2,6},{3,7},{4,0},{5,1},{6,2},{7,3},{8,12},{9,13},{10,... | collective-permute-start | bytes 196616 | tf_op jit(solution)/shard_map/gram/ppermute | solution.py:27
  90.3 1.0 collective-permute-start.31
  91.3 1.3 %collective-permute-start.33 = (bf16[1024,128]{1,0:T(8,128)(2,1)S(1)}, bf16[1024,128]{1,0:T(8,128)(2,1)S(1)}, u32[]{:S(2)}, u32[]{:S(2)}) collective-permute-start(bf16[1024,128]{1,0:T(8,128)(2,1)S(1)} %pad_maximum_fusion.5.refs_2_), channel_id=1, source_target_pairs={{0,2},{1,3},{2,0},{3,1},{4,6},{5,7},{6,4},{7,5},{8,10},{9,11},{10,... | collective-permute-start | bytes 786440 | tf_op jit(solution)/shard_map/gather_range/ppermute | solution.py:27
  92.7 1.0 collective-permute-start.35
  93.7 0.9 collective-permute-start.37
  94.7 1.3 %coords.3.refs_5_ = f32[512,128]{1,0:T(8,128)S(1)} custom-call(s32[1]{0:T(128)} %bitcast.index_ref, s32[1]{0:T(128)} %bitcast.1.group_ref, bf16[256,16384]{1,0:T(8,128)(2,1)S(1)} %get-tuple-element.21.x_ref, bf16[256,8192]{1,0:T(8,128)(2,1)S(1)} %collective-permute-done.2.refs_0_, bf16[1024,128]{1,0:T(8,128)(2,1)S(1)} %pad_maximum_fusion.4.refs_1_, ...), custom_call_target="tpu_custom_call" | custom-call | flops 536870912 | bytes 4194304 | tf_op jit(solution)/shard_map/coords/pallas_call | solution.py:133
  95.9 6.4 %factor.1 = (f32[128,128]{1,0:T(8,128)S(1)}, f32[1024,128]{1,0:T(8,128)}) custom-call(f32[128,128]{1,0:T(8,128)S(1)} %add_add_fusion.gram_ref, f32[1024,128]{1,0:T(8,128)S(1)} %pad_maximum_fusion.range_ref), custom_call_target="tpu_custom_call" | custom-call | flops 10000000 | bytes 20000000 | tf_op jit(solution)/shard_map/factor/pallas_call | solution.py:217
  102.4 1.7 %collective-permute-done.37.refs_4_ = bf16[1024,128]{1,0:T(8,128)(2,1)S(1)} collective-permute-done((bf16[1024,128]{1,0:T(8,128)(2,1)S(1)}, bf16[1024,128]{1,0:T(8,128)(2,1)S(1)}, u32[]{:S(2)}, u32[]{:S(2)}) %collective-permute-start.37) | collective-permute-done | bytes 262176 | tf_op jit(solution)/shard_map/gather_range/ppermute | solution.py:27
  104.1 1.3 %coords.4.part_ref = f32[512,128]{1,0:T(8,128)S(1)} custom-call(s32[1]{0:T(128)} %bitcast.index_ref, s32[1]{0:T(128)} %bitcast.1.group_ref, bf16[256,16384]{1,0:T(8,128)(2,1)S(1)} %get-tuple-element.21.x_ref, bf16[256,8192]{1,0:T(8,128)(2,1)S(1)} %collective-permute-done.2.refs_0_, bf16[1024,128]{1,0:T(8,128)(2,1)S(1)} %collective-permute-done.31.refs_1_, ...), custom_call_target="tpu_custom_call" | custom-call | flops 536870912 | bytes 4194304 | tf_op jit(solution)/shard_map/coords/pallas_call | solution.py:133
  105.5 1.3 %collective-permute-done.38.theirs_ref = f32[256,128]{1,0:T(8,128)S(1)} collective-permute-done((f32[256,128]{1,0:T(8,128)S(1)}, f32[256,128]{1,0:T(8,128)S(1)}, u32[]{:S(2)}, u32[]{:S(2)}) %collective-permute-start.38) | collective-permute-done | bytes 131104 | tf_op jit(solution)/shard_map/coords/ppermute | solution.py:27
  106.8 1.0 coords.5
  (66 shorter events, 2.7 us)
Async XLA Ops:
  1.6 8.0 %collective-permute-start = (bf16[256,128]{1,0:T(8,128)(2,1)S(1)}, bf16[256,128]{1,0:T(8,128)(2,1)S(1)}, u32[]{:S(2)}, u32[]{:S(2)}) collective-permute-start(bf16[256,128]{1,0:T(8,128)(2,1)S(1)} %get-tuple-element.62), channel_id=1, source_target_pairs={{0,8},{1,9},{2,10},{3,11},{4,12},{5,13},{6,14},{7,15},{8,0},{9,1},... | collective-permute-start | bytes 196616 | tf_op jit(solution)/shard_map/gather_sketch/ppermute | solution.py:27
  5.7 6.5 %collective-permute-start.1 = (bf16[256,128]{1,0:T(8,128)(2,1)S(1)}, bf16[256,128]{1,0:T(8,128)(2,1)S(1)}, u32[]{:S(2)}, u32[]{:S(2)}) collective-permute-start(bf16[256,128]{1,0:T(8,128)(2,1)S(1)} %get-tuple-element.63), channel_id=1, source_target_pairs={{0,8},{1,9},{2,10},{3,11},{4,12},{5,13},{6,14},{7,15},{8,0},{9,1},... | collective-permute-start | bytes 196616 | tf_op jit(solution)/shard_map/gather_sketch/ppermute | solution.py:27
  12.1 17.8 %collective-permute-start.2 = (bf16[256,8192]{1,0:T(8,128)(2,1)S(1)}, bf16[256,8192]{1,0:T(8,128)(2,1)S(1)}, u32[]{:S(2)}, u32[]{:S(2)}) collective-permute-start(bf16[256,8192]{1,0:T(8,128)(2,1)S(1)} %get-tuple-element.23), channel_id=1, source_target_pairs={{0,1},{1,0},{2,3},{3,2},{4,5},{5,4},{6,7},{7,6},{8,9},{9,8},{10,11... | collective-permute-start | bytes 12582920 | tf_op jit(solution)/shard_map/split_features/ppermute | solution.py:27
  12.1 6.0 %collective-permute-start.3 = (bf16[512,128]{1,0:T(8,128)(2,1)S(1)}, bf16[512,128]{1,0:T(8,128)(2,1)S(1)}, u32[]{:S(2)}, u32[]{:S(2)}) collective-permute-start(bf16[512,128]{1,0:T(8,128)(2,1)S(1)} %pad_maximum_fusion.8), channel_id=1, source_target_pairs={{0,2},{1,3},{2,0},{3,1},{4,6},{5,7},{6,4},{7,5},{8,10},{9,11},{10,... | collective-permute-start | bytes 393224 | tf_op jit(solution)/shard_map/gather_sketch/ppermute | solution.py:27
  13.9 6.6 %collective-permute-start.9 = (bf16[256,128]{1,0:T(8,128)(2,1)S(1)}, bf16[256,128]{1,0:T(8,128)(2,1)S(1)}, u32[]{:S(2)}, u32[]{:S(2)}) collective-permute-start(bf16[256,128]{1,0:T(8,128)(2,1)S(1)} %get-tuple-element.61), channel_id=1, source_target_pairs={{0,8},{1,9},{2,10},{3,11},{4,12},{5,13},{6,14},{7,15},{8,0},{9,1},... | collective-permute-start | bytes 196616 | tf_op jit(solution)/shard_map/gather_sketch/ppermute | solution.py:27
  14.1 8.7 %collective-permute-start.7 = (bf16[512,128]{1,0:T(8,128)(2,1)S(1)}, bf16[512,128]{1,0:T(8,128)(2,1)S(1)}, u32[]{:S(2)}, u32[]{:S(2)}) collective-permute-start(bf16[512,128]{1,0:T(8,128)(2,1)S(1)} %pad_maximum_fusion.9), channel_id=1, source_target_pairs={{0,4},{1,5},{2,6},{3,7},{4,0},{5,1},{6,2},{7,3},{8,12},{9,13},{10,... | collective-permute-start | bytes 393224 | tf_op jit(solution)/shard_map/gather_sketch/ppermute | solution.py:27
  18.1 10.3 %collective-permute-start.4 = (bf16[1024,128]{1,0:T(8,128)(2,1)S(1)}, bf16[1024,128]{1,0:T(8,128)(2,1)S(1)}, u32[]{:S(2)}, u32[]{:S(2)}) collective-permute-start(bf16[1024,128]{1,0:T(8,128)(2,1)S(1)} %pad_maximum_fusion.1.refs_1_), channel_id=1, source_target_pairs={{0,4},{1,5},{2,6},{3,7},{4,0},{5,1},{6,2},{7,3},{8,12},{9,13},{10,... | collective-permute-start | bytes 786440 | tf_op jit(solution)/shard_map/gather_sketch/ppermute | solution.py:27
  20.5 6.4 %collective-permute-start.10 = (bf16[512,128]{1,0:T(8,128)(2,1)S(1)}, bf16[512,128]{1,0:T(8,128)(2,1)S(1)}, u32[]{:S(2)}, u32[]{:S(2)}) collective-permute-start(bf16[512,128]{1,0:T(8,128)(2,1)S(1)} %pad_maximum_fusion.10), channel_id=1, source_target_pairs={{0,2},{1,3},{2,0},{3,1},{4,6},{5,7},{6,4},{7,5},{8,10},{9,11},{10,... | collective-permute-start | bytes 393224 | tf_op jit(solution)/shard_map/gather_sketch/ppermute | solution.py:27
  21.0 10.0 %collective-permute-start.5 = (bf16[1024,128]{1,0:T(8,128)(2,1)S(1)}, bf16[1024,128]{1,0:T(8,128)(2,1)S(1)}, u32[]{:S(2)}, u32[]{:S(2)}) collective-permute-start(bf16[1024,128]{1,0:T(8,128)(2,1)S(1)} %pad_maximum_fusion.1.refs_1_), channel_id=1, source_target_pairs={{0,16},{16,0},{1,17},{17,1},{2,18},{18,2},{3,19},{19,3},{4,20},{20... | collective-permute-start | bytes 786440 | tf_op jit(solution)/shard_map/gather_sketch/ppermute | solution.py:257
  22.8 8.4 %collective-permute-start.8 = (bf16[1024,128]{1,0:T(8,128)(2,1)S(1)}, bf16[1024,128]{1,0:T(8,128)(2,1)S(1)}, u32[]{:S(2)}, u32[]{:S(2)}) collective-permute-start(bf16[1024,128]{1,0:T(8,128)(2,1)S(1)} %pad_maximum_fusion.2.refs_2_), channel_id=1, source_target_pairs={{0,2},{1,3},{2,0},{3,1},{4,6},{5,7},{6,4},{7,5},{8,10},{9,11},{10,... | collective-permute-start | bytes 786440 | tf_op jit(solution)/shard_map/gather_sketch/ppermute | solution.py:27
  27.0 6.4 %collective-permute-start.11 = (bf16[1024,128]{1,0:T(8,128)(2,1)S(1)}, bf16[1024,128]{1,0:T(8,128)(2,1)S(1)}, u32[]{:S(2)}, u32[]{:S(2)}) collective-permute-start(bf16[1024,128]{1,0:T(8,128)(2,1)S(1)} %pad_maximum_fusion.3.refs_3_), channel_id=1, source_target_pairs={{0,4},{1,5},{2,6},{3,7},{4,0},{5,1},{6,2},{7,3},{8,12},{9,13},{10,... | collective-permute-start | bytes 786440 | tf_op jit(solution)/shard_map/gather_sketch/ppermute | solution.py:27
  28.4 6.9 %collective-permute-start.6 = (bf16[1024,128]{1,0:T(8,128)(2,1)S(1)}, bf16[1024,128]{1,0:T(8,128)(2,1)S(1)}, u32[]{:S(2)}, u32[]{:S(2)}) collective-permute-start(bf16[1024,128]{1,0:T(8,128)(2,1)S(1)} %collective-permute-done.4.refs_1_), channel_id=1, source_target_pairs={{0,16},{16,0},{1,17},{17,1},{2,18},{18,2},{3,19},{19,3},{4,20},{20... | collective-permute-start | bytes 786440 | tf_op jit(solution)/shard_map/gather_sketch/ppermute | solution.py:257
  36.9 1.6 %collective-permute-start.12 = (f32[512,128]{1,0:T(8,128)S(1)}, f32[512,128]{1,0:T(8,128)S(1)}, u32[]{:S(2)}, u32[]{:S(2)}) collective-permute-start(f32[512,128]{1,0:T(8,128)S(1)} %sketched.3), channel_id=1, source_target_pairs={{0,1},{1,0},{2,3},{3,2},{4,5},{5,4},{6,7},{7,6},{8,9},{9,8},{10,11... | collective-permute-start | bytes 786440 | tf_op jit(solution)/shard_map/sketched/ppermute | solution.py:27
  39.4 9.2 %collective-permute-start.22 = (bf16[1024,128]{1,0:T(8,128)(2,1)S(1)}, bf16[1024,128]{1,0:T(8,128)(2,1)S(1)}, u32[]{:S(2)}, u32[]{:S(2)}) collective-permute-start(bf16[1024,128]{1,0:T(8,128)(2,1)S(1)} %get-tuple-element.31), channel_id=1, source_target_pairs={{0,4},{1,5},{2,6},{3,7},{4,0},{5,1},{6,2},{7,3},{8,12},{9,13},{10,... | collective-permute-start | bytes 786440 | tf_op jit(solution)/shard_map/range/ppermute | solution.py:27
  40.3 9.2 %collective-permute-start.19 = (bf16[1024,128]{1,0:T(8,128)(2,1)S(1)}, bf16[1024,128]{1,0:T(8,128)(2,1)S(1)}, u32[]{:S(2)}, u32[]{:S(2)}) collective-permute-start(bf16[1024,128]{1,0:T(8,128)(2,1)S(1)} %get-tuple-element.29), channel_id=1, source_target_pairs={{0,2},{1,3},{2,0},{3,1},{4,6},{5,7},{6,4},{7,5},{8,10},{9,11},{10,... | collective-permute-start | bytes 786440 | tf_op jit(solution)/shard_map/range/ppermute | solution.py:27
  40.7 14.4 %collective-permute-start.16 = (bf16[1024,128]{1,0:T(8,128)(2,1)S(1)}, bf16[1024,128]{1,0:T(8,128)(2,1)S(1)}, u32[]{:S(2)}, u32[]{:S(2)}) collective-permute-start(bf16[1024,128]{1,0:T(8,128)(2,1)S(1)} %get-tuple-element.27), channel_id=1, source_target_pairs={{0,2},{1,3},{2,0},{3,1},{4,6},{5,7},{6,4},{7,5},{8,10},{9,11},{10,... | collective-permute-start | bytes 786440 | tf_op jit(solution)/shard_map/range/ppermute | solution.py:27
  42.3 14.4 %collective-permute-start.13 = (bf16[1024,128]{1,0:T(8,128)(2,1)S(1)}, bf16[1024,128]{1,0:T(8,128)(2,1)S(1)}, u32[]{:S(2)}, u32[]{:S(2)}) collective-permute-start(bf16[1024,128]{1,0:T(8,128)(2,1)S(1)} %get-tuple-element.25), channel_id=1, source_target_pairs={{0,4},{1,5},{2,6},{3,7},{4,0},{5,1},{6,2},{7,3},{8,12},{9,13},{10,... | collective-permute-start | bytes 786440 | tf_op jit(solution)/shard_map/range/ppermute | solution.py:27
  48.9 8.3 %collective-permute-start.23 = (bf16[512,128]{1,0:T(8,128)(2,1)S(1)}, bf16[512,128]{1,0:T(8,128)(2,1)S(1)}, u32[]{:S(2)}, u32[]{:S(2)}) collective-permute-start(bf16[512,128]{1,0:T(8,128)(2,1)S(1)} %fusion.25), channel_id=1, source_target_pairs={{0,2},{1,3},{2,0},{3,1},{4,6},{5,7},{6,4},{7,5},{8,10},{9,11},{10,... | collective-permute-start | bytes 393224 | tf_op jit(solution)/shard_map/range/ppermute | solution.py:27
  49.7 9.4 %collective-permute-start.20 = (bf16[512,128]{1,0:T(8,128)(2,1)S(1)}, bf16[512,128]{1,0:T(8,128)(2,1)S(1)}, u32[]{:S(2)}, u32[]{:S(2)}) collective-permute-start(bf16[512,128]{1,0:T(8,128)(2,1)S(1)} %fusion.22), channel_id=1, source_target_pairs={{0,8},{1,9},{2,10},{3,11},{4,12},{5,13},{6,14},{7,15},{8,0},{9,1},... | collective-permute-start | bytes 393224 | tf_op jit(solution)/shard_map/range/ppermute | solution.py:27
  55.4 7.8 %collective-permute-start.17 = (bf16[512,128]{1,0:T(8,128)(2,1)S(1)}, bf16[512,128]{1,0:T(8,128)(2,1)S(1)}, u32[]{:S(2)}, u32[]{:S(2)}) collective-permute-start(bf16[512,128]{1,0:T(8,128)(2,1)S(1)} %fusion.19), channel_id=1, source_target_pairs={{0,4},{1,5},{2,6},{3,7},{4,0},{5,1},{6,2},{7,3},{8,12},{9,13},{10,... | collective-permute-start | bytes 393224 | tf_op jit(solution)/shard_map/range/ppermute | solution.py:27
  57.0 6.6 %collective-permute-start.14 = (bf16[512,128]{1,0:T(8,128)(2,1)S(1)}, bf16[512,128]{1,0:T(8,128)(2,1)S(1)}, u32[]{:S(2)}, u32[]{:S(2)}) collective-permute-start(bf16[512,128]{1,0:T(8,128)(2,1)S(1)} %fusion.16), channel_id=1, source_target_pairs={{0,2},{1,3},{2,0},{3,1},{4,6},{5,7},{6,4},{7,5},{8,10},{9,11},{10,... | collective-permute-start | bytes 393224 | tf_op jit(solution)/shard_map/range/ppermute | solution.py:27
  57.4 10.0 %collective-permute-start.24 = (bf16[512,128]{1,0:T(8,128)(2,1)S(1)}, bf16[512,128]{1,0:T(8,128)(2,1)S(1)}, u32[]{:S(2)}, u32[]{:S(2)}) collective-permute-start(bf16[512,128]{1,0:T(8,128)(2,1)S(1)} %get-tuple-element.53), channel_id=1, source_target_pairs={{0,8},{1,9},{2,10},{3,11},{4,12},{5,13},{6,14},{7,15},{8,0},{9,1},... | collective-permute-start | bytes 393224 | tf_op jit(solution)/shard_map/range/ppermute | solution.py:27
  59.3 8.3 %collective-permute-start.21 = (bf16[512,128]{1,0:T(8,128)(2,1)S(1)}, bf16[512,128]{1,0:T(8,128)(2,1)S(1)}, u32[]{:S(2)}, u32[]{:S(2)}) collective-permute-start(bf16[512,128]{1,0:T(8,128)(2,1)S(1)} %get-tuple-element.51), channel_id=1, source_target_pairs={{0,4},{1,5},{2,6},{3,7},{4,0},{5,1},{6,2},{7,3},{8,12},{9,13},{10,... | collective-permute-start | bytes 393224 | tf_op jit(solution)/shard_map/range/ppermute | solution.py:27
  63.3 11.7 %collective-permute-start.18 = (bf16[512,128]{1,0:T(8,128)(2,1)S(1)}, bf16[512,128]{1,0:T(8,128)(2,1)S(1)}, u32[]{:S(2)}, u32[]{:S(2)}) collective-permute-start(bf16[512,128]{1,0:T(8,128)(2,1)S(1)} %get-tuple-element.49), channel_id=1, source_target_pairs={{0,8},{1,9},{2,10},{3,11},{4,12},{5,13},{6,14},{7,15},{8,0},{9,1},... | collective-permute-start | bytes 393224 | tf_op jit(solution)/shard_map/range/ppermute | solution.py:27
  63.7 12.8 %collective-permute-start.15 = (bf16[512,128]{1,0:T(8,128)(2,1)S(1)}, bf16[512,128]{1,0:T(8,128)(2,1)S(1)}, u32[]{:S(2)}, u32[]{:S(2)}) collective-permute-start(bf16[512,128]{1,0:T(8,128)(2,1)S(1)} %get-tuple-element.47), channel_id=1, source_target_pairs={{0,8},{1,9},{2,10},{3,11},{4,12},{5,13},{6,14},{7,15},{8,0},{9,1},... | collective-permute-start | bytes 393224 | tf_op jit(solution)/shard_map/range/ppermute | solution.py:27
  77.7 3.7 %collective-permute-start.25 = (f32[128,128]{1,0:T(8,128)S(1)}, f32[128,128]{1,0:T(8,128)S(1)}, u32[]{:S(2)}, u32[]{:S(2)}) collective-permute-start(f32[128,128]{1,0:T(8,128)S(1)} %fusion.33), channel_id=1, source_target_pairs={{0,1},{1,0},{2,3},{3,2},{4,5},{5,4},{6,7},{7,6},{8,9},{9,8},{10,11... | collective-permute-start | bytes 196616 | tf_op jit(solution)/shard_map/gram/ppermute | solution.py:27
  77.8 8.7 %collective-permute-start.27 = (bf16[512,128]{1,0:T(8,128)(2,1)S(1)}, bf16[512,128]{1,0:T(8,128)(2,1)S(1)}, u32[]{:S(2)}, u32[]{:S(2)}) collective-permute-start(bf16[512,128]{1,0:T(8,128)(2,1)S(1)} %pad_maximum_fusion.11), channel_id=1, source_target_pairs={{0,2},{1,3},{2,0},{3,1},{4,6},{5,7},{6,4},{7,5},{8,10},{9,11},{10,... | collective-permute-start | bytes 393224 | tf_op jit(solution)/shard_map/gather_range/ppermute | solution.py:27
  78.3 10.8 %collective-permute-start.32 = (bf16[512,128]{1,0:T(8,128)(2,1)S(1)}, bf16[512,128]{1,0:T(8,128)(2,1)S(1)}, u32[]{:S(2)}, u32[]{:S(2)}) collective-permute-start(bf16[512,128]{1,0:T(8,128)(2,1)S(1)} %pad_maximum_fusion.12), channel_id=1, source_target_pairs={{0,4},{1,5},{2,6},{3,7},{4,0},{5,1},{6,2},{7,3},{8,12},{9,13},{10,... | collective-permute-start | bytes 393224 | tf_op jit(solution)/shard_map/gather_range/ppermute | solution.py:27
  78.4 11.9 %collective-permute-start.34 = (bf16[512,128]{1,0:T(8,128)(2,1)S(1)}, bf16[512,128]{1,0:T(8,128)(2,1)S(1)}, u32[]{:S(2)}, u32[]{:S(2)}) collective-permute-start(bf16[512,128]{1,0:T(8,128)(2,1)S(1)} %pad_maximum_fusion.13), channel_id=1, source_target_pairs={{0,8},{1,9},{2,10},{3,11},{4,12},{5,13},{6,14},{7,15},{8,0},{9,1},... | collective-permute-start | bytes 393224 | tf_op jit(solution)/shard_map/gather_range/ppermute | solution.py:27
  81.4 5.0 %collective-permute-start.26 = (f32[128,128]{1,0:T(8,128)S(1)}, f32[128,128]{1,0:T(8,128)S(1)}, u32[]{:S(2)}, u32[]{:S(2)}) collective-permute-start(f32[128,128]{1,0:T(8,128)S(1)} %add.83), channel_id=1, source_target_pairs={{0,2},{1,3},{2,0},{3,1},{4,6},{5,7},{6,4},{7,5},{8,10},{9,11},{10,... | collective-permute-start | bytes 196616 | tf_op jit(solution)/shard_map/gram/ppermute | solution.py:27
  82.7 8.6 %collective-permute-start.36 = (bf16[512,128]{1,0:T(8,128)(2,1)S(1)}, bf16[512,128]{1,0:T(8,128)(2,1)S(1)}, u32[]{:S(2)}, u32[]{:S(2)}) collective-permute-start(bf16[512,128]{1,0:T(8,128)(2,1)S(1)} %pad_maximum_fusion.14), channel_id=1, source_target_pairs={{0,2},{1,3},{2,0},{3,1},{4,6},{5,7},{6,4},{7,5},{8,10},{9,11},{10,... | collective-permute-start | bytes 393224 | tf_op jit(solution)/shard_map/gather_range/ppermute | solution.py:27
  86.5 6.2 %collective-permute-start.29 = (f32[128,128]{1,0:T(8,128)S(1)}, f32[128,128]{1,0:T(8,128)S(1)}, u32[]{:S(2)}, u32[]{:S(2)}) collective-permute-start(f32[128,128]{1,0:T(8,128)S(1)} %add.84), channel_id=1, source_target_pairs={{0,8},{1,9},{2,10},{3,11},{4,12},{5,13},{6,14},{7,15},{8,0},{9,1},... | collective-permute-start | bytes 196616 | tf_op jit(solution)/shard_map/gram/ppermute | solution.py:27
  86.7 7.0 %collective-permute-start.30 = (f32[128,128]{1,0:T(8,128)S(1)}, f32[128,128]{1,0:T(8,128)S(1)}, u32[]{:S(2)}, u32[]{:S(2)}) collective-permute-start(f32[128,128]{1,0:T(8,128)S(1)} %add.84), channel_id=1, source_target_pairs={{0,12},{1,13},{2,14},{3,15},{4,8},{5,9},{6,10},{7,11},{8,4},{9,5},... | collective-permute-start | bytes 196616 | tf_op jit(solution)/shard_map/gram/ppermute | solution.py:27
  89.1 6.8 %collective-permute-start.28 = (f32[128,128]{1,0:T(8,128)S(1)}, f32[128,128]{1,0:T(8,128)S(1)}, u32[]{:S(2)}, u32[]{:S(2)}) collective-permute-start(f32[128,128]{1,0:T(8,128)S(1)} %add.84), channel_id=1, source_target_pairs={{0,4},{1,5},{2,6},{3,7},{4,0},{5,1},{6,2},{7,3},{8,12},{9,13},{10,... | collective-permute-start | bytes 196616 | tf_op jit(solution)/shard_map/gram/ppermute | solution.py:27
  90.3 12.0 %collective-permute-start.31 = (bf16[1024,128]{1,0:T(8,128)(2,1)S(1)}, bf16[1024,128]{1,0:T(8,128)(2,1)S(1)}, u32[]{:S(2)}, u32[]{:S(2)}) collective-permute-start(bf16[1024,128]{1,0:T(8,128)(2,1)S(1)} %pad_maximum_fusion.4.refs_1_), channel_id=1, source_target_pairs={{0,4},{1,5},{2,6},{3,7},{4,0},{5,1},{6,2},{7,3},{8,12},{9,13},{10,... | collective-permute-start | bytes 786440 | tf_op jit(solution)/shard_map/gather_range/ppermute | solution.py:27
  91.3 11.0 %collective-permute-start.33 = (bf16[1024,128]{1,0:T(8,128)(2,1)S(1)}, bf16[1024,128]{1,0:T(8,128)(2,1)S(1)}, u32[]{:S(2)}, u32[]{:S(2)}) collective-permute-start(bf16[1024,128]{1,0:T(8,128)(2,1)S(1)} %pad_maximum_fusion.5.refs_2_), channel_id=1, source_target_pairs={{0,2},{1,3},{2,0},{3,1},{4,6},{5,7},{6,4},{7,5},{8,10},{9,11},{10,... | collective-permute-start | bytes 786440 | tf_op jit(solution)/shard_map/gather_range/ppermute | solution.py:27
  92.7 9.7 %collective-permute-start.35 = (bf16[1024,128]{1,0:T(8,128)(2,1)S(1)}, bf16[1024,128]{1,0:T(8,128)(2,1)S(1)}, u32[]{:S(2)}, u32[]{:S(2)}) collective-permute-start(bf16[1024,128]{1,0:T(8,128)(2,1)S(1)} %pad_maximum_fusion.6.refs_3_), channel_id=1, source_target_pairs={{0,2},{1,3},{2,0},{3,1},{4,6},{5,7},{6,4},{7,5},{8,10},{9,11},{10,... | collective-permute-start | bytes 786440 | tf_op jit(solution)/shard_map/gather_range/ppermute | solution.py:27
  93.7 10.4 %collective-permute-start.37 = (bf16[1024,128]{1,0:T(8,128)(2,1)S(1)}, bf16[1024,128]{1,0:T(8,128)(2,1)S(1)}, u32[]{:S(2)}, u32[]{:S(2)}) collective-permute-start(bf16[1024,128]{1,0:T(8,128)(2,1)S(1)} %pad_maximum_fusion.7.refs_4_), channel_id=1, source_target_pairs={{0,4},{1,5},{2,6},{3,7},{4,0},{5,1},{6,2},{7,3},{8,12},{9,13},{10,... | collective-permute-start | bytes 786440 | tf_op jit(solution)/shard_map/gather_range/ppermute | solution.py:27
  105.4 1.4 %collective-permute-start.38 = (f32[256,128]{1,0:T(8,128)S(1)}, f32[256,128]{1,0:T(8,128)S(1)}, u32[]{:S(2)}, u32[]{:S(2)}) collective-permute-start(f32[256,128]{1,0:T(8,128)S(1)} %slice.136), channel_id=1, source_target_pairs={{0,1},{1,0},{2,3},{3,2},{4,5},{5,4},{6,7},{7,6},{8,9},{9,8},{10,11... | collective-permute-start | bytes 393224 | tf_op jit(solution)/shard_map/coords/ppermute | solution.py:27

commit v7 on v6

--- a/solution.py
+++ b/solution.py
@@ -21,6 +21,7 @@
 RANGE_PIECES = ((2, HXL, False), (2, HLX, False), (2, LHX, False), (2, HXL, False))
 LOADS, PARTS = 8, 1
 TIED = 2
+LAST = 2
 
 
 def swap(value, bit, n):
@@ -284,7 +285,9 @@
                 far_rows += [(near_owners, start, size, 1), (far_owners, start, size, 1)]
     with jax.named_scope("sketched"):
         part = project(place, near_rows, x, others, near)
-        part = project(place, far_rows, x, others, far, part)
+        early = [i for i in range(len(far)) if i != LAST]
+        part = project(place, [far_rows[i] for i in early], x, others, [far[i] for i in early], part)
+        part = project(place, far_rows[LAST : LAST + 1], x, others, far[LAST : LAST + 1], part)
         theirs = swap(part, 1, n)
         sketched = (part + jnp.concatenate([theirs[rows:], theirs[:rows]])).astype(BF16)
     with jax.named_scope("range"):
@@ -323,7 +326,8 @@
         inverse, basis = factored(math.sqrt(depth), gram, range_rows)
     with jax.named_scope("coords"):
         part = project(place, near_rows, x, others, held)
-        part = project(place, far_rows, x, others, came, after(part, inverse))
+        part = project(place, far_rows[:-1], x, others, came[:-1], after(part, inverse))
+        part = project(place, far_rows[-1:], x, others, came[-1:], part)
         coords, resid_rms = close(depth, part, swap(part[rows:], 1, n), inverse, norm)
     return basis[None], coords, resid_rms.reshape(rows)
 

time: 108 us -> 111 us (1.028)
  waiting for transfers between devices: 40.4 us -> 43.4 us
    ppermute x37, waiting for transfers between devices: 38.5 us -> 42.2 us  [swap(): return lax.ppermute(value, 'tok', [(i, i ^ bit) for i in range(n)])]
    pallas_call x4 -> x6, Pallas kernels: 5.02 us -> 5.35 us  [project(): pl.pallas_call(functools.partial(project_kernel, width, entries, init is...]
  transfers between devices with their start and end apart: 39 -> 39, of which waited for: 20 -> 19; matrix products, arithmetic and copies ran while one was open for 2% -> 2% of each run, Pallas kernels for 12% -> 14%
where the time goes in v7:
time: 111 us
  waiting for transfers between devices  43.4 us (39%)
  starting transfers between devices  43.3 us (39%)
  Pallas kernels  18.3 us (16%)
  other arithmetic  2.49 us (2%)
    ppermute x37, waiting for transfers between devices, swap(): return lax.ppermute(value, 'tok', [(i, i ^ bit) for i in range(n)])  42.2 us
    ppermute x37, starting transfers between devices, swap(): return lax.ppermute(value, 'tok', [(i, i ^ bit) for i in range(n)])  40.3 us
    pallas_call x1, Pallas kernels, factored(): pl.pallas_call(functools.partial(factor_kernel, scale), in_specs=[VMEM] *...  6.41 us
    pallas_call x6, Pallas kernels, project(): pl.pallas_call(functools.partial(project_kernel, width, entries, init is...  5.35 us
    pallas_call x1, Pallas kernels, load(): pl.pallas_call(functools.partial(load_kernel, width), in_specs=[SMEM, ANY...  3.78 us
    ppermute x2, starting transfers between devices, across(): return lax.ppermute(value, 'groups', [(0, 1), (1, 0)])  3.04 us
  transfers between devices with their start and end apart: 39, of which 19 were waited for; matrix products, arithmetic and copies ran while one was open for 2% of the time, Pallas kernels for 14%

profile of v7, /device:TPU:0, one launch (start us, length us, event | category | flops | bytes accessed | tf_op | source)
XLA Modules:
  0.0 110.6 jit_solution(14709242313708813997)
XLA Ops:
  0.6 0.9 slice_bitcast_fusion
  1.6 4.1 %collective-permute-start = (bf16[256,128]{1,0:T(8,128)(2,1)S(1)}, bf16[256,128]{1,0:T(8,128)(2,1)S(1)}, u32[]{:S(2)}, u32[]{:S(2)}) collective-permute-start(bf16[256,128]{1,0:T(8,128)(2,1)S(1)} %get-tuple-element.62), channel_id=1, source_target_pairs={{0,8},{1,9},{2,10},{3,11},{4,12},{5,13},{6,14},{7,15},{8,0},{9,1},... | collective-permute-start | bytes 196616 | tf_op jit(solution)/shard_map/gather_sketch/ppermute | solution.py:28
  5.7 3.8 %split_features.1 = (bf16[256,16384]{1,0:T(8,128)(2,1)S(1)}, f32[256,128]{1,0:T(8,128)S(1)}, bf16[256,8192]{1,0:T(8,128)(2,1)S(1)}) custom-call(s32[1]{0:T(128)} %bitcast.index_ref, bf16[256,16384]{1,0:T(8,128)(2,1)} %x_ref.1), custom_call_target="tpu_custom_call" | custom-call | flops 8388608 | bytes 16777216 | tf_op jit(solution)/shard_map/split_features/pallas_call | solution.py:95
  9.5 2.6 %collective-permute-done.1 = bf16[256,128]{1,0:T(8,128)(2,1)S(1)} collective-permute-done((bf16[256,128]{1,0:T(8,128)(2,1)S(1)}, bf16[256,128]{1,0:T(8,128)(2,1)S(1)}, u32[]{:S(2)}, u32[]{:S(2)}) %collective-permute-start.1) | collective-permute-done | bytes 65568 | tf_op jit(solution)/shard_map/gather_sketch/ppermute | solution.py:28
  12.1 0.4 collective-permute-start.9
  12.6 1.6 %collective-permute-start.3 = (bf16[512,128]{1,0:T(8,128)(2,1)S(1)}, bf16[512,128]{1,0:T(8,128)(2,1)S(1)}, u32[]{:S(2)}, u32[]{:S(2)}) collective-permute-start(bf16[512,128]{1,0:T(8,128)(2,1)S(1)} %pad_maximum_fusion.8), channel_id=1, source_target_pairs={{0,2},{1,3},{2,0},{3,1},{4,6},{5,7},{6,4},{7,5},{8,10},{9,11},{10,... | collective-permute-start | bytes 393224 | tf_op jit(solution)/shard_map/gather_sketch/ppermute | solution.py:28
  14.1 3.6 %collective-permute-start.7 = (bf16[512,128]{1,0:T(8,128)(2,1)S(1)}, bf16[512,128]{1,0:T(8,128)(2,1)S(1)}, u32[]{:S(2)}, u32[]{:S(2)}) collective-permute-start(bf16[512,128]{1,0:T(8,128)(2,1)S(1)} %pad_maximum_fusion.9), channel_id=1, source_target_pairs={{0,4},{1,5},{2,6},{3,7},{4,0},{5,1},{6,2},{7,3},{8,12},{9,13},{10,... | collective-permute-start | bytes 393224 | tf_op jit(solution)/shard_map/gather_sketch/ppermute | solution.py:28
  17.7 1.2 %collective-permute-done.9 = bf16[256,128]{1,0:T(8,128)(2,1)S(1)} collective-permute-done((bf16[256,128]{1,0:T(8,128)(2,1)S(1)}, bf16[256,128]{1,0:T(8,128)(2,1)S(1)}, u32[]{:S(2)}, u32[]{:S(2)}) %collective-permute-start.9) | collective-permute-done | bytes 65568 | tf_op jit(solution)/shard_map/gather_sketch/ppermute | solution.py:28
  19.0 1.8 %collective-permute-start.10 = (bf16[512,128]{1,0:T(8,128)(2,1)S(1)}, bf16[512,128]{1,0:T(8,128)(2,1)S(1)}, u32[]{:S(2)}, u32[]{:S(2)}) collective-permute-start(bf16[512,128]{1,0:T(8,128)(2,1)S(1)} %pad_maximum_fusion.10), channel_id=1, source_target_pairs={{0,2},{1,3},{2,0},{3,1},{4,6},{5,7},{6,4},{7,5},{8,10},{9,11},{10,... | collective-permute-start | bytes 393224 | tf_op jit(solution)/shard_map/gather_sketch/ppermute | solution.py:28
  20.8 1.3 %collective-permute-start.4 = (bf16[1024,128]{1,0:T(8,128)(2,1)S(1)}, bf16[1024,128]{1,0:T(8,128)(2,1)S(1)}, u32[]{:S(2)}, u32[]{:S(2)}) collective-permute-start(bf16[1024,128]{1,0:T(8,128)(2,1)S(1)} %pad_maximum_fusion.1.refs_1_), channel_id=1, source_target_pairs={{0,4},{1,5},{2,6},{3,7},{4,0},{5,1},{6,2},{7,3},{8,12},{9,13},{10,... | collective-permute-start | bytes 786440 | tf_op jit(solution)/shard_map/gather_sketch/ppermute | solution.py:28
  22.1 1.5 %collective-permute-start.6 = (bf16[1024,128]{1,0:T(8,128)(2,1)S(1)}, bf16[1024,128]{1,0:T(8,128)(2,1)S(1)}, u32[]{:S(2)}, u32[]{:S(2)}) collective-permute-start(bf16[1024,128]{1,0:T(8,128)(2,1)S(1)} %pad_maximum_fusion.1.refs_1_), channel_id=1, source_target_pairs={{0,16},{16,0},{1,17},{17,1},{2,18},{18,2},{3,19},{19,3},{4,20},{20... | collective-permute-start | bytes 786440 | tf_op jit(solution)/shard_map/gather_sketch/ppermute | solution.py:258
  23.7 1.6 %collective-permute-start.8 = (bf16[1024,128]{1,0:T(8,128)(2,1)S(1)}, bf16[1024,128]{1,0:T(8,128)(2,1)S(1)}, u32[]{:S(2)}, u32[]{:S(2)}) collective-permute-start(bf16[1024,128]{1,0:T(8,128)(2,1)S(1)} %pad_maximum_fusion.2.refs_2_), channel_id=1, source_target_pairs={{0,2},{1,3},{2,0},{3,1},{4,6},{5,7},{6,4},{7,5},{8,10},{9,11},{10,... | collective-permute-start | bytes 786440 | tf_op jit(solution)/shard_map/gather_sketch/ppermute | solution.py:28
  25.4 4.8 %collective-permute-done.4.refs_1_ = bf16[1024,128]{1,0:T(8,128)(2,1)S(1)} collective-permute-done((bf16[1024,128]{1,0:T(8,128)(2,1)S(1)}, bf16[1024,128]{1,0:T(8,128)(2,1)S(1)}, u32[]{:S(2)}, u32[]{:S(2)}) %collective-permute-start.4) | collective-permute-done | bytes 262176 | tf_op jit(solution)/shard_map/gather_sketch/ppermute | solution.py:28
  30.2 1.5 %collective-permute-start.5 = (bf16[1024,128]{1,0:T(8,128)(2,1)S(1)}, bf16[1024,128]{1,0:T(8,128)(2,1)S(1)}, u32[]{:S(2)}, u32[]{:S(2)}) collective-permute-start(bf16[1024,128]{1,0:T(8,128)(2,1)S(1)} %collective-permute-done.4.refs_1_), channel_id=1, source_target_pairs={{0,16},{16,0},{1,17},{17,1},{2,18},{18,2},{3,19},{19,3},{4,20},{20... | collective-permute-start | bytes 786440 | tf_op jit(solution)/shard_map/gather_sketch/ppermute | solution.py:258
  31.7 1.0 sketched.3.refs_5_
  32.7 1.4 %collective-permute-done.11.refs_4_ = bf16[1024,128]{1,0:T(8,128)(2,1)S(1)} collective-permute-done((bf16[1024,128]{1,0:T(8,128)(2,1)S(1)}, bf16[1024,128]{1,0:T(8,128)(2,1)S(1)}, u32[]{:S(2)}, u32[]{:S(2)}) %collective-permute-start.11) | collective-permute-done | bytes 262176 | tf_op jit(solution)/shard_map/gather_sketch/ppermute | solution.py:28
  34.1 1.2 %sketched.4.refs_2_ = f32[512,128]{1,0:T(8,128)S(1)} custom-call(s32[1]{0:T(128)} %bitcast.index_ref, s32[1]{0:T(128)} %bitcast.1.group_ref, bf16[256,16384]{1,0:T(8,128)(2,1)S(1)} %get-tuple-element.21.x_ref, bf16[256,8192]{1,0:T(8,128)(2,1)S(1)} %collective-permute-done.2.refs_0_, bf16[1024,128]{1,0:T(8,128)(2,1)S(1)} %collective-permute-done.4.refs_1_, ...), custom_call_target="tpu_custom_call" | custom-call | flops 536870912 | bytes 4194304 | tf_op jit(solution)/shard_map/sketched/pallas_call | solution.py:134
  35.3 1.2 %collective-permute-done.5.refs_1_ = bf16[1024,128]{1,0:T(8,128)(2,1)S(1)} collective-permute-done((bf16[1024,128]{1,0:T(8,128)(2,1)S(1)}, bf16[1024,128]{1,0:T(8,128)(2,1)S(1)}, u32[]{:S(2)}, u32[]{:S(2)}) %collective-permute-start.5) | collective-permute-done | bytes 262176 | tf_op jit(solution)/shard_map/gather_sketch/ppermute | solution.py:258
  36.5 0.4 sketched.5
  37.1 1.5 %collective-permute-done.12 = f32[512,128]{1,0:T(8,128)S(1)} collective-permute-done((f32[512,128]{1,0:T(8,128)S(1)}, f32[512,128]{1,0:T(8,128)S(1)}, u32[]{:S(2)}, u32[]{:S(2)}) %collective-permute-start.12) | collective-permute-done | bytes 262176 | tf_op jit(solution)/shard_map/sketched/ppermute | solution.py:28
  38.6 0.9 range.3
  39.6 1.3 %collective-permute-start.22 = (bf16[1024,128]{1,0:T(8,128)(2,1)S(1)}, bf16[1024,128]{1,0:T(8,128)(2,1)S(1)}, u32[]{:S(2)}, u32[]{:S(2)}) collective-permute-start(bf16[1024,128]{1,0:T(8,128)(2,1)S(1)} %get-tuple-element.31), channel_id=1, source_target_pairs={{0,4},{1,5},{2,6},{3,7},{4,0},{5,1},{6,2},{7,3},{8,12},{9,13},{10,... | collective-permute-start | bytes 786440 | tf_op jit(solution)/shard_map/range/ppermute | solution.py:28
  40.8 1.5 %collective-permute-start.19 = (bf16[1024,128]{1,0:T(8,128)(2,1)S(1)}, bf16[1024,128]{1,0:T(8,128)(2,1)S(1)}, u32[]{:S(2)}, u32[]{:S(2)}) collective-permute-start(bf16[1024,128]{1,0:T(8,128)(2,1)S(1)} %get-tuple-element.29), channel_id=1, source_target_pairs={{0,2},{1,3},{2,0},{3,1},{4,6},{5,7},{6,4},{7,5},{8,10},{9,11},{10,... | collective-permute-start | bytes 786440 | tf_op jit(solution)/shard_map/range/ppermute | solution.py:28
  42.3 0.5 collective-permute-start.16
  42.8 0.8 collective-permute-start.13
  43.7 0.9 range.2
  44.6 4.2 %collective-permute-done.22 = bf16[1024,128]{1,0:T(8,128)(2,1)S(1)} collective-permute-done((bf16[1024,128]{1,0:T(8,128)(2,1)S(1)}, bf16[1024,128]{1,0:T(8,128)(2,1)S(1)}, u32[]{:S(2)}, u32[]{:S(2)}) %collective-permute-start.22) | collective-permute-done | bytes 262176 | tf_op jit(solution)/shard_map/range/ppermute | solution.py:28
  48.8 0.2 fusion.7
  49.0 0.7 collective-permute-start.23
  49.7 0.3 collective-permute-done.19
  50.0 0.2 fusion.6
  50.3 1.2 %collective-permute-start.20 = (bf16[512,128]{1,0:T(8,128)(2,1)S(1)}, bf16[512,128]{1,0:T(8,128)(2,1)S(1)}, u32[]{:S(2)}, u32[]{:S(2)}) collective-permute-start(bf16[512,128]{1,0:T(8,128)(2,1)S(1)} %fusion.22), channel_id=1, source_target_pairs={{0,8},{1,9},{2,10},{3,11},{4,12},{5,13},{6,14},{7,15},{8,0},{9,1},... | collective-permute-start | bytes 393224 | tf_op jit(solution)/shard_map/range/ppermute | solution.py:28
  51.5 4.1 %collective-permute-done.16 = bf16[1024,128]{1,0:T(8,128)(2,1)S(1)} collective-permute-done((bf16[1024,128]{1,0:T(8,128)(2,1)S(1)}, bf16[1024,128]{1,0:T(8,128)(2,1)S(1)}, u32[]{:S(2)}, u32[]{:S(2)}) %collective-permute-start.16) | collective-permute-done | bytes 262176 | tf_op jit(solution)/shard_map/range/ppermute | solution.py:28
  55.6 0.2 fusion.5
  55.9 0.9 collective-permute-start.17
  56.8 0.2 fusion.4
  57.1 0.8 collective-permute-start.14
  58.0 1.1 collective-permute-start.24
  59.2 1.2 %collective-permute-start.21 = (bf16[512,128]{1,0:T(8,128)(2,1)S(1)}, bf16[512,128]{1,0:T(8,128)(2,1)S(1)}, u32[]{:S(2)}, u32[]{:S(2)}) collective-permute-start(bf16[512,128]{1,0:T(8,128)(2,1)S(1)} %get-tuple-element.51), channel_id=1, source_target_pairs={{0,4},{1,5},{2,6},{3,7},{4,0},{5,1},{6,2},{7,3},{8,12},{9,13},{10,... | collective-permute-start | bytes 393224 | tf_op jit(solution)/shard_map/range/ppermute | solution.py:28
  60.4 4.4 %collective-permute-done.17 = bf16[512,128]{1,0:T(8,128)(2,1)S(1)} collective-permute-done((bf16[512,128]{1,0:T(8,128)(2,1)S(1)}, bf16[512,128]{1,0:T(8,128)(2,1)S(1)}, u32[]{:S(2)}, u32[]{:S(2)}) %collective-permute-start.17) | collective-permute-done | bytes 131104 | tf_op jit(solution)/shard_map/range/ppermute | solution.py:28
  65.2 3.0 %collective-permute-start.15 = (bf16[512,128]{1,0:T(8,128)(2,1)S(1)}, bf16[512,128]{1,0:T(8,128)(2,1)S(1)}, u32[]{:S(2)}, u32[]{:S(2)}) collective-permute-start(bf16[512,128]{1,0:T(8,128)(2,1)S(1)} %get-tuple-element.47), channel_id=1, source_target_pairs={{0,8},{1,9},{2,10},{3,11},{4,12},{5,13},{6,14},{7,15},{8,0},{9,1},... | collective-permute-start | bytes 393224 | tf_op jit(solution)/shard_map/range/ppermute | solution.py:28
  68.2 1.3 %collective-permute-done.24 = bf16[512,128]{1,0:T(8,128)(2,1)S(1)} collective-permute-done((bf16[512,128]{1,0:T(8,128)(2,1)S(1)}, bf16[512,128]{1,0:T(8,128)(2,1)S(1)}, u32[]{:S(2)}, u32[]{:S(2)}) %collective-permute-start.24) | collective-permute-done | bytes 131104 | tf_op jit(solution)/shard_map/range/ppermute | solution.py:28
  69.8 5.7 %collective-permute-done.18 = bf16[512,128]{1,0:T(8,128)(2,1)S(1)} collective-permute-done((bf16[512,128]{1,0:T(8,128)(2,1)S(1)}, bf16[512,128]{1,0:T(8,128)(2,1)S(1)}, u32[]{:S(2)}, u32[]{:S(2)}) %collective-permute-start.18) | collective-permute-done | bytes 131104 | tf_op jit(solution)/shard_map/range/ppermute | solution.py:28
  75.6 1.3 %collective-permute-done.15 = bf16[512,128]{1,0:T(8,128)(2,1)S(1)} collective-permute-done((bf16[512,128]{1,0:T(8,128)(2,1)S(1)}, bf16[512,128]{1,0:T(8,128)(2,1)S(1)}, u32[]{:S(2)}, u32[]{:S(2)}) %collective-permute-start.15) | collective-permute-done | bytes 131104 | tf_op jit(solution)/shard_map/range/ppermute | solution.py:28
  77.0 1.0 fusion.33
  78.2 1.6 %collective-permute-start.27 = (bf16[512,128]{1,0:T(8,128)(2,1)S(1)}, bf16[512,128]{1,0:T(8,128)(2,1)S(1)}, u32[]{:S(2)}, u32[]{:S(2)}) collective-permute-start(bf16[512,128]{1,0:T(8,128)(2,1)S(1)} %pad_maximum_fusion.11), channel_id=1, source_target_pairs={{0,2},{1,3},{2,0},{3,1},{4,6},{5,7},{6,4},{7,5},{8,10},{9,11},{10,... | collective-permute-start | bytes 393224 | tf_op jit(solution)/shard_map/gather_range/ppermute | solution.py:28
  79.8 0.6 collective-permute-start.31
  80.5 1.6 %collective-permute-start.26 = (f32[128,128]{1,0:T(8,128)S(1)}, f32[128,128]{1,0:T(8,128)S(1)}, u32[]{:S(2)}, u32[]{:S(2)}) collective-permute-start(f32[128,128]{1,0:T(8,128)S(1)} %add.83), channel_id=1, source_target_pairs={{0,2},{1,3},{2,0},{3,1},{4,6},{5,7},{6,4},{7,5},{8,10},{9,11},{10,... | collective-permute-start | bytes 196616 | tf_op jit(solution)/shard_map/gram/ppermute | solution.py:28
  82.1 1.9 %collective-permute-start.36 = (bf16[512,128]{1,0:T(8,128)(2,1)S(1)}, bf16[512,128]{1,0:T(8,128)(2,1)S(1)}, u32[]{:S(2)}, u32[]{:S(2)}) collective-permute-start(bf16[512,128]{1,0:T(8,128)(2,1)S(1)} %pad_maximum_fusion.14), channel_id=1, source_target_pairs={{0,8},{1,9},{2,10},{3,11},{4,12},{5,13},{6,14},{7,15},{8,0},{9,1},... | collective-permute-start | bytes 393224 | tf_op jit(solution)/shard_map/gather_range/ppermute | solution.py:28
  84.0 4.4 %collective-permute-done.26 = f32[128,128]{1,0:T(8,128)S(1)} collective-permute-done((f32[128,128]{1,0:T(8,128)S(1)}, f32[128,128]{1,0:T(8,128)S(1)}, u32[]{:S(2)}, u32[]{:S(2)}) %collective-permute-start.26) | collective-permute-done | bytes 65568 | tf_op jit(solution)/shard_map/gram/ppermute | solution.py:28
  88.5 1.7 %collective-permute-start.30 = (f32[128,128]{1,0:T(8,128)S(1)}, f32[128,128]{1,0:T(8,128)S(1)}, u32[]{:S(2)}, u32[]{:S(2)}) collective-permute-start(f32[128,128]{1,0:T(8,128)S(1)} %add.84), channel_id=1, source_target_pairs={{0,12},{1,13},{2,14},{3,15},{4,8},{5,9},{6,10},{7,11},{8,4},{9,5},... | collective-permute-start | bytes 196616 | tf_op jit(solution)/shard_map/gram/ppermute | solution.py:28
  90.2 1.9 %collective-permute-start.28 = (f32[128,128]{1,0:T(8,128)S(1)}, f32[128,128]{1,0:T(8,128)S(1)}, u32[]{:S(2)}, u32[]{:S(2)}) collective-permute-start(f32[128,128]{1,0:T(8,128)S(1)} %add.84), channel_id=1, source_target_pairs={{0,4},{1,5},{2,6},{3,7},{4,0},{5,1},{6,2},{7,3},{8,12},{9,13},{10,... | collective-permute-start | bytes 196616 | tf_op jit(solution)/shard_map/gram/ppermute | solution.py:28
  92.1 0.3 collective-permute-start.33
  92.5 1.3 %collective-permute-start.35 = (bf16[1024,128]{1,0:T(8,128)(2,1)S(1)}, bf16[1024,128]{1,0:T(8,128)(2,1)S(1)}, u32[]{:S(2)}, u32[]{:S(2)}) collective-permute-start(bf16[1024,128]{1,0:T(8,128)(2,1)S(1)} %pad_maximum_fusion.6.refs_2_), channel_id=1, source_target_pairs={{0,2},{1,3},{2,0},{3,1},{4,6},{5,7},{6,4},{7,5},{8,10},{9,11},{10,... | collective-permute-start | bytes 786440 | tf_op jit(solution)/shard_map/gather_range/ppermute | solution.py:28
  93.8 1.7 %collective-permute-done.29 = f32[128,128]{1,0:T(8,128)S(1)} collective-permute-done((f32[128,128]{1,0:T(8,128)S(1)}, f32[128,128]{1,0:T(8,128)S(1)}, u32[]{:S(2)}, u32[]{:S(2)}) %collective-permute-start.29) | collective-permute-done | bytes 65568 | tf_op jit(solution)/shard_map/gram/ppermute | solution.py:28
  95.5 1.5 %collective-permute-start.37 = (bf16[1024,128]{1,0:T(8,128)(2,1)S(1)}, bf16[1024,128]{1,0:T(8,128)(2,1)S(1)}, u32[]{:S(2)}, u32[]{:S(2)}) collective-permute-start(bf16[1024,128]{1,0:T(8,128)(2,1)S(1)} %pad_maximum_fusion.7.refs_3_), channel_id=1, source_target_pairs={{0,2},{1,3},{2,0},{3,1},{4,6},{5,7},{6,4},{7,5},{8,10},{9,11},{10,... | collective-permute-start | bytes 786440 | tf_op jit(solution)/shard_map/gather_range/ppermute | solution.py:28
  97.0 1.2 %coords.4.refs_4_ = f32[512,128]{1,0:T(8,128)S(1)} custom-call(s32[1]{0:T(128)} %bitcast.index_ref, s32[1]{0:T(128)} %bitcast.1.group_ref, bf16[256,16384]{1,0:T(8,128)(2,1)S(1)} %get-tuple-element.21.x_ref, bf16[256,8192]{1,0:T(8,128)(2,1)S(1)} %collective-permute-done.2.refs_0_, bf16[1024,128]{1,0:T(8,128)(2,1)S(1)} %pad_maximum_fusion.5.refs_1_, ...), custom_call_target="tpu_custom_call" | custom-call | flops 536870912 | bytes 4194304 | tf_op jit(solution)/shard_map/coords/pallas_call | solution.py:134
  98.4 6.4 %factor.1 = (f32[128,128]{1,0:T(8,128)S(1)}, f32[1024,128]{1,0:T(8,128)}) custom-call(f32[128,128]{1,0:T(8,128)S(1)} %add_add_fusion.gram_ref, f32[1024,128]{1,0:T(8,128)S(1)} %pad_maximum_fusion.range_ref), custom_call_target="tpu_custom_call" | custom-call | flops 10000000 | bytes 20000000 | tf_op jit(solution)/shard_map/factor/pallas_call | solution.py:218
  104.8 0.3 collective-permute-done.37.refs_3_
  105.1 1.0 coords.5.refs_2_
  106.1 1.6 %collective-permute-done.32.refs_1_ = bf16[1024,128]{1,0:T(8,128)(2,1)S(1)} collective-permute-done((bf16[1024,128]{1,0:T(8,128)(2,1)S(1)}, bf16[1024,128]{1,0:T(8,128)(2,1)S(1)}, u32[]{:S(2)}, u32[]{:S(2)}) %collective-permute-start.32) | collective-permute-done | bytes 262176 | tf_op jit(solution)/shard_map/gather_range/ppermute | solution.py:28
  107.8 0.4 coords.6.part_ref
  108.3 1.3 %collective-permute-done.38.theirs_ref = f32[256,128]{1,0:T(8,128)S(1)} collective-permute-done((f32[256,128]{1,0:T(8,128)S(1)}, f32[256,128]{1,0:T(8,128)S(1)}, u32[]{:S(2)}, u32[]{:S(2)}) %collective-permute-start.38) | collective-permute-done | bytes 131104 | tf_op jit(solution)/shard_map/coords/ppermute | solution.py:28
  109.6 1.0 coords.7
  (68 shorter events, 2.5 us)
Async XLA Ops:
  1.6 8.0 %collective-permute-start = (bf16[256,128]{1,0:T(8,128)(2,1)S(1)}, bf16[256,128]{1,0:T(8,128)(2,1)S(1)}, u32[]{:S(2)}, u32[]{:S(2)}) collective-permute-start(bf16[256,128]{1,0:T(8,128)(2,1)S(1)} %get-tuple-element.62), channel_id=1, source_target_pairs={{0,8},{1,9},{2,10},{3,11},{4,12},{5,13},{6,14},{7,15},{8,0},{9,1},... | collective-permute-start | bytes 196616 | tf_op jit(solution)/shard_map/gather_sketch/ppermute | solution.py:28
  5.7 6.5 %collective-permute-start.1 = (bf16[256,128]{1,0:T(8,128)(2,1)S(1)}, bf16[256,128]{1,0:T(8,128)(2,1)S(1)}, u32[]{:S(2)}, u32[]{:S(2)}) collective-permute-start(bf16[256,128]{1,0:T(8,128)(2,1)S(1)} %get-tuple-element.63), channel_id=1, source_target_pairs={{0,8},{1,9},{2,10},{3,11},{4,12},{5,13},{6,14},{7,15},{8,0},{9,1},... | collective-permute-start | bytes 196616 | tf_op jit(solution)/shard_map/gather_sketch/ppermute | solution.py:28
  12.1 19.6 %collective-permute-start.2 = (bf16[256,8192]{1,0:T(8,128)(2,1)S(1)}, bf16[256,8192]{1,0:T(8,128)(2,1)S(1)}, u32[]{:S(2)}, u32[]{:S(2)}) collective-permute-start(bf16[256,8192]{1,0:T(8,128)(2,1)S(1)} %get-tuple-element.23), channel_id=1, source_target_pairs={{0,1},{1,0},{2,3},{3,2},{4,5},{5,4},{6,7},{7,6},{8,9},{9,8},{10,11... | collective-permute-start | bytes 12582920 | tf_op jit(solution)/shard_map/split_features/ppermute | solution.py:28
  12.1 6.9 %collective-permute-start.9 = (bf16[256,128]{1,0:T(8,128)(2,1)S(1)}, bf16[256,128]{1,0:T(8,128)(2,1)S(1)}, u32[]{:S(2)}, u32[]{:S(2)}) collective-permute-start(bf16[256,128]{1,0:T(8,128)(2,1)S(1)} %get-tuple-element.61), channel_id=1, source_target_pairs={{0,8},{1,9},{2,10},{3,11},{4,12},{5,13},{6,14},{7,15},{8,0},{9,1},... | collective-permute-start | bytes 196616 | tf_op jit(solution)/shard_map/gather_sketch/ppermute | solution.py:28
  12.6 8.3 %collective-permute-start.3 = (bf16[512,128]{1,0:T(8,128)(2,1)S(1)}, bf16[512,128]{1,0:T(8,128)(2,1)S(1)}, u32[]{:S(2)}, u32[]{:S(2)}) collective-permute-start(bf16[512,128]{1,0:T(8,128)(2,1)S(1)} %pad_maximum_fusion.8), channel_id=1, source_target_pairs={{0,2},{1,3},{2,0},{3,1},{4,6},{5,7},{6,4},{7,5},{8,10},{9,11},{10,... | collective-permute-start | bytes 393224 | tf_op jit(solution)/shard_map/gather_sketch/ppermute | solution.py:28
  14.1 9.5 %collective-permute-start.7 = (bf16[512,128]{1,0:T(8,128)(2,1)S(1)}, bf16[512,128]{1,0:T(8,128)(2,1)S(1)}, u32[]{:S(2)}, u32[]{:S(2)}) collective-permute-start(bf16[512,128]{1,0:T(8,128)(2,1)S(1)} %pad_maximum_fusion.9), channel_id=1, source_target_pairs={{0,4},{1,5},{2,6},{3,7},{4,0},{5,1},{6,2},{7,3},{8,12},{9,13},{10,... | collective-permute-start | bytes 393224 | tf_op jit(solution)/shard_map/gather_sketch/ppermute | solution.py:28
  19.0 6.2 %collective-permute-start.10 = (bf16[512,128]{1,0:T(8,128)(2,1)S(1)}, bf16[512,128]{1,0:T(8,128)(2,1)S(1)}, u32[]{:S(2)}, u32[]{:S(2)}) collective-permute-start(bf16[512,128]{1,0:T(8,128)(2,1)S(1)} %pad_maximum_fusion.10), channel_id=1, source_target_pairs={{0,2},{1,3},{2,0},{3,1},{4,6},{5,7},{6,4},{7,5},{8,10},{9,11},{10,... | collective-permute-start | bytes 393224 | tf_op jit(solution)/shard_map/gather_sketch/ppermute | solution.py:28
  20.8 9.3 %collective-permute-start.4 = (bf16[1024,128]{1,0:T(8,128)(2,1)S(1)}, bf16[1024,128]{1,0:T(8,128)(2,1)S(1)}, u32[]{:S(2)}, u32[]{:S(2)}) collective-permute-start(bf16[1024,128]{1,0:T(8,128)(2,1)S(1)} %pad_maximum_fusion.1.refs_1_), channel_id=1, source_target_pairs={{0,4},{1,5},{2,6},{3,7},{4,0},{5,1},{6,2},{7,3},{8,12},{9,13},{10,... | collective-permute-start | bytes 786440 | tf_op jit(solution)/shard_map/gather_sketch/ppermute | solution.py:28
  22.1 10.6 %collective-permute-start.6 = (bf16[1024,128]{1,0:T(8,128)(2,1)S(1)}, bf16[1024,128]{1,0:T(8,128)(2,1)S(1)}, u32[]{:S(2)}, u32[]{:S(2)}) collective-permute-start(bf16[1024,128]{1,0:T(8,128)(2,1)S(1)} %pad_maximum_fusion.1.refs_1_), channel_id=1, source_target_pairs={{0,16},{16,0},{1,17},{17,1},{2,18},{18,2},{3,19},{19,3},{4,20},{20... | collective-permute-start | bytes 786440 | tf_op jit(solution)/shard_map/gather_sketch/ppermute | solution.py:258
  23.7 9.0 %collective-permute-start.8 = (bf16[1024,128]{1,0:T(8,128)(2,1)S(1)}, bf16[1024,128]{1,0:T(8,128)(2,1)S(1)}, u32[]{:S(2)}, u32[]{:S(2)}) collective-permute-start(bf16[1024,128]{1,0:T(8,128)(2,1)S(1)} %pad_maximum_fusion.2.refs_2_), channel_id=1, source_target_pairs={{0,2},{1,3},{2,0},{3,1},{4,6},{5,7},{6,4},{7,5},{8,10},{9,11},{10,... | collective-permute-start | bytes 786440 | tf_op jit(solution)/shard_map/gather_sketch/ppermute | solution.py:28
  25.2 8.8 %collective-permute-start.11 = (bf16[1024,128]{1,0:T(8,128)(2,1)S(1)}, bf16[1024,128]{1,0:T(8,128)(2,1)S(1)}, u32[]{:S(2)}, u32[]{:S(2)}) collective-permute-start(bf16[1024,128]{1,0:T(8,128)(2,1)S(1)} %pad_maximum_fusion.3.refs_3_), channel_id=1, source_target_pairs={{0,4},{1,5},{2,6},{3,7},{4,0},{5,1},{6,2},{7,3},{8,12},{9,13},{10,... | collective-permute-start | bytes 786440 | tf_op jit(solution)/shard_map/gather_sketch/ppermute | solution.py:28
  30.2 6.4 %collective-permute-start.5 = (bf16[1024,128]{1,0:T(8,128)(2,1)S(1)}, bf16[1024,128]{1,0:T(8,128)(2,1)S(1)}, u32[]{:S(2)}, u32[]{:S(2)}) collective-permute-start(bf16[1024,128]{1,0:T(8,128)(2,1)S(1)} %collective-permute-done.4.refs_1_), channel_id=1, source_target_pairs={{0,16},{16,0},{1,17},{17,1},{2,18},{18,2},{3,19},{19,3},{4,20},{20... | collective-permute-start | bytes 786440 | tf_op jit(solution)/shard_map/gather_sketch/ppermute | solution.py:258
  37.0 1.6 %collective-permute-start.12 = (f32[512,128]{1,0:T(8,128)S(1)}, f32[512,128]{1,0:T(8,128)S(1)}, u32[]{:S(2)}, u32[]{:S(2)}) collective-permute-start(f32[512,128]{1,0:T(8,128)S(1)} %sketched.5), channel_id=1, source_target_pairs={{0,1},{1,0},{2,3},{3,2},{4,5},{5,4},{6,7},{7,6},{8,9},{9,8},{10,11... | collective-permute-start | bytes 786440 | tf_op jit(solution)/shard_map/sketched/ppermute | solution.py:28
  39.6 9.2 %collective-permute-start.22 = (bf16[1024,128]{1,0:T(8,128)(2,1)S(1)}, bf16[1024,128]{1,0:T(8,128)(2,1)S(1)}, u32[]{:S(2)}, u32[]{:S(2)}) collective-permute-start(bf16[1024,128]{1,0:T(8,128)(2,1)S(1)} %get-tuple-element.31), channel_id=1, source_target_pairs={{0,4},{1,5},{2,6},{3,7},{4,0},{5,1},{6,2},{7,3},{8,12},{9,13},{10,... | collective-permute-start | bytes 786440 | tf_op jit(solution)/shard_map/range/ppermute | solution.py:28
  40.8 9.2 %collective-permute-start.19 = (bf16[1024,128]{1,0:T(8,128)(2,1)S(1)}, bf16[1024,128]{1,0:T(8,128)(2,1)S(1)}, u32[]{:S(2)}, u32[]{:S(2)}) collective-permute-start(bf16[1024,128]{1,0:T(8,128)(2,1)S(1)} %get-tuple-element.29), channel_id=1, source_target_pairs={{0,2},{1,3},{2,0},{3,1},{4,6},{5,7},{6,4},{7,5},{8,10},{9,11},{10,... | collective-permute-start | bytes 786440 | tf_op jit(solution)/shard_map/range/ppermute | solution.py:28
  42.3 13.3 %collective-permute-start.16 = (bf16[1024,128]{1,0:T(8,128)(2,1)S(1)}, bf16[1024,128]{1,0:T(8,128)(2,1)S(1)}, u32[]{:S(2)}, u32[]{:S(2)}) collective-permute-start(bf16[1024,128]{1,0:T(8,128)(2,1)S(1)} %get-tuple-element.27), channel_id=1, source_target_pairs={{0,2},{1,3},{2,0},{3,1},{4,6},{5,7},{6,4},{7,5},{8,10},{9,11},{10,... | collective-permute-start | bytes 786440 | tf_op jit(solution)/shard_map/range/ppermute | solution.py:28
  42.8 14.0 %collective-permute-start.13 = (bf16[1024,128]{1,0:T(8,128)(2,1)S(1)}, bf16[1024,128]{1,0:T(8,128)(2,1)S(1)}, u32[]{:S(2)}, u32[]{:S(2)}) collective-permute-start(bf16[1024,128]{1,0:T(8,128)(2,1)S(1)} %get-tuple-element.25), channel_id=1, source_target_pairs={{0,4},{1,5},{2,6},{3,7},{4,0},{5,1},{6,2},{7,3},{8,12},{9,13},{10,... | collective-permute-start | bytes 786440 | tf_op jit(solution)/shard_map/range/ppermute | solution.py:28
  49.0 8.8 %collective-permute-start.23 = (bf16[512,128]{1,0:T(8,128)(2,1)S(1)}, bf16[512,128]{1,0:T(8,128)(2,1)S(1)}, u32[]{:S(2)}, u32[]{:S(2)}) collective-permute-start(bf16[512,128]{1,0:T(8,128)(2,1)S(1)} %fusion.25), channel_id=1, source_target_pairs={{0,2},{1,3},{2,0},{3,1},{4,6},{5,7},{6,4},{7,5},{8,10},{9,11},{10,... | collective-permute-start | bytes 393224 | tf_op jit(solution)/shard_map/range/ppermute | solution.py:28
  50.3 8.8 %collective-permute-start.20 = (bf16[512,128]{1,0:T(8,128)(2,1)S(1)}, bf16[512,128]{1,0:T(8,128)(2,1)S(1)}, u32[]{:S(2)}, u32[]{:S(2)}) collective-permute-start(bf16[512,128]{1,0:T(8,128)(2,1)S(1)} %fusion.22), channel_id=1, source_target_pairs={{0,8},{1,9},{2,10},{3,11},{4,12},{5,13},{6,14},{7,15},{8,0},{9,1},... | collective-permute-start | bytes 393224 | tf_op jit(solution)/shard_map/range/ppermute | solution.py:28
  55.9 8.9 %collective-permute-start.17 = (bf16[512,128]{1,0:T(8,128)(2,1)S(1)}, bf16[512,128]{1,0:T(8,128)(2,1)S(1)}, u32[]{:S(2)}, u32[]{:S(2)}) collective-permute-start(bf16[512,128]{1,0:T(8,128)(2,1)S(1)} %fusion.19), channel_id=1, source_target_pairs={{0,4},{1,5},{2,6},{3,7},{4,0},{5,1},{6,2},{7,3},{8,12},{9,13},{10,... | collective-permute-start | bytes 393224 | tf_op jit(solution)/shard_map/range/ppermute | solution.py:28
  57.1 8.0 %collective-permute-start.14 = (bf16[512,128]{1,0:T(8,128)(2,1)S(1)}, bf16[512,128]{1,0:T(8,128)(2,1)S(1)}, u32[]{:S(2)}, u32[]{:S(2)}) collective-permute-start(bf16[512,128]{1,0:T(8,128)(2,1)S(1)} %fusion.16), channel_id=1, source_target_pairs={{0,2},{1,3},{2,0},{3,1},{4,6},{5,7},{6,4},{7,5},{8,10},{9,11},{10,... | collective-permute-start | bytes 393224 | tf_op jit(solution)/shard_map/range/ppermute | solution.py:28
  58.0 11.5 %collective-permute-start.24 = (bf16[512,128]{1,0:T(8,128)(2,1)S(1)}, bf16[512,128]{1,0:T(8,128)(2,1)S(1)}, u32[]{:S(2)}, u32[]{:S(2)}) collective-permute-start(bf16[512,128]{1,0:T(8,128)(2,1)S(1)} %get-tuple-element.53), channel_id=1, source_target_pairs={{0,8},{1,9},{2,10},{3,11},{4,12},{5,13},{6,14},{7,15},{8,0},{9,1},... | collective-permute-start | bytes 393224 | tf_op jit(solution)/shard_map/range/ppermute | solution.py:28
  59.2 10.4 %collective-permute-start.21 = (bf16[512,128]{1,0:T(8,128)(2,1)S(1)}, bf16[512,128]{1,0:T(8,128)(2,1)S(1)}, u32[]{:S(2)}, u32[]{:S(2)}) collective-permute-start(bf16[512,128]{1,0:T(8,128)(2,1)S(1)} %get-tuple-element.51), channel_id=1, source_target_pairs={{0,4},{1,5},{2,6},{3,7},{4,0},{5,1},{6,2},{7,3},{8,12},{9,13},{10,... | collective-permute-start | bytes 393224 | tf_op jit(solution)/shard_map/range/ppermute | solution.py:28
  65.0 10.5 %collective-permute-start.18 = (bf16[512,128]{1,0:T(8,128)(2,1)S(1)}, bf16[512,128]{1,0:T(8,128)(2,1)S(1)}, u32[]{:S(2)}, u32[]{:S(2)}) collective-permute-start(bf16[512,128]{1,0:T(8,128)(2,1)S(1)} %get-tuple-element.49), channel_id=1, source_target_pairs={{0,8},{1,9},{2,10},{3,11},{4,12},{5,13},{6,14},{7,15},{8,0},{9,1},... | collective-permute-start | bytes 393224 | tf_op jit(solution)/shard_map/range/ppermute | solution.py:28
  65.2 11.6 %collective-permute-start.15 = (bf16[512,128]{1,0:T(8,128)(2,1)S(1)}, bf16[512,128]{1,0:T(8,128)(2,1)S(1)}, u32[]{:S(2)}, u32[]{:S(2)}) collective-permute-start(bf16[512,128]{1,0:T(8,128)(2,1)S(1)} %get-tuple-element.47), channel_id=1, source_target_pairs={{0,8},{1,9},{2,10},{3,11},{4,12},{5,13},{6,14},{7,15},{8,0},{9,1},... | collective-permute-start | bytes 393224 | tf_op jit(solution)/shard_map/range/ppermute | solution.py:28
  78.1 2.4 %collective-permute-start.25 = (f32[128,128]{1,0:T(8,128)S(1)}, f32[128,128]{1,0:T(8,128)S(1)}, u32[]{:S(2)}, u32[]{:S(2)}) collective-permute-start(f32[128,128]{1,0:T(8,128)S(1)} %fusion.33), channel_id=1, source_target_pairs={{0,1},{1,0},{2,3},{3,2},{4,5},{5,4},{6,7},{7,6},{8,9},{9,8},{10,11... | collective-permute-start | bytes 196616 | tf_op jit(solution)/shard_map/gram/ppermute | solution.py:28
  78.2 10.2 %collective-permute-start.27 = (bf16[512,128]{1,0:T(8,128)(2,1)S(1)}, bf16[512,128]{1,0:T(8,128)(2,1)S(1)}, u32[]{:S(2)}, u32[]{:S(2)}) collective-permute-start(bf16[512,128]{1,0:T(8,128)(2,1)S(1)} %pad_maximum_fusion.11), channel_id=1, source_target_pairs={{0,2},{1,3},{2,0},{3,1},{4,6},{5,7},{6,4},{7,5},{8,10},{9,11},{10,... | collective-permute-start | bytes 393224 | tf_op jit(solution)/shard_map/gather_range/ppermute | solution.py:28
  79.8 10.3 %collective-permute-start.31 = (bf16[512,128]{1,0:T(8,128)(2,1)S(1)}, bf16[512,128]{1,0:T(8,128)(2,1)S(1)}, u32[]{:S(2)}, u32[]{:S(2)}) collective-permute-start(bf16[512,128]{1,0:T(8,128)(2,1)S(1)} %pad_maximum_fusion.12), channel_id=1, source_target_pairs={{0,2},{1,3},{2,0},{3,1},{4,6},{5,7},{6,4},{7,5},{8,10},{9,11},{10,... | collective-permute-start | bytes 393224 | tf_op jit(solution)/shard_map/gather_range/ppermute | solution.py:28
  80.4 11.7 %collective-permute-start.34 = (bf16[512,128]{1,0:T(8,128)(2,1)S(1)}, bf16[512,128]{1,0:T(8,128)(2,1)S(1)}, u32[]{:S(2)}, u32[]{:S(2)}) collective-permute-start(bf16[512,128]{1,0:T(8,128)(2,1)S(1)} %pad_maximum_fusion.13), channel_id=1, source_target_pairs={{0,4},{1,5},{2,6},{3,7},{4,0},{5,1},{6,2},{7,3},{8,12},{9,13},{10,... | collective-permute-start | bytes 393224 | tf_op jit(solution)/shard_map/gather_range/ppermute | solution.py:28
  80.5 7.9 %collective-permute-start.26 = (f32[128,128]{1,0:T(8,128)S(1)}, f32[128,128]{1,0:T(8,128)S(1)}, u32[]{:S(2)}, u32[]{:S(2)}) collective-permute-start(f32[128,128]{1,0:T(8,128)S(1)} %add.83), channel_id=1, source_target_pairs={{0,2},{1,3},{2,0},{3,1},{4,6},{5,7},{6,4},{7,5},{8,10},{9,11},{10,... | collective-permute-start | bytes 196616 | tf_op jit(solution)/shard_map/gram/ppermute | solution.py:28
  82.1 10.4 %collective-permute-start.36 = (bf16[512,128]{1,0:T(8,128)(2,1)S(1)}, bf16[512,128]{1,0:T(8,128)(2,1)S(1)}, u32[]{:S(2)}, u32[]{:S(2)}) collective-permute-start(bf16[512,128]{1,0:T(8,128)(2,1)S(1)} %pad_maximum_fusion.14), channel_id=1, source_target_pairs={{0,8},{1,9},{2,10},{3,11},{4,12},{5,13},{6,14},{7,15},{8,0},{9,1},... | collective-permute-start | bytes 393224 | tf_op jit(solution)/shard_map/gather_range/ppermute | solution.py:28
  88.4 7.1 %collective-permute-start.29 = (f32[128,128]{1,0:T(8,128)S(1)}, f32[128,128]{1,0:T(8,128)S(1)}, u32[]{:S(2)}, u32[]{:S(2)}) collective-permute-start(f32[128,128]{1,0:T(8,128)S(1)} %add.84), channel_id=1, source_target_pairs={{0,8},{1,9},{2,10},{3,11},{4,12},{5,13},{6,14},{7,15},{8,0},{9,1},... | collective-permute-start | bytes 196616 | tf_op jit(solution)/shard_map/gram/ppermute | solution.py:28
  88.5 9.8 %collective-permute-start.30 = (f32[128,128]{1,0:T(8,128)S(1)}, f32[128,128]{1,0:T(8,128)S(1)}, u32[]{:S(2)}, u32[]{:S(2)}) collective-permute-start(f32[128,128]{1,0:T(8,128)S(1)} %add.84), channel_id=1, source_target_pairs={{0,12},{1,13},{2,14},{3,15},{4,8},{5,9},{6,10},{7,11},{8,4},{9,5},... | collective-permute-start | bytes 196616 | tf_op jit(solution)/shard_map/gram/ppermute | solution.py:28
  90.2 8.2 %collective-permute-start.28 = (f32[128,128]{1,0:T(8,128)S(1)}, f32[128,128]{1,0:T(8,128)S(1)}, u32[]{:S(2)}, u32[]{:S(2)}) collective-permute-start(f32[128,128]{1,0:T(8,128)S(1)} %add.84), channel_id=1, source_target_pairs={{0,4},{1,5},{2,6},{3,7},{4,0},{5,1},{6,2},{7,3},{8,12},{9,13},{10,... | collective-permute-start | bytes 196616 | tf_op jit(solution)/shard_map/gram/ppermute | solution.py:28
  92.1 12.7 %collective-permute-start.33 = (bf16[1024,128]{1,0:T(8,128)(2,1)S(1)}, bf16[1024,128]{1,0:T(8,128)(2,1)S(1)}, u32[]{:S(2)}, u32[]{:S(2)}) collective-permute-start(bf16[1024,128]{1,0:T(8,128)(2,1)S(1)} %pad_maximum_fusion.5.refs_1_), channel_id=1, source_target_pairs={{0,4},{1,5},{2,6},{3,7},{4,0},{5,1},{6,2},{7,3},{8,12},{9,13},{10,... | collective-permute-start | bytes 786440 | tf_op jit(solution)/shard_map/gather_range/ppermute | solution.py:28
  92.5 12.3 %collective-permute-start.35 = (bf16[1024,128]{1,0:T(8,128)(2,1)S(1)}, bf16[1024,128]{1,0:T(8,128)(2,1)S(1)}, u32[]{:S(2)}, u32[]{:S(2)}) collective-permute-start(bf16[1024,128]{1,0:T(8,128)(2,1)S(1)} %pad_maximum_fusion.6.refs_2_), channel_id=1, source_target_pairs={{0,2},{1,3},{2,0},{3,1},{4,6},{5,7},{6,4},{7,5},{8,10},{9,11},{10,... | collective-permute-start | bytes 786440 | tf_op jit(solution)/shard_map/gather_range/ppermute | solution.py:28
  95.5 9.7 %collective-permute-start.37 = (bf16[1024,128]{1,0:T(8,128)(2,1)S(1)}, bf16[1024,128]{1,0:T(8,128)(2,1)S(1)}, u32[]{:S(2)}, u32[]{:S(2)}) collective-permute-start(bf16[1024,128]{1,0:T(8,128)(2,1)S(1)} %pad_maximum_fusion.7.refs_3_), channel_id=1, source_target_pairs={{0,2},{1,3},{2,0},{3,1},{4,6},{5,7},{6,4},{7,5},{8,10},{9,11},{10,... | collective-permute-start | bytes 786440 | tf_op jit(solution)/shard_map/gather_range/ppermute | solution.py:28
  98.3 9.5 %collective-permute-start.32 = (bf16[1024,128]{1,0:T(8,128)(2,1)S(1)}, bf16[1024,128]{1,0:T(8,128)(2,1)S(1)}, u32[]{:S(2)}, u32[]{:S(2)}) collective-permute-start(bf16[1024,128]{1,0:T(8,128)(2,1)S(1)} %pad_maximum_fusion.4.refs_4_), channel_id=1, source_target_pairs={{0,4},{1,5},{2,6},{3,7},{4,0},{5,1},{6,2},{7,3},{8,12},{9,13},{10,... | collective-permute-start | bytes 786440 | tf_op jit(solution)/shard_map/gather_range/ppermute | solution.py:28
  108.2 1.4 %collective-permute-start.38 = (f32[256,128]{1,0:T(8,128)S(1)}, f32[256,128]{1,0:T(8,128)S(1)}, u32[]{:S(2)}, u32[]{:S(2)}) collective-permute-start(f32[256,128]{1,0:T(8,128)S(1)} %slice.136), channel_id=1, source_target_pairs={{0,1},{1,0},{2,3},{3,2},{4,5},{5,4},{6,7},{7,6},{8,9},{9,8},{10,11... | collective-permute-start | bytes 393224 | tf_op jit(solution)/shard_map/coords/ppermute | solution.py:28

commit v8 on v7

--- a/solution.py
+++ b/solution.py
@@ -326,8 +326,7 @@
         inverse, basis = factored(math.sqrt(depth), gram, range_rows)
     with jax.named_scope("coords"):
         part = project(place, near_rows, x, others, held)
-        part = project(place, far_rows[:-1], x, others, came[:-1], after(part, inverse))
-        part = project(place, far_rows[-1:], x, others, came[-1:], part)
+        part = project(place, far_rows, x, others, came, after(part, inverse))
         coords, resid_rms = close(depth, part, swap(part[rows:], 1, n), inverse, norm)
     return basis[None], coords, resid_rms.reshape(rows)
 

time: 111 us -> 109 us (0.982)
    pallas_call x6 -> x5, Pallas kernels: 5.35 us -> 5.19 us  [project(): pl.pallas_call(functools.partial(project_kernel, width, entries, init is...]
  transfers between devices with their start and end apart: 39 -> 39, of which waited for: 19 -> 19; matrix products, arithmetic and copies ran while one was open for 2% -> 2% of each run, Pallas kernels for 14% -> 13%
where the time goes in v8:
time: 109 us
  waiting for transfers between devices  42.8 us (39%)
  starting transfers between devices  42.6 us (39%)
  Pallas kernels  18.1 us (17%)
  other arithmetic  2.49 us (2%)
    ppermute x37, waiting for transfers between devices, swap(): return lax.ppermute(value, 'tok', [(i, i ^ bit) for i in range(n)])  41.6 us
    ppermute x37, starting transfers between devices, swap(): return lax.ppermute(value, 'tok', [(i, i ^ bit) for i in range(n)])  39.6 us
    pallas_call x1, Pallas kernels, factored(): pl.pallas_call(functools.partial(factor_kernel, scale), in_specs=[VMEM] *...  6.41 us
    pallas_call x5, Pallas kernels, project(): pl.pallas_call(functools.partial(project_kernel, width, entries, init is...  5.19 us
    pallas_call x1, Pallas kernels, load(): pl.pallas_call(functools.partial(load_kernel, width), in_specs=[SMEM, ANY...  3.78 us
    ppermute x2, starting transfers between devices, across(): return lax.ppermute(value, 'groups', [(0, 1), (1, 0)])  3.04 us
  transfers between devices with their start and end apart: 39, of which 19 were waited for; matrix products, arithmetic and copies ran while one was open for 2% of the time, Pallas kernels for 13%

profile of v8, /device:TPU:0, one launch (start us, length us, event | category | flops | bytes accessed | tf_op | source)
XLA Modules:
  0.0 109.1 jit_solution(8494495979617448663)
XLA Ops:
  0.6 0.9 slice_bitcast_fusion
  1.6 4.1 %collective-permute-start = (bf16[256,128]{1,0:T(8,128)(2,1)S(1)}, bf16[256,128]{1,0:T(8,128)(2,1)S(1)}, u32[]{:S(2)}, u32[]{:S(2)}) collective-permute-start(bf16[256,128]{1,0:T(8,128)(2,1)S(1)} %get-tuple-element.62), channel_id=1, source_target_pairs={{0,8},{1,9},{2,10},{3,11},{4,12},{5,13},{6,14},{7,15},{8,0},{9,1},... | collective-permute-start | bytes 196616 | tf_op jit(solution)/shard_map/gather_sketch/ppermute | solution.py:28
  5.7 3.8 %split_features.1 = (bf16[256,16384]{1,0:T(8,128)(2,1)S(1)}, f32[256,128]{1,0:T(8,128)S(1)}, bf16[256,8192]{1,0:T(8,128)(2,1)S(1)}) custom-call(s32[1]{0:T(128)} %bitcast.index_ref, bf16[256,16384]{1,0:T(8,128)(2,1)} %x_ref.1), custom_call_target="tpu_custom_call" | custom-call | flops 8388608 | bytes 16777216 | tf_op jit(solution)/shard_map/split_features/pallas_call | solution.py:95
  9.5 2.6 %collective-permute-done.1 = bf16[256,128]{1,0:T(8,128)(2,1)S(1)} collective-permute-done((bf16[256,128]{1,0:T(8,128)(2,1)S(1)}, bf16[256,128]{1,0:T(8,128)(2,1)S(1)}, u32[]{:S(2)}, u32[]{:S(2)}) %collective-permute-start.1) | collective-permute-done | bytes 65568 | tf_op jit(solution)/shard_map/gather_sketch/ppermute | solution.py:28
  12.1 0.4 collective-permute-start.9
  12.6 1.6 %collective-permute-start.3 = (bf16[512,128]{1,0:T(8,128)(2,1)S(1)}, bf16[512,128]{1,0:T(8,128)(2,1)S(1)}, u32[]{:S(2)}, u32[]{:S(2)}) collective-permute-start(bf16[512,128]{1,0:T(8,128)(2,1)S(1)} %pad_maximum_fusion.8), channel_id=1, source_target_pairs={{0,2},{1,3},{2,0},{3,1},{4,6},{5,7},{6,4},{7,5},{8,10},{9,11},{10,... | collective-permute-start | bytes 393224 | tf_op jit(solution)/shard_map/gather_sketch/ppermute | solution.py:28
  14.1 3.6 %collective-permute-start.7 = (bf16[512,128]{1,0:T(8,128)(2,1)S(1)}, bf16[512,128]{1,0:T(8,128)(2,1)S(1)}, u32[]{:S(2)}, u32[]{:S(2)}) collective-permute-start(bf16[512,128]{1,0:T(8,128)(2,1)S(1)} %pad_maximum_fusion.9), channel_id=1, source_target_pairs={{0,4},{1,5},{2,6},{3,7},{4,0},{5,1},{6,2},{7,3},{8,12},{9,13},{10,... | collective-permute-start | bytes 393224 | tf_op jit(solution)/shard_map/gather_sketch/ppermute | solution.py:28
  17.7 1.2 %collective-permute-done.9 = bf16[256,128]{1,0:T(8,128)(2,1)S(1)} collective-permute-done((bf16[256,128]{1,0:T(8,128)(2,1)S(1)}, bf16[256,128]{1,0:T(8,128)(2,1)S(1)}, u32[]{:S(2)}, u32[]{:S(2)}) %collective-permute-start.9) | collective-permute-done | bytes 65568 | tf_op jit(solution)/shard_map/gather_sketch/ppermute | solution.py:28
  19.0 1.8 %collective-permute-start.10 = (bf16[512,128]{1,0:T(8,128)(2,1)S(1)}, bf16[512,128]{1,0:T(8,128)(2,1)S(1)}, u32[]{:S(2)}, u32[]{:S(2)}) collective-permute-start(bf16[512,128]{1,0:T(8,128)(2,1)S(1)} %pad_maximum_fusion.10), channel_id=1, source_target_pairs={{0,2},{1,3},{2,0},{3,1},{4,6},{5,7},{6,4},{7,5},{8,10},{9,11},{10,... | collective-permute-start | bytes 393224 | tf_op jit(solution)/shard_map/gather_sketch/ppermute | solution.py:28
  20.8 1.3 %collective-permute-start.4 = (bf16[1024,128]{1,0:T(8,128)(2,1)S(1)}, bf16[1024,128]{1,0:T(8,128)(2,1)S(1)}, u32[]{:S(2)}, u32[]{:S(2)}) collective-permute-start(bf16[1024,128]{1,0:T(8,128)(2,1)S(1)} %pad_maximum_fusion.1.refs_1_), channel_id=1, source_target_pairs={{0,4},{1,5},{2,6},{3,7},{4,0},{5,1},{6,2},{7,3},{8,12},{9,13},{10,... | collective-permute-start | bytes 786440 | tf_op jit(solution)/shard_map/gather_sketch/ppermute | solution.py:28
  22.1 1.5 %collective-permute-start.6 = (bf16[1024,128]{1,0:T(8,128)(2,1)S(1)}, bf16[1024,128]{1,0:T(8,128)(2,1)S(1)}, u32[]{:S(2)}, u32[]{:S(2)}) collective-permute-start(bf16[1024,128]{1,0:T(8,128)(2,1)S(1)} %pad_maximum_fusion.1.refs_1_), channel_id=1, source_target_pairs={{0,16},{16,0},{1,17},{17,1},{2,18},{18,2},{3,19},{19,3},{4,20},{20... | collective-permute-start | bytes 786440 | tf_op jit(solution)/shard_map/gather_sketch/ppermute | solution.py:258
  23.7 1.6 %collective-permute-start.8 = (bf16[1024,128]{1,0:T(8,128)(2,1)S(1)}, bf16[1024,128]{1,0:T(8,128)(2,1)S(1)}, u32[]{:S(2)}, u32[]{:S(2)}) collective-permute-start(bf16[1024,128]{1,0:T(8,128)(2,1)S(1)} %pad_maximum_fusion.2.refs_2_), channel_id=1, source_target_pairs={{0,2},{1,3},{2,0},{3,1},{4,6},{5,7},{6,4},{7,5},{8,10},{9,11},{10,... | collective-permute-start | bytes 786440 | tf_op jit(solution)/shard_map/gather_sketch/ppermute | solution.py:28
  25.4 4.8 %collective-permute-done.4.refs_1_ = bf16[1024,128]{1,0:T(8,128)(2,1)S(1)} collective-permute-done((bf16[1024,128]{1,0:T(8,128)(2,1)S(1)}, bf16[1024,128]{1,0:T(8,128)(2,1)S(1)}, u32[]{:S(2)}, u32[]{:S(2)}) %collective-permute-start.4) | collective-permute-done | bytes 262176 | tf_op jit(solution)/shard_map/gather_sketch/ppermute | solution.py:28
  30.2 1.5 %collective-permute-start.5 = (bf16[1024,128]{1,0:T(8,128)(2,1)S(1)}, bf16[1024,128]{1,0:T(8,128)(2,1)S(1)}, u32[]{:S(2)}, u32[]{:S(2)}) collective-permute-start(bf16[1024,128]{1,0:T(8,128)(2,1)S(1)} %collective-permute-done.4.refs_1_), channel_id=1, source_target_pairs={{0,16},{16,0},{1,17},{17,1},{2,18},{18,2},{3,19},{19,3},{4,20},{20... | collective-permute-start | bytes 786440 | tf_op jit(solution)/shard_map/gather_sketch/ppermute | solution.py:258
  31.7 1.0 sketched.3.refs_5_
  32.7 1.4 %collective-permute-done.11.refs_4_ = bf16[1024,128]{1,0:T(8,128)(2,1)S(1)} collective-permute-done((bf16[1024,128]{1,0:T(8,128)(2,1)S(1)}, bf16[1024,128]{1,0:T(8,128)(2,1)S(1)}, u32[]{:S(2)}, u32[]{:S(2)}) %collective-permute-start.11) | collective-permute-done | bytes 262176 | tf_op jit(solution)/shard_map/gather_sketch/ppermute | solution.py:28
  34.1 1.2 %sketched.4.refs_2_ = f32[512,128]{1,0:T(8,128)S(1)} custom-call(s32[1]{0:T(128)} %bitcast.index_ref, s32[1]{0:T(128)} %bitcast.1.group_ref, bf16[256,16384]{1,0:T(8,128)(2,1)S(1)} %get-tuple-element.21.x_ref, bf16[256,8192]{1,0:T(8,128)(2,1)S(1)} %collective-permute-done.2.refs_0_, bf16[1024,128]{1,0:T(8,128)(2,1)S(1)} %collective-permute-done.4.refs_1_, ...), custom_call_target="tpu_custom_call" | custom-call | flops 536870912 | bytes 4194304 | tf_op jit(solution)/shard_map/sketched/pallas_call | solution.py:134
  35.3 1.2 %collective-permute-done.5.refs_1_ = bf16[1024,128]{1,0:T(8,128)(2,1)S(1)} collective-permute-done((bf16[1024,128]{1,0:T(8,128)(2,1)S(1)}, bf16[1024,128]{1,0:T(8,128)(2,1)S(1)}, u32[]{:S(2)}, u32[]{:S(2)}) %collective-permute-start.5) | collective-permute-done | bytes 262176 | tf_op jit(solution)/shard_map/gather_sketch/ppermute | solution.py:258
  36.5 0.4 sketched.5
  37.1 1.5 %collective-permute-done.12 = f32[512,128]{1,0:T(8,128)S(1)} collective-permute-done((f32[512,128]{1,0:T(8,128)S(1)}, f32[512,128]{1,0:T(8,128)S(1)}, u32[]{:S(2)}, u32[]{:S(2)}) %collective-permute-start.12) | collective-permute-done | bytes 262176 | tf_op jit(solution)/shard_map/sketched/ppermute | solution.py:28
  38.6 0.9 range.3
  39.6 1.3 %collective-permute-start.22 = (bf16[1024,128]{1,0:T(8,128)(2,1)S(1)}, bf16[1024,128]{1,0:T(8,128)(2,1)S(1)}, u32[]{:S(2)}, u32[]{:S(2)}) collective-permute-start(bf16[1024,128]{1,0:T(8,128)(2,1)S(1)} %get-tuple-element.31), channel_id=1, source_target_pairs={{0,4},{1,5},{2,6},{3,7},{4,0},{5,1},{6,2},{7,3},{8,12},{9,13},{10,... | collective-permute-start | bytes 786440 | tf_op jit(solution)/shard_map/range/ppermute | solution.py:28
  40.8 1.5 %collective-permute-start.19 = (bf16[1024,128]{1,0:T(8,128)(2,1)S(1)}, bf16[1024,128]{1,0:T(8,128)(2,1)S(1)}, u32[]{:S(2)}, u32[]{:S(2)}) collective-permute-start(bf16[1024,128]{1,0:T(8,128)(2,1)S(1)} %get-tuple-element.29), channel_id=1, source_target_pairs={{0,2},{1,3},{2,0},{3,1},{4,6},{5,7},{6,4},{7,5},{8,10},{9,11},{10,... | collective-permute-start | bytes 786440 | tf_op jit(solution)/shard_map/range/ppermute | solution.py:28
  42.3 0.5 collective-permute-start.16
  42.8 0.8 collective-permute-start.13
  43.7 0.9 range.2
  44.6 4.2 %collective-permute-done.22 = bf16[1024,128]{1,0:T(8,128)(2,1)S(1)} collective-permute-done((bf16[1024,128]{1,0:T(8,128)(2,1)S(1)}, bf16[1024,128]{1,0:T(8,128)(2,1)S(1)}, u32[]{:S(2)}, u32[]{:S(2)}) %collective-permute-start.22) | collective-permute-done | bytes 262176 | tf_op jit(solution)/shard_map/range/ppermute | solution.py:28
  49.0 0.7 collective-permute-start.23
  49.7 0.3 collective-permute-done.19
  50.0 0.2 fusion.6
  50.3 1.2 %collective-permute-start.20 = (bf16[512,128]{1,0:T(8,128)(2,1)S(1)}, bf16[512,128]{1,0:T(8,128)(2,1)S(1)}, u32[]{:S(2)}, u32[]{:S(2)}) collective-permute-start(bf16[512,128]{1,0:T(8,128)(2,1)S(1)} %fusion.22), channel_id=1, source_target_pairs={{0,8},{1,9},{2,10},{3,11},{4,12},{5,13},{6,14},{7,15},{8,0},{9,1},... | collective-permute-start | bytes 393224 | tf_op jit(solution)/shard_map/range/ppermute | solution.py:28
  51.5 4.1 %collective-permute-done.16 = bf16[1024,128]{1,0:T(8,128)(2,1)S(1)} collective-permute-done((bf16[1024,128]{1,0:T(8,128)(2,1)S(1)}, bf16[1024,128]{1,0:T(8,128)(2,1)S(1)}, u32[]{:S(2)}, u32[]{:S(2)}) %collective-permute-start.16) | collective-permute-done | bytes 262176 | tf_op jit(solution)/shard_map/range/ppermute | solution.py:28
  55.6 0.2 fusion.5
  55.9 0.9 collective-permute-start.17
  56.8 0.2 fusion.4
  57.1 0.8 collective-permute-start.14
  58.0 1.1 collective-permute-start.24
  59.2 1.2 %collective-permute-start.21 = (bf16[512,128]{1,0:T(8,128)(2,1)S(1)}, bf16[512,128]{1,0:T(8,128)(2,1)S(1)}, u32[]{:S(2)}, u32[]{:S(2)}) collective-permute-start(bf16[512,128]{1,0:T(8,128)(2,1)S(1)} %get-tuple-element.51), channel_id=1, source_target_pairs={{0,4},{1,5},{2,6},{3,7},{4,0},{5,1},{6,2},{7,3},{8,12},{9,13},{10,... | collective-permute-start | bytes 393224 | tf_op jit(solution)/shard_map/range/ppermute | solution.py:28
  60.4 4.4 %collective-permute-done.17 = bf16[512,128]{1,0:T(8,128)(2,1)S(1)} collective-permute-done((bf16[512,128]{1,0:T(8,128)(2,1)S(1)}, bf16[512,128]{1,0:T(8,128)(2,1)S(1)}, u32[]{:S(2)}, u32[]{:S(2)}) %collective-permute-start.17) | collective-permute-done | bytes 131104 | tf_op jit(solution)/shard_map/range/ppermute | solution.py:28
  65.2 3.0 %collective-permute-start.15 = (bf16[512,128]{1,0:T(8,128)(2,1)S(1)}, bf16[512,128]{1,0:T(8,128)(2,1)S(1)}, u32[]{:S(2)}, u32[]{:S(2)}) collective-permute-start(bf16[512,128]{1,0:T(8,128)(2,1)S(1)} %get-tuple-element.47), channel_id=1, source_target_pairs={{0,8},{1,9},{2,10},{3,11},{4,12},{5,13},{6,14},{7,15},{8,0},{9,1},... | collective-permute-start | bytes 393224 | tf_op jit(solution)/shard_map/range/ppermute | solution.py:28
  68.2 1.3 %collective-permute-done.24 = bf16[512,128]{1,0:T(8,128)(2,1)S(1)} collective-permute-done((bf16[512,128]{1,0:T(8,128)(2,1)S(1)}, bf16[512,128]{1,0:T(8,128)(2,1)S(1)}, u32[]{:S(2)}, u32[]{:S(2)}) %collective-permute-start.24) | collective-permute-done | bytes 131104 | tf_op jit(solution)/shard_map/range/ppermute | solution.py:28
  69.8 5.7 %collective-permute-done.18 = bf16[512,128]{1,0:T(8,128)(2,1)S(1)} collective-permute-done((bf16[512,128]{1,0:T(8,128)(2,1)S(1)}, bf16[512,128]{1,0:T(8,128)(2,1)S(1)}, u32[]{:S(2)}, u32[]{:S(2)}) %collective-permute-start.18) | collective-permute-done | bytes 131104 | tf_op jit(solution)/shard_map/range/ppermute | solution.py:28
  75.6 1.3 %collective-permute-done.15 = bf16[512,128]{1,0:T(8,128)(2,1)S(1)} collective-permute-done((bf16[512,128]{1,0:T(8,128)(2,1)S(1)}, bf16[512,128]{1,0:T(8,128)(2,1)S(1)}, u32[]{:S(2)}, u32[]{:S(2)}) %collective-permute-start.15) | collective-permute-done | bytes 131104 | tf_op jit(solution)/shard_map/range/ppermute | solution.py:28
  77.0 1.0 fusion.33
  78.2 1.6 %collective-permute-start.27 = (bf16[512,128]{1,0:T(8,128)(2,1)S(1)}, bf16[512,128]{1,0:T(8,128)(2,1)S(1)}, u32[]{:S(2)}, u32[]{:S(2)}) collective-permute-start(bf16[512,128]{1,0:T(8,128)(2,1)S(1)} %pad_maximum_fusion.11), channel_id=1, source_target_pairs={{0,2},{1,3},{2,0},{3,1},{4,6},{5,7},{6,4},{7,5},{8,10},{9,11},{10,... | collective-permute-start | bytes 393224 | tf_op jit(solution)/shard_map/gather_range/ppermute | solution.py:28
  79.9 1.9 %collective-permute-start.34 = (bf16[512,128]{1,0:T(8,128)(2,1)S(1)}, bf16[512,128]{1,0:T(8,128)(2,1)S(1)}, u32[]{:S(2)}, u32[]{:S(2)}) collective-permute-start(bf16[512,128]{1,0:T(8,128)(2,1)S(1)} %pad_maximum_fusion.13), channel_id=1, source_target_pairs={{0,8},{1,9},{2,10},{3,11},{4,12},{5,13},{6,14},{7,15},{8,0},{9,1},... | collective-permute-start | bytes 393224 | tf_op jit(solution)/shard_map/gather_range/ppermute | solution.py:28
  81.8 0.9 collective-permute-start.26
  82.7 1.3 %collective-permute-start.36 = (bf16[512,128]{1,0:T(8,128)(2,1)S(1)}, bf16[512,128]{1,0:T(8,128)(2,1)S(1)}, u32[]{:S(2)}, u32[]{:S(2)}) collective-permute-start(bf16[512,128]{1,0:T(8,128)(2,1)S(1)} %pad_maximum_fusion.14), channel_id=1, source_target_pairs={{0,2},{1,3},{2,0},{3,1},{4,6},{5,7},{6,4},{7,5},{8,10},{9,11},{10,... | collective-permute-start | bytes 393224 | tf_op jit(solution)/shard_map/gather_range/ppermute | solution.py:28
  83.9 2.9 %collective-permute-done.26 = f32[128,128]{1,0:T(8,128)S(1)} collective-permute-done((f32[128,128]{1,0:T(8,128)S(1)}, f32[128,128]{1,0:T(8,128)S(1)}, u32[]{:S(2)}, u32[]{:S(2)}) %collective-permute-start.26) | collective-permute-done | bytes 65568 | tf_op jit(solution)/shard_map/gram/ppermute | solution.py:28
  86.9 1.1 %collective-permute-start.29 = (f32[128,128]{1,0:T(8,128)S(1)}, f32[128,128]{1,0:T(8,128)S(1)}, u32[]{:S(2)}, u32[]{:S(2)}) collective-permute-start(f32[128,128]{1,0:T(8,128)S(1)} %add.84), channel_id=1, source_target_pairs={{0,8},{1,9},{2,10},{3,11},{4,12},{5,13},{6,14},{7,15},{8,0},{9,1},... | collective-permute-start | bytes 196616 | tf_op jit(solution)/shard_map/gram/ppermute | solution.py:28
  88.0 1.6 %collective-permute-start.30 = (f32[128,128]{1,0:T(8,128)S(1)}, f32[128,128]{1,0:T(8,128)S(1)}, u32[]{:S(2)}, u32[]{:S(2)}) collective-permute-start(f32[128,128]{1,0:T(8,128)S(1)} %add.84), channel_id=1, source_target_pairs={{0,12},{1,13},{2,14},{3,15},{4,8},{5,9},{6,10},{7,11},{8,4},{9,5},... | collective-permute-start | bytes 196616 | tf_op jit(solution)/shard_map/gram/ppermute | solution.py:28
  89.6 0.9 collective-permute-start.28
  90.5 1.4 %collective-permute-done.34 = bf16[512,128]{1,0:T(8,128)(2,1)S(1)} collective-permute-done((bf16[512,128]{1,0:T(8,128)(2,1)S(1)}, bf16[512,128]{1,0:T(8,128)(2,1)S(1)}, u32[]{:S(2)}, u32[]{:S(2)}) %collective-permute-start.34) | collective-permute-done | bytes 131104 | tf_op jit(solution)/shard_map/gather_range/ppermute | solution.py:28
  92.0 0.4 collective-permute-start.33
  92.3 1.3 %collective-permute-done.29 = f32[128,128]{1,0:T(8,128)S(1)} collective-permute-done((f32[128,128]{1,0:T(8,128)S(1)}, f32[128,128]{1,0:T(8,128)S(1)}, u32[]{:S(2)}, u32[]{:S(2)}) %collective-permute-start.29) | collective-permute-done | bytes 65568 | tf_op jit(solution)/shard_map/gram/ppermute | solution.py:28
  93.6 0.8 collective-permute-start.35
  94.4 0.4 collective-permute-done.30
  94.8 1.3 %collective-permute-start.37 = (bf16[1024,128]{1,0:T(8,128)(2,1)S(1)}, bf16[1024,128]{1,0:T(8,128)(2,1)S(1)}, u32[]{:S(2)}, u32[]{:S(2)}) collective-permute-start(bf16[1024,128]{1,0:T(8,128)(2,1)S(1)} %pad_maximum_fusion.7.refs_4_), channel_id=1, source_target_pairs={{0,4},{1,5},{2,6},{3,7},{4,0},{5,1},{6,2},{7,3},{8,12},{9,13},{10,... | collective-permute-start | bytes 786440 | tf_op jit(solution)/shard_map/gather_range/ppermute | solution.py:28
  96.2 1.3 %coords.3.refs_5_ = f32[512,128]{1,0:T(8,128)S(1)} custom-call(s32[1]{0:T(128)} %bitcast.index_ref, s32[1]{0:T(128)} %bitcast.1.group_ref, bf16[256,16384]{1,0:T(8,128)(2,1)S(1)} %get-tuple-element.21.x_ref, bf16[256,8192]{1,0:T(8,128)(2,1)S(1)} %collective-permute-done.2.refs_0_, bf16[1024,128]{1,0:T(8,128)(2,1)S(1)} %pad_maximum_fusion.4.refs_1_, ...), custom_call_target="tpu_custom_call" | custom-call | flops 536870912 | bytes 4194304 | tf_op jit(solution)/shard_map/coords/pallas_call | solution.py:134
  97.5 6.4 %factor.1 = (f32[128,128]{1,0:T(8,128)S(1)}, f32[1024,128]{1,0:T(8,128)}) custom-call(f32[128,128]{1,0:T(8,128)S(1)} %add_add_fusion.gram_ref, f32[1024,128]{1,0:T(8,128)S(1)} %pad_maximum_fusion.range_ref), custom_call_target="tpu_custom_call" | custom-call | flops 10000000 | bytes 20000000 | tf_op jit(solution)/shard_map/factor/pallas_call | solution.py:218
  103.9 1.6 %collective-permute-done.37.refs_4_ = bf16[1024,128]{1,0:T(8,128)(2,1)S(1)} collective-permute-done((bf16[1024,128]{1,0:T(8,128)(2,1)S(1)}, bf16[1024,128]{1,0:T(8,128)(2,1)S(1)}, u32[]{:S(2)}, u32[]{:S(2)}) %collective-permute-start.37) | collective-permute-done | bytes 262176 | tf_op jit(solution)/shard_map/gather_range/ppermute | solution.py:28
  105.5 1.3 %coords.4.part_ref = f32[512,128]{1,0:T(8,128)S(1)} custom-call(s32[1]{0:T(128)} %bitcast.index_ref, s32[1]{0:T(128)} %bitcast.1.group_ref, bf16[256,16384]{1,0:T(8,128)(2,1)S(1)} %get-tuple-element.21.x_ref, bf16[256,8192]{1,0:T(8,128)(2,1)S(1)} %collective-permute-done.2.refs_0_, bf16[1024,128]{1,0:T(8,128)(2,1)S(1)} %collective-permute-done.31.refs_1_, ...), custom_call_target="tpu_custom_call" | custom-call | flops 536870912 | bytes 4194304 | tf_op jit(solution)/shard_map/coords/pallas_call | solution.py:134
  106.8 1.3 %collective-permute-done.38.theirs_ref = f32[256,128]{1,0:T(8,128)S(1)} collective-permute-done((f32[256,128]{1,0:T(8,128)S(1)}, f32[256,128]{1,0:T(8,128)S(1)}, u32[]{:S(2)}, u32[]{:S(2)}) %collective-permute-start.38) | collective-permute-done | bytes 131104 | tf_op jit(solution)/shard_map/coords/ppermute | solution.py:28
  108.2 1.0 coords.5
  (67 shorter events, 2.5 us)
Async XLA Ops:
  1.6 8.0 %collective-permute-start = (bf16[256,128]{1,0:T(8,128)(2,1)S(1)}, bf16[256,128]{1,0:T(8,128)(2,1)S(1)}, u32[]{:S(2)}, u32[]{:S(2)}) collective-permute-start(bf16[256,128]{1,0:T(8,128)(2,1)S(1)} %get-tuple-element.62), channel_id=1, source_target_pairs={{0,8},{1,9},{2,10},{3,11},{4,12},{5,13},{6,14},{7,15},{8,0},{9,1},... | collective-permute-start | bytes 196616 | tf_op jit(solution)/shard_map/gather_sketch/ppermute | solution.py:28
  5.7 6.5 %collective-permute-start.1 = (bf16[256,128]{1,0:T(8,128)(2,1)S(1)}, bf16[256,128]{1,0:T(8,128)(2,1)S(1)}, u32[]{:S(2)}, u32[]{:S(2)}) collective-permute-start(bf16[256,128]{1,0:T(8,128)(2,1)S(1)} %get-tuple-element.63), channel_id=1, source_target_pairs={{0,8},{1,9},{2,10},{3,11},{4,12},{5,13},{6,14},{7,15},{8,0},{9,1},... | collective-permute-start | bytes 196616 | tf_op jit(solution)/shard_map/gather_sketch/ppermute | solution.py:28
  12.1 19.6 %collective-permute-start.2 = (bf16[256,8192]{1,0:T(8,128)(2,1)S(1)}, bf16[256,8192]{1,0:T(8,128)(2,1)S(1)}, u32[]{:S(2)}, u32[]{:S(2)}) collective-permute-start(bf16[256,8192]{1,0:T(8,128)(2,1)S(1)} %get-tuple-element.23), channel_id=1, source_target_pairs={{0,1},{1,0},{2,3},{3,2},{4,5},{5,4},{6,7},{7,6},{8,9},{9,8},{10,11... | collective-permute-start | bytes 12582920 | tf_op jit(solution)/shard_map/split_features/ppermute | solution.py:28
  12.1 6.9 %collective-permute-start.9 = (bf16[256,128]{1,0:T(8,128)(2,1)S(1)}, bf16[256,128]{1,0:T(8,128)(2,1)S(1)}, u32[]{:S(2)}, u32[]{:S(2)}) collective-permute-start(bf16[256,128]{1,0:T(8,128)(2,1)S(1)} %get-tuple-element.61), channel_id=1, source_target_pairs={{0,8},{1,9},{2,10},{3,11},{4,12},{5,13},{6,14},{7,15},{8,0},{9,1},... | collective-permute-start | bytes 196616 | tf_op jit(solution)/shard_map/gather_sketch/ppermute | solution.py:28
  12.6 8.3 %collective-permute-start.3 = (bf16[512,128]{1,0:T(8,128)(2,1)S(1)}, bf16[512,128]{1,0:T(8,128)(2,1)S(1)}, u32[]{:S(2)}, u32[]{:S(2)}) collective-permute-start(bf16[512,128]{1,0:T(8,128)(2,1)S(1)} %pad_maximum_fusion.8), channel_id=1, source_target_pairs={{0,2},{1,3},{2,0},{3,1},{4,6},{5,7},{6,4},{7,5},{8,10},{9,11},{10,... | collective-permute-start | bytes 393224 | tf_op jit(solution)/shard_map/gather_sketch/ppermute | solution.py:28
  14.1 9.5 %collective-permute-start.7 = (bf16[512,128]{1,0:T(8,128)(2,1)S(1)}, bf16[512,128]{1,0:T(8,128)(2,1)S(1)}, u32[]{:S(2)}, u32[]{:S(2)}) collective-permute-start(bf16[512,128]{1,0:T(8,128)(2,1)S(1)} %pad_maximum_fusion.9), channel_id=1, source_target_pairs={{0,4},{1,5},{2,6},{3,7},{4,0},{5,1},{6,2},{7,3},{8,12},{9,13},{10,... | collective-permute-start | bytes 393224 | tf_op jit(solution)/shard_map/gather_sketch/ppermute | solution.py:28
  19.0 6.2 %collective-permute-start.10 = (bf16[512,128]{1,0:T(8,128)(2,1)S(1)}, bf16[512,128]{1,0:T(8,128)(2,1)S(1)}, u32[]{:S(2)}, u32[]{:S(2)}) collective-permute-start(bf16[512,128]{1,0:T(8,128)(2,1)S(1)} %pad_maximum_fusion.10), channel_id=1, source_target_pairs={{0,2},{1,3},{2,0},{3,1},{4,6},{5,7},{6,4},{7,5},{8,10},{9,11},{10,... | collective-permute-start | bytes 393224 | tf_op jit(solution)/shard_map/gather_sketch/ppermute | solution.py:28
  20.8 9.3 %collective-permute-start.4 = (bf16[1024,128]{1,0:T(8,128)(2,1)S(1)}, bf16[1024,128]{1,0:T(8,128)(2,1)S(1)}, u32[]{:S(2)}, u32[]{:S(2)}) collective-permute-start(bf16[1024,128]{1,0:T(8,128)(2,1)S(1)} %pad_maximum_fusion.1.refs_1_), channel_id=1, source_target_pairs={{0,4},{1,5},{2,6},{3,7},{4,0},{5,1},{6,2},{7,3},{8,12},{9,13},{10,... | collective-permute-start | bytes 786440 | tf_op jit(solution)/shard_map/gather_sketch/ppermute | solution.py:28
  22.1 10.6 %collective-permute-start.6 = (bf16[1024,128]{1,0:T(8,128)(2,1)S(1)}, bf16[1024,128]{1,0:T(8,128)(2,1)S(1)}, u32[]{:S(2)}, u32[]{:S(2)}) collective-permute-start(bf16[1024,128]{1,0:T(8,128)(2,1)S(1)} %pad_maximum_fusion.1.refs_1_), channel_id=1, source_target_pairs={{0,16},{16,0},{1,17},{17,1},{2,18},{18,2},{3,19},{19,3},{4,20},{20... | collective-permute-start | bytes 786440 | tf_op jit(solution)/shard_map/gather_sketch/ppermute | solution.py:258
  23.7 9.0 %collective-permute-start.8 = (bf16[1024,128]{1,0:T(8,128)(2,1)S(1)}, bf16[1024,128]{1,0:T(8,128)(2,1)S(1)}, u32[]{:S(2)}, u32[]{:S(2)}) collective-permute-start(bf16[1024,128]{1,0:T(8,128)(2,1)S(1)} %pad_maximum_fusion.2.refs_2_), channel_id=1, source_target_pairs={{0,2},{1,3},{2,0},{3,1},{4,6},{5,7},{6,4},{7,5},{8,10},{9,11},{10,... | collective-permute-start | bytes 786440 | tf_op jit(solution)/shard_map/gather_sketch/ppermute | solution.py:28
  25.2 8.8 %collective-permute-start.11 = (bf16[1024,128]{1,0:T(8,128)(2,1)S(1)}, bf16[1024,128]{1,0:T(8,128)(2,1)S(1)}, u32[]{:S(2)}, u32[]{:S(2)}) collective-permute-start(bf16[1024,128]{1,0:T(8,128)(2,1)S(1)} %pad_maximum_fusion.3.refs_3_), channel_id=1, source_target_pairs={{0,4},{1,5},{2,6},{3,7},{4,0},{5,1},{6,2},{7,3},{8,12},{9,13},{10,... | collective-permute-start | bytes 786440 | tf_op jit(solution)/shard_map/gather_sketch/ppermute | solution.py:28
  30.2 6.4 %collective-permute-start.5 = (bf16[1024,128]{1,0:T(8,128)(2,1)S(1)}, bf16[1024,128]{1,0:T(8,128)(2,1)S(1)}, u32[]{:S(2)}, u32[]{:S(2)}) collective-permute-start(bf16[1024,128]{1,0:T(8,128)(2,1)S(1)} %collective-permute-done.4.refs_1_), channel_id=1, source_target_pairs={{0,16},{16,0},{1,17},{17,1},{2,18},{18,2},{3,19},{19,3},{4,20},{20... | collective-permute-start | bytes 786440 | tf_op jit(solution)/shard_map/gather_sketch/ppermute | solution.py:258
  37.0 1.6 %collective-permute-start.12 = (f32[512,128]{1,0:T(8,128)S(1)}, f32[512,128]{1,0:T(8,128)S(1)}, u32[]{:S(2)}, u32[]{:S(2)}) collective-permute-start(f32[512,128]{1,0:T(8,128)S(1)} %sketched.5), channel_id=1, source_target_pairs={{0,1},{1,0},{2,3},{3,2},{4,5},{5,4},{6,7},{7,6},{8,9},{9,8},{10,11... | collective-permute-start | bytes 786440 | tf_op jit(solution)/shard_map/sketched/ppermute | solution.py:28
  39.6 9.2 %collective-permute-start.22 = (bf16[1024,128]{1,0:T(8,128)(2,1)S(1)}, bf16[1024,128]{1,0:T(8,128)(2,1)S(1)}, u32[]{:S(2)}, u32[]{:S(2)}) collective-permute-start(bf16[1024,128]{1,0:T(8,128)(2,1)S(1)} %get-tuple-element.31), channel_id=1, source_target_pairs={{0,4},{1,5},{2,6},{3,7},{4,0},{5,1},{6,2},{7,3},{8,12},{9,13},{10,... | collective-permute-start | bytes 786440 | tf_op jit(solution)/shard_map/range/ppermute | solution.py:28
  40.8 9.2 %collective-permute-start.19 = (bf16[1024,128]{1,0:T(8,128)(2,1)S(1)}, bf16[1024,128]{1,0:T(8,128)(2,1)S(1)}, u32[]{:S(2)}, u32[]{:S(2)}) collective-permute-start(bf16[1024,128]{1,0:T(8,128)(2,1)S(1)} %get-tuple-element.29), channel_id=1, source_target_pairs={{0,2},{1,3},{2,0},{3,1},{4,6},{5,7},{6,4},{7,5},{8,10},{9,11},{10,... | collective-permute-start | bytes 786440 | tf_op jit(solution)/shard_map/range/ppermute | solution.py:28
  42.3 13.3 %collective-permute-start.16 = (bf16[1024,128]{1,0:T(8,128)(2,1)S(1)}, bf16[1024,128]{1,0:T(8,128)(2,1)S(1)}, u32[]{:S(2)}, u32[]{:S(2)}) collective-permute-start(bf16[1024,128]{1,0:T(8,128)(2,1)S(1)} %get-tuple-element.27), channel_id=1, source_target_pairs={{0,2},{1,3},{2,0},{3,1},{4,6},{5,7},{6,4},{7,5},{8,10},{9,11},{10,... | collective-permute-start | bytes 786440 | tf_op jit(solution)/shard_map/range/ppermute | solution.py:28
  42.8 14.0 %collective-permute-start.13 = (bf16[1024,128]{1,0:T(8,128)(2,1)S(1)}, bf16[1024,128]{1,0:T(8,128)(2,1)S(1)}, u32[]{:S(2)}, u32[]{:S(2)}) collective-permute-start(bf16[1024,128]{1,0:T(8,128)(2,1)S(1)} %get-tuple-element.25), channel_id=1, source_target_pairs={{0,4},{1,5},{2,6},{3,7},{4,0},{5,1},{6,2},{7,3},{8,12},{9,13},{10,... | collective-permute-start | bytes 786440 | tf_op jit(solution)/shard_map/range/ppermute | solution.py:28
  49.0 8.8 %collective-permute-start.23 = (bf16[512,128]{1,0:T(8,128)(2,1)S(1)}, bf16[512,128]{1,0:T(8,128)(2,1)S(1)}, u32[]{:S(2)}, u32[]{:S(2)}) collective-permute-start(bf16[512,128]{1,0:T(8,128)(2,1)S(1)} %fusion.25), channel_id=1, source_target_pairs={{0,2},{1,3},{2,0},{3,1},{4,6},{5,7},{6,4},{7,5},{8,10},{9,11},{10,... | collective-permute-start | bytes 393224 | tf_op jit(solution)/shard_map/range/ppermute | solution.py:28
  50.3 8.8 %collective-permute-start.20 = (bf16[512,128]{1,0:T(8,128)(2,1)S(1)}, bf16[512,128]{1,0:T(8,128)(2,1)S(1)}, u32[]{:S(2)}, u32[]{:S(2)}) collective-permute-start(bf16[512,128]{1,0:T(8,128)(2,1)S(1)} %fusion.22), channel_id=1, source_target_pairs={{0,8},{1,9},{2,10},{3,11},{4,12},{5,13},{6,14},{7,15},{8,0},{9,1},... | collective-permute-start | bytes 393224 | tf_op jit(solution)/shard_map/range/ppermute | solution.py:28
  55.9 8.9 %collective-permute-start.17 = (bf16[512,128]{1,0:T(8,128)(2,1)S(1)}, bf16[512,128]{1,0:T(8,128)(2,1)S(1)}, u32[]{:S(2)}, u32[]{:S(2)}) collective-permute-start(bf16[512,128]{1,0:T(8,128)(2,1)S(1)} %fusion.19), channel_id=1, source_target_pairs={{0,4},{1,5},{2,6},{3,7},{4,0},{5,1},{6,2},{7,3},{8,12},{9,13},{10,... | collective-permute-start | bytes 393224 | tf_op jit(solution)/shard_map/range/ppermute | solution.py:28
  57.1 8.0 %collective-permute-start.14 = (bf16[512,128]{1,0:T(8,128)(2,1)S(1)}, bf16[512,128]{1,0:T(8,128)(2,1)S(1)}, u32[]{:S(2)}, u32[]{:S(2)}) collective-permute-start(bf16[512,128]{1,0:T(8,128)(2,1)S(1)} %fusion.16), channel_id=1, source_target_pairs={{0,2},{1,3},{2,0},{3,1},{4,6},{5,7},{6,4},{7,5},{8,10},{9,11},{10,... | collective-permute-start | bytes 393224 | tf_op jit(solution)/shard_map/range/ppermute | solution.py:28
  58.0 11.5 %collective-permute-start.24 = (bf16[512,128]{1,0:T(8,128)(2,1)S(1)}, bf16[512,128]{1,0:T(8,128)(2,1)S(1)}, u32[]{:S(2)}, u32[]{:S(2)}) collective-permute-start(bf16[512,128]{1,0:T(8,128)(2,1)S(1)} %get-tuple-element.53), channel_id=1, source_target_pairs={{0,8},{1,9},{2,10},{3,11},{4,12},{5,13},{6,14},{7,15},{8,0},{9,1},... | collective-permute-start | bytes 393224 | tf_op jit(solution)/shard_map/range/ppermute | solution.py:28
  59.2 10.4 %collective-permute-start.21 = (bf16[512,128]{1,0:T(8,128)(2,1)S(1)}, bf16[512,128]{1,0:T(8,128)(2,1)S(1)}, u32[]{:S(2)}, u32[]{:S(2)}) collective-permute-start(bf16[512,128]{1,0:T(8,128)(2,1)S(1)} %get-tuple-element.51), channel_id=1, source_target_pairs={{0,4},{1,5},{2,6},{3,7},{4,0},{5,1},{6,2},{7,3},{8,12},{9,13},{10,... | collective-permute-start | bytes 393224 | tf_op jit(solution)/shard_map/range/ppermute | solution.py:28
  65.0 10.5 %collective-permute-start.18 = (bf16[512,128]{1,0:T(8,128)(2,1)S(1)}, bf16[512,128]{1,0:T(8,128)(2,1)S(1)}, u32[]{:S(2)}, u32[]{:S(2)}) collective-permute-start(bf16[512,128]{1,0:T(8,128)(2,1)S(1)} %get-tuple-element.49), channel_id=1, source_target_pairs={{0,8},{1,9},{2,10},{3,11},{4,12},{5,13},{6,14},{7,15},{8,0},{9,1},... | collective-permute-start | bytes 393224 | tf_op jit(solution)/shard_map/range/ppermute | solution.py:28
  65.2 11.6 %collective-permute-start.15 = (bf16[512,128]{1,0:T(8,128)(2,1)S(1)}, bf16[512,128]{1,0:T(8,128)(2,1)S(1)}, u32[]{:S(2)}, u32[]{:S(2)}) collective-permute-start(bf16[512,128]{1,0:T(8,128)(2,1)S(1)} %get-tuple-element.47), channel_id=1, source_target_pairs={{0,8},{1,9},{2,10},{3,11},{4,12},{5,13},{6,14},{7,15},{8,0},{9,1},... | collective-permute-start | bytes 393224 | tf_op jit(solution)/shard_map/range/ppermute | solution.py:28
  78.1 3.7 %collective-permute-start.25 = (f32[128,128]{1,0:T(8,128)S(1)}, f32[128,128]{1,0:T(8,128)S(1)}, u32[]{:S(2)}, u32[]{:S(2)}) collective-permute-start(f32[128,128]{1,0:T(8,128)S(1)} %fusion.33), channel_id=1, source_target_pairs={{0,1},{1,0},{2,3},{3,2},{4,5},{5,4},{6,7},{7,6},{8,9},{9,8},{10,11... | collective-permute-start | bytes 196616 | tf_op jit(solution)/shard_map/gram/ppermute | solution.py:28
  78.2 8.7 %collective-permute-start.27 = (bf16[512,128]{1,0:T(8,128)(2,1)S(1)}, bf16[512,128]{1,0:T(8,128)(2,1)S(1)}, u32[]{:S(2)}, u32[]{:S(2)}) collective-permute-start(bf16[512,128]{1,0:T(8,128)(2,1)S(1)} %pad_maximum_fusion.11), channel_id=1, source_target_pairs={{0,2},{1,3},{2,0},{3,1},{4,6},{5,7},{6,4},{7,5},{8,10},{9,11},{10,... | collective-permute-start | bytes 393224 | tf_op jit(solution)/shard_map/gather_range/ppermute | solution.py:28
  79.8 9.8 %collective-permute-start.32 = (bf16[512,128]{1,0:T(8,128)(2,1)S(1)}, bf16[512,128]{1,0:T(8,128)(2,1)S(1)}, u32[]{:S(2)}, u32[]{:S(2)}) collective-permute-start(bf16[512,128]{1,0:T(8,128)(2,1)S(1)} %pad_maximum_fusion.12), channel_id=1, source_target_pairs={{0,4},{1,5},{2,6},{3,7},{4,0},{5,1},{6,2},{7,3},{8,12},{9,13},{10,... | collective-permute-start | bytes 393224 | tf_op jit(solution)/shard_map/gather_range/ppermute | solution.py:28
  79.9 12.0 %collective-permute-start.34 = (bf16[512,128]{1,0:T(8,128)(2,1)S(1)}, bf16[512,128]{1,0:T(8,128)(2,1)S(1)}, u32[]{:S(2)}, u32[]{:S(2)}) collective-permute-start(bf16[512,128]{1,0:T(8,128)(2,1)S(1)} %pad_maximum_fusion.13), channel_id=1, source_target_pairs={{0,8},{1,9},{2,10},{3,11},{4,12},{5,13},{6,14},{7,15},{8,0},{9,1},... | collective-permute-start | bytes 393224 | tf_op jit(solution)/shard_map/gather_range/ppermute | solution.py:28
  81.8 5.1 %collective-permute-start.26 = (f32[128,128]{1,0:T(8,128)S(1)}, f32[128,128]{1,0:T(8,128)S(1)}, u32[]{:S(2)}, u32[]{:S(2)}) collective-permute-start(f32[128,128]{1,0:T(8,128)S(1)} %add.83), channel_id=1, source_target_pairs={{0,2},{1,3},{2,0},{3,1},{4,6},{5,7},{6,4},{7,5},{8,10},{9,11},{10,... | collective-permute-start | bytes 196616 | tf_op jit(solution)/shard_map/gram/ppermute | solution.py:28
  82.7 9.3 %collective-permute-start.36 = (bf16[512,128]{1,0:T(8,128)(2,1)S(1)}, bf16[512,128]{1,0:T(8,128)(2,1)S(1)}, u32[]{:S(2)}, u32[]{:S(2)}) collective-permute-start(bf16[512,128]{1,0:T(8,128)(2,1)S(1)} %pad_maximum_fusion.14), channel_id=1, source_target_pairs={{0,2},{1,3},{2,0},{3,1},{4,6},{5,7},{6,4},{7,5},{8,10},{9,11},{10,... | collective-permute-start | bytes 393224 | tf_op jit(solution)/shard_map/gather_range/ppermute | solution.py:28
  86.9 6.7 %collective-permute-start.29 = (f32[128,128]{1,0:T(8,128)S(1)}, f32[128,128]{1,0:T(8,128)S(1)}, u32[]{:S(2)}, u32[]{:S(2)}) collective-permute-start(f32[128,128]{1,0:T(8,128)S(1)} %add.84), channel_id=1, source_target_pairs={{0,8},{1,9},{2,10},{3,11},{4,12},{5,13},{6,14},{7,15},{8,0},{9,1},... | collective-permute-start | bytes 196616 | tf_op jit(solution)/shard_map/gram/ppermute | solution.py:28
  88.0 6.8 %collective-permute-start.30 = (f32[128,128]{1,0:T(8,128)S(1)}, f32[128,128]{1,0:T(8,128)S(1)}, u32[]{:S(2)}, u32[]{:S(2)}) collective-permute-start(f32[128,128]{1,0:T(8,128)S(1)} %add.84), channel_id=1, source_target_pairs={{0,12},{1,13},{2,14},{3,15},{4,8},{5,9},{6,10},{7,11},{8,4},{9,5},... | collective-permute-start | bytes 196616 | tf_op jit(solution)/shard_map/gram/ppermute | solution.py:28
  89.6 7.8 %collective-permute-start.28 = (f32[128,128]{1,0:T(8,128)S(1)}, f32[128,128]{1,0:T(8,128)S(1)}, u32[]{:S(2)}, u32[]{:S(2)}) collective-permute-start(f32[128,128]{1,0:T(8,128)S(1)} %add.84), channel_id=1, source_target_pairs={{0,4},{1,5},{2,6},{3,7},{4,0},{5,1},{6,2},{7,3},{8,12},{9,13},{10,... | collective-permute-start | bytes 196616 | tf_op jit(solution)/shard_map/gram/ppermute | solution.py:28
  91.9 12.0 %collective-permute-start.31 = (bf16[1024,128]{1,0:T(8,128)(2,1)S(1)}, bf16[1024,128]{1,0:T(8,128)(2,1)S(1)}, u32[]{:S(2)}, u32[]{:S(2)}) collective-permute-start(bf16[1024,128]{1,0:T(8,128)(2,1)S(1)} %pad_maximum_fusion.4.refs_1_), channel_id=1, source_target_pairs={{0,4},{1,5},{2,6},{3,7},{4,0},{5,1},{6,2},{7,3},{8,12},{9,13},{10,... | collective-permute-start | bytes 786440 | tf_op jit(solution)/shard_map/gather_range/ppermute | solution.py:28
  92.0 11.9 %collective-permute-start.33 = (bf16[1024,128]{1,0:T(8,128)(2,1)S(1)}, bf16[1024,128]{1,0:T(8,128)(2,1)S(1)}, u32[]{:S(2)}, u32[]{:S(2)}) collective-permute-start(bf16[1024,128]{1,0:T(8,128)(2,1)S(1)} %pad_maximum_fusion.5.refs_2_), channel_id=1, source_target_pairs={{0,2},{1,3},{2,0},{3,1},{4,6},{5,7},{6,4},{7,5},{8,10},{9,11},{10,... | collective-permute-start | bytes 786440 | tf_op jit(solution)/shard_map/gather_range/ppermute | solution.py:28
  93.6 10.3 %collective-permute-start.35 = (bf16[1024,128]{1,0:T(8,128)(2,1)S(1)}, bf16[1024,128]{1,0:T(8,128)(2,1)S(1)}, u32[]{:S(2)}, u32[]{:S(2)}) collective-permute-start(bf16[1024,128]{1,0:T(8,128)(2,1)S(1)} %pad_maximum_fusion.6.refs_3_), channel_id=1, source_target_pairs={{0,2},{1,3},{2,0},{3,1},{4,6},{5,7},{6,4},{7,5},{8,10},{9,11},{10,... | collective-permute-start | bytes 786440 | tf_op jit(solution)/shard_map/gather_range/ppermute | solution.py:28
  94.8 10.6 %collective-permute-start.37 = (bf16[1024,128]{1,0:T(8,128)(2,1)S(1)}, bf16[1024,128]{1,0:T(8,128)(2,1)S(1)}, u32[]{:S(2)}, u32[]{:S(2)}) collective-permute-start(bf16[1024,128]{1,0:T(8,128)(2,1)S(1)} %pad_maximum_fusion.7.refs_4_), channel_id=1, source_target_pairs={{0,4},{1,5},{2,6},{3,7},{4,0},{5,1},{6,2},{7,3},{8,12},{9,13},{10,... | collective-permute-start | bytes 786440 | tf_op jit(solution)/shard_map/gather_range/ppermute | solution.py:28
  106.7 1.4 %collective-permute-start.38 = (f32[256,128]{1,0:T(8,128)S(1)}, f32[256,128]{1,0:T(8,128)S(1)}, u32[]{:S(2)}, u32[]{:S(2)}) collective-permute-start(f32[256,128]{1,0:T(8,128)S(1)} %slice.136), channel_id=1, source_target_pairs={{0,1},{1,0},{2,3},{3,2},{4,5},{5,4},{6,7},{7,6},{8,9},{9,8},{10,11... | collective-permute-start | bytes 393224 | tf_op jit(solution)/shard_map/coords/ppermute | solution.py:28
